TPU v7x, 32 devices: a whole 2x2x4 slice. The times are simulated.
32 devices in a mesh: pair: 8 (over y, x, core), vir: 4 (over z).
Axes of the slice: x: 2, y: 2, z: 4, core: 2. Of those that a mesh axis runs over, the one named last changes fastest.
Arguments:
- amplitudes: bfloat16 [2048, 2048], P('pair', 'vir'), may hold values from -6 to 6
- integrals: bfloat16 [2, 512, 128, 128], P(None, ('pair', 'vir')), may hold values from -0.0625 to 0.0625
- tile_blocks: int32 [2, 512, 2], P(None, ('pair', 'vir')), may hold values from 0 to 15
- mirror_row: int32 [2048], P('pair'), may hold values from 0 to 2047, as said below
Outputs:
- symmetric: bfloat16 [2048, 2048], P('pair', 'vir')
Inputs may be any that keep to these rules, and one draw needn't show every extreme that they name: mirror_row is an involution without fixed points; the mirrors of the rows of pair block k (rows k * 256 to (k + 1) * 256 - 1) all lie in block k XOR 1, in an arbitrary order.
All inputs are finite; a program needn't handle non-finite values.
Results may differ from a plain program's by a relative error of at most 0.015.
Values may be sent and summed in bfloat16 or wider, within the bound.
No kernel may reach another device: no remote copies, remote signals or barrier semaphores. Data moves between devices by JAX's collectives and lax.ppermute only.
A program may use at most 128 MiB of HBM per device.

v0:
```python
import math

import jax
import jax.numpy as jnp
from jax import lax
from jax.sharding import PartitionSpec as P

TILE = 128
SUB = 8


def from_partner(array, axis, apart):
    return lax.ppermute(array, axis, [(i, i ^ 1 << apart) for i in range(lax.axis_size(axis))])


def add_tiles(running, column_grid, tile_set, blocks):
    slot_count = tile_set.size // (TILE * TILE)
    block_count = column_grid.shape[1]
    group = math.gcd(slot_count, 64)
    grouped_tiles = tile_set.reshape(slot_count // group, group, TILE, TILE)
    grouped_blocks = blocks.reshape(slot_count // group, group, 2)
    block_ids = jnp.arange(block_count, dtype=jnp.int32)

    def one_group(total, item):
        tiles_now, blocks_now = item
        source_hot = (blocks_now[:, 1][:, None] == block_ids[None, :]).astype(jnp.bfloat16)
        target_hot = (blocks_now[:, 0][:, None] == block_ids[None, :]).astype(jnp.bfloat16)
        picked = jnp.einsum(
            "rnc,mn->rmc", column_grid, source_hot, preferred_element_type=jnp.float32
        ).astype(jnp.bfloat16)
        products = jnp.einsum("rmc,mca->rma", picked, tiles_now, preferred_element_type=jnp.float32)
        upper_part = products.astype(jnp.bfloat16)
        rest = products - upper_part.astype(jnp.float32)
        middle_part = rest.astype(jnp.bfloat16)
        lower_part = (rest - middle_part.astype(jnp.float32)).astype(jnp.bfloat16)
        stacked = jnp.stack([upper_part, middle_part, lower_part], axis=0)
        placed = jnp.einsum("prma,mn->rna", stacked, target_hot, preferred_element_type=jnp.float32)
        return (total + placed, None)

    running, _ = lax.scan(one_group, running, (grouped_tiles, grouped_blocks))
    return running


def swap_virtuals(rows):
    row_count = rows.shape[0]
    shaped = rows.reshape(row_count, -1, 2, SUB, SUB)
    flipped = jnp.transpose(shaped[:, :, ::-1], (0, 1, 2, 4, 3))
    return flipped.reshape(row_count, -1)


def local(amplitudes, integrals, tile_blocks, mirror_row):
    pair_rows = amplitudes.shape[0]
    gathered = lax.all_gather(amplitudes, "vir", axis=1, tiled=True)
    column_grid = gathered.reshape(pair_rows, -1, TILE)
    running = jnp.zeros(column_grid.shape, jnp.float32)
    running = add_tiles(
        running,
        column_grid,
        lax.all_gather(integrals, "pair", axis=1, tiled=True),
        lax.all_gather(tile_blocks, "pair", axis=1, tiled=True),
    )
    partial_value = running.reshape(pair_rows, -1)
    ladder = lax.psum_scatter(partial_value, "vir", scatter_dimension=1, tiled=True).astype(
        jnp.bfloat16
    )
    partner_rows = from_partner(ladder, "pair", 0)
    partner_first = (lax.axis_index("pair") ^ 1) * pair_rows
    partner = jnp.take(partner_rows, mirror_row - partner_first, axis=0)
    swapped = swap_virtuals(partner)
    return (ladder.astype(jnp.float32) + swapped.astype(jnp.float32)).astype(jnp.bfloat16)


def solution(mesh):
    in_specs = (
        P("pair", "vir"),
        P(None, ("pair", "vir"), None, None),
        P(None, ("pair", "vir"), None),
        P("pair"),
    )
    out_specs = P("pair", "vir")
    return jax.shard_map(local, mesh=mesh, in_specs=in_specs, out_specs=out_specs, check_vma=False)
```

profile of v0, /device:TPU:0, one launch (start us, length us, event | category | flops | bytes accessed | tf_op | source)
XLA Modules:
  0.0 298.5 jit_solution(9231083484077960171)
XLA Ops:
  8.8 10.7 %all_gather.9 = s32[2,128,2]{2,0,1:T(2,128)S(1)} all-gather(s32[2,16,2]{2,0,1:T(2,128)S(1)} %copy.15), channel_id=1, replica_groups=mesh['pair'=8,'vir'=4] {'pair'}, dimensions={1}, use_global_device_ids=true | all-gather | bytes 2304 | tf_op jit(solution)/shard_map/all_gather | solution.py:60
  19.7 19.9 %all-gather.5.cloned.1.call-done = bf16[256,2048]{1,0:T(8,128)(2,1)} async-done(((bf16[256,512]{1,0:T(8,128)(2,1)}), bf16[256,2048]{1,0:T(8,128)(2,1)}) %all-gather.5.cloned.1.call-update) | async-done | bytes 1048592 | tf_op jit(solution)/shard_map/all_gather | solution.py:53
  41.0 54.4 %all-gather.3.cloned.1.call-done = bf16[2,128,128,128]{3,2,1,0:T(8,128)(2,1)} async-done(((bf16[2,16,128,128]{3,2,1,0:T(8,128)(2,1)}), bf16[2,128,128,128]{3,2,1,0:T(8,128)(2,1)}) %all-gather.3.cloned.1.call-update) | async-done | bytes 8388624 | tf_op jit(solution)/shard_map/all_gather | solution.py:59
  95.4 12.0 %copy.17 = bf16[2,128,128,128]{2,3,1,0:T(8,128)(2,1)} copy(bf16[2,128,128,128]{3,2,1,0:T(8,128)(2,1)} %all-gather.3.cloned.1.call-done) | data formatting | bytes 16777216 | tf_op jit(solution)/shard_map/all_gather | solution.py:59
  107.4 131.5 %while.12 = (s32[]{:T(128)}, f32[256,16,128]{2,1,0:T(8,128)}, s32[4,64,2]{1,0,2:T(4,128)S(1)}, bf16[4,64,128,128]{2,3,1,0:T(8,128)(2,1)}, bf16[256,16,128]{2,1,0:T(8,128)(2,1)S(1)}, /*index=5*/s32[]{:T(128)}, s32[]{:T(128)}) while((s32[]{:T(128)}, f32[256,16,128]{2,1,0:T(8,128)}, s32[4,64,2]{1,0,2:T(4,128)S(1)}, ...), condition=%wide.region_2.3_spmd.clone.clone, body=%wide.region_0.2_spmd.clone.clone.sunk | while | flops 732956672 | bytes 99617944 | solution.py:40
  108.7 6.2 %fusion.34 = f32[64,128,256]{2,1,0:T(8,128)S(1)} fusion(bf16[256,64,128]{2,1,0:T(8,128)(2,1)S(1)} %convert_bitcast_fusion.3, bf16[4,64,128,128]{2,3,1,0:T(8,128)(2,1)} %get-tuple-element.159, s32[]{:T(128)} %get-tuple-element.149), kind=kOutput, calls=%fused_computation.10.clone.1 | convolution fusion | flops 536870912 | bytes 14680576 | tf_op jit(solution)/shard_map/while/body/eval_jaxpr/rmc,mca->rma/dot_general | solution.py:31
  114.9 3.7 %fusion.35 = (bf16[1,256,64,128]{1,3,2,0:T(8,128)(2,1)S(1)}, bf16[1,256,64,128]{1,3,2,0:T(8,128)(2,1)}) fusion(f32[64,128,256]{2,1,0:T(8,128)S(1)} %fusion.34), kind=kLoop, calls=%fused_computation.8.clone.1 | loop fusion | flops 14680064 | bytes 16777216 | tf_op jit(solution)/shard_map/while/body/eval_jaxpr/stack | solution.py:36
  119.2 10.1 %convert_reduce_fusion.2 = bf16[256,64,128]{0,2,1:T(8,128)(2,1)} fusion(bf16[1,256,64,128]{1,3,2,0:T(8,128)(2,1)} %get-tuple-element.139, bf16[1,256,64,128]{1,3,2,0:T(8,128)(2,1)S(1)} %get-tuple-element.140, bf16[1,256,64,128]{1,3,2,0:T(8,128)(2,1)S(1)} %fusion.36), kind=kLoop, calls=%fused_computation.2.clone.1 | loop fusion | flops 41943040 | bytes 16777216 | tf_op jit(solution)/shard_map/while/body/eval_jaxpr/prma,mn->rna/reduce_sum | solution.py:37
  129.3 6.7 %copy.32 = bf16[256,64,128]{2,1,0:T(8,128)(2,1)} copy(bf16[256,64,128]{0,2,1:T(8,128)(2,1)} %convert_reduce_fusion.2) | data formatting | bytes 8388608 | tf_op jit(solution)/shard_map/while/body/eval_jaxpr/prma,mn->rna/reduce_sum | solution.py:37
  135.9 3.0 bitcast_add_fusion.2
  141.6 6.2 %fusion.34 = f32[64,128,256]{2,1,0:T(8,128)S(1)} fusion(bf16[256,64,128]{2,1,0:T(8,128)(2,1)S(1)} %convert_bitcast_fusion.3, bf16[4,64,128,128]{2,3,1,0:T(8,128)(2,1)} %get-tuple-element.159, s32[]{:T(128)} %get-tuple-element.149), kind=kOutput, calls=%fused_computation.10.clone.1 | convolution fusion | flops 536870912 | bytes 14680576 | tf_op jit(solution)/shard_map/while/body/eval_jaxpr/rmc,mca->rma/dot_general | solution.py:31
  147.8 3.7 %fusion.35 = (bf16[1,256,64,128]{1,3,2,0:T(8,128)(2,1)S(1)}, bf16[1,256,64,128]{1,3,2,0:T(8,128)(2,1)}) fusion(f32[64,128,256]{2,1,0:T(8,128)S(1)} %fusion.34), kind=kLoop, calls=%fused_computation.8.clone.1 | loop fusion | flops 14680064 | bytes 16777216 | tf_op jit(solution)/shard_map/while/body/eval_jaxpr/stack | solution.py:36
  152.1 10.1 %convert_reduce_fusion.2 = bf16[256,64,128]{0,2,1:T(8,128)(2,1)} fusion(bf16[1,256,64,128]{1,3,2,0:T(8,128)(2,1)} %get-tuple-element.139, bf16[1,256,64,128]{1,3,2,0:T(8,128)(2,1)S(1)} %get-tuple-element.140, bf16[1,256,64,128]{1,3,2,0:T(8,128)(2,1)S(1)} %fusion.36), kind=kLoop, calls=%fused_computation.2.clone.1 | loop fusion | flops 41943040 | bytes 16777216 | tf_op jit(solution)/shard_map/while/body/eval_jaxpr/prma,mn->rna/reduce_sum | solution.py:37
  162.2 6.7 %copy.32 = bf16[256,64,128]{2,1,0:T(8,128)(2,1)} copy(bf16[256,64,128]{0,2,1:T(8,128)(2,1)} %convert_reduce_fusion.2) | data formatting | bytes 8388608 | tf_op jit(solution)/shard_map/while/body/eval_jaxpr/prma,mn->rna/reduce_sum | solution.py:37
  174.4 6.2 %fusion.34 = f32[64,128,256]{2,1,0:T(8,128)S(1)} fusion(bf16[256,64,128]{2,1,0:T(8,128)(2,1)S(1)} %convert_bitcast_fusion.3, bf16[4,64,128,128]{2,3,1,0:T(8,128)(2,1)} %get-tuple-element.159, s32[]{:T(128)} %get-tuple-element.149), kind=kOutput, calls=%fused_computation.10.clone.1 | convolution fusion | flops 536870912 | bytes 14680576 | tf_op jit(solution)/shard_map/while/body/eval_jaxpr/rmc,mca->rma/dot_general | solution.py:31
  180.6 3.7 %fusion.35 = (bf16[1,256,64,128]{1,3,2,0:T(8,128)(2,1)S(1)}, bf16[1,256,64,128]{1,3,2,0:T(8,128)(2,1)}) fusion(f32[64,128,256]{2,1,0:T(8,128)S(1)} %fusion.34), kind=kLoop, calls=%fused_computation.8.clone.1 | loop fusion | flops 14680064 | bytes 16777216 | tf_op jit(solution)/shard_map/while/body/eval_jaxpr/stack | solution.py:36
  184.9 10.1 %convert_reduce_fusion.2 = bf16[256,64,128]{0,2,1:T(8,128)(2,1)} fusion(bf16[1,256,64,128]{1,3,2,0:T(8,128)(2,1)} %get-tuple-element.139, bf16[1,256,64,128]{1,3,2,0:T(8,128)(2,1)S(1)} %get-tuple-element.140, bf16[1,256,64,128]{1,3,2,0:T(8,128)(2,1)S(1)} %fusion.36), kind=kLoop, calls=%fused_computation.2.clone.1 | loop fusion | flops 41943040 | bytes 16777216 | tf_op jit(solution)/shard_map/while/body/eval_jaxpr/prma,mn->rna/reduce_sum | solution.py:37
  195.0 6.7 %copy.32 = bf16[256,64,128]{2,1,0:T(8,128)(2,1)} copy(bf16[256,64,128]{0,2,1:T(8,128)(2,1)} %convert_reduce_fusion.2) | data formatting | bytes 8388608 | tf_op jit(solution)/shard_map/while/body/eval_jaxpr/prma,mn->rna/reduce_sum | solution.py:37
  207.3 6.2 %fusion.34 = f32[64,128,256]{2,1,0:T(8,128)S(1)} fusion(bf16[256,64,128]{2,1,0:T(8,128)(2,1)S(1)} %convert_bitcast_fusion.3, bf16[4,64,128,128]{2,3,1,0:T(8,128)(2,1)} %get-tuple-element.159, s32[]{:T(128)} %get-tuple-element.149), kind=kOutput, calls=%fused_computation.10.clone.1 | convolution fusion | flops 536870912 | bytes 14680576 | tf_op jit(solution)/shard_map/while/body/eval_jaxpr/rmc,mca->rma/dot_general | solution.py:31
  213.5 3.7 %fusion.35 = (bf16[1,256,64,128]{1,3,2,0:T(8,128)(2,1)S(1)}, bf16[1,256,64,128]{1,3,2,0:T(8,128)(2,1)}) fusion(f32[64,128,256]{2,1,0:T(8,128)S(1)} %fusion.34), kind=kLoop, calls=%fused_computation.8.clone.1 | loop fusion | flops 14680064 | bytes 16777216 | tf_op jit(solution)/shard_map/while/body/eval_jaxpr/stack | solution.py:36
  217.8 10.1 %convert_reduce_fusion.2 = bf16[256,64,128]{0,2,1:T(8,128)(2,1)} fusion(bf16[1,256,64,128]{1,3,2,0:T(8,128)(2,1)} %get-tuple-element.139, bf16[1,256,64,128]{1,3,2,0:T(8,128)(2,1)S(1)} %get-tuple-element.140, bf16[1,256,64,128]{1,3,2,0:T(8,128)(2,1)S(1)} %fusion.36), kind=kLoop, calls=%fused_computation.2.clone.1 | loop fusion | flops 41943040 | bytes 16777216 | tf_op jit(solution)/shard_map/while/body/eval_jaxpr/prma,mn->rna/reduce_sum | solution.py:37
  227.9 6.7 %copy.32 = bf16[256,64,128]{2,1,0:T(8,128)(2,1)} copy(bf16[256,64,128]{0,2,1:T(8,128)(2,1)} %convert_reduce_fusion.2) | data formatting | bytes 8388608 | tf_op jit(solution)/shard_map/while/body/eval_jaxpr/prma,mn->rna/reduce_sum | solution.py:37
  238.9 3.8 %copy.28 = f32[32,8,16,128]{3,1,2,0:T(8,128)} copy(f32[32,8,16,128]{3,2,1,0:T(8,128)} %bitcast.86) | data formatting | bytes 4194304
  242.7 44.0 %reduce-scatter.2.cloned.1.call-done = f32[256,512]{1,0:T(8,128)} async-done(((f32[256,2048]{1,0:T(8,128)}), f32[256,512]{1,0:T(8,128)}) %reduce-scatter.2.cloned.1.call-update) | async-done | bytes 524304 | tf_op jit(solution)/shard_map/reduce_scatter | solution.py:63
  (62 shorter events, 30.9 us)
Async XLA Ops:
  6.5 33.1 %all-gather.5.cloned.1.call-start = ((), (), s32[]{:S(2)}) async-start(), calls=%async_computation.2 | async-start | bytes 1310720 | tf_op jit(solution)/shard_map/all_gather | solution.py:53
  7.3 88.2 %all-gather.3.cloned.1.call-start = ((), (), s32[]{:S(2)}) async-start(), calls=%async_computation.1 | async-start | bytes 9437184 | tf_op jit(solution)/shard_map/all_gather | solution.py:59
  8.0 278.7 %reduce-scatter.2.cloned.1.call-start = ((), (), s32[]{:S(2)}) async-start(), calls=%async_computation.3 | async-start | bytes 2621440 | tf_op jit(solution)/shard_map/reduce_scatter | solution.py:63
  129.3 6.7 %copy-start = (f32[256,16,128]{2,1,0:T(8,128)S(1)}, f32[256,16,128]{2,1,0:T(8,128)}, u32[]{:S(2)}) copy-start(f32[256,16,128]{2,1,0:T(8,128)} %get-tuple-element.150) | copy-start | bytes 6291460 | tf_op jit(solution)/shard_map/while
  138.9 1.3 copy-start.1
  162.2 6.7 %copy-start = (f32[256,16,128]{2,1,0:T(8,128)S(1)}, f32[256,16,128]{2,1,0:T(8,128)}, u32[]{:S(2)}) copy-start(f32[256,16,128]{2,1,0:T(8,128)} %get-tuple-element.150) | copy-start | bytes 6291460 | tf_op jit(solution)/shard_map/while
  171.8 1.3 copy-start.1
  195.0 6.7 %copy-start = (f32[256,16,128]{2,1,0:T(8,128)S(1)}, f32[256,16,128]{2,1,0:T(8,128)}, u32[]{:S(2)}) copy-start(f32[256,16,128]{2,1,0:T(8,128)} %get-tuple-element.150) | copy-start | bytes 6291460 | tf_op jit(solution)/shard_map/while
  204.7 1.3 copy-start.1
  227.9 6.7 %copy-start = (f32[256,16,128]{2,1,0:T(8,128)S(1)}, f32[256,16,128]{2,1,0:T(8,128)}, u32[]{:S(2)}) copy-start(f32[256,16,128]{2,1,0:T(8,128)} %get-tuple-element.150) | copy-start | bytes 6291460 | tf_op jit(solution)/shard_map/while
  237.5 1.3 copy-start.1
  238.9 49.1 %copy-start.3 = (s32[256]{0:T(256)S(1)}, s32[256]{0:T(256)}, u32[]{:S(2)}) copy-start(s32[256]{0:T(256)} %param.9) | copy-start | bytes 3076
  286.7 4.5 %copy-start.2 = (f32[256,512]{1,0:T(8,128)S(1)}, f32[256,512]{1,0:T(8,128)}, u32[]{:S(2)}) copy-start(f32[256,512]{1,0:T(8,128)} %reduce-scatter.2.cloned.1.call-done) | copy-start | bytes 1572868
  287.9 1.6 collective-permute-start
Sparse Core Ops, SparseCore 0:
  8.9 30.6 all-gather.4
  41.5 53.8 all-gather.2
  242.8 43.8 reduce-scatter.1
where the time goes:
time: 300 us; the launch traced here: 299 us
  waiting for transfers between devices  121 us (40%)
  other arithmetic  59.5 us (20%)
  local copies, waits for them, and re-layouts  51.8 us (17%)
  matrix products  41.9 us (14%)
  between operations  13.2 us (4%)
  blocking collectives  10.7 us (4%)
    all_gather x1, waiting for transfers between devices, local(): lax.all_gather(integrals, 'pair', axis=1, tiled=True)  54.4 us
    reduce_scatter x1, waiting for transfers between devices, local(): lax.psum_scatter(partial_value, 'vir', scatter_dimension=1, tiled=True)  44 us
    reduce_sum x4, other arithmetic, one_group(): jnp.einsum('prma,mn->rna', stacked, target_hot, preferred_element_type=jn...  40.4 us
    reduce_sum x4, local copies, waits for them, and re-layouts, one_group(): jnp.einsum('prma,mn->rna', stacked, target_hot, preferred_element_type=jn...  26.6 us
    dot_general x4, matrix products, one_group(): jnp.einsum('rmc,mca->rma', picked, tiles_now, preferred_element_type=jnp....  24.8 us
    all_gather x1, waiting for transfers between devices, local(): gathered = lax.all_gather(amplitudes, 'vir', axis=1, tiled=True)  19.9 us
    another operation x8, other arithmetic, one_group(): stacked = jnp.stack([upper_part, middle_part, lower_part], axis=0)  17.1 us
    all_gather x1, local copies, waits for them, and re-layouts, local(): lax.all_gather(integrals, 'pair', axis=1, tiled=True)  12 us
  transfers between devices with their start and end apart: 4, of which 4 were waited for; matrix products, arithmetic and copies ran while one was open for 1% of the time, Pallas kernels for 0%

commit v1 on v0

v1 whole, which is shorter than its diff:
```python
import functools

import jax
import jax.numpy as jnp
from jax import lax
from jax.experimental import pallas as pl
from jax.experimental.pallas import tpu as pltpu
from jax.sharding import PartitionSpec as P

TILE = 128
SUB = 8
F32 = jnp.float32
BF16 = jnp.bfloat16
VMEM = pl.BlockSpec(memory_space=pltpu.VMEM)
SMEM = pl.BlockSpec(memory_space=pltpu.SMEM)


def call(body, out_shape, in_specs, scratch=(), megabytes=32, flops=0, moved=0):
    many = isinstance(out_shape, (list, tuple))
    return pl.pallas_call(
        body,
        out_shape=out_shape,
        in_specs=in_specs,
        out_specs=[VMEM] * len(out_shape) if many else VMEM,
        scratch_shapes=list(scratch),
        compiler_params=pltpu.CompilerParams(vmem_limit_bytes=megabytes << 20),
        cost_estimate=pl.CostEstimate(flops=flops, bytes_accessed=moved, transcendentals=0),
    )


def swap_matrix():
    source = lax.broadcasted_iota(jnp.int32, (TILE, TILE), 0)
    target = lax.broadcasted_iota(jnp.int32, (TILE, TILE), 1)
    h, a, b = target // (SUB * SUB), target // SUB % SUB, target % SUB
    return source == (1 - h) * SUB * SUB + b * SUB + a


def order_rows_kernel(amp_ref, mirror_ref, out_ref):
    rows = amp_ref.shape[0]
    pair = lax.axis_index("pair")
    own = lax.broadcasted_iota(jnp.int32, (1, rows), 1)
    place = jnp.where(pair % 2 == 1, mirror_ref[...] - (pair - 1) * rows, own)
    hot = (lax.broadcasted_iota(jnp.int32, (rows, rows), 0) == place).astype(BF16)
    out_ref[...] = jnp.dot(hot, amp_ref[...], preferred_element_type=F32).astype(BF16)


def add_products(grid_ref, acc_ref, tiles_ref, blocks_ref):
    count = tiles_ref.shape[0]

    @pl.loop(0, count, unroll=4)
    def _(t):
        to, come = blocks_ref[2 * t], blocks_ref[2 * t + 1]
        acc_ref[to] += jnp.dot(grid_ref[come], tiles_ref[t], preferred_element_type=F32)


def fold(acc_ref, swap, block, rows):
    upper = acc_ref[block, rows:].astype(BF16)
    return acc_ref[block, :rows] + jnp.dot(upper, swap, preferred_element_type=F32)


def first_kernel(n_vir, n_sets, *refs):
    own, other = refs[:n_vir], refs[n_vir : 2 * n_vir]
    tiles = refs[2 * n_vir : 2 * n_vir + n_sets]
    blocks = refs[2 * n_vir + n_sets : 2 * n_vir + 2 * n_sets]
    grid_ref, sum_ref, acc_ref = refs[2 * n_vir + 2 * n_sets :]
    rows, width = own[0].shape
    per = width // TILE
    core = lax.axis_index("pair") % 2
    vir = lax.axis_index("vir")
    for shift in range(n_vir):
        first = (vir + n_vir - shift) % n_vir * per
        for k in range(per):
            columns = slice(k * TILE, (k + 1) * TILE)
            grid_ref[first + k, pl.ds(pl.multiple_of(core * rows, rows), rows)] = own[shift][:, columns]
            grid_ref[first + k, pl.ds(pl.multiple_of((1 - core) * rows, rows), rows)] = other[shift][:, columns]
    acc_ref[...] = jnp.zeros_like(acc_ref)
    for tiles_ref, blocks_ref in zip(tiles, blocks):
        add_products(grid_ref, acc_ref, tiles_ref, blocks_ref)
    swap = swap_matrix().astype(BF16)

    @pl.loop(0, sum_ref.shape[0])
    def _(block):
        sum_ref[block] = fold(acc_ref, swap, block, rows)


def second_kernel(n_vir, n_sets, *refs):
    grid_ref, sum_ref = refs[:2]
    tiles, blocks = refs[2 : 2 + n_sets], refs[2 + n_sets : 2 + 2 * n_sets]
    keep_ref, send_ref, acc_ref = refs[2 + 2 * n_sets :]
    rows = sum_ref.shape[1]
    half = keep_ref.shape[1]
    core = lax.axis_index("pair") % 2
    vir = lax.axis_index("vir")
    acc_ref[...] = jnp.zeros_like(acc_ref)
    for tiles_ref, blocks_ref in zip(tiles, blocks):
        add_products(grid_ref, acc_ref, tiles_ref, blocks_ref)
    swap = swap_matrix().astype(BF16)
    for shift in range(n_vir):
        first = (vir + shift) % n_vir * 2 * half
        for k in range(half):
            block = first + core * half + k
            keep_ref[shift, k] = (sum_ref[block] + fold(acc_ref, swap, block, rows)).astype(BF16)
            block = first + (1 - core) * half + k
            send_ref[shift, k] = (sum_ref[block] + fold(acc_ref, swap, block, rows)).astype(BF16)


def join_kernel(keep_ref, come_ref, *outs):
    for shift, out_ref in enumerate(outs):
        out_ref[...] = (keep_ref[shift].astype(F32) + come_ref[shift].astype(F32)).astype(BF16)


def total_kernel(*refs):
    total = refs[0][...].astype(F32)
    for ref in refs[1:-1]:
        total += ref[...].astype(F32)
    refs[-1][...] = total.astype(BF16)


def finish_kernel(own_ref, other_ref, mirror_ref, out_ref):
    half, rows, _ = own_ref.shape
    pair = lax.axis_index("pair")
    core = pair % 2
    position = lax.broadcasted_iota(jnp.int32, (rows, 1), 0)
    place = jnp.where(core == 1, mirror_ref[...] - (pair - 1) * rows, position)
    hot = (lax.broadcasted_iota(jnp.int32, (rows, rows), 1) == place).astype(BF16)
    same = lax.broadcasted_iota(jnp.int32, (TILE, TILE), 0) == lax.broadcasted_iota(jnp.int32, (TILE, TILE), 1)
    swap = jnp.where(core == 1, swap_matrix().astype(F32), same.astype(F32)).astype(BF16)
    for which in range(2):
        for k in range(half):
            values = jnp.where(core == which, own_ref[k].astype(F32), other_ref[k].astype(F32)).astype(BF16)
            values = jnp.dot(values, swap, preferred_element_type=F32).astype(BF16)
            column = (which * half + k) * TILE
            out_ref[:, column : column + TILE] = jnp.dot(hot, values, preferred_element_type=F32).astype(BF16)


def local(amplitudes, integrals, tile_blocks, mirror_row):
    rows, width = amplitudes.shape
    slabs, tile_dev = integrals.shape[:2]
    n_pair, n_vir = lax.axis_size("pair"), lax.axis_size("vir")
    per = width // TILE
    n_blk = per * n_vir

    def across(array, bits):
        return lax.ppermute(array, "pair", [(i, i ^ bits) for i in range(n_pair)])

    def along(array, shift):
        return lax.ppermute(array, "vir", [(i, (i + shift) % n_vir) for i in range(n_vir)])

    own = [integrals[s] for s in range(slabs)]
    flat_blocks = tile_blocks.reshape(slabs, -1)
    tiles = {}
    for s in range(slabs):
        tiles[1, s] = across(own[s], 2)
        tiles[2, slabs - 1 - s] = across(own[slabs - 1 - s], 4)
    for s in range(slabs):
        tiles[3, s] = across(tiles[1, s], 4) if s % 2 == 0 else across(tiles[2, s], 2)
    chips = n_pair // 2
    done = 4
    while done < chips:
        for d in range(done):
            for s in range(slabs):
                tiles[d + done, s] = across(own[s] if d == 0 else tiles[d, s], 2 * done)
        done *= 2
    blocks = {d: across(flat_blocks, 2 * d) if d else flat_blocks for d in range(chips)}

    rows_in_order = call(
        order_rows_kernel, jax.ShapeDtypeStruct((rows, width), BF16), [VMEM, VMEM], megabytes=8
    )(amplitudes, mirror_row.reshape(1, rows))
    mine = [rows_in_order] + [along(rows_in_order, shift) for shift in range(1, n_vir)]
    others = [across(piece, 1) for piece in mine]

    early = [(d, s) for d in range(3) for s in range(slabs)]
    late = [(d, s) for d in range(3, chips) for s in range(slabs)]
    for s in range(slabs):
        tiles[0, s] = own[s]
    product_flops = 2 * tile_dev * 2 * rows * TILE * TILE
    grid, partial_sum = call(
        functools.partial(first_kernel, n_vir, len(early)),
        [
            jax.ShapeDtypeStruct((n_blk, 2 * rows, TILE), BF16),
            jax.ShapeDtypeStruct((n_blk, rows, TILE), F32),
        ],
        [VMEM] * (2 * n_vir + len(early)) + [SMEM] * len(early),
        [pltpu.VMEM((n_blk, 2 * rows, TILE), F32)],
        megabytes=40,
        flops=product_flops * len(early),
        moved=8 << 20,
    )(*mine, *others, *[tiles[key] for key in early], *[blocks[d][s] for d, s in early])
    piece = jax.ShapeDtypeStruct((n_vir, per // 2, rows, TILE), BF16)
    keep, send = call(
        functools.partial(second_kernel, n_vir, len(late)),
        [piece, piece],
        [VMEM] * (2 + len(late)) + [SMEM] * len(late),
        [pltpu.VMEM((n_blk, 2 * rows, TILE), F32)],
        megabytes=40,
        flops=product_flops * len(late),
        moved=6 << 20,
    )(grid, partial_sum, *[tiles[key] for key in late], *[blocks[d][s] for d, s in late])
    one = jax.ShapeDtypeStruct((per // 2, rows, TILE), BF16)
    parts = call(join_kernel, [one] * n_vir, [VMEM, VMEM], megabytes=8)(keep, across(send, 1))
    arrived = [parts[0]] + [along(parts[shift], shift) for shift in range(1, n_vir)]
    total = call(total_kernel, one, [VMEM] * n_vir, megabytes=8)(*arrived)
    return call(
        finish_kernel, jax.ShapeDtypeStruct((rows, width), BF16), [VMEM] * 3, megabytes=8
    )(total, across(total, 1), mirror_row.reshape(rows, 1))


def solution(mesh):
    in_specs = (
        P("pair", "vir"),
        P(None, ("pair", "vir"), None, None),
        P(None, ("pair", "vir"), None),
        P("pair"),
    )
    out_specs = P("pair", "vir")
    return jax.shard_map(local, mesh=mesh, in_specs=in_specs, out_specs=out_specs, check_vma=False)
```

time: 300 us -> 81.8 us (0.27)
  waiting for transfers between devices: 121 us -> 34 us
  other arithmetic: 59.5 us -> 0 us
  local copies, waits for them, and re-layouts: 51.8 us -> 4.32 us
  matrix products: 41.9 us -> 0 us
  starting transfers between devices: 0.15 us -> 25.6 us
  Pallas kernels: 0 us -> 17 us
  between operations: 13.2 us -> 0.14 us
  blocking collectives: 10.7 us -> 0 us
    all_gather x2 -> x0, waiting for transfers between devices: 74.3 us -> none  [the longest x1 54.4 us: local(): lax.all_gather(integrals, 'pair', axis=1, tiled=True)]
    reduce_scatter x1 -> x0, waiting for transfers between devices: 44 us -> none  [local(): lax.psum_scatter(partial_value, 'vir', scatter_dimension=1, tiled=True)]
    dot_general x12 -> x0, matrix products: 41.9 us -> none  [the longest x4 24.8 us: one_group(): jnp.einsum('rmc,mca->rma', picked, tiles_now, preferred_element_type=jnp....]
    reduce_sum x4 -> x0, other arithmetic: 40.4 us -> none  [one_group(): jnp.einsum('prma,mn->rna', stacked, target_hot, preferred_element_type=jn...]
    ppermute x1 -> x21, waiting for transfers between devices: 1.48 us -> 34 us  [the longest x6 17.7 us: along(): lax.ppermute(array, 'vir', [(i, (i + shift) % n_vir) for i in range(n_vir)])]
    reduce_sum x4 -> x0, local copies, waits for them, and re-layouts: 26.6 us -> none  [one_group(): jnp.einsum('prma,mn->rna', stacked, target_hot, preferred_element_type=jn...]
    ppermute x1 -> x21, starting transfers between devices: 0.07 us -> 25.6 us  [the longest x6 13.6 us: along(): lax.ppermute(array, 'vir', [(i, (i + shift) % n_vir) for i in range(n_vir)])]
    another operation x8 -> x0, other arithmetic: 17.1 us -> none  [one_group(): stacked = jnp.stack([upper_part, middle_part, lower_part], axis=0)]
  transfers between devices with their start and end apart: 4 -> 21, of which waited for: 4 -> 9; matrix products, arithmetic and copies ran while one was open for 1% -> 2% of each run, Pallas kernels for 0% -> 14%
where the time goes in v1:
time: 81.8 us; the launch traced here: 81 us
  waiting for transfers between devices  34 us (42%)
  starting transfers between devices  25.6 us (31%)
  Pallas kernels  17 us (21%)
  local copies, waits for them, and re-layouts  4.32 us (5%)
    ppermute x6, waiting for transfers between devices, along(): lax.ppermute(array, 'vir', [(i, (i + shift) % n_vir) for i in range(n_vir)])  17.7 us
    ppermute x15, waiting for transfers between devices, across(): return lax.ppermute(array, 'pair', [(i, i ^ bits) for i in range(n_pair)])  16.3 us
    ppermute x6, starting transfers between devices, along(): lax.ppermute(array, 'vir', [(i, (i + shift) % n_vir) for i in range(n_vir)])  13.6 us
    ppermute x15, starting transfers between devices, across(): return lax.ppermute(array, 'pair', [(i, i ^ bits) for i in range(n_pair)])  12 us
    pallas_call x1, Pallas kernels, local(): call(functools.partial(first_kernel, n_vir, len(early)), [jax.ShapeDtypeS...  11.5 us
    pallas_call x1, Pallas kernels, local(): call(functools.partial(second_kernel, n_vir, len(late)), [piece, piece],...  3.73 us
    unnamed x9, local copies, waits for them, and re-layouts  2.47 us
  transfers between devices with their start and end apart: 21, of which 9 were waited for; matrix products, arithmetic and copies ran while one was open for 2% of the time, Pallas kernels for 14%

profile of v1, /device:TPU:0, one launch (start us, length us, event | category | flops | bytes accessed | tf_op | source)
XLA Modules:
  0.0 81.0 jit_solution(8033099973779900320)
XLA Ops:
  0.0 0.8 %copy.10 = s32[2,16,2]{2,1,0:T(8,128)S(1)} copy(s32[2,16,2]{1,2,0:T(2,128)} %param.6) | data formatting | bytes 512 | tf_op args[2]
  0.9 3.0 %collective-permute-start.12 = (s32[2,32]{1,0:T(2,128)S(1)}, s32[2,32]{1,0:T(2,128)S(1)}, u32[]{:S(2)}, u32[]{:S(2)}) collective-permute-start(s32[2,32]{1,0:T(2,128)S(1)} %reshape.14), channel_id=1, source_target_pairs={{0,16},{4,20},{8,24},{12,28},{16,0},{20,4},{24,8},{28,12},{1,17},{... | collective-permute-start | bytes 776 | tf_op jit(solution)/shard_map/ppermute | solution.py:144
  4.0 0.9 %copy-done = bf16[256,512]{1,0:T(8,128)(2,1)S(1)} copy-done((bf16[256,512]{1,0:T(8,128)(2,1)S(1)}, bf16[256,512]{1,0:T(8,128)(2,1)}, u32[]{:S(2)}) %copy-start) | copy-done | bytes 262168
  5.8 1.6 %collective-permute-start = (bf16[256,512]{1,0:T(8,128)(2,1)S(1)}, bf16[256,512]{1,0:T(8,128)(2,1)S(1)}, u32[]{:S(2)}, u32[]{:S(2)}) collective-permute-start(bf16[256,512]{1,0:T(8,128)(2,1)S(1)} %shard_map.46.refs_0_), channel_id=1, source_target_pairs={{0,1},{1,2},{2,3},{3,0},{4,5},{5,6},{6,7},{7,4},{8,9},{9,10},{10,1... | collective-permute-start | bytes 786440 | tf_op jit(solution)/shard_map/ppermute | solution.py:147
  7.5 2.6 %collective-permute-start.1 = (bf16[256,512]{1,0:T(8,128)(2,1)S(1)}, bf16[256,512]{1,0:T(8,128)(2,1)S(1)}, u32[]{:S(2)}, u32[]{:S(2)}) collective-permute-start(bf16[256,512]{1,0:T(8,128)(2,1)S(1)} %shard_map.46.refs_0_), channel_id=1, source_target_pairs={{0,2},{1,3},{2,0},{3,1},{4,6},{5,7},{6,4},{7,5},{8,10},{9,11},{10,... | collective-permute-start | bytes 786440 | tf_op jit(solution)/shard_map/ppermute | solution.py:147
  10.0 1.3 %collective-permute-start.2 = (bf16[256,512]{1,0:T(8,128)(2,1)S(1)}, bf16[256,512]{1,0:T(8,128)(2,1)S(1)}, u32[]{:S(2)}, u32[]{:S(2)}) collective-permute-start(bf16[256,512]{1,0:T(8,128)(2,1)S(1)} %shard_map.46.refs_0_), channel_id=1, source_target_pairs={{0,3},{1,0},{2,1},{3,2},{4,7},{5,4},{6,5},{7,6},{8,11},{9,8},{10,9... | collective-permute-start | bytes 786440 | tf_op jit(solution)/shard_map/ppermute | solution.py:147
  11.4 1.5 %collective-permute-start.11 = (s32[2,32]{1,0:T(2,128)S(1)}, s32[2,32]{1,0:T(2,128)S(1)}, u32[]{:S(2)}, u32[]{:S(2)}) collective-permute-start(s32[2,32]{1,0:T(2,128)S(1)} %reshape.14), channel_id=1, source_target_pairs={{0,8},{4,12},{8,0},{12,4},{16,24},{20,28},{24,16},{28,20},{1,9},{5... | collective-permute-start | bytes 776 | tf_op jit(solution)/shard_map/ppermute | solution.py:144
  13.4 1.3 %slice_bitcast_fusion = (bf16[16,128,128]{2,1,0:T(8,128)(2,1)S(1)}, bf16[16,128,128]{2,1,0:T(8,128)(2,1)S(1)}) fusion(bf16[2,16,128,128]{3,2,1,0:T(8,128)(2,1)} %param.5), kind=kLoop, calls=%fused_computation | loop fusion | bytes 2097152 | tf_op jit(solution)/shard_map/squeeze | solution.py:149
  15.0 1.5 %collective-permute-start.7 = (bf16[16,128,128]{2,1,0:T(8,128)(2,1)S(1)}, bf16[16,128,128]{2,1,0:T(8,128)(2,1)S(1)}, u32[]{:S(2)}, u32[]{:S(2)}) collective-permute-start(bf16[16,128,128]{2,1,0:T(8,128)(2,1)S(1)} %get-tuple-element.22.refs_8_), channel_id=1, source_target_pairs={{0,8},{4,12},{8,0},{12,4},{16,24},{20,28},{24,16},{28,20},{1,9},{5... | collective-permute-start | bytes 1572872 | tf_op jit(solution)/shard_map/ppermute | solution.py:144
  16.4 0.9 %collective-permute-done.15 = s32[2,32]{1,0:T(2,128)S(1)} collective-permute-done((s32[2,32]{1,0:T(2,128)S(1)}, s32[2,32]{1,0:T(2,128)S(1)}, u32[]{:S(2)}, u32[]{:S(2)}) %collective-permute-start.15) | collective-permute-done | bytes 288 | tf_op jit(solution)/shard_map/ppermute | solution.py:144
  17.9 9.0 %collective-permute-done.1.refs_2_ = bf16[256,512]{1,0:T(8,128)(2,1)S(1)} collective-permute-done((bf16[256,512]{1,0:T(8,128)(2,1)S(1)}, bf16[256,512]{1,0:T(8,128)(2,1)S(1)}, u32[]{:S(2)}, u32[]{:S(2)}) %collective-permute-start.1) | collective-permute-done | bytes 262176 | tf_op jit(solution)/shard_map/ppermute | solution.py:147
  27.8 1.6 %collective-permute-start.8 = (bf16[16,128,128]{2,1,0:T(8,128)(2,1)S(1)}, bf16[16,128,128]{2,1,0:T(8,128)(2,1)S(1)}, u32[]{:S(2)}, u32[]{:S(2)}) collective-permute-start(bf16[16,128,128]{2,1,0:T(8,128)(2,1)S(1)} %get-tuple-element.21.refs_9_), channel_id=1, source_target_pairs={{0,8},{4,12},{8,0},{12,4},{16,24},{20,28},{24,16},{28,20},{1,9},{5... | collective-permute-start | bytes 1572872 | tf_op jit(solution)/shard_map/ppermute | solution.py:144
  29.8 1.6 %collective-permute-start.13 = (bf16[16,128,128]{2,1,0:T(8,128)(2,1)S(1)}, bf16[16,128,128]{2,1,0:T(8,128)(2,1)S(1)}, u32[]{:S(2)}, u32[]{:S(2)}) collective-permute-start(bf16[16,128,128]{2,1,0:T(8,128)(2,1)S(1)} %collective-permute-done.7.refs_10_), channel_id=1, source_target_pairs={{0,16},{4,20},{8,24},{12,28},{16,0},{20,4},{24,8},{28,12},{1,17},{... | collective-permute-start | bytes 1572872 | tf_op jit(solution)/shard_map/ppermute | solution.py:144
  32.2 10.4 %collective-permute-done.8.refs_11_ = bf16[16,128,128]{2,1,0:T(8,128)(2,1)S(1)} collective-permute-done((bf16[16,128,128]{2,1,0:T(8,128)(2,1)S(1)}, bf16[16,128,128]{2,1,0:T(8,128)(2,1)S(1)}, u32[]{:S(2)}, u32[]{:S(2)}) %collective-permute-start.8) | collective-permute-done | bytes 524320 | tf_op jit(solution)/shard_map/ppermute | solution.py:144
  42.6 1.5 %collective-permute-done.9.refs_12_ = bf16[16,128,128]{2,1,0:T(8,128)(2,1)S(1)} collective-permute-done((bf16[16,128,128]{2,1,0:T(8,128)(2,1)S(1)}, bf16[16,128,128]{2,1,0:T(8,128)(2,1)S(1)}, u32[]{:S(2)}, u32[]{:S(2)}) %collective-permute-start.9) | collective-permute-done | bytes 524320 | tf_op jit(solution)/shard_map/ppermute | solution.py:144
  44.1 11.5 %shard_map.47 = (bf16[16,512,128]{2,1,0:T(8,128)(2,1)S(1)}, f32[16,256,128]{2,1,0:T(8,128)S(1)}) custom-call(bf16[256,512]{1,0:T(8,128)(2,1)S(1)} %shard_map.46.refs_0_, bf16[256,512]{1,0:T(8,128)(2,1)S(1)} %collective-permute-done.refs_1_, bf16[256,512]{1,0:T(8,128)(2,1)S(1)} %collective-permute-done.1.refs_2_, ...), custom_call_target="tpu_custom_call" | custom-call | flops 1610612736 | bytes 8388608 | tf_op jit(solution)/shard_map/pallas_call | solution.py:177
  55.7 3.7 %shard_map.48 = (bf16[4,2,256,128]{3,2,1,0:T(8,128)(2,1)S(1)}, bf16[4,2,256,128]{3,2,1,0:T(8,128)(2,1)S(1)}) custom-call(bf16[16,512,128]{2,1,0:T(8,128)(2,1)S(1)} %get-tuple-element.13.refs_0_, f32[16,256,128]{2,1,0:T(8,128)S(1)} %get-tuple-element.14.refs_1_, bf16[16,128,128]{2,1,0:T(8,128)(2,1)S(1)} %collective-permute-done.13.refs_2_, ...), custom_call_target="tpu_custom_call" | custom-call | flops 536870912 | bytes 6291456 | tf_op jit(solution)/shard_map/pallas_call | solution.py:190
  59.5 1.9 %collective-permute-done.16.come_ref = bf16[4,2,256,128]{3,2,1,0:T(8,128)(2,1)S(1)} collective-permute-done((bf16[4,2,256,128]{3,2,1,0:T(8,128)(2,1)S(1)}, bf16[4,2,256,128]{3,2,1,0:T(8,128)(2,1)S(1)}, u32[]{:S(2)}, u32[]{:S(2)}) %collective-permute-start.16) | collective-permute-done | bytes 524320 | tf_op jit(solution)/shard_map/ppermute | solution.py:144
  61.5 5.6 %collective-permute-start.17 = (bf16[2,256,128]{2,1,0:T(8,128)(2,1)S(1)}, bf16[2,256,128]{2,1,0:T(8,128)(2,1)S(1)}, u32[]{:S(2)}, u32[]{:S(2)}) collective-permute-start(bf16[2,256,128]{2,1,0:T(8,128)(2,1)S(1)} %get-tuple-element.18), channel_id=1, source_target_pairs={{0,1},{1,2},{2,3},{3,0},{4,5},{5,6},{6,7},{7,4},{8,9},{9,10},{10,1... | collective-permute-start | bytes 393224 | tf_op jit(solution)/shard_map/ppermute | solution.py:147
  67.1 2.1 %collective-permute-start.18 = (bf16[2,256,128]{2,1,0:T(8,128)(2,1)S(1)}, bf16[2,256,128]{2,1,0:T(8,128)(2,1)S(1)}, u32[]{:S(2)}, u32[]{:S(2)}) collective-permute-start(bf16[2,256,128]{2,1,0:T(8,128)(2,1)S(1)} %get-tuple-element.19), channel_id=1, source_target_pairs={{0,2},{1,3},{2,0},{3,1},{4,6},{5,7},{6,4},{7,5},{8,10},{9,11},{10,... | collective-permute-start | bytes 393224 | tf_op jit(solution)/shard_map/ppermute | solution.py:147
  69.5 3.5 %collective-permute-done.17.refs_1_ = bf16[2,256,128]{2,1,0:T(8,128)(2,1)S(1)} collective-permute-done((bf16[2,256,128]{2,1,0:T(8,128)(2,1)S(1)}, bf16[2,256,128]{2,1,0:T(8,128)(2,1)S(1)}, u32[]{:S(2)}, u32[]{:S(2)}) %collective-permute-start.17) | collective-permute-done | bytes 131104 | tf_op jit(solution)/shard_map/ppermute | solution.py:147
  73.0 5.1 %collective-permute-done.18.refs_2_ = bf16[2,256,128]{2,1,0:T(8,128)(2,1)S(1)} collective-permute-done((bf16[2,256,128]{2,1,0:T(8,128)(2,1)S(1)}, bf16[2,256,128]{2,1,0:T(8,128)(2,1)S(1)}, u32[]{:S(2)}, u32[]{:S(2)}) %collective-permute-start.18) | collective-permute-done | bytes 131104 | tf_op jit(solution)/shard_map/ppermute | solution.py:147
  78.5 1.2 %collective-permute-done.20.other_ref = bf16[2,256,128]{2,1,0:T(8,128)(2,1)S(1)} collective-permute-done((bf16[2,256,128]{2,1,0:T(8,128)(2,1)S(1)}, bf16[2,256,128]{2,1,0:T(8,128)(2,1)S(1)}, u32[]{:S(2)}, u32[]{:S(2)}) %collective-permute-start.20) | collective-permute-done | bytes 131104 | tf_op jit(solution)/shard_map/ppermute | solution.py:144
  79.7 1.3 %shard_map.51 = bf16[256,512]{1,0:T(8,128)(2,1)} custom-call(bf16[2,256,128]{2,1,0:T(8,128)(2,1)S(1)} %shard_map.50.own_ref, bf16[2,256,128]{2,1,0:T(8,128)(2,1)S(1)} %collective-permute-done.20.other_ref, s32[256,1]{1,0:T(8,128)S(1)} %copy.11.mirror_ref), custom_call_target="tpu_custom_call" | custom-call | tf_op jit(solution)/shard_map/pallas_call | solution.py:203
  (44 shorter events, 5.2 us)
Async XLA Ops:
  0.0 27.4 %copy-start.3 = (s32[2,16,2]{1,2,0:T(2,128)S(1)}, s32[2,16,2]{1,2,0:T(2,128)}, u32[]{:S(2)}) copy-start(s32[2,16,2]{1,2,0:T(2,128)} %param.6) | copy-start | bytes 772
  0.9 12.0 %collective-permute-start.12 = (s32[2,32]{1,0:T(2,128)S(1)}, s32[2,32]{1,0:T(2,128)S(1)}, u32[]{:S(2)}, u32[]{:S(2)}) collective-permute-start(s32[2,32]{1,0:T(2,128)S(1)} %reshape.14), channel_id=1, source_target_pairs={{0,16},{4,20},{8,24},{12,28},{16,0},{20,4},{24,8},{28,12},{1,17},{... | collective-permute-start | bytes 776 | tf_op jit(solution)/shard_map/ppermute | solution.py:144
  4.0 0.9 %copy-start = (bf16[256,512]{1,0:T(8,128)(2,1)S(1)}, bf16[256,512]{1,0:T(8,128)(2,1)}, u32[]{:S(2)}) copy-start(bf16[256,512]{1,0:T(8,128)(2,1)} %amp_ref.1) | copy-start | bytes 786436
  5.8 12.0 %collective-permute-start = (bf16[256,512]{1,0:T(8,128)(2,1)S(1)}, bf16[256,512]{1,0:T(8,128)(2,1)S(1)}, u32[]{:S(2)}, u32[]{:S(2)}) collective-permute-start(bf16[256,512]{1,0:T(8,128)(2,1)S(1)} %shard_map.46.refs_0_), channel_id=1, source_target_pairs={{0,1},{1,2},{2,3},{3,0},{4,5},{5,6},{6,7},{7,4},{8,9},{9,10},{10,1... | collective-permute-start | bytes 786440 | tf_op jit(solution)/shard_map/ppermute | solution.py:147
  7.5 19.4 %collective-permute-start.1 = (bf16[256,512]{1,0:T(8,128)(2,1)S(1)}, bf16[256,512]{1,0:T(8,128)(2,1)S(1)}, u32[]{:S(2)}, u32[]{:S(2)}) collective-permute-start(bf16[256,512]{1,0:T(8,128)(2,1)S(1)} %shard_map.46.refs_0_), channel_id=1, source_target_pairs={{0,2},{1,3},{2,0},{3,1},{4,6},{5,7},{6,4},{7,5},{8,10},{9,11},{10,... | collective-permute-start | bytes 786440 | tf_op jit(solution)/shard_map/ppermute | solution.py:147
  10.0 16.8 %collective-permute-start.2 = (bf16[256,512]{1,0:T(8,128)(2,1)S(1)}, bf16[256,512]{1,0:T(8,128)(2,1)S(1)}, u32[]{:S(2)}, u32[]{:S(2)}) collective-permute-start(bf16[256,512]{1,0:T(8,128)(2,1)S(1)} %shard_map.46.refs_0_), channel_id=1, source_target_pairs={{0,3},{1,0},{2,1},{3,2},{4,7},{5,4},{6,5},{7,6},{8,11},{9,8},{10,9... | collective-permute-start | bytes 786440 | tf_op jit(solution)/shard_map/ppermute | solution.py:147
  11.4 3.6 %collective-permute-start.11 = (s32[2,32]{1,0:T(2,128)S(1)}, s32[2,32]{1,0:T(2,128)S(1)}, u32[]{:S(2)}, u32[]{:S(2)}) collective-permute-start(s32[2,32]{1,0:T(2,128)S(1)} %reshape.14), channel_id=1, source_target_pairs={{0,8},{4,12},{8,0},{12,4},{16,24},{20,28},{24,16},{28,20},{1,9},{5... | collective-permute-start | bytes 776 | tf_op jit(solution)/shard_map/ppermute | solution.py:144
  12.9 4.5 %collective-permute-start.15 = (s32[2,32]{1,0:T(2,128)S(1)}, s32[2,32]{1,0:T(2,128)S(1)}, u32[]{:S(2)}, u32[]{:S(2)}) collective-permute-start(s32[2,32]{1,0:T(2,128)S(1)} %reshape.14), channel_id=1, source_target_pairs={{0,24},{4,28},{8,16},{12,20},{16,8},{20,12},{24,0},{28,4},{1,25},{... | collective-permute-start | bytes 776 | tf_op jit(solution)/shard_map/ppermute | solution.py:144
  15.0 14.9 %collective-permute-start.7 = (bf16[16,128,128]{2,1,0:T(8,128)(2,1)S(1)}, bf16[16,128,128]{2,1,0:T(8,128)(2,1)S(1)}, u32[]{:S(2)}, u32[]{:S(2)}) collective-permute-start(bf16[16,128,128]{2,1,0:T(8,128)(2,1)S(1)} %get-tuple-element.22.refs_8_), channel_id=1, source_target_pairs={{0,8},{4,12},{8,0},{12,4},{16,24},{20,28},{24,16},{28,20},{1,9},{5... | collective-permute-start | bytes 1572872 | tf_op jit(solution)/shard_map/ppermute | solution.py:144
  17.4 14.1 %collective-permute-start.10 = (bf16[16,128,128]{2,1,0:T(8,128)(2,1)S(1)}, bf16[16,128,128]{2,1,0:T(8,128)(2,1)S(1)}, u32[]{:S(2)}, u32[]{:S(2)}) collective-permute-start(bf16[16,128,128]{2,1,0:T(8,128)(2,1)S(1)} %get-tuple-element.21.refs_9_), channel_id=1, source_target_pairs={{0,16},{4,20},{8,24},{12,28},{16,0},{20,4},{24,8},{28,12},{1,17},{... | collective-permute-start | bytes 1572872 | tf_op jit(solution)/shard_map/ppermute | solution.py:144
  17.9 9.9 %collective-permute-start.3 = (bf16[256,512]{1,0:T(8,128)(2,1)S(1)}, bf16[256,512]{1,0:T(8,128)(2,1)S(1)}, u32[]{:S(2)}, u32[]{:S(2)}) collective-permute-start(bf16[256,512]{1,0:T(8,128)(2,1)S(1)} %shard_map.46.refs_0_), channel_id=1, source_target_pairs={{0,4},{4,0},{8,12},{12,8},{16,20},{20,16},{24,28},{28,24},{1,5},{5... | collective-permute-start | bytes 786440 | tf_op jit(solution)/shard_map/ppermute | solution.py:144
  26.9 2.5 %collective-permute-start.4 = (bf16[256,512]{1,0:T(8,128)(2,1)S(1)}, bf16[256,512]{1,0:T(8,128)(2,1)}, u32[]{:S(2)}, u32[]{:S(2)}) collective-permute-start(bf16[256,512]{1,0:T(8,128)(2,1)S(1)} %collective-permute-done.refs_1_), channel_id=1, source_target_pairs={{0,4},{4,0},{8,12},{12,8},{16,20},{20,16},{24,28},{28,24},{1,5},{5... | collective-permute-start | bytes 786440 | tf_op jit(solution)/shard_map/ppermute | solution.py:144
  26.9 3.0 %collective-permute-start.5 = (bf16[256,512]{1,0:T(8,128)(2,1)S(1)}, bf16[256,512]{1,0:T(8,128)(2,1)}, u32[]{:S(2)}, u32[]{:S(2)}) collective-permute-start(bf16[256,512]{1,0:T(8,128)(2,1)S(1)} %collective-permute-done.1.refs_2_), channel_id=1, source_target_pairs={{0,4},{4,0},{8,12},{12,8},{16,20},{20,16},{24,28},{28,24},{1,5},{5... | collective-permute-start | bytes 786440 | tf_op jit(solution)/shard_map/ppermute | solution.py:144
  27.8 14.9 %collective-permute-start.8 = (bf16[16,128,128]{2,1,0:T(8,128)(2,1)S(1)}, bf16[16,128,128]{2,1,0:T(8,128)(2,1)S(1)}, u32[]{:S(2)}, u32[]{:S(2)}) collective-permute-start(bf16[16,128,128]{2,1,0:T(8,128)(2,1)S(1)} %get-tuple-element.21.refs_9_), channel_id=1, source_target_pairs={{0,8},{4,12},{8,0},{12,4},{16,24},{20,28},{24,16},{28,20},{1,9},{5... | collective-permute-start | bytes 1572872 | tf_op jit(solution)/shard_map/ppermute | solution.py:144
  29.3 14.8 %collective-permute-start.9 = (bf16[16,128,128]{2,1,0:T(8,128)(2,1)S(1)}, bf16[16,128,128]{2,1,0:T(8,128)(2,1)S(1)}, u32[]{:S(2)}, u32[]{:S(2)}) collective-permute-start(bf16[16,128,128]{2,1,0:T(8,128)(2,1)S(1)} %get-tuple-element.22.refs_8_), channel_id=1, source_target_pairs={{0,16},{4,20},{8,24},{12,28},{16,0},{20,4},{24,8},{28,12},{1,17},{... | collective-permute-start | bytes 1572872 | tf_op jit(solution)/shard_map/ppermute | solution.py:144
  29.8 2.3 %collective-permute-start.6 = (bf16[256,512]{1,0:T(8,128)(2,1)S(1)}, bf16[256,512]{1,0:T(8,128)(2,1)S(1)}, u32[]{:S(2)}, u32[]{:S(2)}) collective-permute-start(bf16[256,512]{1,0:T(8,128)(2,1)S(1)} %collective-permute-done.2.refs_3_), channel_id=1, source_target_pairs={{0,4},{4,0},{8,12},{12,8},{16,20},{20,16},{24,28},{28,24},{1,5},{5... | collective-permute-start | bytes 786440 | tf_op jit(solution)/shard_map/ppermute | solution.py:144
  29.8 25.8 %collective-permute-start.13 = (bf16[16,128,128]{2,1,0:T(8,128)(2,1)S(1)}, bf16[16,128,128]{2,1,0:T(8,128)(2,1)S(1)}, u32[]{:S(2)}, u32[]{:S(2)}) collective-permute-start(bf16[16,128,128]{2,1,0:T(8,128)(2,1)S(1)} %collective-permute-done.7.refs_10_), channel_id=1, source_target_pairs={{0,16},{4,20},{8,24},{12,28},{16,0},{20,4},{24,8},{28,12},{1,17},{... | collective-permute-start | bytes 1572872 | tf_op jit(solution)/shard_map/ppermute | solution.py:144
  31.4 24.2 %collective-permute-start.14 = (bf16[16,128,128]{2,1,0:T(8,128)(2,1)S(1)}, bf16[16,128,128]{2,1,0:T(8,128)(2,1)S(1)}, u32[]{:S(2)}, u32[]{:S(2)}) collective-permute-start(bf16[16,128,128]{2,1,0:T(8,128)(2,1)S(1)} %collective-permute-done.10.refs_13_), channel_id=1, source_target_pairs={{0,8},{4,12},{8,0},{12,4},{16,24},{20,28},{24,16},{28,20},{1,9},{5... | collective-permute-start | bytes 1572872 | tf_op jit(solution)/shard_map/ppermute | solution.py:144
  55.7 22.7 %copy-start.2 = (s32[256]{0:T(256)S(1)}, s32[256]{0:T(256)}, u32[]{:S(2)}) copy-start(s32[256]{0:T(256)} %param.7) | copy-start | bytes 3076
  59.4 2.0 %collective-permute-start.16 = (bf16[4,2,256,128]{3,2,1,0:T(8,128)(2,1)S(1)}, bf16[4,2,256,128]{3,2,1,0:T(8,128)(2,1)S(1)}, u32[]{:S(2)}, u32[]{:S(2)}) collective-permute-start(bf16[4,2,256,128]{3,2,1,0:T(8,128)(2,1)S(1)} %get-tuple-element.16), channel_id=1, source_target_pairs={{0,4},{4,0},{8,12},{12,8},{16,20},{20,16},{24,28},{28,24},{1,5},{5... | collective-permute-start | bytes 1572872 | tf_op jit(solution)/shard_map/ppermute | solution.py:144
  61.5 11.5 %collective-permute-start.17 = (bf16[2,256,128]{2,1,0:T(8,128)(2,1)S(1)}, bf16[2,256,128]{2,1,0:T(8,128)(2,1)S(1)}, u32[]{:S(2)}, u32[]{:S(2)}) collective-permute-start(bf16[2,256,128]{2,1,0:T(8,128)(2,1)S(1)} %get-tuple-element.18), channel_id=1, source_target_pairs={{0,1},{1,2},{2,3},{3,0},{4,5},{5,6},{6,7},{7,4},{8,9},{9,10},{10,1... | collective-permute-start | bytes 393224 | tf_op jit(solution)/shard_map/ppermute | solution.py:147
  67.1 11.1 %collective-permute-start.18 = (bf16[2,256,128]{2,1,0:T(8,128)(2,1)S(1)}, bf16[2,256,128]{2,1,0:T(8,128)(2,1)S(1)}, u32[]{:S(2)}, u32[]{:S(2)}) collective-permute-start(bf16[2,256,128]{2,1,0:T(8,128)(2,1)S(1)} %get-tuple-element.19), channel_id=1, source_target_pairs={{0,2},{1,3},{2,0},{3,1},{4,6},{5,7},{6,4},{7,5},{8,10},{9,11},{10,... | collective-permute-start | bytes 393224 | tf_op jit(solution)/shard_map/ppermute | solution.py:147
  69.2 8.9 %collective-permute-start.19 = (bf16[2,256,128]{2,1,0:T(8,128)(2,1)S(1)}, bf16[2,256,128]{2,1,0:T(8,128)(2,1)S(1)}, u32[]{:S(2)}, u32[]{:S(2)}) collective-permute-start(bf16[2,256,128]{2,1,0:T(8,128)(2,1)S(1)} %get-tuple-element.20), channel_id=1, source_target_pairs={{0,3},{1,0},{2,1},{3,2},{4,7},{5,4},{6,5},{7,6},{8,11},{9,8},{10,9... | collective-permute-start | bytes 393224 | tf_op jit(solution)/shard_map/ppermute | solution.py:147
  78.2 1.4 %collective-permute-start.20 = (bf16[2,256,128]{2,1,0:T(8,128)(2,1)S(1)}, bf16[2,256,128]{2,1,0:T(8,128)(2,1)S(1)}, u32[]{:S(2)}, u32[]{:S(2)}) collective-permute-start(bf16[2,256,128]{2,1,0:T(8,128)(2,1)S(1)} %shard_map.50.own_ref), channel_id=1, source_target_pairs={{0,4},{4,0},{8,12},{12,8},{16,20},{20,16},{24,28},{28,24},{1,5},{5... | collective-permute-start | bytes 393224 | tf_op jit(solution)/shard_map/ppermute | solution.py:144
  (1 other events, 0.7 us)

commit v2 on v1

v2 whole, which is shorter than its diff:
```python
import functools

import jax
import jax.numpy as jnp
from jax import lax
from jax.experimental import pallas as pl
from jax.experimental.pallas import tpu as pltpu
from jax.sharding import PartitionSpec as P

TILE = 128
SUB = 8
F32 = jnp.float32
BF16 = jnp.bfloat16
VMEM = pl.BlockSpec(memory_space=pltpu.VMEM)
SMEM = pl.BlockSpec(memory_space=pltpu.SMEM)


def call(body, out_shape, in_specs, scratch=(), megabytes=32, flops=0, moved=0):
    many = isinstance(out_shape, (list, tuple))
    return pl.pallas_call(
        body,
        out_shape=out_shape,
        in_specs=in_specs,
        out_specs=[VMEM] * len(out_shape) if many else VMEM,
        scratch_shapes=list(scratch),
        compiler_params=pltpu.CompilerParams(vmem_limit_bytes=megabytes << 20),
        cost_estimate=pl.CostEstimate(flops=flops, bytes_accessed=moved, transcendentals=0),
    )


def iota(shape, dimension):
    return lax.broadcasted_iota(jnp.int32, shape, dimension)


def swap_matrix():
    target = iota((TILE, TILE), 1)
    h, a, b = target // (SUB * SUB), target // SUB % SUB, target % SUB
    return iota((TILE, TILE), 0) == (1 - h) * SUB * SUB + b * SUB + a


def swap_columns(tiles_ref, swapped_ref):
    swap = swap_matrix().astype(BF16)

    @pl.loop(0, tiles_ref.shape[0], unroll=4)
    def _(t):
        swapped_ref[t] = jnp.dot(tiles_ref[t], swap, preferred_element_type=F32).astype(BF16)


def swap_kernel(*refs):
    count = len(refs) // 2
    for tiles_ref, swapped_ref in zip(refs[:count], refs[count:]):
        swap_columns(tiles_ref, swapped_ref)


def add_products(grid_ref, acc_ref, tiles_ref, swapped_ref, blocks_ref, first):
    @pl.loop(0, tiles_ref.shape[0], unroll=4)
    def _(t):
        to, come = blocks_ref[2 * (first + t)], blocks_ref[2 * (first + t) + 1]
        both = jnp.concatenate([tiles_ref[t], swapped_ref[t]], axis=0)
        acc_ref[to] += jnp.dot(grid_ref[come], both, preferred_element_type=F32)


def first_kernel(n_vir, n_sets, *refs):
    own, other = refs[:n_vir], refs[n_vir : 2 * n_vir]
    tiles = refs[2 * n_vir : 2 * n_vir + n_sets]
    swapped = refs[2 * n_vir + n_sets : 2 * n_vir + 2 * n_sets]
    blocks_ref, row_ref, column_ref, grid_ref, sum_ref = refs[2 * n_vir + 2 * n_sets :]
    rows, width = own[0].shape
    per = width // TILE
    pair = lax.axis_index("pair")
    vir = lax.axis_index("vir")
    upper = pair % 2 == 1
    base = (pair ^ 1) * rows
    wanted = jnp.where(upper, row_ref[...] - base - iota((rows, rows), 0), column_ref[...] - base - iota((rows, rows), 1))
    hot = jnp.where(wanted == 0, 1.0, 0.0).astype(BF16)
    for shift in range(n_vir):
        first = (vir ^ shift) * per
        for k in range(per):
            columns = slice(k * TILE, (k + 1) * TILE)
            mine, others = own[shift][:, columns], other[shift][:, columns]
            grid_ref[first + k, :, :TILE] = jnp.where(upper, others, mine)
            moved = jnp.dot(hot, jnp.where(upper, mine, others), preferred_element_type=F32)
            grid_ref[first + k, :, TILE:] = moved.astype(BF16)
    sum_ref[...] = jnp.zeros_like(sum_ref)
    for which in range(n_sets):
        first = which * tiles[which].shape[0]
        add_products(grid_ref, sum_ref, tiles[which], swapped[which], blocks_ref, first)


def second_kernel(n_vir, n_sets, first, *refs):
    grid_ref, sum_ref, blocks_ref = refs[:3]
    tiles = refs[3 : 3 + n_sets]
    keep_ref, send_ref, acc_ref, swapped_ref = refs[3 + n_sets :]
    half = keep_ref.shape[1]
    core = lax.axis_index("pair") % 2
    vir = lax.axis_index("vir")
    acc_ref[...] = sum_ref[...]
    for which, tiles_ref in enumerate(tiles):
        swap_columns(tiles_ref, swapped_ref)
        add_products(grid_ref, acc_ref, tiles_ref, swapped_ref, blocks_ref, first + which * tiles_ref.shape[0])
    for shift in range(n_vir):
        block = (vir ^ shift) * 2 * half
        for k in range(half):
            keep_ref[shift, k] = acc_ref[block + core * half + k].astype(BF16)
            send_ref[shift, k] = acc_ref[block + (1 - core) * half + k].astype(BF16)


def join_kernel(keep_ref, come_ref, *outs):
    for shift, out_ref in enumerate(outs):
        out_ref[...] = (keep_ref[shift].astype(F32) + come_ref[shift].astype(F32)).astype(BF16)


def total_kernel(*refs):
    total = refs[0][...].astype(F32)
    for ref in refs[1:-1]:
        total += ref[...].astype(F32)
    refs[-1][...] = total.astype(BF16)


def finish_kernel(own_ref, other_ref, column_ref, out_ref):
    half, rows, _ = own_ref.shape
    pair = lax.axis_index("pair")
    upper = pair % 2 == 1
    place = jnp.where(upper, column_ref[...] - (pair ^ 1) * rows, iota((rows, 1), 0))
    hot = (iota((rows, rows), 1) == place).astype(BF16)
    same = (iota((TILE, TILE), 0) == iota((TILE, TILE), 1)).astype(F32)
    swap = jnp.where(upper, swap_matrix().astype(F32), same).astype(BF16)
    for which in range(2):
        for k in range(half):
            values = jnp.where(upper == (which == 1), own_ref[k], other_ref[k])
            values = jnp.dot(values, swap, preferred_element_type=F32).astype(BF16)
            column = (which * half + k) * TILE
            out_ref[:, column : column + TILE] = jnp.dot(hot, values, preferred_element_type=F32).astype(BF16)


def local(amplitudes, integrals, tile_blocks, mirror_row):
    rows, width = amplitudes.shape
    slabs, tile_dev = integrals.shape[:2]
    n_pair, n_vir = lax.axis_size("pair"), lax.axis_size("vir")
    chips = n_pair // 2
    per = width // TILE
    n_blk = per * n_vir
    count = slabs * tile_dev

    def across(array, bits):
        return lax.ppermute(array, "pair", [(i, i ^ bits) for i in range(n_pair)])

    def along(array, bits):
        return lax.ppermute(array, "vir", [(i, i ^ bits) for i in range(n_vir)])

    tiles_x, tiles_y = across(integrals, 2), across(integrals, 4)
    shifts = list(range(n_vir // 2, n_vir)) + list(range(1, n_vir // 2))
    pieces = {shift: along(amplitudes, shift) for shift in shifts}
    pieces[0] = amplitudes
    late = [across(tiles_x[s], 4) if s % 2 == 0 else across(tiles_y[s], 2) for s in range(slabs)]

    blocks, _ = lax.optimization_barrier((tile_blocks.reshape(-1), pieces[1]))
    reach = 1
    while reach < chips:
        blocks = jnp.concatenate([blocks, across(blocks, 2 * reach)])
        reach *= 2
    reach = 4
    farther = [integrals, tiles_x, tiles_y, jnp.stack(late)] if reach < chips else []
    while reach < chips:
        farther += [across(array, 2 * reach) for array in farther]
        reach *= 2
    late += [array[s] for array in farther[4:] for s in range(slabs)]

    mine = [pieces[shift] for shift in range(n_vir)]
    others = [across(piece, 1) for piece in mine]
    row, column = mirror_row.reshape(1, rows), mirror_row.reshape(rows, 1)

    early = [array.reshape(count, TILE, TILE) for array in (integrals, tiles_x, tiles_y)]
    swapped = call(
        swap_kernel,
        [jax.ShapeDtypeStruct((count, TILE, TILE), BF16)] * len(early),
        [VMEM] * len(early),
        megabytes=16,
    )(*early)
    grid, partial_sum = call(
        functools.partial(first_kernel, n_vir, len(early)),
        [
            jax.ShapeDtypeStruct((n_blk, rows, 2 * TILE), BF16),
            jax.ShapeDtypeStruct((n_blk, rows, TILE), F32),
        ],
        [VMEM] * (2 * n_vir + 2 * len(early)) + [SMEM, VMEM, VMEM],
        megabytes=32,
    )(*mine, *others, *early, *swapped, blocks, row, column)
    piece = jax.ShapeDtypeStruct((n_vir, per // 2, rows, TILE), BF16)
    keep, send = call(
        functools.partial(second_kernel, n_vir, len(late), len(early) * count),
        [piece, piece],
        [VMEM, VMEM, SMEM] + [VMEM] * len(late),
        [pltpu.VMEM((n_blk, rows, TILE), F32), pltpu.VMEM((tile_dev, TILE, TILE), BF16)],
        megabytes=32,
    )(grid, partial_sum, blocks, *late)
    one = jax.ShapeDtypeStruct((per // 2, rows, TILE), BF16)
    parts = call(join_kernel, [one] * n_vir, [VMEM, VMEM], megabytes=8)(keep, across(send, 1))
    arrived = [along(parts[shift], shift) for shift in shifts]
    total = call(total_kernel, one, [VMEM] * n_vir, megabytes=8)(parts[0], *arrived)
    return call(
        finish_kernel, jax.ShapeDtypeStruct((rows, width), BF16), [VMEM] * 3, megabytes=8
    )(total, across(total, 1), column)


def solution(mesh):
    in_specs = (
        P("pair", "vir"),
        P(None, ("pair", "vir"), None, None),
        P(None, ("pair", "vir"), None),
        P("pair"),
    )
    out_specs = P("pair", "vir")
    return jax.shard_map(local, mesh=mesh, in_specs=in_specs, out_specs=out_specs, check_vma=False)
```

time: 81.8 us -> 80.4 us (0.983)
  starting transfers between devices: 25.6 us -> 19.3 us
  Pallas kernels: 17 us -> 20.4 us
  waiting for transfers between devices: 34 us -> 36.5 us
  local copies, waits for them, and re-layouts: 4.32 us -> 3.42 us
    pallas_call x3, Pallas kernels: 4.02 us -> 9.5 us  [the longest x1 5.23 us: local(): call(functools.partial(second_kernel, n_vir, len(late), len(early) * coun...]
    ppermute x6, starting transfers between devices: 13.6 us -> 8.64 us  [along(): return lax.ppermute(array, 'vir', [(i, i ^ bits) for i in range(n_vir)])]
    ppermute x15 -> x12, waiting for transfers between devices: 16.3 us -> 20 us  [across(): return lax.ppermute(array, 'pair', [(i, i ^ bits) for i in range(n_pair)])]
    pallas_call x1, Pallas kernels: 11.5 us -> 9.46 us  [local(): call(functools.partial(first_kernel, n_vir, len(early)), [jax.ShapeDtypeS...]
    ppermute x15 -> x12, starting transfers between devices: 12 us -> 10.7 us  [across(): return lax.ppermute(array, 'pair', [(i, i ^ bits) for i in range(n_pair)])]
    ppermute x6, waiting for transfers between devices: 17.7 us -> 16.6 us  [along(): return lax.ppermute(array, 'vir', [(i, i ^ bits) for i in range(n_vir)])]
    unnamed x9 -> x15, local copies, waits for them, and re-layouts: 2.47 us -> 1.5 us
    squeeze x6 -> x2, local copies, waits for them, and re-layouts: 1.46 us -> 1.68 us  [the longest x1 0.85 us: local(): tiles_x[s]]
  transfers between devices with their start and end apart: 21 -> 18, of which waited for: 9 -> 7; matrix products, arithmetic and copies ran while one was open for 2% -> 4% of each run, Pallas kernels for 14% -> 17%
where the time goes in v2:
time: 80.4 us; the launch traced here: 80 us
  waiting for transfers between devices  36.5 us (45%)
  Pallas kernels  20.4 us (25%)
  starting transfers between devices  19.3 us (24%)
  local copies, waits for them, and re-layouts  3.42 us (4%)
    ppermute x12, waiting for transfers between devices, across(): return lax.ppermute(array, 'pair', [(i, i ^ bits) for i in range(n_pair)])  20 us
    ppermute x6, waiting for transfers between devices, along(): return lax.ppermute(array, 'vir', [(i, i ^ bits) for i in range(n_vir)])  16.6 us
    ppermute x12, starting transfers between devices, across(): return lax.ppermute(array, 'pair', [(i, i ^ bits) for i in range(n_pair)])  10.7 us
    pallas_call x1, Pallas kernels, local(): call(functools.partial(first_kernel, n_vir, len(early)), [jax.ShapeDtypeS...  9.46 us
    ppermute x6, starting transfers between devices, along(): return lax.ppermute(array, 'vir', [(i, i ^ bits) for i in range(n_vir)])  8.64 us
    pallas_call x1, Pallas kernels, local(): call(functools.partial(second_kernel, n_vir, len(late), len(early) * coun...  5.23 us
    pallas_call x1, Pallas kernels, local(): call(swap_kernel, [jax.ShapeDtypeStruct((count, TILE, TILE), BF16)] * len...  4.2 us
  transfers between devices with their start and end apart: 18, of which 7 were waited for; matrix products, arithmetic and copies ran while one was open for 4% of the time, Pallas kernels for 17%

profile of v2, /device:TPU:0, one launch (start us, length us, event | category | flops | bytes accessed | tf_op | source)
XLA Modules:
  0.0 80.0 jit_solution(17293866061728313430)
XLA Ops:
  0.0 2.9 %collective-permute-start.7 = (bf16[2,16,128,128]{3,2,1,0:T(8,128)(2,1)}, bf16[2,16,128,128]{3,2,1,0:T(8,128)(2,1)S(1)}, u32[]{:S(2)}, u32[]{:S(2)}) collective-permute-start(bf16[2,16,128,128]{3,2,1,0:T(8,128)(2,1)} %param.5), channel_id=1, source_target_pairs={{0,8},{4,12},{8,0},{12,4},{16,24},{20,28},{24,16},{28,20},{1,9},{5... | collective-permute-start | bytes 3145736 | tf_op jit(solution)/shard_map/ppermute | solution.py:146
  2.9 1.5 %collective-permute-start.8 = (bf16[2,16,128,128]{3,2,1,0:T(8,128)(2,1)}, bf16[2,16,128,128]{3,2,1,0:T(8,128)(2,1)S(1)}, u32[]{:S(2)}, u32[]{:S(2)}) collective-permute-start(bf16[2,16,128,128]{3,2,1,0:T(8,128)(2,1)} %param.5), channel_id=1, source_target_pairs={{0,16},{4,20},{8,24},{12,28},{16,0},{20,4},{24,8},{28,12},{1,17},{... | collective-permute-start | bytes 3145736 | tf_op jit(solution)/shard_map/ppermute | solution.py:146
  4.5 1.6 %collective-permute-start = (bf16[256,512]{1,0:T(8,128)(2,1)}, bf16[256,512]{1,0:T(8,128)(2,1)S(1)}, u32[]{:S(2)}, u32[]{:S(2)}) collective-permute-start(bf16[256,512]{1,0:T(8,128)(2,1)} %refs_0_.1), channel_id=1, source_target_pairs={{0,1},{1,0},{2,3},{3,2},{4,5},{5,4},{6,7},{7,6},{8,9},{9,8},{10,11... | collective-permute-start | bytes 786440 | tf_op jit(solution)/shard_map/ppermute | solution.py:149
  6.0 2.6 %collective-permute-start.1 = (bf16[256,512]{1,0:T(8,128)(2,1)}, bf16[256,512]{1,0:T(8,128)(2,1)}, u32[]{:S(2)}, u32[]{:S(2)}) collective-permute-start(bf16[256,512]{1,0:T(8,128)(2,1)} %refs_0_.1), channel_id=1, source_target_pairs={{0,2},{1,3},{2,0},{3,1},{4,6},{5,7},{6,4},{7,5},{8,10},{9,11},{10,... | collective-permute-start | bytes 786440 | tf_op jit(solution)/shard_map/ppermute | solution.py:149
  8.9 0.8 copy.6
  9.7 7.0 %collective-permute-done.refs_1_ = bf16[256,512]{1,0:T(8,128)(2,1)S(1)} collective-permute-done((bf16[256,512]{1,0:T(8,128)(2,1)}, bf16[256,512]{1,0:T(8,128)(2,1)S(1)}, u32[]{:S(2)}, u32[]{:S(2)}) %collective-permute-start) | collective-permute-done | bytes 262176 | tf_op jit(solution)/shard_map/ppermute | solution.py:149
  16.7 9.6 %collective-permute-done.7 = bf16[2,16,128,128]{3,2,1,0:T(8,128)(2,1)S(1)} collective-permute-done((bf16[2,16,128,128]{3,2,1,0:T(8,128)(2,1)}, bf16[2,16,128,128]{3,2,1,0:T(8,128)(2,1)S(1)}, u32[]{:S(2)}, u32[]{:S(2)}) %collective-permute-start.7) | collective-permute-done | bytes 1048608 | tf_op jit(solution)/shard_map/ppermute | solution.py:146
  26.4 1.7 %collective-permute-start.9 = (s32[64]{0:T(128)S(1)}, s32[64]{0:T(128)S(1)}, u32[]{:S(2)}, u32[]{:S(2)}) collective-permute-start(s32[64]{0:T(128)S(1)} %reshape.21), channel_id=1, source_target_pairs={{0,8},{4,12},{8,0},{12,4},{16,24},{20,28},{24,16},{28,20},{1,9},{5... | collective-permute-start | bytes 776 | tf_op jit(solution)/shard_map/ppermute | solution.py:146
  28.1 0.9 %slice_bitcast_fusion.1 = bf16[16,128,128]{2,1,0:T(8,128)(2,1)} fusion(bf16[2,16,128,128]{3,2,1,0:T(8,128)(2,1)S(1)} %collective-permute-done.7), kind=kLoop, calls=%fused_computation.1 | loop fusion | bytes 1048576 | tf_op jit(solution)/shard_map/squeeze | solution.py:155
  28.9 1.5 %collective-permute-start.11 = (bf16[16,128,128]{2,1,0:T(8,128)(2,1)}, bf16[16,128,128]{2,1,0:T(8,128)(2,1)}, u32[]{:S(2)}, u32[]{:S(2)}) collective-permute-start(bf16[16,128,128]{2,1,0:T(8,128)(2,1)} %slice_bitcast_fusion.1), channel_id=1, source_target_pairs={{0,16},{4,20},{8,24},{12,28},{16,0},{20,4},{24,8},{28,12},{1,17},{... | collective-permute-start | bytes 1572872 | tf_op jit(solution)/shard_map/ppermute | solution.py:146
  30.4 0.8 %slice_bitcast_fusion = bf16[16,128,128]{2,1,0:T(8,128)(2,1)} fusion(bf16[2,16,128,128]{3,2,1,0:T(8,128)(2,1)S(1)} %collective-permute-done.8), kind=kLoop, calls=%fused_computation | loop fusion | bytes 1048576 | tf_op jit(solution)/shard_map/squeeze | solution.py:155
  31.9 1.3 %collective-permute-start.10 = (s32[128]{0:T(128)S(1)}, s32[128]{0:T(128)S(1)}, u32[]{:S(2)}, u32[]{:S(2)}) collective-permute-start(s32[128]{0:T(128)S(1)} %pad_add_fusion.1), channel_id=1, source_target_pairs={{0,16},{4,20},{8,24},{12,28},{16,0},{20,4},{24,8},{28,12},{1,17},{... | collective-permute-start | bytes 1544 | tf_op jit(solution)/shard_map/ppermute | solution.py:146
  33.2 0.7 copy-done.4
  34.4 7.4 %collective-permute-done.10 = s32[128]{0:T(128)S(1)} collective-permute-done((s32[128]{0:T(128)S(1)}, s32[128]{0:T(128)S(1)}, u32[]{:S(2)}, u32[]{:S(2)}) %collective-permute-start.10) | collective-permute-done | bytes 544 | tf_op jit(solution)/shard_map/ppermute | solution.py:146
  42.1 4.2 %shard_map.46 = (bf16[32,128,128]{2,1,0:T(8,128)(2,1)S(1)}, bf16[32,128,128]{2,1,0:T(8,128)(2,1)S(1)}, bf16[32,128,128]{2,1,0:T(8,128)(2,1)S(1)}) custom-call(bf16[32,128,128]{2,1,0:T(8,128)(2,1)S(1)} %bitcast.13, bf16[32,128,128]{2,1,0:T(8,128)(2,1)S(1)} %bitcast.9, bf16[32,128,128]{2,1,0:T(8,128)(2,1)S(1)} %bitcast.11), custom_call_target="tpu_custom_call" | custom-call | tf_op jit(solution)/shard_map/pallas_call | solution.py:174
  46.4 9.5 %shard_map.47 = (bf16[16,256,256]{2,1,0:T(8,128)(2,1)S(1)}, f32[16,256,128]{2,1,0:T(8,128)S(1)}) custom-call(bf16[256,512]{1,0:T(8,128)(2,1)S(1)} %copy-done.1, bf16[256,512]{1,0:T(8,128)(2,1)S(1)} %copy-done.3, bf16[256,512]{1,0:T(8,128)(2,1)} %collective-permute-done.1.refs_2_, bf16[256,512]{1,0:T(8,128)(2,1)} %collective-permute-done.2.refs_3_, ...), custom_call_target="tpu_custom_call" | custom-call | tf_op jit(solution)/shard_map/pallas_call | solution.py:180
  55.9 5.2 %shard_map.48 = (bf16[4,2,256,128]{3,2,1,0:T(8,128)(2,1)S(1)}, bf16[4,2,256,128]{3,2,1,0:T(8,128)(2,1)S(1)}) custom-call(bf16[16,256,256]{2,1,0:T(8,128)(2,1)S(1)} %get-tuple-element.21.refs_0_, f32[16,256,128]{2,1,0:T(8,128)S(1)} %get-tuple-element.22.refs_1_, s32[256]{0:T(256)S(1)} %pad_add_fusion.refs_14_.refs_2_, ...), custom_call_target="tpu_custom_call" | custom-call | tf_op jit(solution)/shard_map/pallas_call | solution.py:190
  61.7 1.5 %collective-permute-done.13.come_ref = bf16[4,2,256,128]{3,2,1,0:T(8,128)(2,1)S(1)} collective-permute-done((bf16[4,2,256,128]{3,2,1,0:T(8,128)(2,1)S(1)}, bf16[4,2,256,128]{3,2,1,0:T(8,128)(2,1)S(1)}, u32[]{:S(2)}, u32[]{:S(2)}) %collective-permute-start.13) | collective-permute-done | bytes 524320 | tf_op jit(solution)/shard_map/ppermute | solution.py:146
  63.3 2.6 %collective-permute-start.14 = (bf16[2,256,128]{2,1,0:T(8,128)(2,1)S(1)}, bf16[2,256,128]{2,1,0:T(8,128)(2,1)S(1)}, u32[]{:S(2)}, u32[]{:S(2)}) collective-permute-start(bf16[2,256,128]{2,1,0:T(8,128)(2,1)S(1)} %get-tuple-element.26), channel_id=1, source_target_pairs={{0,2},{1,3},{2,0},{3,1},{4,6},{5,7},{6,4},{7,5},{8,10},{9,11},{10,... | collective-permute-start | bytes 393224 | tf_op jit(solution)/shard_map/ppermute | solution.py:149
  65.9 1.3 %collective-permute-start.15 = (bf16[2,256,128]{2,1,0:T(8,128)(2,1)S(1)}, bf16[2,256,128]{2,1,0:T(8,128)(2,1)S(1)}, u32[]{:S(2)}, u32[]{:S(2)}) collective-permute-start(bf16[2,256,128]{2,1,0:T(8,128)(2,1)S(1)} %get-tuple-element.27), channel_id=1, source_target_pairs={{0,3},{1,2},{2,1},{3,0},{4,7},{5,6},{6,5},{7,4},{8,11},{9,10},{10,... | collective-permute-start | bytes 393224 | tf_op jit(solution)/shard_map/ppermute | solution.py:149
  67.6 8.7 %collective-permute-done.14.refs_1_ = bf16[2,256,128]{2,1,0:T(8,128)(2,1)S(1)} collective-permute-done((bf16[2,256,128]{2,1,0:T(8,128)(2,1)S(1)}, bf16[2,256,128]{2,1,0:T(8,128)(2,1)S(1)}, u32[]{:S(2)}, u32[]{:S(2)}) %collective-permute-start.14) | collective-permute-done | bytes 131104 | tf_op jit(solution)/shard_map/ppermute | solution.py:149
  76.3 0.8 %collective-permute-done.16.refs_3_ = bf16[2,256,128]{2,1,0:T(8,128)(2,1)S(1)} collective-permute-done((bf16[2,256,128]{2,1,0:T(8,128)(2,1)S(1)}, bf16[2,256,128]{2,1,0:T(8,128)(2,1)S(1)}, u32[]{:S(2)}, u32[]{:S(2)}) %collective-permute-start.16) | collective-permute-done | bytes 131104 | tf_op jit(solution)/shard_map/ppermute | solution.py:149
  77.3 1.3 %collective-permute-done.17.other_ref = bf16[2,256,128]{2,1,0:T(8,128)(2,1)S(1)} collective-permute-done((bf16[2,256,128]{2,1,0:T(8,128)(2,1)S(1)}, bf16[2,256,128]{2,1,0:T(8,128)(2,1)S(1)}, u32[]{:S(2)}, u32[]{:S(2)}) %collective-permute-start.17) | collective-permute-done | bytes 131104 | tf_op jit(solution)/shard_map/ppermute | solution.py:146
  78.6 1.3 %shard_map.51 = bf16[256,512]{1,0:T(8,128)(2,1)} custom-call(bf16[2,256,128]{2,1,0:T(8,128)(2,1)S(1)} %shard_map.50.own_ref, bf16[2,256,128]{2,1,0:T(8,128)(2,1)S(1)} %collective-permute-done.17.other_ref, s32[256,1]{1,0:T(8,128)S(1)} %copy.7.refs_16_.column_ref), custom_call_target="tpu_custom_call" | custom-call | tf_op jit(solution)/shard_map/pallas_call | solution.py:201
  (39 shorter events, 2.9 us)
Async XLA Ops:
  0.0 42.1 %copy-start = (bf16[2,16,128,128]{3,2,1,0:T(8,128)(2,1)S(1)}, bf16[2,16,128,128]{3,2,1,0:T(8,128)(2,1)}, u32[]{:S(2)}) copy-start(bf16[2,16,128,128]{3,2,1,0:T(8,128)(2,1)} %param.5) | copy-start | bytes 3145732
  0.0 41.9 %copy-start.6 = (s32[256]{0:T(256)S(1)}, s32[256]{0:T(256)}, u32[]{:S(2)}) copy-start(s32[256]{0:T(256)} %param.7) | copy-start | bytes 3076
  0.0 26.4 %collective-permute-start.7 = (bf16[2,16,128,128]{3,2,1,0:T(8,128)(2,1)}, bf16[2,16,128,128]{3,2,1,0:T(8,128)(2,1)S(1)}, u32[]{:S(2)}, u32[]{:S(2)}) collective-permute-start(bf16[2,16,128,128]{3,2,1,0:T(8,128)(2,1)} %param.5), channel_id=1, source_target_pairs={{0,8},{4,12},{8,0},{12,4},{16,24},{20,28},{24,16},{28,20},{1,9},{5... | collective-permute-start | bytes 3145736 | tf_op jit(solution)/shard_map/ppermute | solution.py:146
  2.9 26.0 %collective-permute-start.8 = (bf16[2,16,128,128]{3,2,1,0:T(8,128)(2,1)}, bf16[2,16,128,128]{3,2,1,0:T(8,128)(2,1)S(1)}, u32[]{:S(2)}, u32[]{:S(2)}) collective-permute-start(bf16[2,16,128,128]{3,2,1,0:T(8,128)(2,1)} %param.5), channel_id=1, source_target_pairs={{0,16},{4,20},{8,24},{12,28},{16,0},{20,4},{24,8},{28,12},{1,17},{... | collective-permute-start | bytes 3145736 | tf_op jit(solution)/shard_map/ppermute | solution.py:146
  4.5 12.3 %collective-permute-start = (bf16[256,512]{1,0:T(8,128)(2,1)}, bf16[256,512]{1,0:T(8,128)(2,1)S(1)}, u32[]{:S(2)}, u32[]{:S(2)}) collective-permute-start(bf16[256,512]{1,0:T(8,128)(2,1)} %refs_0_.1), channel_id=1, source_target_pairs={{0,1},{1,0},{2,3},{3,2},{4,5},{5,4},{6,7},{7,6},{8,9},{9,8},{10,11... | collective-permute-start | bytes 786440 | tf_op jit(solution)/shard_map/ppermute | solution.py:149
  6.0 25.8 %collective-permute-start.1 = (bf16[256,512]{1,0:T(8,128)(2,1)}, bf16[256,512]{1,0:T(8,128)(2,1)}, u32[]{:S(2)}, u32[]{:S(2)}) collective-permute-start(bf16[256,512]{1,0:T(8,128)(2,1)} %refs_0_.1), channel_id=1, source_target_pairs={{0,2},{1,3},{2,0},{3,1},{4,6},{5,7},{6,4},{7,5},{8,10},{9,11},{10,... | collective-permute-start | bytes 786440 | tf_op jit(solution)/shard_map/ppermute | solution.py:149
  8.6 24.6 %collective-permute-start.2 = (bf16[256,512]{1,0:T(8,128)(2,1)}, bf16[256,512]{1,0:T(8,128)(2,1)}, u32[]{:S(2)}, u32[]{:S(2)}) collective-permute-start(bf16[256,512]{1,0:T(8,128)(2,1)} %refs_0_.1), channel_id=1, source_target_pairs={{0,3},{1,2},{2,1},{3,0},{4,7},{5,6},{6,5},{7,4},{8,11},{9,10},{10,... | collective-permute-start | bytes 786440 | tf_op jit(solution)/shard_map/ppermute | solution.py:149
  16.7 11.3 %copy-start.2 = (bf16[256,512]{1,0:T(8,128)(2,1)}, bf16[256,512]{1,0:T(8,128)(2,1)S(1)}, u32[]{:S(2)}) copy-start(bf16[256,512]{1,0:T(8,128)(2,1)S(1)} %collective-permute-done.refs_1_) | copy-start | bytes 786436
  16.7 16.5 %collective-permute-start.3 = (bf16[256,512]{1,0:T(8,128)(2,1)}, bf16[256,512]{1,0:T(8,128)(2,1)S(1)}, u32[]{:S(2)}, u32[]{:S(2)}) collective-permute-start(bf16[256,512]{1,0:T(8,128)(2,1)} %refs_0_.1), channel_id=1, source_target_pairs={{0,4},{4,0},{8,12},{12,8},{16,20},{20,16},{24,28},{28,24},{1,5},{5... | collective-permute-start | bytes 786440 | tf_op jit(solution)/shard_map/ppermute | solution.py:146
  26.4 4.9 %collective-permute-start.9 = (s32[64]{0:T(128)S(1)}, s32[64]{0:T(128)S(1)}, u32[]{:S(2)}, u32[]{:S(2)}) collective-permute-start(s32[64]{0:T(128)S(1)} %reshape.21), channel_id=1, source_target_pairs={{0,8},{4,12},{8,0},{12,4},{16,24},{20,28},{24,16},{28,20},{1,9},{5... | collective-permute-start | bytes 776 | tf_op jit(solution)/shard_map/ppermute | solution.py:146
  28.9 17.4 %copy-start.1 = (bf16[256,512]{1,0:T(8,128)(2,1)S(1)}, bf16[256,512]{1,0:T(8,128)(2,1)}, u32[]{:S(2)}) copy-start(bf16[256,512]{1,0:T(8,128)(2,1)} %refs_0_.1) | copy-start | bytes 786436
  28.9 26.9 %collective-permute-start.11 = (bf16[16,128,128]{2,1,0:T(8,128)(2,1)}, bf16[16,128,128]{2,1,0:T(8,128)(2,1)}, u32[]{:S(2)}, u32[]{:S(2)}) collective-permute-start(bf16[16,128,128]{2,1,0:T(8,128)(2,1)} %slice_bitcast_fusion.1), channel_id=1, source_target_pairs={{0,16},{4,20},{8,24},{12,28},{16,0},{20,4},{24,8},{28,12},{1,17},{... | collective-permute-start | bytes 1572872 | tf_op jit(solution)/shard_map/ppermute | solution.py:146
  31.3 24.6 %collective-permute-start.12 = (bf16[16,128,128]{2,1,0:T(8,128)(2,1)}, bf16[16,128,128]{2,1,0:T(8,128)(2,1)}, u32[]{:S(2)}, u32[]{:S(2)}) collective-permute-start(bf16[16,128,128]{2,1,0:T(8,128)(2,1)} %slice_bitcast_fusion), channel_id=1, source_target_pairs={{0,8},{4,12},{8,0},{12,4},{16,24},{20,28},{24,16},{28,20},{1,9},{5... | collective-permute-start | bytes 1572872 | tf_op jit(solution)/shard_map/ppermute | solution.py:146
  31.9 10.0 %collective-permute-start.10 = (s32[128]{0:T(128)S(1)}, s32[128]{0:T(128)S(1)}, u32[]{:S(2)}, u32[]{:S(2)}) collective-permute-start(s32[128]{0:T(128)S(1)} %pad_add_fusion.1), channel_id=1, source_target_pairs={{0,16},{4,20},{8,24},{12,28},{16,0},{20,4},{24,8},{28,12},{1,17},{... | collective-permute-start | bytes 1544 | tf_op jit(solution)/shard_map/ppermute | solution.py:146
  33.2 13.1 %collective-permute-start.4 = (bf16[256,512]{1,0:T(8,128)(2,1)}, bf16[256,512]{1,0:T(8,128)(2,1)}, u32[]{:S(2)}, u32[]{:S(2)}) collective-permute-start(bf16[256,512]{1,0:T(8,128)(2,1)} %copy-done.2), channel_id=1, source_target_pairs={{0,4},{4,0},{8,12},{12,8},{16,20},{20,16},{24,28},{28,24},{1,5},{5... | collective-permute-start | bytes 786440 | tf_op jit(solution)/shard_map/ppermute | solution.py:146
  33.9 12.4 %collective-permute-start.5 = (bf16[256,512]{1,0:T(8,128)(2,1)}, bf16[256,512]{1,0:T(8,128)(2,1)}, u32[]{:S(2)}, u32[]{:S(2)}) collective-permute-start(bf16[256,512]{1,0:T(8,128)(2,1)} %collective-permute-done.1.refs_2_), channel_id=1, source_target_pairs={{0,4},{4,0},{8,12},{12,8},{16,20},{20,16},{24,28},{28,24},{1,5},{5... | collective-permute-start | bytes 786440 | tf_op jit(solution)/shard_map/ppermute | solution.py:146
  41.9 4.5 %collective-permute-start.6 = (bf16[256,512]{1,0:T(8,128)(2,1)}, bf16[256,512]{1,0:T(8,128)(2,1)}, u32[]{:S(2)}, u32[]{:S(2)}) collective-permute-start(bf16[256,512]{1,0:T(8,128)(2,1)} %collective-permute-done.2.refs_3_), channel_id=1, source_target_pairs={{0,4},{4,0},{8,12},{12,8},{16,20},{20,16},{24,28},{28,24},{1,5},{5... | collective-permute-start | bytes 786440 | tf_op jit(solution)/shard_map/ppermute | solution.py:146
  42.0 4.4 %copy-start.3 = (bf16[256,512]{1,0:T(8,128)(2,1)S(1)}, bf16[256,512]{1,0:T(8,128)(2,1)}, u32[]{:S(2)}) copy-start(bf16[256,512]{1,0:T(8,128)(2,1)} %copy-done.2) | copy-start | bytes 786436
  42.0 4.4 %copy-start.5 = (bf16[256,512]{1,0:T(8,128)(2,1)S(1)}, bf16[256,512]{1,0:T(8,128)(2,1)}, u32[]{:S(2)}) copy-start(bf16[256,512]{1,0:T(8,128)(2,1)} %copy-done.4) | copy-start | bytes 786436
  61.1 2.1 %collective-permute-start.13 = (bf16[4,2,256,128]{3,2,1,0:T(8,128)(2,1)S(1)}, bf16[4,2,256,128]{3,2,1,0:T(8,128)(2,1)S(1)}, u32[]{:S(2)}, u32[]{:S(2)}) collective-permute-start(bf16[4,2,256,128]{3,2,1,0:T(8,128)(2,1)S(1)} %get-tuple-element.24), channel_id=1, source_target_pairs={{0,4},{4,0},{8,12},{12,8},{16,20},{20,16},{24,28},{28,24},{1,5},{5... | collective-permute-start | bytes 1572872 | tf_op jit(solution)/shard_map/ppermute | solution.py:146
  63.3 13.0 %collective-permute-start.14 = (bf16[2,256,128]{2,1,0:T(8,128)(2,1)S(1)}, bf16[2,256,128]{2,1,0:T(8,128)(2,1)S(1)}, u32[]{:S(2)}, u32[]{:S(2)}) collective-permute-start(bf16[2,256,128]{2,1,0:T(8,128)(2,1)S(1)} %get-tuple-element.26), channel_id=1, source_target_pairs={{0,2},{1,3},{2,0},{3,1},{4,6},{5,7},{6,4},{7,5},{8,10},{9,11},{10,... | collective-permute-start | bytes 393224 | tf_op jit(solution)/shard_map/ppermute | solution.py:149
  65.9 10.4 %collective-permute-start.15 = (bf16[2,256,128]{2,1,0:T(8,128)(2,1)S(1)}, bf16[2,256,128]{2,1,0:T(8,128)(2,1)S(1)}, u32[]{:S(2)}, u32[]{:S(2)}) collective-permute-start(bf16[2,256,128]{2,1,0:T(8,128)(2,1)S(1)} %get-tuple-element.27), channel_id=1, source_target_pairs={{0,3},{1,2},{2,1},{3,0},{4,7},{5,6},{6,5},{7,4},{8,11},{9,10},{10,... | collective-permute-start | bytes 393224 | tf_op jit(solution)/shard_map/ppermute | solution.py:149
  67.3 9.9 %collective-permute-start.16 = (bf16[2,256,128]{2,1,0:T(8,128)(2,1)S(1)}, bf16[2,256,128]{2,1,0:T(8,128)(2,1)S(1)}, u32[]{:S(2)}, u32[]{:S(2)}) collective-permute-start(bf16[2,256,128]{2,1,0:T(8,128)(2,1)S(1)} %get-tuple-element.28), channel_id=1, source_target_pairs={{0,1},{1,0},{2,3},{3,2},{4,5},{5,4},{6,7},{7,6},{8,9},{9,8},{10,11... | collective-permute-start | bytes 393224 | tf_op jit(solution)/shard_map/ppermute | solution.py:149
  77.2 1.4 %collective-permute-start.17 = (bf16[2,256,128]{2,1,0:T(8,128)(2,1)S(1)}, bf16[2,256,128]{2,1,0:T(8,128)(2,1)S(1)}, u32[]{:S(2)}, u32[]{:S(2)}) collective-permute-start(bf16[2,256,128]{2,1,0:T(8,128)(2,1)S(1)} %shard_map.50.own_ref), channel_id=1, source_target_pairs={{0,4},{4,0},{8,12},{12,8},{16,20},{20,16},{24,28},{28,24},{1,5},{5... | collective-permute-start | bytes 393224 | tf_op jit(solution)/shard_map/ppermute | solution.py:146
  (1 other events, 0.7 us)

commit v3 on v2

v3 whole, which is shorter than its diff:
```python
import functools

import jax
import jax.numpy as jnp
from jax import lax
from jax.experimental import pallas as pl
from jax.experimental.pallas import tpu as pltpu
from jax.sharding import PartitionSpec as P

TILE = 128
SUB = 8
EXTRA = 16
F32 = jnp.float32
BF16 = jnp.bfloat16
VMEM = pl.BlockSpec(memory_space=pltpu.VMEM)
SMEM = pl.BlockSpec(memory_space=pltpu.SMEM)


def call(body, out_shape, in_specs, scratch=(), megabytes=32, aliases=None):
    many = isinstance(out_shape, (list, tuple))
    return pl.pallas_call(
        body,
        out_shape=out_shape,
        in_specs=in_specs,
        out_specs=[VMEM] * len(out_shape) if many else VMEM,
        scratch_shapes=list(scratch),
        compiler_params=pltpu.CompilerParams(vmem_limit_bytes=megabytes << 20),
        input_output_aliases=aliases or {},
        cost_estimate=pl.CostEstimate(flops=0, bytes_accessed=0, transcendentals=0),
    )


def iota(shape, dimension):
    return lax.broadcasted_iota(jnp.int32, shape, dimension)


def swap_matrix():
    target = iota((TILE, TILE), 1)
    h, a, b = target // (SUB * SUB), target // SUB % SUB, target % SUB
    return iota((TILE, TILE), 0) == (1 - h) * SUB * SUB + b * SUB + a


def pack_kernel(integrals_ref, blocks_ref, *refs):
    outs, sems = refs[:-1], refs[-1]
    length = integrals_ref.shape[1]
    copies = [
        pltpu.make_async_copy(integrals_ref.at[s], out_ref.at[pl.ds(0, length)], sems.at[s])
        for s, out_ref in enumerate(outs)
    ]
    for copy in copies:
        copy.start()
    lane = iota((EXTRA, TILE), 1)
    for s, out_ref in enumerate(outs):
        ids = jnp.zeros((EXTRA, TILE), jnp.int32)
        for t in range(length // TILE):
            for which in range(2):
                ids = jnp.where(lane == 2 * t + which, blocks_ref[s, which, t], ids)
        out_ref[length:, :] = ids.astype(F32).astype(BF16)
    for copy in copies:
        copy.wait()


def add_products(grid_ref, acc_refs, tiles_ref, blocks_ref):
    empty = jnp.zeros((TILE, TILE), BF16)

    @pl.loop(0, blocks_ref.shape[0] // 4, unroll=4)
    def _(t):
        to = [blocks_ref[4 * t + 2 * k] for k in range(2)]
        come = [blocks_ref[4 * t + 2 * k + 1] for k in range(2)]
        tiles = [tiles_ref[pl.ds(pl.multiple_of((2 * t + k) * TILE, TILE), TILE), :] for k in range(2)]
        left = jnp.concatenate([grid_ref[come[0]], grid_ref[come[1]]], axis=1)
        right = jnp.concatenate(
            [jnp.concatenate([tiles[0], empty], axis=1), jnp.concatenate([empty, tiles[1]], axis=1)], axis=0
        )
        products = jnp.dot(left, right, preferred_element_type=F32)
        for k in range(2):
            acc_refs[k][to[k]] += products[:, k * TILE : (k + 1) * TILE]


def first_kernel(n_vir, n_sets, *refs):
    own, other = refs[:n_vir], refs[n_vir : 2 * n_vir]
    tiles = refs[2 * n_vir : 2 * n_vir + n_sets]
    blocks = refs[2 * n_vir + n_sets : 2 * n_vir + 2 * n_sets]
    row_ref, column_ref, grid_ref, *acc_refs = refs[2 * n_vir + 2 * n_sets :]
    rows, width = own[0].shape
    per = width // TILE
    pair = lax.axis_index("pair")
    vir = lax.axis_index("vir")
    upper = pair % 2 == 1
    base = (pair ^ 1) * rows
    wanted = jnp.where(upper, row_ref[...] - base - iota((rows, rows), 0), column_ref[...] - base - iota((rows, rows), 1))
    hot = jnp.where(wanted == 0, 1.0, 0.0).astype(BF16)
    for shift in range(n_vir):
        first = (vir ^ shift) * per
        mine, others = own[shift][...], other[shift][...]
        kept = jnp.where(upper, others, mine)
        moved = jnp.dot(hot, jnp.where(upper, mine, others), preferred_element_type=F32).astype(BF16)
        for k in range(per):
            columns = slice(k * TILE, (k + 1) * TILE)
            grid_ref[first + k, :rows] = kept[:, columns]
            grid_ref[first + k, rows:] = moved[:, columns]
    for acc_ref in acc_refs:
        acc_ref[...] = jnp.zeros_like(acc_ref)
    for tiles_ref, blocks_ref in zip(tiles, blocks):
        add_products(grid_ref, acc_refs, tiles_ref, blocks_ref)


def second_kernel(n_vir, n_sets, *refs):
    grid_ref = refs[0]
    tiles, blocks = refs[3 : 3 + n_sets], refs[3 + n_sets : 3 + 2 * n_sets]
    keep_ref, send_ref, *acc_refs = refs[3 + 2 * n_sets :]
    half, rows = keep_ref.shape[1:3]
    core = lax.axis_index("pair") % 2
    vir = lax.axis_index("vir")
    for tiles_ref, blocks_ref in zip(tiles, blocks):
        add_products(grid_ref, acc_refs, tiles_ref, blocks_ref)
    swap = swap_matrix().astype(BF16)
    for shift in range(n_vir):
        for k in range(half):
            for out_ref, side in ((keep_ref, core), (send_ref, 1 - core)):
                block = ((vir ^ shift) * 2 + side) * half + k
                lower = acc_refs[0][block, :rows] + acc_refs[1][block, :rows]
                upper = (acc_refs[0][block, rows:] + acc_refs[1][block, rows:]).astype(BF16)
                out_ref[shift, k] = (lower + jnp.dot(upper, swap, preferred_element_type=F32)).astype(BF16)


def join_kernel(keep_ref, come_ref, *outs):
    for shift, out_ref in enumerate(outs):
        out_ref[...] = (keep_ref[shift].astype(F32) + come_ref[shift].astype(F32)).astype(BF16)


def total_kernel(*refs):
    total = refs[0][...].astype(F32)
    for ref in refs[1:-1]:
        total += ref[...].astype(F32)
    refs[-1][...] = total.astype(BF16)


def finish_kernel(own_ref, other_ref, column_ref, out_ref):
    half, rows, _ = own_ref.shape
    pair = lax.axis_index("pair")
    upper = pair % 2 == 1
    place = jnp.where(upper, column_ref[...] - (pair ^ 1) * rows, iota((rows, 1), 0))
    hot = (iota((rows, rows), 1) == place).astype(BF16)
    same = (iota((TILE, TILE), 0) == iota((TILE, TILE), 1)).astype(F32)
    swap = jnp.where(upper, swap_matrix().astype(F32), same).astype(BF16)
    for which in range(2):
        for k in range(half):
            values = jnp.where(upper == (which == 1), own_ref[k], other_ref[k])
            values = jnp.dot(values, swap, preferred_element_type=F32).astype(BF16)
            column = (which * half + k) * TILE
            out_ref[:, column : column + TILE] = jnp.dot(hot, values, preferred_element_type=F32).astype(BF16)


def local(amplitudes, integrals, tile_blocks, mirror_row):
    rows, width = amplitudes.shape
    slabs, tile_dev = integrals.shape[:2]
    n_pair, n_vir = lax.axis_size("pair"), lax.axis_size("vir")
    chips = n_pair // 2
    per = width // TILE
    n_blk = per * n_vir
    length = tile_dev * TILE

    def across(array, bits):
        return lax.ppermute(array, "pair", [(i, i ^ bits) for i in range(n_pair)])

    def along(array, bits):
        return lax.ppermute(array, "vir", [(i, i ^ bits) for i in range(n_vir)])

    packed = call(
        pack_kernel,
        [jax.ShapeDtypeStruct((length + EXTRA, TILE), BF16)] * slabs,
        [pl.BlockSpec(memory_space=pl.ANY), SMEM],
        [pltpu.SemaphoreType.DMA((slabs,))],
        megabytes=8,
    )(integrals.reshape(slabs, length, TILE), tile_blocks.transpose(0, 2, 1))
    tiles = {(0, s): packed[s] for s in range(slabs)}
    for s in range(slabs):
        tiles[1, s] = across(packed[s], 2)
        tiles[2, slabs - 1 - s] = across(packed[slabs - 1 - s], 4)
    for s in range(slabs):
        tiles[3, s] = across(tiles[1, s], 4) if s % 2 == 0 else across(tiles[2, s], 2)
    reach = 4
    while reach < chips:
        tiles |= {(d + reach, s): across(tiles[d, s], 2 * reach) for d in range(reach) for s in range(slabs)}
        reach *= 2

    pieces = {0: amplitudes}
    reach = 1
    while reach < n_vir:
        pieces |= {shift + reach: along(pieces[shift], reach) for shift in range(reach)}
        reach *= 2
    mine = [pieces[shift] for shift in range(n_vir)]
    others = [across(piece, 1) for piece in mine]
    row, column = mirror_row.reshape(1, rows), mirror_row.reshape(rows, 1)

    def ids(key):
        return tiles[key][length, : 2 * tile_dev].astype(jnp.int32)

    early = [(d, s) for d in range(3) for s in range(slabs)]
    late = [(d, s) for d in range(3, chips) for s in range(slabs)]
    sums = jax.ShapeDtypeStruct((n_blk, 2 * rows, TILE), F32)
    grid, *sums_so_far = call(
        functools.partial(first_kernel, n_vir, len(early)),
        [jax.ShapeDtypeStruct((n_blk, 2 * rows, TILE), BF16), sums, sums],
        [VMEM] * (2 * n_vir + len(early)) + [SMEM] * len(early) + [VMEM, VMEM],
        megabytes=32,
    )(*mine, *others, *[tiles[key] for key in early], *[ids(key) for key in early], row, column)
    piece = jax.ShapeDtypeStruct((n_vir, per // 2, rows, TILE), BF16)
    keep, send, *_ = call(
        functools.partial(second_kernel, n_vir, len(late)),
        [piece, piece, sums, sums],
        [VMEM] * (3 + len(late)) + [SMEM] * len(late),
        megabytes=32,
        aliases={1: 2, 2: 3},
    )(grid, *sums_so_far, *[tiles[key] for key in late], *[ids(key) for key in late])
    one = jax.ShapeDtypeStruct((per // 2, rows, TILE), BF16)
    parts = call(join_kernel, [one] * n_vir, [VMEM, VMEM], megabytes=8)(keep, across(send, 1))
    arrived = [along(parts[shift], shift) for shift in range(n_vir - 1, 0, -1)]
    total = call(total_kernel, one, [VMEM] * n_vir, megabytes=8)(parts[0], *arrived)
    return call(
        finish_kernel, jax.ShapeDtypeStruct((rows, width), BF16), [VMEM] * 3, megabytes=8
    )(total, across(total, 1), column)


def solution(mesh):
    in_specs = (
        P("pair", "vir"),
        P(None, ("pair", "vir"), None, None),
        P(None, ("pair", "vir"), None),
        P("pair"),
    )
    out_specs = P("pair", "vir")
    return jax.shard_map(local, mesh=mesh, in_specs=in_specs, out_specs=out_specs, check_vma=False)
```

time: 80.4 us -> 73.2 us (0.910)
  Pallas kernels: 20.4 us -> 13.9 us
  local copies, waits for them, and re-layouts: 3.42 us -> 4.33 us
  starting transfers between devices: 19.3 us -> 18.4 us
    ppermute x12, waiting for transfers between devices: 20 us -> 6.46 us  [across(): return lax.ppermute(array, 'pair', [(i, i ^ bits) for i in range(n_pair)])]
    ppermute x6, waiting for transfers between devices: 16.6 us -> 29.8 us  [along(): return lax.ppermute(array, 'vir', [(i, i ^ bits) for i in range(n_vir)])]
    pallas_call x2, Pallas kernels: 9.43 us -> 3.96 us  [the longest x1 3.27 us: local(): call(functools.partial(second_kernel, n_vir, len(late)), [piece, piece, s...]
    unnamed x15 -> x8, local copies, waits for them, and re-layouts: 1.5 us -> 3.53 us
    squeeze x2 -> x0, local copies, waits for them, and re-layouts: 1.68 us -> none  [the longest x1 0.85 us: local(): tiles_x[s]]
    ppermute x12, starting transfers between devices: 10.7 us -> 9.21 us  [across(): return lax.ppermute(array, 'pair', [(i, i ^ bits) for i in range(n_pair)])]
    pallas_call x1, Pallas kernels: 9.46 us -> 8.43 us  [local(): call(functools.partial(first_kernel, n_vir, len(early)), [jax.ShapeDtypeS...]
  transfers between devices with their start and end apart: 18 -> 18, of which waited for: 7 -> 9; matrix products, arithmetic and copies ran while one was open for 4% -> 1% of each run, Pallas kernels for 17% -> 12%
where the time goes in v3:
time: 73.2 us; the launch traced here: 73 us
  waiting for transfers between devices  36.2 us (49%)
  starting transfers between devices  18.4 us (25%)
  Pallas kernels  13.9 us (19%)
  local copies, waits for them, and re-layouts  4.33 us (6%)
    ppermute x6, waiting for transfers between devices, along(): return lax.ppermute(array, 'vir', [(i, i ^ bits) for i in range(n_vir)])  29.8 us
    ppermute x12, starting transfers between devices, across(): return lax.ppermute(array, 'pair', [(i, i ^ bits) for i in range(n_pair)])  9.21 us
    ppermute x6, starting transfers between devices, along(): return lax.ppermute(array, 'vir', [(i, i ^ bits) for i in range(n_vir)])  9.16 us
    pallas_call x1, Pallas kernels, local(): call(functools.partial(first_kernel, n_vir, len(early)), [jax.ShapeDtypeS...  8.43 us
    ppermute x12, waiting for transfers between devices, across(): return lax.ppermute(array, 'pair', [(i, i ^ bits) for i in range(n_pair)])  6.46 us
    unnamed x8, local copies, waits for them, and re-layouts  3.53 us
    pallas_call x1, Pallas kernels, local(): call(functools.partial(second_kernel, n_vir, len(late)), [piece, piece, s...  3.27 us
  transfers between devices with their start and end apart: 18, of which 9 were waited for; matrix products, arithmetic and copies ran while one was open for 1% of the time, Pallas kernels for 12%

profile of v3, /device:TPU:0, one launch (start us, length us, event | category | flops | bytes accessed | tf_op | source)
XLA Modules:
  0.0 73.0 jit_solution(6773208943977753931)
XLA Ops:
  0.0 1.2 %copy-done = bf16[2,16,128,128]{3,2,1,0:T(8,128)(2,1)S(1)} copy-done((bf16[2,16,128,128]{3,2,1,0:T(8,128)(2,1)S(1)}, bf16[2,16,128,128]{3,2,1,0:T(8,128)(2,1)}, u32[]{:S(2)}) %copy-start) | copy-done | bytes 1048600
  1.2 0.7 copy-done.3
  1.9 0.7 shard_map.46
  2.6 3.0 %collective-permute-start.7 = (bf16[2064,128]{1,0:T(8,128)(2,1)S(1)}, bf16[2064,128]{1,0:T(8,128)(2,1)S(1)}, u32[]{:S(2)}, u32[]{:S(2)}) collective-permute-start(bf16[2064,128]{1,0:T(8,128)(2,1)S(1)} %get-tuple-element.16.refs_8_), channel_id=1, source_target_pairs={{0,8},{4,12},{8,0},{12,4},{16,24},{20,28},{24,16},{28,20},{1,9},{5... | collective-permute-start | bytes 1585160 | tf_op jit(solution)/shard_map/ppermute | solution.py:165
  5.6 2.6 %collective-permute-start.1 = (bf16[256,512]{1,0:T(8,128)(2,1)}, bf16[256,512]{1,0:T(8,128)(2,1)}, u32[]{:S(2)}, u32[]{:S(2)}) collective-permute-start(bf16[256,512]{1,0:T(8,128)(2,1)} %refs_0_.1), channel_id=1, source_target_pairs={{0,2},{1,3},{2,0},{3,1},{4,6},{5,7},{6,4},{7,5},{8,10},{9,11},{10,... | collective-permute-start | bytes 786440 | tf_op jit(solution)/shard_map/ppermute | solution.py:168
  8.2 1.5 %collective-permute-start.10 = (bf16[2064,128]{1,0:T(8,128)(2,1)S(1)}, bf16[2064,128]{1,0:T(8,128)(2,1)S(1)}, u32[]{:S(2)}, u32[]{:S(2)}) collective-permute-start(bf16[2064,128]{1,0:T(8,128)(2,1)S(1)} %get-tuple-element.17.refs_9_), channel_id=1, source_target_pairs={{0,16},{4,20},{8,24},{12,28},{16,0},{20,4},{24,8},{28,12},{1,17},{... | collective-permute-start | bytes 1585160 | tf_op jit(solution)/shard_map/ppermute | solution.py:165
  9.7 1.6 %collective-permute-start = (bf16[256,512]{1,0:T(8,128)(2,1)}, bf16[256,512]{1,0:T(8,128)(2,1)}, u32[]{:S(2)}, u32[]{:S(2)}) collective-permute-start(bf16[256,512]{1,0:T(8,128)(2,1)} %refs_0_.1), channel_id=1, source_target_pairs={{0,1},{1,0},{2,3},{3,2},{4,5},{5,4},{6,7},{7,6},{8,9},{9,8},{10,11... | collective-permute-start | bytes 786440 | tf_op jit(solution)/shard_map/ppermute | solution.py:168
  11.8 8.5 %collective-permute-done.1.refs_2_ = bf16[256,512]{1,0:T(8,128)(2,1)} collective-permute-done((bf16[256,512]{1,0:T(8,128)(2,1)}, bf16[256,512]{1,0:T(8,128)(2,1)}, u32[]{:S(2)}, u32[]{:S(2)}) %collective-permute-start.1) | collective-permute-done | bytes 262176 | tf_op jit(solution)/shard_map/ppermute | solution.py:168
  20.8 0.8 %copy.7.refs_21_.column_ref = s32[256,1]{1,0:T(8,128)S(1)} copy(s32[256,1]{0,1:T(1,128)} %bitcast.41) | data formatting | bytes 2048 | tf_op jit(solution)/shard_map/reshape | solution.py:195
  22.3 0.9 %collective-permute-done.10.refs_13_ = bf16[2064,128]{1,0:T(8,128)(2,1)S(1)} collective-permute-done((bf16[2064,128]{1,0:T(8,128)(2,1)S(1)}, bf16[2064,128]{1,0:T(8,128)(2,1)S(1)}, u32[]{:S(2)}, u32[]{:S(2)}) %collective-permute-start.10) | collective-permute-done | bytes 528416 | tf_op jit(solution)/shard_map/ppermute | solution.py:165
  23.2 1.5 %collective-permute-start.11 = (bf16[2064,128]{1,0:T(8,128)(2,1)S(1)}, bf16[2064,128]{1,0:T(8,128)(2,1)S(1)}, u32[]{:S(2)}, u32[]{:S(2)}) collective-permute-start(bf16[2064,128]{1,0:T(8,128)(2,1)S(1)} %collective-permute-done.7.refs_10_), channel_id=1, source_target_pairs={{0,16},{4,20},{8,24},{12,28},{16,0},{20,4},{24,8},{28,12},{1,17},{... | collective-permute-start | bytes 1585160 | tf_op jit(solution)/shard_map/ppermute | solution.py:165
  24.7 12.5 %collective-permute-done.2.refs_3_ = bf16[256,512]{1,0:T(8,128)(2,1)S(1)} collective-permute-done((bf16[256,512]{1,0:T(8,128)(2,1)}, bf16[256,512]{1,0:T(8,128)(2,1)S(1)}, u32[]{:S(2)}, u32[]{:S(2)}) %collective-permute-start.2) | collective-permute-done | bytes 262176 | tf_op jit(solution)/shard_map/ppermute | solution.py:168
  37.7 1.5 %collective-permute-start.12 = (bf16[2064,128]{1,0:T(8,128)(2,1)S(1)}, bf16[2064,128]{1,0:T(8,128)(2,1)S(1)}, u32[]{:S(2)}, u32[]{:S(2)}) collective-permute-start(bf16[2064,128]{1,0:T(8,128)(2,1)S(1)} %collective-permute-done.10.refs_13_), channel_id=1, source_target_pairs={{0,8},{4,12},{8,0},{12,4},{16,24},{20,28},{24,16},{28,20},{1,9},{5... | collective-permute-start | bytes 1585160 | tf_op jit(solution)/shard_map/ppermute | solution.py:165
  39.3 0.9 %copy-done.1 = bf16[256,512]{1,0:T(8,128)(2,1)S(1)} copy-done((bf16[256,512]{1,0:T(8,128)(2,1)S(1)}, bf16[256,512]{1,0:T(8,128)(2,1)}, u32[]{:S(2)}) %copy-start.1) | copy-done | bytes 262168
  40.9 8.4 %shard_map.47 = (bf16[16,512,128]{2,1,0:T(8,128)(2,1)S(1)}, f32[16,512,128]{2,1,0:T(8,128)S(1)}, f32[16,512,128]{2,1,0:T(8,128)S(1)}) custom-call(bf16[256,512]{1,0:T(8,128)(2,1)S(1)} %copy-done.1, bf16[256,512]{1,0:T(8,128)(2,1)} %collective-permute-done.refs_1_, bf16[256,512]{1,0:T(8,128)(2,1)} %collective-permute-done.1.refs_2_, ...), custom_call_target="tpu_custom_call" | custom-call | tf_op jit(solution)/shard_map/pallas_call | solution.py:203
  49.4 2.4 %collective-permute-done.12.refs_4_ = bf16[2064,128]{1,0:T(8,128)(2,1)S(1)} collective-permute-done((bf16[2064,128]{1,0:T(8,128)(2,1)S(1)}, bf16[2064,128]{1,0:T(8,128)(2,1)S(1)}, u32[]{:S(2)}, u32[]{:S(2)}) %collective-permute-start.12) | collective-permute-done | bytes 528416 | tf_op jit(solution)/shard_map/ppermute | solution.py:165
  51.7 3.3 %shard_map.48 = (bf16[4,2,256,128]{3,2,1,0:T(8,128)(2,1)S(1)}, bf16[4,2,256,128]{3,2,1,0:T(8,128)(2,1)S(1)}, f32[16,512,128]{2,1,0:T(8,128)S(1)}, f32[16,512,128]{2,1,0:T(8,128)S(1)}) custom-call(bf16[16,512,128]{2,1,0:T(8,128)(2,1)S(1)} %get-tuple-element.18.refs_0_, ...), custom_call_target="tpu_custom_call", output_to_operand_aliasing={{2}: (1, {}), {3}: (2, {})} | custom-call | tf_op jit(solution)/shard_map/pallas_call | solution.py:210
  55.1 1.9 %collective-permute-done.13.come_ref = bf16[4,2,256,128]{3,2,1,0:T(8,128)(2,1)S(1)} collective-permute-done((bf16[4,2,256,128]{3,2,1,0:T(8,128)(2,1)S(1)}, bf16[4,2,256,128]{3,2,1,0:T(8,128)(2,1)S(1)}, u32[]{:S(2)}, u32[]{:S(2)}) %collective-permute-start.13) | collective-permute-done | bytes 524320 | tf_op jit(solution)/shard_map/ppermute | solution.py:165
  57.1 1.5 %collective-permute-start.14 = (bf16[2,256,128]{2,1,0:T(8,128)(2,1)S(1)}, bf16[2,256,128]{2,1,0:T(8,128)(2,1)S(1)}, u32[]{:S(2)}, u32[]{:S(2)}) collective-permute-start(bf16[2,256,128]{2,1,0:T(8,128)(2,1)S(1)} %get-tuple-element.24), channel_id=1, source_target_pairs={{0,3},{1,2},{2,1},{3,0},{4,7},{5,6},{6,5},{7,4},{8,11},{9,10},{10,... | collective-permute-start | bytes 393224 | tf_op jit(solution)/shard_map/ppermute | solution.py:168
  58.6 2.9 %collective-permute-start.16 = (bf16[2,256,128]{2,1,0:T(8,128)(2,1)S(1)}, bf16[2,256,128]{2,1,0:T(8,128)(2,1)S(1)}, u32[]{:S(2)}, u32[]{:S(2)}) collective-permute-start(bf16[2,256,128]{2,1,0:T(8,128)(2,1)S(1)} %get-tuple-element.26), channel_id=1, source_target_pairs={{0,1},{1,0},{2,3},{3,2},{4,5},{5,4},{6,7},{7,6},{8,9},{9,8},{10,11... | collective-permute-start | bytes 393224 | tf_op jit(solution)/shard_map/ppermute | solution.py:168
  61.5 3.9 %collective-permute-done.14.refs_1_ = bf16[2,256,128]{2,1,0:T(8,128)(2,1)S(1)} collective-permute-done((bf16[2,256,128]{2,1,0:T(8,128)(2,1)S(1)}, bf16[2,256,128]{2,1,0:T(8,128)(2,1)S(1)}, u32[]{:S(2)}, u32[]{:S(2)}) %collective-permute-start.14) | collective-permute-done | bytes 131104 | tf_op jit(solution)/shard_map/ppermute | solution.py:168
  65.4 4.7 %collective-permute-done.15.refs_2_ = bf16[2,256,128]{2,1,0:T(8,128)(2,1)S(1)} collective-permute-done((bf16[2,256,128]{2,1,0:T(8,128)(2,1)S(1)}, bf16[2,256,128]{2,1,0:T(8,128)(2,1)S(1)}, u32[]{:S(2)}, u32[]{:S(2)}) %collective-permute-start.15) | collective-permute-done | bytes 131104 | tf_op jit(solution)/shard_map/ppermute | solution.py:168
  70.3 1.3 %collective-permute-done.17.other_ref = bf16[2,256,128]{2,1,0:T(8,128)(2,1)S(1)} collective-permute-done((bf16[2,256,128]{2,1,0:T(8,128)(2,1)S(1)}, bf16[2,256,128]{2,1,0:T(8,128)(2,1)S(1)}, u32[]{:S(2)}, u32[]{:S(2)}) %collective-permute-start.17) | collective-permute-done | bytes 131104 | tf_op jit(solution)/shard_map/ppermute | solution.py:165
  71.6 1.3 %shard_map.51 = bf16[256,512]{1,0:T(8,128)(2,1)} custom-call(bf16[2,256,128]{2,1,0:T(8,128)(2,1)S(1)} %shard_map.50.own_ref, bf16[2,256,128]{2,1,0:T(8,128)(2,1)S(1)} %collective-permute-done.17.other_ref, s32[256,1]{1,0:T(8,128)S(1)} %copy.7.refs_21_.column_ref), custom_call_target="tpu_custom_call" | custom-call | tf_op jit(solution)/shard_map/pallas_call | solution.py:221
  (34 shorter events, 3.3 us)
Async XLA Ops:
  0.0 1.2 %copy-start = (bf16[2,16,128,128]{3,2,1,0:T(8,128)(2,1)S(1)}, bf16[2,16,128,128]{3,2,1,0:T(8,128)(2,1)}, u32[]{:S(2)}) copy-start(bf16[2,16,128,128]{3,2,1,0:T(8,128)(2,1)} %param.5) | copy-start | bytes 3145732
  1.2 0.7 copy-start.3
  2.6 19.1 %collective-permute-start.7 = (bf16[2064,128]{1,0:T(8,128)(2,1)S(1)}, bf16[2064,128]{1,0:T(8,128)(2,1)S(1)}, u32[]{:S(2)}, u32[]{:S(2)}) collective-permute-start(bf16[2064,128]{1,0:T(8,128)(2,1)S(1)} %get-tuple-element.16.refs_8_), channel_id=1, source_target_pairs={{0,8},{4,12},{8,0},{12,4},{16,24},{20,28},{24,16},{28,20},{1,9},{5... | collective-permute-start | bytes 1585160 | tf_op jit(solution)/shard_map/ppermute | solution.py:165
  5.6 14.7 %collective-permute-start.1 = (bf16[256,512]{1,0:T(8,128)(2,1)}, bf16[256,512]{1,0:T(8,128)(2,1)}, u32[]{:S(2)}, u32[]{:S(2)}) collective-permute-start(bf16[256,512]{1,0:T(8,128)(2,1)} %refs_0_.1), channel_id=1, source_target_pairs={{0,2},{1,3},{2,0},{3,1},{4,6},{5,7},{6,4},{7,5},{8,10},{9,11},{10,... | collective-permute-start | bytes 786440 | tf_op jit(solution)/shard_map/ppermute | solution.py:168
  8.2 15.0 %collective-permute-start.10 = (bf16[2064,128]{1,0:T(8,128)(2,1)S(1)}, bf16[2064,128]{1,0:T(8,128)(2,1)S(1)}, u32[]{:S(2)}, u32[]{:S(2)}) collective-permute-start(bf16[2064,128]{1,0:T(8,128)(2,1)S(1)} %get-tuple-element.17.refs_9_), channel_id=1, source_target_pairs={{0,16},{4,20},{8,24},{12,28},{16,0},{20,4},{24,8},{28,12},{1,17},{... | collective-permute-start | bytes 1585160 | tf_op jit(solution)/shard_map/ppermute | solution.py:165
  9.7 12.0 %collective-permute-start = (bf16[256,512]{1,0:T(8,128)(2,1)}, bf16[256,512]{1,0:T(8,128)(2,1)}, u32[]{:S(2)}, u32[]{:S(2)}) collective-permute-start(bf16[256,512]{1,0:T(8,128)(2,1)} %refs_0_.1), channel_id=1, source_target_pairs={{0,1},{1,0},{2,3},{3,2},{4,5},{5,4},{6,7},{7,6},{8,9},{9,8},{10,11... | collective-permute-start | bytes 786440 | tf_op jit(solution)/shard_map/ppermute | solution.py:168
  11.3 25.9 %collective-permute-start.9 = (bf16[2064,128]{1,0:T(8,128)(2,1)S(1)}, bf16[2064,128]{1,0:T(8,128)(2,1)S(1)}, u32[]{:S(2)}, u32[]{:S(2)}) collective-permute-start(bf16[2064,128]{1,0:T(8,128)(2,1)S(1)} %get-tuple-element.16.refs_8_), channel_id=1, source_target_pairs={{0,16},{4,20},{8,24},{12,28},{16,0},{20,4},{24,8},{28,12},{1,17},{... | collective-permute-start | bytes 1585160 | tf_op jit(solution)/shard_map/ppermute | solution.py:165
  20.3 17.4 %collective-permute-start.8 = (bf16[2064,128]{1,0:T(8,128)(2,1)S(1)}, bf16[2064,128]{1,0:T(8,128)(2,1)S(1)}, u32[]{:S(2)}, u32[]{:S(2)}) collective-permute-start(bf16[2064,128]{1,0:T(8,128)(2,1)S(1)} %get-tuple-element.17.refs_9_), channel_id=1, source_target_pairs={{0,8},{4,12},{8,0},{12,4},{16,24},{20,28},{24,16},{28,20},{1,9},{5... | collective-permute-start | bytes 1585160 | tf_op jit(solution)/shard_map/ppermute | solution.py:165
  21.7 2.9 %collective-permute-start.3 = (bf16[256,512]{1,0:T(8,128)(2,1)}, bf16[256,512]{1,0:T(8,128)(2,1)S(1)}, u32[]{:S(2)}, u32[]{:S(2)}) collective-permute-start(bf16[256,512]{1,0:T(8,128)(2,1)} %refs_0_.1), channel_id=1, source_target_pairs={{0,4},{4,0},{8,12},{12,8},{16,20},{20,16},{24,28},{28,24},{1,5},{5... | collective-permute-start | bytes 786440 | tf_op jit(solution)/shard_map/ppermute | solution.py:165
  21.8 15.4 %collective-permute-start.2 = (bf16[256,512]{1,0:T(8,128)(2,1)}, bf16[256,512]{1,0:T(8,128)(2,1)S(1)}, u32[]{:S(2)}, u32[]{:S(2)}) collective-permute-start(bf16[256,512]{1,0:T(8,128)(2,1)} %collective-permute-done.refs_1_), channel_id=1, source_target_pairs={{0,2},{1,3},{2,0},{3,1},{4,6},{5,7},{6,4},{7,5},{8,10},{9,11},{10,... | collective-permute-start | bytes 786440 | tf_op jit(solution)/shard_map/ppermute | solution.py:168
  23.2 26.2 %collective-permute-start.11 = (bf16[2064,128]{1,0:T(8,128)(2,1)S(1)}, bf16[2064,128]{1,0:T(8,128)(2,1)S(1)}, u32[]{:S(2)}, u32[]{:S(2)}) collective-permute-start(bf16[2064,128]{1,0:T(8,128)(2,1)S(1)} %collective-permute-done.7.refs_10_), channel_id=1, source_target_pairs={{0,16},{4,20},{8,24},{12,28},{16,0},{20,4},{24,8},{28,12},{1,17},{... | collective-permute-start | bytes 1585160 | tf_op jit(solution)/shard_map/ppermute | solution.py:165
  24.7 14.6 %collective-permute-start.4 = (bf16[256,512]{1,0:T(8,128)(2,1)}, bf16[256,512]{1,0:T(8,128)(2,1)S(1)}, u32[]{:S(2)}, u32[]{:S(2)}) collective-permute-start(bf16[256,512]{1,0:T(8,128)(2,1)} %collective-permute-done.refs_1_), channel_id=1, source_target_pairs={{0,4},{4,0},{8,12},{12,8},{16,20},{20,16},{24,28},{28,24},{1,5},{5... | collective-permute-start | bytes 786440 | tf_op jit(solution)/shard_map/ppermute | solution.py:165
  37.2 2.0 %collective-permute-start.5 = (bf16[256,512]{1,0:T(8,128)(2,1)}, bf16[256,512]{1,0:T(8,128)(2,1)S(1)}, u32[]{:S(2)}, u32[]{:S(2)}) collective-permute-start(bf16[256,512]{1,0:T(8,128)(2,1)} %collective-permute-done.1.refs_2_), channel_id=1, source_target_pairs={{0,4},{4,0},{8,12},{12,8},{16,20},{20,16},{24,28},{28,24},{1,5},{5... | collective-permute-start | bytes 786440 | tf_op jit(solution)/shard_map/ppermute | solution.py:165
  37.2 2.0 %collective-permute-start.6 = (bf16[256,512]{1,0:T(8,128)(2,1)S(1)}, bf16[256,512]{1,0:T(8,128)(2,1)S(1)}, u32[]{:S(2)}, u32[]{:S(2)}) collective-permute-start(bf16[256,512]{1,0:T(8,128)(2,1)S(1)} %collective-permute-done.2.refs_3_), channel_id=1, source_target_pairs={{0,4},{4,0},{8,12},{12,8},{16,20},{20,16},{24,28},{28,24},{1,5},{5... | collective-permute-start | bytes 786440 | tf_op jit(solution)/shard_map/ppermute | solution.py:165
  37.7 14.0 %collective-permute-start.12 = (bf16[2064,128]{1,0:T(8,128)(2,1)S(1)}, bf16[2064,128]{1,0:T(8,128)(2,1)S(1)}, u32[]{:S(2)}, u32[]{:S(2)}) collective-permute-start(bf16[2064,128]{1,0:T(8,128)(2,1)S(1)} %collective-permute-done.10.refs_13_), channel_id=1, source_target_pairs={{0,8},{4,12},{8,0},{12,4},{16,24},{20,28},{24,16},{28,20},{1,9},{5... | collective-permute-start | bytes 1585160 | tf_op jit(solution)/shard_map/ppermute | solution.py:165
  39.3 1.0 %copy-start.1 = (bf16[256,512]{1,0:T(8,128)(2,1)S(1)}, bf16[256,512]{1,0:T(8,128)(2,1)}, u32[]{:S(2)}) copy-start(bf16[256,512]{1,0:T(8,128)(2,1)} %refs_0_.1) | copy-start | bytes 786436
  40.2 0.7 copy-start.2
  55.0 2.0 %collective-permute-start.13 = (bf16[4,2,256,128]{3,2,1,0:T(8,128)(2,1)S(1)}, bf16[4,2,256,128]{3,2,1,0:T(8,128)(2,1)S(1)}, u32[]{:S(2)}, u32[]{:S(2)}) collective-permute-start(bf16[4,2,256,128]{3,2,1,0:T(8,128)(2,1)S(1)} %get-tuple-element.22), channel_id=1, source_target_pairs={{0,4},{4,0},{8,12},{12,8},{16,20},{20,16},{24,28},{28,24},{1,5},{5... | collective-permute-start | bytes 1572872 | tf_op jit(solution)/shard_map/ppermute | solution.py:165
  57.1 8.3 %collective-permute-start.14 = (bf16[2,256,128]{2,1,0:T(8,128)(2,1)S(1)}, bf16[2,256,128]{2,1,0:T(8,128)(2,1)S(1)}, u32[]{:S(2)}, u32[]{:S(2)}) collective-permute-start(bf16[2,256,128]{2,1,0:T(8,128)(2,1)S(1)} %get-tuple-element.24), channel_id=1, source_target_pairs={{0,3},{1,2},{2,1},{3,0},{4,7},{5,6},{6,5},{7,4},{8,11},{9,10},{10,... | collective-permute-start | bytes 393224 | tf_op jit(solution)/shard_map/ppermute | solution.py:168
  58.6 11.6 %collective-permute-start.15 = (bf16[2,256,128]{2,1,0:T(8,128)(2,1)S(1)}, bf16[2,256,128]{2,1,0:T(8,128)(2,1)S(1)}, u32[]{:S(2)}, u32[]{:S(2)}) collective-permute-start(bf16[2,256,128]{2,1,0:T(8,128)(2,1)S(1)} %get-tuple-element.25), channel_id=1, source_target_pairs={{0,2},{1,3},{2,0},{3,1},{4,6},{5,7},{6,4},{7,5},{8,10},{9,11},{10,... | collective-permute-start | bytes 393224 | tf_op jit(solution)/shard_map/ppermute | solution.py:168
  58.6 11.6 %collective-permute-start.16 = (bf16[2,256,128]{2,1,0:T(8,128)(2,1)S(1)}, bf16[2,256,128]{2,1,0:T(8,128)(2,1)S(1)}, u32[]{:S(2)}, u32[]{:S(2)}) collective-permute-start(bf16[2,256,128]{2,1,0:T(8,128)(2,1)S(1)} %get-tuple-element.26), channel_id=1, source_target_pairs={{0,1},{1,0},{2,3},{3,2},{4,5},{5,4},{6,7},{7,6},{8,9},{9,8},{10,11... | collective-permute-start | bytes 393224 | tf_op jit(solution)/shard_map/ppermute | solution.py:168
  70.2 1.4 %collective-permute-start.17 = (bf16[2,256,128]{2,1,0:T(8,128)(2,1)S(1)}, bf16[2,256,128]{2,1,0:T(8,128)(2,1)S(1)}, u32[]{:S(2)}, u32[]{:S(2)}) collective-permute-start(bf16[2,256,128]{2,1,0:T(8,128)(2,1)S(1)} %shard_map.50.own_ref), channel_id=1, source_target_pairs={{0,4},{4,0},{8,12},{12,8},{16,20},{20,16},{24,28},{28,24},{1,5},{5... | collective-permute-start | bytes 393224 | tf_op jit(solution)/shard_map/ppermute | solution.py:165

commit v4 on v3

--- a/solution.py
+++ b/solution.py
@@ -16,13 +16,13 @@
 SMEM = pl.BlockSpec(memory_space=pltpu.SMEM)
 
 
-def call(body, out_shape, in_specs, scratch=(), megabytes=32, aliases=None):
+def call(body, out_shape, in_specs, scratch=(), megabytes=32, aliases=None, out_specs=None):
     many = isinstance(out_shape, (list, tuple))
     return pl.pallas_call(
         body,
         out_shape=out_shape,
         in_specs=in_specs,
-        out_specs=[VMEM] * len(out_shape) if many else VMEM,
+        out_specs=out_specs or ([VMEM] * len(out_shape) if many else VMEM),
         scratch_shapes=list(scratch),
         compiler_params=pltpu.CompilerParams(vmem_limit_bytes=megabytes << 20),
         input_output_aliases=aliases or {},
@@ -40,24 +40,31 @@
     return iota((TILE, TILE), 0) == (1 - h) * SUB * SUB + b * SUB + a
 
 
-def pack_kernel(integrals_ref, blocks_ref, *refs):
-    outs, sems = refs[:-1], refs[-1]
-    length = integrals_ref.shape[1]
+def pack_kernel(integrals_ref, blocks_ref, out_ref, ids_ref, sems):
+    slabs, length = integrals_ref.shape[:2]
     copies = [
-        pltpu.make_async_copy(integrals_ref.at[s], out_ref.at[pl.ds(0, length)], sems.at[s])
-        for s, out_ref in enumerate(outs)
+        pltpu.make_async_copy(integrals_ref.at[s], out_ref.at[s, pl.ds(0, length)], sems.at[s]) for s in range(slabs)
     ]
     for copy in copies:
         copy.start()
     lane = iota((EXTRA, TILE), 1)
-    for s, out_ref in enumerate(outs):
+    for s in range(slabs):
         ids = jnp.zeros((EXTRA, TILE), jnp.int32)
         for t in range(length // TILE):
             for which in range(2):
                 ids = jnp.where(lane == 2 * t + which, blocks_ref[s, which, t], ids)
-        out_ref[length:, :] = ids.astype(F32).astype(BF16)
+        ids_ref[s] = ids.astype(F32).astype(BF16)
+        copies.append(
+            pltpu.make_async_copy(ids_ref.at[s], out_ref.at[s, pl.ds(length, EXTRA)], sems.at[slabs + s])
+        )
+        copies[-1].start()
     for copy in copies:
         copy.wait()
+
+
+def cut_kernel(x_ref, y_ref, *outs):
+    for s, out_ref in enumerate(outs):
+        out_ref[...] = (x_ref if s % 2 == 0 else y_ref)[s]
 
 
 def add_products(grid_ref, acc_refs, tiles_ref, blocks_ref):
@@ -102,7 +109,8 @@
     for acc_ref in acc_refs:
         acc_ref[...] = jnp.zeros_like(acc_ref)
     for tiles_ref, blocks_ref in zip(tiles, blocks):
-        add_products(grid_ref, acc_refs, tiles_ref, blocks_ref)
+        for s in range(tiles_ref.shape[0]):
+            add_products(grid_ref, acc_refs, tiles_ref.at[s], blocks_ref.at[s])
 
 
 def second_kernel(n_vir, n_sets, *refs):
@@ -113,7 +121,8 @@
     core = lax.axis_index("pair") % 2
     vir = lax.axis_index("vir")
     for tiles_ref, blocks_ref in zip(tiles, blocks):
-        add_products(grid_ref, acc_refs, tiles_ref, blocks_ref)
+        for s in range(tiles_ref.shape[0]):
+            add_products(grid_ref, acc_refs, tiles_ref.at[s], blocks_ref.at[s])
     swap = swap_matrix().astype(BF16)
     for shift in range(n_vir):
         for k in range(half):
@@ -169,21 +178,13 @@
 
     packed = call(
         pack_kernel,
-        [jax.ShapeDtypeStruct((length + EXTRA, TILE), BF16)] * slabs,
+        jax.ShapeDtypeStruct((slabs, length + EXTRA, TILE), BF16),
         [pl.BlockSpec(memory_space=pl.ANY), SMEM],
-        [pltpu.SemaphoreType.DMA((slabs,))],
-        megabytes=8,
+        [pltpu.VMEM((slabs, EXTRA, TILE), BF16), pltpu.SemaphoreType.DMA((2 * slabs,))],
+        out_specs=pl.BlockSpec(memory_space=pl.ANY),
+        megabytes=56,
     )(integrals.reshape(slabs, length, TILE), tile_blocks.transpose(0, 2, 1))
-    tiles = {(0, s): packed[s] for s in range(slabs)}
-    for s in range(slabs):
-        tiles[1, s] = across(packed[s], 2)
-        tiles[2, slabs - 1 - s] = across(packed[slabs - 1 - s], 4)
-    for s in range(slabs):
-        tiles[3, s] = across(tiles[1, s], 4) if s % 2 == 0 else across(tiles[2, s], 2)
-    reach = 4
-    while reach < chips:
-        tiles |= {(d + reach, s): across(tiles[d, s], 2 * reach) for d in range(reach) for s in range(slabs)}
-        reach *= 2
+    early = [packed, across(packed, 2), across(packed, 4)]
 
     pieces = {0: amplitudes}
     reach = 1
@@ -192,20 +193,28 @@
         reach *= 2
     mine = [pieces[shift] for shift in range(n_vir)]
     others = [across(piece, 1) for piece in mine]
+    tiles_x, tiles_y, *_ = lax.optimization_barrier((*early[1:], *others[:2], *mine[:-1]))
+    slab = jax.ShapeDtypeStruct((length + EXTRA, TILE), BF16)
+    halves = call(cut_kernel, [slab] * slabs, [VMEM, VMEM], megabytes=8)(tiles_x, tiles_y)
+    late = [across(half, 4 if s % 2 == 0 else 2) for s, half in enumerate(halves)]
+    reach = 4
+    while reach < chips:
+        farther = early + late if reach == 4 else late
+        late = late + [across(array, 2 * reach) for array in farther]
+        reach *= 2
+    late = [array.reshape(-1, length + EXTRA, TILE) for array in late]
     row, column = mirror_row.reshape(1, rows), mirror_row.reshape(rows, 1)
 
-    def ids(key):
-        return tiles[key][length, : 2 * tile_dev].astype(jnp.int32)
-
-    early = [(d, s) for d in range(3) for s in range(slabs)]
-    late = [(d, s) for d in range(3, chips) for s in range(slabs)]
+    def ids(array):
+        return array[:, length, : 2 * tile_dev].astype(jnp.int32)
+
     sums = jax.ShapeDtypeStruct((n_blk, 2 * rows, TILE), F32)
     grid, *sums_so_far = call(
         functools.partial(first_kernel, n_vir, len(early)),
         [jax.ShapeDtypeStruct((n_blk, 2 * rows, TILE), BF16), sums, sums],
         [VMEM] * (2 * n_vir + len(early)) + [SMEM] * len(early) + [VMEM, VMEM],
         megabytes=32,
-    )(*mine, *others, *[tiles[key] for key in early], *[ids(key) for key in early], row, column)
+    )(*mine, *others, *early, *[ids(array) for array in early], row, column)
     piece = jax.ShapeDtypeStruct((n_vir, per // 2, rows, TILE), BF16)
     keep, send, *_ = call(
         functools.partial(second_kernel, n_vir, len(late)),
@@ -213,11 +222,20 @@
         [VMEM] * (3 + len(late)) + [SMEM] * len(late),
         megabytes=32,
         aliases={1: 2, 2: 3},
-    )(grid, *sums_so_far, *[tiles[key] for key in late], *[ids(key) for key in late])
+    )(grid, *sums_so_far, *late, *[ids(array) for array in late])
     one = jax.ShapeDtypeStruct((per // 2, rows, TILE), BF16)
     parts = call(join_kernel, [one] * n_vir, [VMEM, VMEM], megabytes=8)(keep, across(send, 1))
-    arrived = [along(parts[shift], shift) for shift in range(n_vir - 1, 0, -1)]
-    total = call(total_kernel, one, [VMEM] * n_vir, megabytes=8)(parts[0], *arrived)
+    parts = dict(enumerate(parts))
+    reach = 1
+    while reach < n_vir:
+        sent = [shift for shift in reversed(parts) if shift & reach]
+        arrived = {shift: along(parts.pop(shift), reach) for shift in sent}
+        for shift in sent:
+            kept = shift ^ reach
+            if 2 * reach < n_vir:
+                parts[kept] = call(total_kernel, one, [VMEM] * 2, megabytes=8)(parts[kept], arrived[shift])
+        reach *= 2
+    total = call(total_kernel, one, [VMEM] * 2, megabytes=8)(parts[0], *arrived.values())
     return call(
         finish_kernel, jax.ShapeDtypeStruct((rows, width), BF16), [VMEM] * 3, megabytes=8
     )(total, across(total, 1), column)

time: 73.2 us -> 104 us (1.42)
  Pallas kernels: 13.9 us -> 48.3 us
  starting transfers between devices: 18.4 us -> 13.7 us
  local copies, waits for them, and re-layouts: 4.33 us -> 5.53 us
    pallas_call x2 -> x5, Pallas kernels: 0.76 us -> 34.7 us  [the longest x1 33.7 us: local(): call(pack_kernel, jax.ShapeDtypeStruct((slabs, length + EXTRA, TILE), BF1...]
    ppermute x12 -> x10, starting transfers between devices: 9.21 us -> 5.89 us  [across(): return lax.ppermute(array, 'pair', [(i, i ^ bits) for i in range(n_pair)])]
    ppermute x12 -> x10, waiting for transfers between devices: 6.46 us -> 4.35 us  [across(): return lax.ppermute(array, 'pair', [(i, i ^ bits) for i in range(n_pair)])]
    unnamed x8 -> x22, local copies, waits for them, and re-layouts: 3.53 us -> 5.4 us
    ppermute x6, waiting for transfers between devices: 29.8 us -> 31.2 us  [along(): return lax.ppermute(array, 'vir', [(i, i ^ bits) for i in range(n_vir)])]
    ppermute x6, starting transfers between devices: 9.16 us -> 7.8 us  [along(): return lax.ppermute(array, 'vir', [(i, i ^ bits) for i in range(n_vir)])]
  transfers between devices with their start and end apart: 18 -> 16, of which waited for: 9 -> 9; matrix products, arithmetic and copies ran while one was open for 1% -> 1% of each run, Pallas kernels for 12% -> 9%
where the time goes in v4:
time: 104 us
  Pallas kernels  48.3 us (46%)
  waiting for transfers between devices  35.6 us (34%)
  starting transfers between devices  13.7 us (13%)
  local copies, waits for them, and re-layouts  5.53 us (5%)
    pallas_call x1, Pallas kernels, local(): call(pack_kernel, jax.ShapeDtypeStruct((slabs, length + EXTRA, TILE), BF1...  33.7 us
    ppermute x6, waiting for transfers between devices, along(): return lax.ppermute(array, 'vir', [(i, i ^ bits) for i in range(n_vir)])  31.2 us
    pallas_call x1, Pallas kernels, local(): call(functools.partial(first_kernel, n_vir, len(early)), [jax.ShapeDtypeS...  8.38 us
    ppermute x6, starting transfers between devices, along(): return lax.ppermute(array, 'vir', [(i, i ^ bits) for i in range(n_vir)])  7.8 us
    ppermute x10, starting transfers between devices, across(): return lax.ppermute(array, 'pair', [(i, i ^ bits) for i in range(n_pair)])  5.89 us
    unnamed x22, local copies, waits for them, and re-layouts  5.4 us
    ppermute x10, waiting for transfers between devices, across(): return lax.ppermute(array, 'pair', [(i, i ^ bits) for i in range(n_pair)])  4.35 us
    pallas_call x1, Pallas kernels, local(): call(functools.partial(second_kernel, n_vir, len(late)), [piece, piece, s...  3.78 us
  transfers between devices with their start and end apart: 16, of which 9 were waited for; matrix products, arithmetic and copies ran while one was open for 1% of the time, Pallas kernels for 9%

profile of v4, /device:TPU:0, one launch (start us, length us, event | category | flops | bytes accessed | tf_op | source)
XLA Modules:
  0.0 103.9 jit_solution(3758708400290111402)
XLA Ops:
  0.0 33.7 %shard_map.46.refs_8_ = bf16[2,2064,128]{2,1,0:T(8,128)(2,1)} custom-call(bf16[2,2048,128]{2,1,0:T(8,128)(2,1)} %bitcast.26, s32[2,2,16]{2,1,0:T(2,128)} %bitcast.27), custom_call_target="tpu_custom_call" | custom-call | tf_op jit(solution)/shard_map/pallas_call | solution.py:179
  33.8 3.0 %collective-permute-start.8 = (bf16[2,2064,128]{2,1,0:T(8,128)(2,1)}, bf16[2,2064,128]{2,1,0:T(8,128)(2,1)S(1)}, u32[]{:S(2)}, u32[]{:S(2)}) collective-permute-start(bf16[2,2064,128]{2,1,0:T(8,128)(2,1)} %shard_map.46.refs_8_), channel_id=1, source_target_pairs={{0,16},{4,20},{8,24},{12,28},{16,0},{20,4},{24,8},{28,12},{1,17},{... | collective-permute-start | bytes 3170312 | tf_op jit(solution)/shard_map/ppermute | solution.py:174
  36.8 1.5 %collective-permute-start.7 = (bf16[2,2064,128]{2,1,0:T(8,128)(2,1)}, bf16[2,2064,128]{2,1,0:T(8,128)(2,1)S(1)}, u32[]{:S(2)}, u32[]{:S(2)}) collective-permute-start(bf16[2,2064,128]{2,1,0:T(8,128)(2,1)} %shard_map.46.refs_8_), channel_id=1, source_target_pairs={{0,8},{4,12},{8,0},{12,4},{16,24},{20,28},{24,16},{28,20},{1,9},{5... | collective-permute-start | bytes 3170312 | tf_op jit(solution)/shard_map/ppermute | solution.py:174
  38.3 1.6 %collective-permute-start = (bf16[256,512]{1,0:T(8,128)(2,1)S(1)}, bf16[256,512]{1,0:T(8,128)(2,1)}, u32[]{:S(2)}, u32[]{:S(2)}) collective-permute-start(bf16[256,512]{1,0:T(8,128)(2,1)S(1)} %copy-done.1), channel_id=1, source_target_pairs={{0,1},{1,0},{2,3},{3,2},{4,5},{5,4},{6,7},{7,6},{8,9},{9,8},{10,11... | collective-permute-start | bytes 786440 | tf_op jit(solution)/shard_map/ppermute | solution.py:177
  39.9 2.6 %collective-permute-start.1 = (bf16[256,512]{1,0:T(8,128)(2,1)S(1)}, bf16[256,512]{1,0:T(8,128)(2,1)S(1)}, u32[]{:S(2)}, u32[]{:S(2)}) collective-permute-start(bf16[256,512]{1,0:T(8,128)(2,1)S(1)} %copy-done.1), channel_id=1, source_target_pairs={{0,2},{1,3},{2,0},{3,1},{4,6},{5,7},{6,4},{7,5},{8,10},{9,11},{10,... | collective-permute-start | bytes 786440 | tf_op jit(solution)/shard_map/ppermute | solution.py:177
  42.5 7.4 %collective-permute-done.refs_1_ = bf16[256,512]{1,0:T(8,128)(2,1)} collective-permute-done((bf16[256,512]{1,0:T(8,128)(2,1)S(1)}, bf16[256,512]{1,0:T(8,128)(2,1)}, u32[]{:S(2)}, u32[]{:S(2)}) %collective-permute-start) | collective-permute-done | bytes 262176 | tf_op jit(solution)/shard_map/ppermute | solution.py:177
  50.4 10.8 %collective-permute-done.1.refs_2_ = bf16[256,512]{1,0:T(8,128)(2,1)S(1)} collective-permute-done((bf16[256,512]{1,0:T(8,128)(2,1)S(1)}, bf16[256,512]{1,0:T(8,128)(2,1)S(1)}, u32[]{:S(2)}, u32[]{:S(2)}) %collective-permute-start.1) | collective-permute-done | bytes 262176 | tf_op jit(solution)/shard_map/ppermute | solution.py:177
  61.9 0.9 shard_map.48
  64.4 2.1 %collective-permute-done.2.refs_3_ = bf16[256,512]{1,0:T(8,128)(2,1)} collective-permute-done((bf16[256,512]{1,0:T(8,128)(2,1)}, bf16[256,512]{1,0:T(8,128)(2,1)}, u32[]{:S(2)}, u32[]{:S(2)}) %collective-permute-start.2) | collective-permute-done | bytes 262176 | tf_op jit(solution)/shard_map/ppermute | solution.py:177
  67.0 1.2 %collective-permute-done.6.refs_7_ = bf16[256,512]{1,0:T(8,128)(2,1)S(1)} collective-permute-done((bf16[256,512]{1,0:T(8,128)(2,1)}, bf16[256,512]{1,0:T(8,128)(2,1)S(1)}, u32[]{:S(2)}, u32[]{:S(2)}) %collective-permute-start.6) | collective-permute-done | bytes 262176 | tf_op jit(solution)/shard_map/ppermute | solution.py:174
  68.2 0.9 copy-done.2
  69.2 0.9 copy-done.4
  70.1 0.9 copy-done.6
  71.1 0.9 copy-done.8
  72.0 8.4 %shard_map.47 = (bf16[16,512,128]{2,1,0:T(8,128)(2,1)S(1)}, f32[16,512,128]{2,1,0:T(8,128)S(1)}, f32[16,512,128]{2,1,0:T(8,128)S(1)}) custom-call(bf16[256,512]{1,0:T(8,128)(2,1)S(1)} %copy-done.2, bf16[256,512]{1,0:T(8,128)(2,1)} %collective-permute-done.refs_1_, bf16[256,512]{1,0:T(8,128)(2,1)S(1)} %copy-done.6, ...), custom_call_target="tpu_custom_call" | custom-call | tf_op jit(solution)/shard_map/pallas_call | solution.py:212
  81.1 3.8 %shard_map.49 = (bf16[4,2,256,128]{3,2,1,0:T(8,128)(2,1)S(1)}, bf16[4,2,256,128]{3,2,1,0:T(8,128)(2,1)S(1)}, f32[16,512,128]{2,1,0:T(8,128)S(1)}, f32[16,512,128]{2,1,0:T(8,128)S(1)}) custom-call(bf16[16,512,128]{2,1,0:T(8,128)(2,1)S(1)} %get-tuple-element.18.refs_0_, ...), custom_call_target="tpu_custom_call", output_to_operand_aliasing={{2}: (1, {}), {3}: (2, {})} | custom-call | tf_op jit(solution)/shard_map/pallas_call | solution.py:219
  85.1 1.8 %collective-permute-done.11.come_ref = bf16[4,2,256,128]{3,2,1,0:T(8,128)(2,1)S(1)} collective-permute-done((bf16[4,2,256,128]{3,2,1,0:T(8,128)(2,1)S(1)}, bf16[4,2,256,128]{3,2,1,0:T(8,128)(2,1)S(1)}, u32[]{:S(2)}, u32[]{:S(2)}) %collective-permute-start.11) | collective-permute-done | bytes 524320 | tf_op jit(solution)/shard_map/ppermute | solution.py:174
  87.1 2.0 %collective-permute-start.12 = (bf16[2,256,128]{2,1,0:T(8,128)(2,1)S(1)}, bf16[2,256,128]{2,1,0:T(8,128)(2,1)S(1)}, u32[]{:S(2)}, u32[]{:S(2)}) collective-permute-start(bf16[2,256,128]{2,1,0:T(8,128)(2,1)S(1)} %get-tuple-element.28), channel_id=1, source_target_pairs={{0,1},{1,0},{2,3},{3,2},{4,5},{5,4},{6,7},{7,6},{8,9},{9,8},{10,11... | collective-permute-start | bytes 393224 | tf_op jit(solution)/shard_map/ppermute | solution.py:177
  89.1 4.3 %collective-permute-done.13.refs_1_ = bf16[2,256,128]{2,1,0:T(8,128)(2,1)S(1)} collective-permute-done((bf16[2,256,128]{2,1,0:T(8,128)(2,1)S(1)}, bf16[2,256,128]{2,1,0:T(8,128)(2,1)S(1)}, u32[]{:S(2)}, u32[]{:S(2)}) %collective-permute-start.13) | collective-permute-done | bytes 131104 | tf_op jit(solution)/shard_map/ppermute | solution.py:177
  93.5 1.0 %collective-permute-start.14 = (bf16[2,256,128]{2,1,0:T(8,128)(2,1)S(1)}, bf16[2,256,128]{2,1,0:T(8,128)(2,1)S(1)}, u32[]{:S(2)}, u32[]{:S(2)}) collective-permute-start(bf16[2,256,128]{2,1,0:T(8,128)(2,1)S(1)} %shard_map.52), channel_id=1, source_target_pairs={{0,2},{1,3},{2,0},{3,1},{4,6},{5,7},{6,4},{7,5},{8,10},{9,11},{10,... | collective-permute-start | bytes 393224 | tf_op jit(solution)/shard_map/ppermute | solution.py:177
  94.5 0.9 collective-permute-done.12.refs_1_
  95.5 5.7 %collective-permute-done.14.refs_1_ = bf16[2,256,128]{2,1,0:T(8,128)(2,1)S(1)} collective-permute-done((bf16[2,256,128]{2,1,0:T(8,128)(2,1)S(1)}, bf16[2,256,128]{2,1,0:T(8,128)(2,1)S(1)}, u32[]{:S(2)}, u32[]{:S(2)}) %collective-permute-start.14) | collective-permute-done | bytes 131104 | tf_op jit(solution)/shard_map/ppermute | solution.py:177
  101.3 1.3 %collective-permute-done.15.other_ref = bf16[2,256,128]{2,1,0:T(8,128)(2,1)S(1)} collective-permute-done((bf16[2,256,128]{2,1,0:T(8,128)(2,1)S(1)}, bf16[2,256,128]{2,1,0:T(8,128)(2,1)S(1)}, u32[]{:S(2)}, u32[]{:S(2)}) %collective-permute-start.15) | collective-permute-done | bytes 131104 | tf_op jit(solution)/shard_map/ppermute | solution.py:174
  102.6 1.3 %shard_map.54 = bf16[256,512]{1,0:T(8,128)(2,1)} custom-call(bf16[2,256,128]{2,1,0:T(8,128)(2,1)S(1)} %shard_map.53.own_ref, bf16[2,256,128]{2,1,0:T(8,128)(2,1)S(1)} %collective-permute-done.15.other_ref, s32[256,1]{1,0:T(8,128)S(1)} %copy.7.refs_15_.column_ref), custom_call_target="tpu_custom_call" | custom-call | tf_op jit(solution)/shard_map/pallas_call | solution.py:239
  (45 shorter events, 4.6 us)
Async XLA Ops:
  0.0 38.3 %copy-start.1 = (bf16[256,512]{1,0:T(8,128)(2,1)S(1)}, bf16[256,512]{1,0:T(8,128)(2,1)}, u32[]{:S(2)}) copy-start(bf16[256,512]{1,0:T(8,128)(2,1)} %refs_0_.1) | copy-start | bytes 786436
  33.7 30.4 %copy-start = (bf16[2,2064,128]{2,1,0:T(8,128)(2,1)S(1)}, bf16[2,2064,128]{2,1,0:T(8,128)(2,1)}, u32[]{:S(2)}) copy-start(bf16[2,2064,128]{2,1,0:T(8,128)(2,1)} %shard_map.46.refs_8_) | copy-start | bytes 3170308
  33.7 30.4 %copy-start.9 = (s32[256]{0:T(256)S(1)}, s32[256]{0:T(256)}, u32[]{:S(2)}) copy-start(s32[256]{0:T(256)} %param.7) | copy-start | bytes 3076
  33.8 28.1 %collective-permute-start.8 = (bf16[2,2064,128]{2,1,0:T(8,128)(2,1)}, bf16[2,2064,128]{2,1,0:T(8,128)(2,1)S(1)}, u32[]{:S(2)}, u32[]{:S(2)}) collective-permute-start(bf16[2,2064,128]{2,1,0:T(8,128)(2,1)} %shard_map.46.refs_8_), channel_id=1, source_target_pairs={{0,16},{4,20},{8,24},{12,28},{16,0},{20,4},{24,8},{28,12},{1,17},{... | collective-permute-start | bytes 3170312 | tf_op jit(solution)/shard_map/ppermute | solution.py:174
  36.8 25.1 %collective-permute-start.7 = (bf16[2,2064,128]{2,1,0:T(8,128)(2,1)}, bf16[2,2064,128]{2,1,0:T(8,128)(2,1)S(1)}, u32[]{:S(2)}, u32[]{:S(2)}) collective-permute-start(bf16[2,2064,128]{2,1,0:T(8,128)(2,1)} %shard_map.46.refs_8_), channel_id=1, source_target_pairs={{0,8},{4,12},{8,0},{12,4},{16,24},{20,28},{24,16},{28,20},{1,9},{5... | collective-permute-start | bytes 3170312 | tf_op jit(solution)/shard_map/ppermute | solution.py:174
  38.3 11.6 %collective-permute-start = (bf16[256,512]{1,0:T(8,128)(2,1)S(1)}, bf16[256,512]{1,0:T(8,128)(2,1)}, u32[]{:S(2)}, u32[]{:S(2)}) collective-permute-start(bf16[256,512]{1,0:T(8,128)(2,1)S(1)} %copy-done.1), channel_id=1, source_target_pairs={{0,1},{1,0},{2,3},{3,2},{4,5},{5,4},{6,7},{7,6},{8,9},{9,8},{10,11... | collective-permute-start | bytes 786440 | tf_op jit(solution)/shard_map/ppermute | solution.py:177
  39.9 10.0 %collective-permute-start.3 = (bf16[256,512]{1,0:T(8,128)(2,1)S(1)}, bf16[256,512]{1,0:T(8,128)(2,1)S(1)}, u32[]{:S(2)}, u32[]{:S(2)}) collective-permute-start(bf16[256,512]{1,0:T(8,128)(2,1)S(1)} %copy-done.1), channel_id=1, source_target_pairs={{0,4},{4,0},{8,12},{12,8},{16,20},{20,16},{24,28},{28,24},{1,5},{5... | collective-permute-start | bytes 786440 | tf_op jit(solution)/shard_map/ppermute | solution.py:174
  39.9 21.3 %collective-permute-start.1 = (bf16[256,512]{1,0:T(8,128)(2,1)S(1)}, bf16[256,512]{1,0:T(8,128)(2,1)S(1)}, u32[]{:S(2)}, u32[]{:S(2)}) collective-permute-start(bf16[256,512]{1,0:T(8,128)(2,1)S(1)} %copy-done.1), channel_id=1, source_target_pairs={{0,2},{1,3},{2,0},{3,1},{4,6},{5,7},{6,4},{7,5},{8,10},{9,11},{10,... | collective-permute-start | bytes 786440 | tf_op jit(solution)/shard_map/ppermute | solution.py:177
  49.9 11.3 %collective-permute-start.4 = (bf16[256,512]{1,0:T(8,128)(2,1)}, bf16[256,512]{1,0:T(8,128)(2,1)S(1)}, u32[]{:S(2)}, u32[]{:S(2)}) collective-permute-start(bf16[256,512]{1,0:T(8,128)(2,1)} %collective-permute-done.refs_1_), channel_id=1, source_target_pairs={{0,4},{4,0},{8,12},{12,8},{16,20},{20,16},{24,28},{28,24},{1,5},{5... | collective-permute-start | bytes 786440 | tf_op jit(solution)/shard_map/ppermute | solution.py:174
  49.9 13.8 %copy-start.3 = (bf16[256,512]{1,0:T(8,128)(2,1)}, bf16[256,512]{1,0:T(8,128)(2,1)S(1)}, u32[]{:S(2)}) copy-start(bf16[256,512]{1,0:T(8,128)(2,1)S(1)} %collective-permute-done.3.refs_4_) | copy-start | bytes 786436
  49.9 16.6 %collective-permute-start.2 = (bf16[256,512]{1,0:T(8,128)(2,1)}, bf16[256,512]{1,0:T(8,128)(2,1)}, u32[]{:S(2)}, u32[]{:S(2)}) collective-permute-start(bf16[256,512]{1,0:T(8,128)(2,1)} %collective-permute-done.refs_1_), channel_id=1, source_target_pairs={{0,2},{1,3},{2,0},{3,1},{4,6},{5,7},{6,4},{7,5},{8,10},{9,11},{10,... | collective-permute-start | bytes 786440 | tf_op jit(solution)/shard_map/ppermute | solution.py:177
  63.6 16.8 %collective-permute-start.9 = (bf16[2064,128]{1,0:T(8,128)(2,1)}, bf16[2064,128]{1,0:T(8,128)(2,1)}, u32[]{:S(2)}, u32[]{:S(2)}) collective-permute-start(bf16[2064,128]{1,0:T(8,128)(2,1)} %get-tuple-element.23), channel_id=1, source_target_pairs={{0,16},{4,20},{8,24},{12,28},{16,0},{20,4},{24,8},{28,12},{1,17},{... | collective-permute-start | bytes 1585160 | tf_op jit(solution)/shard_map/ppermute | solution.py:174
  64.3 2.8 %collective-permute-start.5 = (bf16[256,512]{1,0:T(8,128)(2,1)}, bf16[256,512]{1,0:T(8,128)(2,1)S(1)}, u32[]{:S(2)}, u32[]{:S(2)}) collective-permute-start(bf16[256,512]{1,0:T(8,128)(2,1)} %copy-done.5), channel_id=1, source_target_pairs={{0,4},{4,0},{8,12},{12,8},{16,20},{20,16},{24,28},{28,24},{1,5},{5... | collective-permute-start | bytes 786440 | tf_op jit(solution)/shard_map/ppermute | solution.py:174
  66.5 1.7 %collective-permute-start.6 = (bf16[256,512]{1,0:T(8,128)(2,1)}, bf16[256,512]{1,0:T(8,128)(2,1)S(1)}, u32[]{:S(2)}, u32[]{:S(2)}) collective-permute-start(bf16[256,512]{1,0:T(8,128)(2,1)} %collective-permute-done.2.refs_3_), channel_id=1, source_target_pairs={{0,4},{4,0},{8,12},{12,8},{16,20},{20,16},{24,28},{28,24},{1,5},{5... | collective-permute-start | bytes 786440 | tf_op jit(solution)/shard_map/ppermute | solution.py:174
  66.5 14.6 %collective-permute-start.10 = (bf16[2064,128]{1,0:T(8,128)(2,1)}, bf16[2064,128]{1,0:T(8,128)(2,1)S(1)}, u32[]{:S(2)}, u32[]{:S(2)}) collective-permute-start(bf16[2064,128]{1,0:T(8,128)(2,1)} %copy-done.10), channel_id=1, source_target_pairs={{0,8},{4,12},{8,0},{12,4},{16,24},{20,28},{24,16},{28,20},{1,9},{5... | collective-permute-start | bytes 1585160 | tf_op jit(solution)/shard_map/ppermute | solution.py:174
  68.2 1.0 copy-start.2
  69.2 0.9 copy-start.4
  70.1 0.9 copy-start.6
  71.1 0.9 copy-start.8
  84.9 2.0 %collective-permute-start.11 = (bf16[4,2,256,128]{3,2,1,0:T(8,128)(2,1)S(1)}, bf16[4,2,256,128]{3,2,1,0:T(8,128)(2,1)S(1)}, u32[]{:S(2)}, u32[]{:S(2)}) collective-permute-start(bf16[4,2,256,128]{3,2,1,0:T(8,128)(2,1)S(1)} %get-tuple-element.26), channel_id=1, source_target_pairs={{0,4},{4,0},{8,12},{12,8},{16,20},{20,16},{24,28},{28,24},{1,5},{5... | collective-permute-start | bytes 1572872 | tf_op jit(solution)/shard_map/ppermute | solution.py:174
  87.0 6.4 %collective-permute-start.13 = (bf16[2,256,128]{2,1,0:T(8,128)(2,1)S(1)}, bf16[2,256,128]{2,1,0:T(8,128)(2,1)S(1)}, u32[]{:S(2)}, u32[]{:S(2)}) collective-permute-start(bf16[2,256,128]{2,1,0:T(8,128)(2,1)S(1)} %get-tuple-element.30), channel_id=1, source_target_pairs={{0,1},{1,0},{2,3},{3,2},{4,5},{5,4},{6,7},{7,6},{8,9},{9,8},{10,11... | collective-permute-start | bytes 393224 | tf_op jit(solution)/shard_map/ppermute | solution.py:177
  87.1 8.3 %collective-permute-start.12 = (bf16[2,256,128]{2,1,0:T(8,128)(2,1)S(1)}, bf16[2,256,128]{2,1,0:T(8,128)(2,1)S(1)}, u32[]{:S(2)}, u32[]{:S(2)}) collective-permute-start(bf16[2,256,128]{2,1,0:T(8,128)(2,1)S(1)} %get-tuple-element.28), channel_id=1, source_target_pairs={{0,1},{1,0},{2,3},{3,2},{4,5},{5,4},{6,7},{7,6},{8,9},{9,8},{10,11... | collective-permute-start | bytes 393224 | tf_op jit(solution)/shard_map/ppermute | solution.py:177
  93.5 7.7 %collective-permute-start.14 = (bf16[2,256,128]{2,1,0:T(8,128)(2,1)S(1)}, bf16[2,256,128]{2,1,0:T(8,128)(2,1)S(1)}, u32[]{:S(2)}, u32[]{:S(2)}) collective-permute-start(bf16[2,256,128]{2,1,0:T(8,128)(2,1)S(1)} %shard_map.52), channel_id=1, source_target_pairs={{0,2},{1,3},{2,0},{3,1},{4,6},{5,7},{6,4},{7,5},{8,10},{9,11},{10,... | collective-permute-start | bytes 393224 | tf_op jit(solution)/shard_map/ppermute | solution.py:177
  101.2 1.4 %collective-permute-start.15 = (bf16[2,256,128]{2,1,0:T(8,128)(2,1)S(1)}, bf16[2,256,128]{2,1,0:T(8,128)(2,1)S(1)}, u32[]{:S(2)}, u32[]{:S(2)}) collective-permute-start(bf16[2,256,128]{2,1,0:T(8,128)(2,1)S(1)} %shard_map.53.own_ref), channel_id=1, source_target_pairs={{0,4},{4,0},{8,12},{12,8},{16,20},{20,16},{24,28},{28,24},{1,5},{5... | collective-permute-start | bytes 393224 | tf_op jit(solution)/shard_map/ppermute | solution.py:174
  (3 other events, 2.3 us)

commit v5 on v4

--- a/solution.py
+++ b/solution.py
@@ -40,7 +40,7 @@
     return iota((TILE, TILE), 0) == (1 - h) * SUB * SUB + b * SUB + a
 
 
-def pack_kernel(integrals_ref, blocks_ref, out_ref, ids_ref, sems):
+def pack_kernel(integrals_ref, blocks_ref, out_ref, sems):
     slabs, length = integrals_ref.shape[:2]
     copies = [
         pltpu.make_async_copy(integrals_ref.at[s], out_ref.at[s, pl.ds(0, length)], sems.at[s]) for s in range(slabs)
@@ -53,11 +53,7 @@
         for t in range(length // TILE):
             for which in range(2):
                 ids = jnp.where(lane == 2 * t + which, blocks_ref[s, which, t], ids)
-        ids_ref[s] = ids.astype(F32).astype(BF16)
-        copies.append(
-            pltpu.make_async_copy(ids_ref.at[s], out_ref.at[s, pl.ds(length, EXTRA)], sems.at[slabs + s])
-        )
-        copies[-1].start()
+        out_ref[s, length:, :] = ids.astype(F32).astype(BF16)
     for copy in copies:
         copy.wait()
 
@@ -179,18 +175,17 @@
     packed = call(
         pack_kernel,
         jax.ShapeDtypeStruct((slabs, length + EXTRA, TILE), BF16),
-        [pl.BlockSpec(memory_space=pl.ANY), SMEM],
-        [pltpu.VMEM((slabs, EXTRA, TILE), BF16), pltpu.SemaphoreType.DMA((2 * slabs,))],
-        out_specs=pl.BlockSpec(memory_space=pl.ANY),
-        megabytes=56,
+        [pl.BlockSpec(memory_space=pltpu.HBM), SMEM],
+        [pltpu.SemaphoreType.DMA((slabs,))],
+        megabytes=8,
     )(integrals.reshape(slabs, length, TILE), tile_blocks.transpose(0, 2, 1))
     early = [packed, across(packed, 2), across(packed, 4)]
 
     pieces = {0: amplitudes}
-    reach = 1
-    while reach < n_vir:
-        pieces |= {shift + reach: along(pieces[shift], reach) for shift in range(reach)}
-        reach *= 2
+    reach = n_vir // 2
+    while reach:
+        pieces |= {shift + reach: along(piece, reach) for shift, piece in pieces.items()}
+        reach //= 2
     mine = [pieces[shift] for shift in range(n_vir)]
     others = [across(piece, 1) for piece in mine]
     tiles_x, tiles_y, *_ = lax.optimization_barrier((*early[1:], *others[:2], *mine[:-1]))
@@ -226,16 +221,16 @@
     one = jax.ShapeDtypeStruct((per // 2, rows, TILE), BF16)
     parts = call(join_kernel, [one] * n_vir, [VMEM, VMEM], megabytes=8)(keep, across(send, 1))
     parts = dict(enumerate(parts))
-    reach = 1
+    reach, arrived = 1, []
     while reach < n_vir:
-        sent = [shift for shift in reversed(parts) if shift & reach]
-        arrived = {shift: along(parts.pop(shift), reach) for shift in sent}
-        for shift in sent:
-            kept = shift ^ reach
-            if 2 * reach < n_vir:
-                parts[kept] = call(total_kernel, one, [VMEM] * 2, megabytes=8)(parts[kept], arrived[shift])
+        far = {shift: along(parts[shift], reach) for shift in parts if shift & reach and shift > reach}
+        for shift, array in far.items():
+            parts[shift ^ reach] = call(total_kernel, one, [VMEM] * 2, megabytes=8)(parts[shift ^ reach], array)
+        near, *_ = lax.optimization_barrier((parts[reach], *far.values()))
+        arrived.append(along(near, reach))
+        parts = {shift: part for shift, part in parts.items() if not shift & reach}
         reach *= 2
-    total = call(total_kernel, one, [VMEM] * 2, megabytes=8)(parts[0], *arrived.values())
+    total = call(total_kernel, one, [VMEM] * (1 + len(arrived)), megabytes=8)(parts[0], *arrived)
     return call(
         finish_kernel, jax.ShapeDtypeStruct((rows, width), BF16), [VMEM] * 3, megabytes=8
     )(total, across(total, 1), column)

time: 104 us -> 72.5 us (0.70)
  Pallas kernels: 48.3 us -> 15.3 us
  waiting for transfers between devices: 35.6 us -> 29.2 us
  starting transfers between devices: 13.7 us -> 18 us
  local copies, waits for them, and re-layouts: 5.53 us -> 8.78 us
    pallas_call x1, Pallas kernels: 33.7 us -> 0.69 us  [local(): call(pack_kernel, jax.ShapeDtypeStruct((slabs, length + EXTRA, TILE), BF1...]
    ppermute x6, waiting for transfers between devices: 31.2 us -> 20 us  [along(): return lax.ppermute(array, 'vir', [(i, i ^ bits) for i in range(n_vir)])]
    ppermute x10, waiting for transfers between devices: 4.35 us -> 9.14 us  [across(): return lax.ppermute(array, 'pair', [(i, i ^ bits) for i in range(n_pair)])]
    unnamed x22 -> x24, local copies, waits for them, and re-layouts: 5.4 us -> 8.64 us
    ppermute x6, starting transfers between devices: 7.8 us -> 10.7 us  [along(): return lax.ppermute(array, 'vir', [(i, i ^ bits) for i in range(n_vir)])]
    ppermute x10, starting transfers between devices: 5.89 us -> 7.3 us  [across(): return lax.ppermute(array, 'pair', [(i, i ^ bits) for i in range(n_pair)])]
  transfers between devices with their start and end apart: 16 -> 16, of which waited for: 9 -> 9; matrix products, arithmetic and copies ran while one was open for 1% -> 1% of each run, Pallas kernels for 9% -> 13%
where the time goes in v5:
time: 72.5 us; the launch traced here: 72.1 us
  waiting for transfers between devices  29.2 us (40%)
  starting transfers between devices  18 us (25%)
  Pallas kernels  15.3 us (21%)
  local copies, waits for them, and re-layouts  8.78 us (12%)
    ppermute x6, waiting for transfers between devices, along(): return lax.ppermute(array, 'vir', [(i, i ^ bits) for i in range(n_vir)])  20 us
    ppermute x6, starting transfers between devices, along(): return lax.ppermute(array, 'vir', [(i, i ^ bits) for i in range(n_vir)])  10.7 us
    ppermute x10, waiting for transfers between devices, across(): return lax.ppermute(array, 'pair', [(i, i ^ bits) for i in range(n_pair)])  9.14 us
    unnamed x24, local copies, waits for them, and re-layouts  8.64 us
    pallas_call x1, Pallas kernels, local(): call(functools.partial(first_kernel, n_vir, len(early)), [jax.ShapeDtypeS...  8.42 us
    ppermute x10, starting transfers between devices, across(): return lax.ppermute(array, 'pair', [(i, i ^ bits) for i in range(n_pair)])  7.3 us
    pallas_call x1, Pallas kernels, local(): call(functools.partial(second_kernel, n_vir, len(late)), [piece, piece, s...  3.77 us
  transfers between devices with their start and end apart: 16, of which 9 were waited for; matrix products, arithmetic and copies ran while one was open for 1% of the time, Pallas kernels for 13%

profile of v5, /device:TPU:0, one launch (start us, length us, event | category | flops | bytes accessed | tf_op | source)
XLA Modules:
  0.0 72.1 jit_solution(9028042996916198340)
XLA Ops:
  0.0 1.2 %copy-done = bf16[2,16,128,128]{3,2,1,0:T(8,128)(2,1)S(1)} copy-done((bf16[2,16,128,128]{3,2,1,0:T(8,128)(2,1)S(1)}, bf16[2,16,128,128]{3,2,1,0:T(8,128)(2,1)}, u32[]{:S(2)}) %copy-start) | copy-done | bytes 1048600
  2.6 3.0 %collective-permute-start.8 = (bf16[2,2064,128]{2,1,0:T(8,128)(2,1)S(1)}, bf16[2,2064,128]{2,1,0:T(8,128)(2,1)S(1)}, u32[]{:S(2)}, u32[]{:S(2)}) collective-permute-start(bf16[2,2064,128]{2,1,0:T(8,128)(2,1)S(1)} %shard_map.46.refs_8_), channel_id=1, source_target_pairs={{0,16},{4,20},{8,24},{12,28},{16,0},{20,4},{24,8},{28,12},{1,17},{... | collective-permute-start | bytes 3170312 | tf_op jit(solution)/shard_map/ppermute | solution.py:170
  5.7 1.5 %collective-permute-start.7 = (bf16[2,2064,128]{2,1,0:T(8,128)(2,1)S(1)}, bf16[2,2064,128]{2,1,0:T(8,128)(2,1)S(1)}, u32[]{:S(2)}, u32[]{:S(2)}) collective-permute-start(bf16[2,2064,128]{2,1,0:T(8,128)(2,1)S(1)} %shard_map.46.refs_8_), channel_id=1, source_target_pairs={{0,8},{4,12},{8,0},{12,4},{16,24},{20,28},{24,16},{28,20},{1,9},{5... | collective-permute-start | bytes 3170312 | tf_op jit(solution)/shard_map/ppermute | solution.py:170
  7.1 1.6 %collective-permute-start = (bf16[256,512]{1,0:T(8,128)(2,1)S(1)}, bf16[256,512]{1,0:T(8,128)(2,1)S(1)}, u32[]{:S(2)}, u32[]{:S(2)}) collective-permute-start(bf16[256,512]{1,0:T(8,128)(2,1)S(1)} %copy-done.1), channel_id=1, source_target_pairs={{0,1},{1,0},{2,3},{3,2},{4,5},{5,4},{6,7},{7,6},{8,9},{9,8},{10,11... | collective-permute-start | bytes 786440 | tf_op jit(solution)/shard_map/ppermute | solution.py:173
  8.7 2.6 %collective-permute-start.1 = (bf16[256,512]{1,0:T(8,128)(2,1)S(1)}, bf16[256,512]{1,0:T(8,128)(2,1)}, u32[]{:S(2)}, u32[]{:S(2)}) collective-permute-start(bf16[256,512]{1,0:T(8,128)(2,1)S(1)} %copy-done.1), channel_id=1, source_target_pairs={{0,2},{1,3},{2,0},{3,1},{4,6},{5,7},{6,4},{7,5},{8,10},{9,11},{10,... | collective-permute-start | bytes 786440 | tf_op jit(solution)/shard_map/ppermute | solution.py:173
  11.3 8.8 %collective-permute-done.refs_1_ = bf16[256,512]{1,0:T(8,128)(2,1)S(1)} collective-permute-done((bf16[256,512]{1,0:T(8,128)(2,1)S(1)}, bf16[256,512]{1,0:T(8,128)(2,1)S(1)}, u32[]{:S(2)}, u32[]{:S(2)}) %collective-permute-start) | collective-permute-done | bytes 262176 | tf_op jit(solution)/shard_map/ppermute | solution.py:173
  20.8 1.8 %collective-permute-done.1.refs_2_ = bf16[256,512]{1,0:T(8,128)(2,1)} collective-permute-done((bf16[256,512]{1,0:T(8,128)(2,1)S(1)}, bf16[256,512]{1,0:T(8,128)(2,1)}, u32[]{:S(2)}, u32[]{:S(2)}) %collective-permute-start.1) | collective-permute-done | bytes 262176 | tf_op jit(solution)/shard_map/ppermute | solution.py:173
  24.5 4.5 %collective-permute-done.8.refs_10_.y_ref = bf16[2,2064,128]{2,1,0:T(8,128)(2,1)S(1)} collective-permute-done((bf16[2,2064,128]{2,1,0:T(8,128)(2,1)S(1)}, bf16[2,2064,128]{2,1,0:T(8,128)(2,1)S(1)}, u32[]{:S(2)}, u32[]{:S(2)}) %collective-permute-start.8) | collective-permute-done | bytes 1056800 | tf_op jit(solution)/shard_map/ppermute | solution.py:170
  29.0 1.5 %collective-permute-done.7.refs_9_.x_ref = bf16[2,2064,128]{2,1,0:T(8,128)(2,1)S(1)} collective-permute-done((bf16[2,2064,128]{2,1,0:T(8,128)(2,1)S(1)}, bf16[2,2064,128]{2,1,0:T(8,128)(2,1)S(1)}, u32[]{:S(2)}, u32[]{:S(2)}) %collective-permute-start.7) | collective-permute-done | bytes 1056800 | tf_op jit(solution)/shard_map/ppermute | solution.py:170
  33.2 1.6 %collective-permute-start.10 = (bf16[2064,128]{1,0:T(8,128)(2,1)}, bf16[2064,128]{1,0:T(8,128)(2,1)S(1)}, u32[]{:S(2)}, u32[]{:S(2)}) collective-permute-start(bf16[2064,128]{1,0:T(8,128)(2,1)} %copy-done.11), channel_id=1, source_target_pairs={{0,8},{4,12},{8,0},{12,4},{16,24},{20,28},{24,16},{28,20},{1,9},{5... | collective-permute-start | bytes 1585160 | tf_op jit(solution)/shard_map/ppermute | solution.py:170
  35.8 0.9 %copy-done.4 = bf16[256,512]{1,0:T(8,128)(2,1)S(1)} copy-done((bf16[256,512]{1,0:T(8,128)(2,1)S(1)}, bf16[256,512]{1,0:T(8,128)(2,1)}, u32[]{:S(2)}) %copy-start.4) | copy-done | bytes 262168
  36.8 0.9 %copy-done.6 = bf16[256,512]{1,0:T(8,128)(2,1)S(1)} copy-done((bf16[256,512]{1,0:T(8,128)(2,1)S(1)}, bf16[256,512]{1,0:T(8,128)(2,1)}, u32[]{:S(2)}) %copy-start.6) | copy-done | bytes 262168
  37.7 0.9 %copy-done.8 = bf16[256,512]{1,0:T(8,128)(2,1)S(1)} copy-done((bf16[256,512]{1,0:T(8,128)(2,1)S(1)}, bf16[256,512]{1,0:T(8,128)(2,1)}, u32[]{:S(2)}) %copy-start.8) | copy-done | bytes 262168
  38.7 8.4 %shard_map.47 = (bf16[16,512,128]{2,1,0:T(8,128)(2,1)S(1)}, f32[16,512,128]{2,1,0:T(8,128)S(1)}, f32[16,512,128]{2,1,0:T(8,128)S(1)}) custom-call(bf16[256,512]{1,0:T(8,128)(2,1)S(1)} %copy-done.2, bf16[256,512]{1,0:T(8,128)(2,1)S(1)} %copy-done.4, bf16[256,512]{1,0:T(8,128)(2,1)} %collective-permute-done.1.refs_2_, ...), custom_call_target="tpu_custom_call" | custom-call | tf_op jit(solution)/shard_map/pallas_call | solution.py:207
  47.8 3.8 %shard_map.49 = (bf16[4,2,256,128]{3,2,1,0:T(8,128)(2,1)S(1)}, bf16[4,2,256,128]{3,2,1,0:T(8,128)(2,1)S(1)}, f32[16,512,128]{2,1,0:T(8,128)S(1)}, f32[16,512,128]{2,1,0:T(8,128)S(1)}) custom-call(bf16[16,512,128]{2,1,0:T(8,128)(2,1)S(1)} %get-tuple-element.19.refs_0_, ...), custom_call_target="tpu_custom_call", output_to_operand_aliasing={{2}: (1, {}), {3}: (2, {})} | custom-call | tf_op jit(solution)/shard_map/pallas_call | solution.py:214
  51.7 1.8 %collective-permute-done.11.come_ref = bf16[4,2,256,128]{3,2,1,0:T(8,128)(2,1)S(1)} collective-permute-done((bf16[4,2,256,128]{3,2,1,0:T(8,128)(2,1)S(1)}, bf16[4,2,256,128]{3,2,1,0:T(8,128)(2,1)S(1)}, u32[]{:S(2)}, u32[]{:S(2)}) %collective-permute-start.11) | collective-permute-done | bytes 524320 | tf_op jit(solution)/shard_map/ppermute | solution.py:170
  53.7 1.8 %collective-permute-start.12 = (bf16[2,256,128]{2,1,0:T(8,128)(2,1)S(1)}, bf16[2,256,128]{2,1,0:T(8,128)(2,1)S(1)}, u32[]{:S(2)}, u32[]{:S(2)}) collective-permute-start(bf16[2,256,128]{2,1,0:T(8,128)(2,1)S(1)} %get-tuple-element.30), channel_id=1, source_target_pairs={{0,1},{1,0},{2,3},{3,2},{4,5},{5,4},{6,7},{7,6},{8,9},{9,8},{10,11... | collective-permute-start | bytes 393224 | tf_op jit(solution)/shard_map/ppermute | solution.py:173
  55.4 3.9 %collective-permute-done.12.refs_1_ = bf16[2,256,128]{2,1,0:T(8,128)(2,1)S(1)} collective-permute-done((bf16[2,256,128]{2,1,0:T(8,128)(2,1)S(1)}, bf16[2,256,128]{2,1,0:T(8,128)(2,1)S(1)}, u32[]{:S(2)}, u32[]{:S(2)}) %collective-permute-start.12) | collective-permute-done | bytes 131104 | tf_op jit(solution)/shard_map/ppermute | solution.py:173
  59.3 1.8 %collective-permute-start.13 = (bf16[2,256,128]{2,1,0:T(8,128)(2,1)S(1)}, bf16[2,256,128]{2,1,0:T(8,128)(2,1)S(1)}, u32[]{:S(2)}, u32[]{:S(2)}) collective-permute-start(bf16[2,256,128]{2,1,0:T(8,128)(2,1)S(1)} %get-tuple-element.31), channel_id=1, source_target_pairs={{0,1},{1,0},{2,3},{3,2},{4,5},{5,4},{6,7},{7,6},{8,9},{9,8},{10,11... | collective-permute-start | bytes 393224 | tf_op jit(solution)/shard_map/ppermute | solution.py:173
  61.1 2.6 %collective-permute-start.14 = (bf16[2,256,128]{2,1,0:T(8,128)(2,1)S(1)}, bf16[2,256,128]{2,1,0:T(8,128)(2,1)S(1)}, u32[]{:S(2)}, u32[]{:S(2)}) collective-permute-start(bf16[2,256,128]{2,1,0:T(8,128)(2,1)S(1)} %shard_map.51), channel_id=1, source_target_pairs={{0,2},{1,3},{2,0},{3,1},{4,6},{5,7},{6,4},{7,5},{8,10},{9,11},{10,... | collective-permute-start | bytes 393224 | tf_op jit(solution)/shard_map/ppermute | solution.py:173
  63.6 2.3 %collective-permute-done.13.refs_1_ = bf16[2,256,128]{2,1,0:T(8,128)(2,1)S(1)} collective-permute-done((bf16[2,256,128]{2,1,0:T(8,128)(2,1)S(1)}, bf16[2,256,128]{2,1,0:T(8,128)(2,1)S(1)}, u32[]{:S(2)}, u32[]{:S(2)}) %collective-permute-start.13) | collective-permute-done | bytes 131104 | tf_op jit(solution)/shard_map/ppermute | solution.py:173
  65.9 3.4 %collective-permute-done.14.refs_2_ = bf16[2,256,128]{2,1,0:T(8,128)(2,1)S(1)} collective-permute-done((bf16[2,256,128]{2,1,0:T(8,128)(2,1)S(1)}, bf16[2,256,128]{2,1,0:T(8,128)(2,1)S(1)}, u32[]{:S(2)}, u32[]{:S(2)}) %collective-permute-start.14) | collective-permute-done | bytes 131104 | tf_op jit(solution)/shard_map/ppermute | solution.py:173
  69.4 1.3 %collective-permute-done.15.other_ref = bf16[2,256,128]{2,1,0:T(8,128)(2,1)S(1)} collective-permute-done((bf16[2,256,128]{2,1,0:T(8,128)(2,1)S(1)}, bf16[2,256,128]{2,1,0:T(8,128)(2,1)S(1)}, u32[]{:S(2)}, u32[]{:S(2)}) %collective-permute-start.15) | collective-permute-done | bytes 131104 | tf_op jit(solution)/shard_map/ppermute | solution.py:170
  70.7 1.3 %shard_map.53 = bf16[256,512]{1,0:T(8,128)(2,1)} custom-call(bf16[2,256,128]{2,1,0:T(8,128)(2,1)S(1)} %shard_map.52.own_ref, bf16[2,256,128]{2,1,0:T(8,128)(2,1)S(1)} %collective-permute-done.15.other_ref, s32[256,1]{1,0:T(8,128)S(1)} %copy.7.refs_15_.column_ref), custom_call_target="tpu_custom_call" | custom-call | tf_op jit(solution)/shard_map/pallas_call | solution.py:234
  (46 shorter events, 8.8 us)
Async XLA Ops:
  0.0 1.2 %copy-start = (bf16[2,16,128,128]{3,2,1,0:T(8,128)(2,1)S(1)}, bf16[2,16,128,128]{3,2,1,0:T(8,128)(2,1)}, u32[]{:S(2)}) copy-start(bf16[2,16,128,128]{3,2,1,0:T(8,128)(2,1)} %param.5) | copy-start | bytes 3145732
  1.9 5.2 %copy-start.1 = (bf16[256,512]{1,0:T(8,128)(2,1)S(1)}, bf16[256,512]{1,0:T(8,128)(2,1)}, u32[]{:S(2)}) copy-start(bf16[256,512]{1,0:T(8,128)(2,1)} %refs_0_.1) | copy-start | bytes 786436
  2.6 29.9 %copy-start.9 = (s32[256]{0:T(256)S(1)}, s32[256]{0:T(256)}, u32[]{:S(2)}) copy-start(s32[256]{0:T(256)} %param.7) | copy-start | bytes 3076
  2.6 26.4 %collective-permute-start.8 = (bf16[2,2064,128]{2,1,0:T(8,128)(2,1)S(1)}, bf16[2,2064,128]{2,1,0:T(8,128)(2,1)S(1)}, u32[]{:S(2)}, u32[]{:S(2)}) collective-permute-start(bf16[2,2064,128]{2,1,0:T(8,128)(2,1)S(1)} %shard_map.46.refs_8_), channel_id=1, source_target_pairs={{0,16},{4,20},{8,24},{12,28},{16,0},{20,4},{24,8},{28,12},{1,17},{... | collective-permute-start | bytes 3170312 | tf_op jit(solution)/shard_map/ppermute | solution.py:170
  5.7 24.8 %collective-permute-start.7 = (bf16[2,2064,128]{2,1,0:T(8,128)(2,1)S(1)}, bf16[2,2064,128]{2,1,0:T(8,128)(2,1)S(1)}, u32[]{:S(2)}, u32[]{:S(2)}) collective-permute-start(bf16[2,2064,128]{2,1,0:T(8,128)(2,1)S(1)} %shard_map.46.refs_8_), channel_id=1, source_target_pairs={{0,8},{4,12},{8,0},{12,4},{16,24},{20,28},{24,16},{28,20},{1,9},{5... | collective-permute-start | bytes 3170312 | tf_op jit(solution)/shard_map/ppermute | solution.py:170
  7.1 13.0 %collective-permute-start = (bf16[256,512]{1,0:T(8,128)(2,1)S(1)}, bf16[256,512]{1,0:T(8,128)(2,1)S(1)}, u32[]{:S(2)}, u32[]{:S(2)}) collective-permute-start(bf16[256,512]{1,0:T(8,128)(2,1)S(1)} %copy-done.1), channel_id=1, source_target_pairs={{0,1},{1,0},{2,3},{3,2},{4,5},{5,4},{6,7},{7,6},{8,9},{9,8},{10,11... | collective-permute-start | bytes 786440 | tf_op jit(solution)/shard_map/ppermute | solution.py:173
  8.7 13.9 %collective-permute-start.1 = (bf16[256,512]{1,0:T(8,128)(2,1)S(1)}, bf16[256,512]{1,0:T(8,128)(2,1)}, u32[]{:S(2)}, u32[]{:S(2)}) collective-permute-start(bf16[256,512]{1,0:T(8,128)(2,1)S(1)} %copy-done.1), channel_id=1, source_target_pairs={{0,2},{1,3},{2,0},{3,1},{4,6},{5,7},{6,4},{7,5},{8,10},{9,11},{10,... | collective-permute-start | bytes 786440 | tf_op jit(solution)/shard_map/ppermute | solution.py:173
  11.3 11.7 %collective-permute-start.3 = (bf16[256,512]{1,0:T(8,128)(2,1)S(1)}, bf16[256,512]{1,0:T(8,128)(2,1)S(1)}, u32[]{:S(2)}, u32[]{:S(2)}) collective-permute-start(bf16[256,512]{1,0:T(8,128)(2,1)S(1)} %copy-done.1), channel_id=1, source_target_pairs={{0,4},{4,0},{8,12},{12,8},{16,20},{20,16},{24,28},{28,24},{1,5},{5... | collective-permute-start | bytes 786440 | tf_op jit(solution)/shard_map/ppermute | solution.py:170
  20.1 3.6 %collective-permute-start.4 = (bf16[256,512]{1,0:T(8,128)(2,1)S(1)}, bf16[256,512]{1,0:T(8,128)(2,1)S(1)}, u32[]{:S(2)}, u32[]{:S(2)}) collective-permute-start(bf16[256,512]{1,0:T(8,128)(2,1)S(1)} %collective-permute-done.refs_1_), channel_id=1, source_target_pairs={{0,4},{4,0},{8,12},{12,8},{16,20},{20,16},{24,28},{28,24},{1,5},{5... | collective-permute-start | bytes 786440 | tf_op jit(solution)/shard_map/ppermute | solution.py:170
  22.6 10.1 %collective-permute-start.2 = (bf16[256,512]{1,0:T(8,128)(2,1)}, bf16[256,512]{1,0:T(8,128)(2,1)}, u32[]{:S(2)}, u32[]{:S(2)}) collective-permute-start(bf16[256,512]{1,0:T(8,128)(2,1)} %collective-permute-done.1.refs_2_), channel_id=1, source_target_pairs={{0,1},{1,0},{2,3},{3,2},{4,5},{5,4},{6,7},{7,6},{8,9},{9,8},{10,11... | collective-permute-start | bytes 786440 | tf_op jit(solution)/shard_map/ppermute | solution.py:173
  31.3 0.8 %copy-start.11 = (bf16[2064,128]{1,0:T(8,128)(2,1)}, bf16[2064,128]{1,0:T(8,128)(2,1)S(1)}, u32[]{:S(2)}) copy-start(bf16[2064,128]{1,0:T(8,128)(2,1)S(1)} %get-tuple-element.25) | copy-start | bytes 1585156
  32.1 15.0 %collective-permute-start.9 = (bf16[2064,128]{1,0:T(8,128)(2,1)}, bf16[2064,128]{1,0:T(8,128)(2,1)}, u32[]{:S(2)}, u32[]{:S(2)}) collective-permute-start(bf16[2064,128]{1,0:T(8,128)(2,1)} %get-tuple-element.24), channel_id=1, source_target_pairs={{0,16},{4,20},{8,24},{12,28},{16,0},{20,4},{24,8},{28,12},{1,17},{... | collective-permute-start | bytes 1585160 | tf_op jit(solution)/shard_map/ppermute | solution.py:170
  32.6 2.2 %collective-permute-start.5 = (bf16[256,512]{1,0:T(8,128)(2,1)}, bf16[256,512]{1,0:T(8,128)(2,1)S(1)}, u32[]{:S(2)}, u32[]{:S(2)}) collective-permute-start(bf16[256,512]{1,0:T(8,128)(2,1)} %collective-permute-done.1.refs_2_), channel_id=1, source_target_pairs={{0,4},{4,0},{8,12},{12,8},{16,20},{20,16},{24,28},{28,24},{1,5},{5... | collective-permute-start | bytes 786440 | tf_op jit(solution)/shard_map/ppermute | solution.py:170
  32.7 2.1 %collective-permute-start.6 = (bf16[256,512]{1,0:T(8,128)(2,1)}, bf16[256,512]{1,0:T(8,128)(2,1)S(1)}, u32[]{:S(2)}, u32[]{:S(2)}) collective-permute-start(bf16[256,512]{1,0:T(8,128)(2,1)} %collective-permute-done.2.refs_3_), channel_id=1, source_target_pairs={{0,4},{4,0},{8,12},{12,8},{16,20},{20,16},{24,28},{28,24},{1,5},{5... | collective-permute-start | bytes 786440 | tf_op jit(solution)/shard_map/ppermute | solution.py:170
  33.2 14.6 %collective-permute-start.10 = (bf16[2064,128]{1,0:T(8,128)(2,1)}, bf16[2064,128]{1,0:T(8,128)(2,1)S(1)}, u32[]{:S(2)}, u32[]{:S(2)}) collective-permute-start(bf16[2064,128]{1,0:T(8,128)(2,1)} %copy-done.11), channel_id=1, source_target_pairs={{0,8},{4,12},{8,0},{12,4},{16,24},{20,28},{24,16},{28,20},{1,9},{5... | collective-permute-start | bytes 1585160 | tf_op jit(solution)/shard_map/ppermute | solution.py:170
  34.9 1.0 %copy-start.2 = (bf16[256,512]{1,0:T(8,128)(2,1)S(1)}, bf16[256,512]{1,0:T(8,128)(2,1)}, u32[]{:S(2)}) copy-start(bf16[256,512]{1,0:T(8,128)(2,1)} %refs_0_.1) | copy-start | bytes 786436
  35.8 0.9 %copy-start.4 = (bf16[256,512]{1,0:T(8,128)(2,1)S(1)}, bf16[256,512]{1,0:T(8,128)(2,1)}, u32[]{:S(2)}) copy-start(bf16[256,512]{1,0:T(8,128)(2,1)} %copy-done.3) | copy-start | bytes 786436
  36.8 0.9 %copy-start.6 = (bf16[256,512]{1,0:T(8,128)(2,1)S(1)}, bf16[256,512]{1,0:T(8,128)(2,1)}, u32[]{:S(2)}) copy-start(bf16[256,512]{1,0:T(8,128)(2,1)} %copy-done.5) | copy-start | bytes 786436
  37.7 0.9 %copy-start.8 = (bf16[256,512]{1,0:T(8,128)(2,1)S(1)}, bf16[256,512]{1,0:T(8,128)(2,1)}, u32[]{:S(2)}) copy-start(bf16[256,512]{1,0:T(8,128)(2,1)} %copy-done.7) | copy-start | bytes 786436
  51.6 2.0 %collective-permute-start.11 = (bf16[4,2,256,128]{3,2,1,0:T(8,128)(2,1)S(1)}, bf16[4,2,256,128]{3,2,1,0:T(8,128)(2,1)S(1)}, u32[]{:S(2)}, u32[]{:S(2)}) collective-permute-start(bf16[4,2,256,128]{3,2,1,0:T(8,128)(2,1)S(1)} %get-tuple-element.27), channel_id=1, source_target_pairs={{0,4},{4,0},{8,12},{12,8},{16,20},{20,16},{24,28},{28,24},{1,5},{5... | collective-permute-start | bytes 1572872 | tf_op jit(solution)/shard_map/ppermute | solution.py:170
  53.7 5.6 %collective-permute-start.12 = (bf16[2,256,128]{2,1,0:T(8,128)(2,1)S(1)}, bf16[2,256,128]{2,1,0:T(8,128)(2,1)S(1)}, u32[]{:S(2)}, u32[]{:S(2)}) collective-permute-start(bf16[2,256,128]{2,1,0:T(8,128)(2,1)S(1)} %get-tuple-element.30), channel_id=1, source_target_pairs={{0,1},{1,0},{2,3},{3,2},{4,5},{5,4},{6,7},{7,6},{8,9},{9,8},{10,11... | collective-permute-start | bytes 393224 | tf_op jit(solution)/shard_map/ppermute | solution.py:173
  59.3 6.6 %collective-permute-start.13 = (bf16[2,256,128]{2,1,0:T(8,128)(2,1)S(1)}, bf16[2,256,128]{2,1,0:T(8,128)(2,1)S(1)}, u32[]{:S(2)}, u32[]{:S(2)}) collective-permute-start(bf16[2,256,128]{2,1,0:T(8,128)(2,1)S(1)} %get-tuple-element.31), channel_id=1, source_target_pairs={{0,1},{1,0},{2,3},{3,2},{4,5},{5,4},{6,7},{7,6},{8,9},{9,8},{10,11... | collective-permute-start | bytes 393224 | tf_op jit(solution)/shard_map/ppermute | solution.py:173
  61.1 8.2 %collective-permute-start.14 = (bf16[2,256,128]{2,1,0:T(8,128)(2,1)S(1)}, bf16[2,256,128]{2,1,0:T(8,128)(2,1)S(1)}, u32[]{:S(2)}, u32[]{:S(2)}) collective-permute-start(bf16[2,256,128]{2,1,0:T(8,128)(2,1)S(1)} %shard_map.51), channel_id=1, source_target_pairs={{0,2},{1,3},{2,0},{3,1},{4,6},{5,7},{6,4},{7,5},{8,10},{9,11},{10,... | collective-permute-start | bytes 393224 | tf_op jit(solution)/shard_map/ppermute | solution.py:173
  69.3 1.4 %collective-permute-start.15 = (bf16[2,256,128]{2,1,0:T(8,128)(2,1)S(1)}, bf16[2,256,128]{2,1,0:T(8,128)(2,1)S(1)}, u32[]{:S(2)}, u32[]{:S(2)}) collective-permute-start(bf16[2,256,128]{2,1,0:T(8,128)(2,1)S(1)} %shard_map.52.own_ref), channel_id=1, source_target_pairs={{0,4},{4,0},{8,12},{12,8},{16,20},{20,16},{24,28},{28,24},{1,5},{5... | collective-permute-start | bytes 393224 | tf_op jit(solution)/shard_map/ppermute | solution.py:170
  (4 other events, 2.8 us)

commit v6 on v5

--- a/solution.py
+++ b/solution.py
@@ -188,9 +188,9 @@
         reach //= 2
     mine = [pieces[shift] for shift in range(n_vir)]
     others = [across(piece, 1) for piece in mine]
-    tiles_x, tiles_y, *_ = lax.optimization_barrier((*early[1:], *others[:2], *mine[:-1]))
+    tiles_x, tiles_y, *_ = lax.optimization_barrier((*early[1:], *others[:-1], *mine[:-1]))
     slab = jax.ShapeDtypeStruct((length + EXTRA, TILE), BF16)
-    halves = call(cut_kernel, [slab] * slabs, [VMEM, VMEM], megabytes=8)(tiles_x, tiles_y)
+    halves = call(cut_kernel, [slab] * slabs, [VMEM, VMEM], megabytes=4)(tiles_x, tiles_y)
     late = [across(half, 4 if s % 2 == 0 else 2) for s, half in enumerate(halves)]
     reach = 4
     while reach < chips:
@@ -208,29 +208,20 @@
         functools.partial(first_kernel, n_vir, len(early)),
         [jax.ShapeDtypeStruct((n_blk, 2 * rows, TILE), BF16), sums, sums],
         [VMEM] * (2 * n_vir + len(early)) + [SMEM] * len(early) + [VMEM, VMEM],
-        megabytes=32,
+        megabytes=20,
     )(*mine, *others, *early, *[ids(array) for array in early], row, column)
     piece = jax.ShapeDtypeStruct((n_vir, per // 2, rows, TILE), BF16)
     keep, send, *_ = call(
         functools.partial(second_kernel, n_vir, len(late)),
         [piece, piece, sums, sums],
         [VMEM] * (3 + len(late)) + [SMEM] * len(late),
-        megabytes=32,
+        megabytes=24,
         aliases={1: 2, 2: 3},
     )(grid, *sums_so_far, *late, *[ids(array) for array in late])
     one = jax.ShapeDtypeStruct((per // 2, rows, TILE), BF16)
-    parts = call(join_kernel, [one] * n_vir, [VMEM, VMEM], megabytes=8)(keep, across(send, 1))
-    parts = dict(enumerate(parts))
-    reach, arrived = 1, []
-    while reach < n_vir:
-        far = {shift: along(parts[shift], reach) for shift in parts if shift & reach and shift > reach}
-        for shift, array in far.items():
-            parts[shift ^ reach] = call(total_kernel, one, [VMEM] * 2, megabytes=8)(parts[shift ^ reach], array)
-        near, *_ = lax.optimization_barrier((parts[reach], *far.values()))
-        arrived.append(along(near, reach))
-        parts = {shift: part for shift, part in parts.items() if not shift & reach}
-        reach *= 2
-    total = call(total_kernel, one, [VMEM] * (1 + len(arrived)), megabytes=8)(parts[0], *arrived)
+    parts = call(join_kernel, [one] * n_vir, [VMEM, VMEM], megabytes=4)(keep, across(send, 1))
+    arrived = [along(parts[shift], shift) for shift in range(n_vir - 1, 0, -1)]
+    total = call(total_kernel, one, [VMEM] * n_vir, megabytes=4)(parts[0], *arrived)
     return call(
         finish_kernel, jax.ShapeDtypeStruct((rows, width), BF16), [VMEM] * 3, megabytes=8
     )(total, across(total, 1), column)

time: 72.5 us -> 72.6 us (level)
  local copies, waits for them, and re-layouts: 8.78 us -> 10.4 us
  starting transfers between devices: 18 us -> 17 us
    unnamed x24 -> x28, local copies, waits for them, and re-layouts: 8.64 us -> 10.3 us
    ppermute x10, waiting for transfers between devices: 9.14 us -> 7.88 us  [across(): return lax.ppermute(array, 'pair', [(i, i ^ bits) for i in range(n_pair)])]
    ppermute x6, starting transfers between devices: 10.7 us -> 9.63 us  [along(): return lax.ppermute(array, 'vir', [(i, i ^ bits) for i in range(n_vir)])]
    ppermute x6, waiting for transfers between devices: 20 us -> 20.9 us  [along(): return lax.ppermute(array, 'vir', [(i, i ^ bits) for i in range(n_vir)])]
  transfers between devices with their start and end apart: 16 -> 16, of which waited for: 9 -> 8; matrix products, arithmetic and copies ran while one was open for 1% -> 1% of each run, Pallas kernels for 13% -> 13%
where the time goes in v6:
time: 72.6 us; the launch traced here: 72.2 us
  waiting for transfers between devices  28.7 us (40%)
  starting transfers between devices  17 us (23%)
  Pallas kernels  15.3 us (21%)
  local copies, waits for them, and re-layouts  10.4 us (14%)
    ppermute x6, waiting for transfers between devices, along(): return lax.ppermute(array, 'vir', [(i, i ^ bits) for i in range(n_vir)])  20.9 us
    unnamed x28, local copies, waits for them, and re-layouts  10.3 us
    ppermute x6, starting transfers between devices, along(): return lax.ppermute(array, 'vir', [(i, i ^ bits) for i in range(n_vir)])  9.63 us
    pallas_call x1, Pallas kernels, local(): call(functools.partial(first_kernel, n_vir, len(early)), [jax.ShapeDtypeS...  8.45 us
    ppermute x10, waiting for transfers between devices, across(): return lax.ppermute(array, 'pair', [(i, i ^ bits) for i in range(n_pair)])  7.88 us
    ppermute x10, starting transfers between devices, across(): return lax.ppermute(array, 'pair', [(i, i ^ bits) for i in range(n_pair)])  7.34 us
    pallas_call x1, Pallas kernels, local(): call(functools.partial(second_kernel, n_vir, len(late)), [piece, piece, s...  3.78 us
  transfers between devices with their start and end apart: 16, of which 8 were waited for; matrix products, arithmetic and copies ran while one was open for 1% of the time, Pallas kernels for 13%

profile of v6, /device:TPU:0, one launch (start us, length us, event | category | flops | bytes accessed | tf_op | source)
XLA Modules:
  0.0 72.2 jit_solution(16484022353088405060)
XLA Ops:
  0.0 1.2 %copy-done = bf16[2,16,128,128]{3,2,1,0:T(8,128)(2,1)S(1)} copy-done((bf16[2,16,128,128]{3,2,1,0:T(8,128)(2,1)S(1)}, bf16[2,16,128,128]{3,2,1,0:T(8,128)(2,1)}, u32[]{:S(2)}) %copy-start) | copy-done | bytes 1048600
  2.6 3.0 %collective-permute-start.8 = (bf16[2,2064,128]{2,1,0:T(8,128)(2,1)S(1)}, bf16[2,2064,128]{2,1,0:T(8,128)(2,1)S(1)}, u32[]{:S(2)}, u32[]{:S(2)}) collective-permute-start(bf16[2,2064,128]{2,1,0:T(8,128)(2,1)S(1)} %shard_map.46.refs_8_), channel_id=1, source_target_pairs={{0,16},{4,20},{8,24},{12,28},{16,0},{20,4},{24,8},{28,12},{1,17},{... | collective-permute-start | bytes 3170312 | tf_op jit(solution)/shard_map/ppermute | solution.py:170
  5.7 1.5 %collective-permute-start.7 = (bf16[2,2064,128]{2,1,0:T(8,128)(2,1)S(1)}, bf16[2,2064,128]{2,1,0:T(8,128)(2,1)S(1)}, u32[]{:S(2)}, u32[]{:S(2)}) collective-permute-start(bf16[2,2064,128]{2,1,0:T(8,128)(2,1)S(1)} %shard_map.46.refs_8_), channel_id=1, source_target_pairs={{0,8},{4,12},{8,0},{12,4},{16,24},{20,28},{24,16},{28,20},{1,9},{5... | collective-permute-start | bytes 3170312 | tf_op jit(solution)/shard_map/ppermute | solution.py:170
  7.1 2.6 %collective-permute-start.1 = (bf16[256,512]{1,0:T(8,128)(2,1)S(1)}, bf16[256,512]{1,0:T(8,128)(2,1)}, u32[]{:S(2)}, u32[]{:S(2)}) collective-permute-start(bf16[256,512]{1,0:T(8,128)(2,1)S(1)} %copy-done.1), channel_id=1, source_target_pairs={{0,2},{1,3},{2,0},{3,1},{4,6},{5,7},{6,4},{7,5},{8,10},{9,11},{10,... | collective-permute-start | bytes 786440 | tf_op jit(solution)/shard_map/ppermute | solution.py:173
  9.7 1.6 %collective-permute-start = (bf16[256,512]{1,0:T(8,128)(2,1)S(1)}, bf16[256,512]{1,0:T(8,128)(2,1)S(1)}, u32[]{:S(2)}, u32[]{:S(2)}) collective-permute-start(bf16[256,512]{1,0:T(8,128)(2,1)S(1)} %copy-done.1), channel_id=1, source_target_pairs={{0,1},{1,0},{2,3},{3,2},{4,5},{5,4},{6,7},{7,6},{8,9},{9,8},{10,11... | collective-permute-start | bytes 786440 | tf_op jit(solution)/shard_map/ppermute | solution.py:173
  11.3 10.0 %collective-permute-done.1.refs_2_ = bf16[256,512]{1,0:T(8,128)(2,1)} collective-permute-done((bf16[256,512]{1,0:T(8,128)(2,1)S(1)}, bf16[256,512]{1,0:T(8,128)(2,1)}, u32[]{:S(2)}, u32[]{:S(2)}) %collective-permute-start.1) | collective-permute-done | bytes 262176 | tf_op jit(solution)/shard_map/ppermute | solution.py:173
  23.3 1.0 %collective-permute-start.2 = (bf16[256,512]{1,0:T(8,128)(2,1)}, bf16[256,512]{1,0:T(8,128)(2,1)}, u32[]{:S(2)}, u32[]{:S(2)}) collective-permute-start(bf16[256,512]{1,0:T(8,128)(2,1)} %collective-permute-done.1.refs_2_), channel_id=1, source_target_pairs={{0,1},{1,0},{2,3},{3,2},{4,5},{5,4},{6,7},{7,6},{8,9},{9,8},{10,11... | collective-permute-start | bytes 786440 | tf_op jit(solution)/shard_map/ppermute | solution.py:173
  25.7 3.3 %collective-permute-done.8.refs_10_.y_ref = bf16[2,2064,128]{2,1,0:T(8,128)(2,1)S(1)} collective-permute-done((bf16[2,2064,128]{2,1,0:T(8,128)(2,1)S(1)}, bf16[2,2064,128]{2,1,0:T(8,128)(2,1)S(1)}, u32[]{:S(2)}, u32[]{:S(2)}) %collective-permute-start.8) | collective-permute-done | bytes 1056800 | tf_op jit(solution)/shard_map/ppermute | solution.py:170
  29.0 1.5 %collective-permute-done.7.refs_9_.x_ref = bf16[2,2064,128]{2,1,0:T(8,128)(2,1)S(1)} collective-permute-done((bf16[2,2064,128]{2,1,0:T(8,128)(2,1)S(1)}, bf16[2,2064,128]{2,1,0:T(8,128)(2,1)S(1)}, u32[]{:S(2)}, u32[]{:S(2)}) %collective-permute-start.7) | collective-permute-done | bytes 1056800 | tf_op jit(solution)/shard_map/ppermute | solution.py:170
  30.4 0.9 %shard_map.48 = (bf16[2064,128]{1,0:T(8,128)(2,1)}, bf16[2064,128]{1,0:T(8,128)(2,1)S(1)}) custom-call(bf16[2,2064,128]{2,1,0:T(8,128)(2,1)S(1)} %collective-permute-done.7.refs_9_.x_ref, bf16[2,2064,128]{2,1,0:T(8,128)(2,1)S(1)} %collective-permute-done.8.refs_10_.y_ref), custom_call_target="tpu_custom_call" | custom-call | tf_op jit(solution)/shard_map/pallas_call | solution.py:193
  32.7 1.7 %collective-permute-start.10 = (bf16[2064,128]{1,0:T(8,128)(2,1)}, bf16[2064,128]{1,0:T(8,128)(2,1)S(1)}, u32[]{:S(2)}, u32[]{:S(2)}) collective-permute-start(bf16[2064,128]{1,0:T(8,128)(2,1)} %copy-done.13), channel_id=1, source_target_pairs={{0,8},{4,12},{8,0},{12,4},{16,24},{20,28},{24,16},{28,20},{1,9},{5... | collective-permute-start | bytes 1585160 | tf_op jit(solution)/shard_map/ppermute | solution.py:170
  34.4 0.9 %copy-done.2 = bf16[256,512]{1,0:T(8,128)(2,1)S(1)} copy-done((bf16[256,512]{1,0:T(8,128)(2,1)S(1)}, bf16[256,512]{1,0:T(8,128)(2,1)}, u32[]{:S(2)}) %copy-start.2) | copy-done | bytes 262168
  35.4 0.9 %copy-done.4 = bf16[256,512]{1,0:T(8,128)(2,1)S(1)} copy-done((bf16[256,512]{1,0:T(8,128)(2,1)S(1)}, bf16[256,512]{1,0:T(8,128)(2,1)}, u32[]{:S(2)}) %copy-start.4) | copy-done | bytes 262168
  36.3 0.9 %copy-done.6 = bf16[256,512]{1,0:T(8,128)(2,1)S(1)} copy-done((bf16[256,512]{1,0:T(8,128)(2,1)S(1)}, bf16[256,512]{1,0:T(8,128)(2,1)}, u32[]{:S(2)}) %copy-start.6) | copy-done | bytes 262168
  37.3 0.9 %copy-done.8 = bf16[256,512]{1,0:T(8,128)(2,1)S(1)} copy-done((bf16[256,512]{1,0:T(8,128)(2,1)S(1)}, bf16[256,512]{1,0:T(8,128)(2,1)}, u32[]{:S(2)}) %copy-start.8) | copy-done | bytes 262168
  38.2 0.9 %copy-done.10 = bf16[256,512]{1,0:T(8,128)(2,1)S(1)} copy-done((bf16[256,512]{1,0:T(8,128)(2,1)S(1)}, bf16[256,512]{1,0:T(8,128)(2,1)}, u32[]{:S(2)}) %copy-start.10) | copy-done | bytes 262168
  39.2 8.4 %shard_map.47 = (bf16[16,512,128]{2,1,0:T(8,128)(2,1)S(1)}, f32[16,512,128]{2,1,0:T(8,128)S(1)}, f32[16,512,128]{2,1,0:T(8,128)S(1)}) custom-call(bf16[256,512]{1,0:T(8,128)(2,1)S(1)} %copy-done.2, bf16[256,512]{1,0:T(8,128)(2,1)S(1)} %copy-done.4, bf16[256,512]{1,0:T(8,128)(2,1)} %collective-permute-done.1.refs_2_, ...), custom_call_target="tpu_custom_call" | custom-call | tf_op jit(solution)/shard_map/pallas_call | solution.py:207
  48.3 3.8 %shard_map.49 = (bf16[4,2,256,128]{3,2,1,0:T(8,128)(2,1)S(1)}, bf16[4,2,256,128]{3,2,1,0:T(8,128)(2,1)S(1)}, f32[16,512,128]{2,1,0:T(8,128)S(1)}, f32[16,512,128]{2,1,0:T(8,128)S(1)}) custom-call(bf16[16,512,128]{2,1,0:T(8,128)(2,1)S(1)} %get-tuple-element.18.refs_0_, ...), custom_call_target="tpu_custom_call", output_to_operand_aliasing={{2}: (1, {}), {3}: (2, {})} | custom-call | tf_op jit(solution)/shard_map/pallas_call | solution.py:214
  52.3 1.8 %collective-permute-done.11.come_ref = bf16[4,2,256,128]{3,2,1,0:T(8,128)(2,1)S(1)} collective-permute-done((bf16[4,2,256,128]{3,2,1,0:T(8,128)(2,1)S(1)}, bf16[4,2,256,128]{3,2,1,0:T(8,128)(2,1)S(1)}, u32[]{:S(2)}, u32[]{:S(2)}) %collective-permute-start.11) | collective-permute-done | bytes 524320 | tf_op jit(solution)/shard_map/ppermute | solution.py:170
  54.2 3.8 %collective-permute-start.12 = (bf16[2,256,128]{2,1,0:T(8,128)(2,1)S(1)}, bf16[2,256,128]{2,1,0:T(8,128)(2,1)S(1)}, u32[]{:S(2)}, u32[]{:S(2)}) collective-permute-start(bf16[2,256,128]{2,1,0:T(8,128)(2,1)S(1)} %get-tuple-element.28), channel_id=1, source_target_pairs={{0,3},{1,2},{2,1},{3,0},{4,7},{5,6},{6,5},{7,4},{8,11},{9,10},{10,... | collective-permute-start | bytes 393224 | tf_op jit(solution)/shard_map/ppermute | solution.py:173
  58.7 3.8 %collective-permute-done.12.refs_1_ = bf16[2,256,128]{2,1,0:T(8,128)(2,1)S(1)} collective-permute-done((bf16[2,256,128]{2,1,0:T(8,128)(2,1)S(1)}, bf16[2,256,128]{2,1,0:T(8,128)(2,1)S(1)}, u32[]{:S(2)}, u32[]{:S(2)}) %collective-permute-start.12) | collective-permute-done | bytes 131104 | tf_op jit(solution)/shard_map/ppermute | solution.py:173
  62.5 6.9 %collective-permute-done.13.refs_2_ = bf16[2,256,128]{2,1,0:T(8,128)(2,1)S(1)} collective-permute-done((bf16[2,256,128]{2,1,0:T(8,128)(2,1)S(1)}, bf16[2,256,128]{2,1,0:T(8,128)(2,1)S(1)}, u32[]{:S(2)}, u32[]{:S(2)}) %collective-permute-start.13) | collective-permute-done | bytes 131104 | tf_op jit(solution)/shard_map/ppermute | solution.py:173
  69.6 1.3 %collective-permute-done.15.other_ref = bf16[2,256,128]{2,1,0:T(8,128)(2,1)S(1)} collective-permute-done((bf16[2,256,128]{2,1,0:T(8,128)(2,1)S(1)}, bf16[2,256,128]{2,1,0:T(8,128)(2,1)S(1)}, u32[]{:S(2)}, u32[]{:S(2)}) %collective-permute-start.15) | collective-permute-done | bytes 131104 | tf_op jit(solution)/shard_map/ppermute | solution.py:170
  70.9 1.3 %shard_map.52 = bf16[256,512]{1,0:T(8,128)(2,1)} custom-call(bf16[2,256,128]{2,1,0:T(8,128)(2,1)S(1)} %shard_map.51.own_ref, bf16[2,256,128]{2,1,0:T(8,128)(2,1)S(1)} %collective-permute-done.15.other_ref, s32[256,1]{1,0:T(8,128)S(1)} %copy.7.refs_15_.column_ref), custom_call_target="tpu_custom_call" | custom-call | tf_op jit(solution)/shard_map/pallas_call | solution.py:225
  (49 shorter events, 7.9 us)
Async XLA Ops:
  0.0 1.2 %copy-start = (bf16[2,16,128,128]{3,2,1,0:T(8,128)(2,1)S(1)}, bf16[2,16,128,128]{3,2,1,0:T(8,128)(2,1)}, u32[]{:S(2)}) copy-start(bf16[2,16,128,128]{3,2,1,0:T(8,128)(2,1)} %param.5) | copy-start | bytes 3145732
  1.9 5.2 %copy-start.1 = (bf16[256,512]{1,0:T(8,128)(2,1)S(1)}, bf16[256,512]{1,0:T(8,128)(2,1)}, u32[]{:S(2)}) copy-start(bf16[256,512]{1,0:T(8,128)(2,1)} %refs_0_.1) | copy-start | bytes 786436
  2.6 29.9 %copy-start.11 = (s32[256]{0:T(256)S(1)}, s32[256]{0:T(256)}, u32[]{:S(2)}) copy-start(s32[256]{0:T(256)} %param.7) | copy-start | bytes 3076
  2.6 26.4 %collective-permute-start.8 = (bf16[2,2064,128]{2,1,0:T(8,128)(2,1)S(1)}, bf16[2,2064,128]{2,1,0:T(8,128)(2,1)S(1)}, u32[]{:S(2)}, u32[]{:S(2)}) collective-permute-start(bf16[2,2064,128]{2,1,0:T(8,128)(2,1)S(1)} %shard_map.46.refs_8_), channel_id=1, source_target_pairs={{0,16},{4,20},{8,24},{12,28},{16,0},{20,4},{24,8},{28,12},{1,17},{... | collective-permute-start | bytes 3170312 | tf_op jit(solution)/shard_map/ppermute | solution.py:170
  5.7 24.8 %collective-permute-start.7 = (bf16[2,2064,128]{2,1,0:T(8,128)(2,1)S(1)}, bf16[2,2064,128]{2,1,0:T(8,128)(2,1)S(1)}, u32[]{:S(2)}, u32[]{:S(2)}) collective-permute-start(bf16[2,2064,128]{2,1,0:T(8,128)(2,1)S(1)} %shard_map.46.refs_8_), channel_id=1, source_target_pairs={{0,8},{4,12},{8,0},{12,4},{16,24},{20,28},{24,16},{28,20},{1,9},{5... | collective-permute-start | bytes 3170312 | tf_op jit(solution)/shard_map/ppermute | solution.py:170
  7.1 14.2 %collective-permute-start.1 = (bf16[256,512]{1,0:T(8,128)(2,1)S(1)}, bf16[256,512]{1,0:T(8,128)(2,1)}, u32[]{:S(2)}, u32[]{:S(2)}) collective-permute-start(bf16[256,512]{1,0:T(8,128)(2,1)S(1)} %copy-done.1), channel_id=1, source_target_pairs={{0,2},{1,3},{2,0},{3,1},{4,6},{5,7},{6,4},{7,5},{8,10},{9,11},{10,... | collective-permute-start | bytes 786440 | tf_op jit(solution)/shard_map/ppermute | solution.py:173
  9.7 11.7 %collective-permute-start = (bf16[256,512]{1,0:T(8,128)(2,1)S(1)}, bf16[256,512]{1,0:T(8,128)(2,1)S(1)}, u32[]{:S(2)}, u32[]{:S(2)}) collective-permute-start(bf16[256,512]{1,0:T(8,128)(2,1)S(1)} %copy-done.1), channel_id=1, source_target_pairs={{0,1},{1,0},{2,3},{3,2},{4,5},{5,4},{6,7},{7,6},{8,9},{9,8},{10,11... | collective-permute-start | bytes 786440 | tf_op jit(solution)/shard_map/ppermute | solution.py:173
  11.3 11.3 %collective-permute-start.3 = (bf16[256,512]{1,0:T(8,128)(2,1)S(1)}, bf16[256,512]{1,0:T(8,128)(2,1)S(1)}, u32[]{:S(2)}, u32[]{:S(2)}) collective-permute-start(bf16[256,512]{1,0:T(8,128)(2,1)S(1)} %copy-done.1), channel_id=1, source_target_pairs={{0,4},{4,0},{8,12},{12,8},{16,20},{20,16},{24,28},{28,24},{1,5},{5... | collective-permute-start | bytes 786440 | tf_op jit(solution)/shard_map/ppermute | solution.py:170
  21.4 2.9 %collective-permute-start.5 = (bf16[256,512]{1,0:T(8,128)(2,1)}, bf16[256,512]{1,0:T(8,128)(2,1)S(1)}, u32[]{:S(2)}, u32[]{:S(2)}) collective-permute-start(bf16[256,512]{1,0:T(8,128)(2,1)} %collective-permute-done.1.refs_2_), channel_id=1, source_target_pairs={{0,4},{4,0},{8,12},{12,8},{16,20},{20,16},{24,28},{28,24},{1,5},{5... | collective-permute-start | bytes 786440 | tf_op jit(solution)/shard_map/ppermute | solution.py:170
  21.4 3.6 %collective-permute-start.4 = (bf16[256,512]{1,0:T(8,128)(2,1)S(1)}, bf16[256,512]{1,0:T(8,128)(2,1)S(1)}, u32[]{:S(2)}, u32[]{:S(2)}) collective-permute-start(bf16[256,512]{1,0:T(8,128)(2,1)S(1)} %collective-permute-done.refs_1_), channel_id=1, source_target_pairs={{0,4},{4,0},{8,12},{12,8},{16,20},{20,16},{24,28},{28,24},{1,5},{5... | collective-permute-start | bytes 786440 | tf_op jit(solution)/shard_map/ppermute | solution.py:170
  23.3 9.3 %collective-permute-start.2 = (bf16[256,512]{1,0:T(8,128)(2,1)}, bf16[256,512]{1,0:T(8,128)(2,1)}, u32[]{:S(2)}, u32[]{:S(2)}) collective-permute-start(bf16[256,512]{1,0:T(8,128)(2,1)} %collective-permute-done.1.refs_2_), channel_id=1, source_target_pairs={{0,1},{1,0},{2,3},{3,2},{4,5},{5,4},{6,7},{7,6},{8,9},{9,8},{10,11... | collective-permute-start | bytes 786440 | tf_op jit(solution)/shard_map/ppermute | solution.py:173
  32.1 15.5 %collective-permute-start.9 = (bf16[2064,128]{1,0:T(8,128)(2,1)}, bf16[2064,128]{1,0:T(8,128)(2,1)}, u32[]{:S(2)}, u32[]{:S(2)}) collective-permute-start(bf16[2064,128]{1,0:T(8,128)(2,1)} %get-tuple-element.23), channel_id=1, source_target_pairs={{0,16},{4,20},{8,24},{12,28},{16,0},{20,4},{24,8},{28,12},{1,17},{... | collective-permute-start | bytes 1585160 | tf_op jit(solution)/shard_map/ppermute | solution.py:170
  32.6 1.8 %collective-permute-start.6 = (bf16[256,512]{1,0:T(8,128)(2,1)}, bf16[256,512]{1,0:T(8,128)(2,1)S(1)}, u32[]{:S(2)}, u32[]{:S(2)}) collective-permute-start(bf16[256,512]{1,0:T(8,128)(2,1)} %collective-permute-done.2.refs_3_), channel_id=1, source_target_pairs={{0,4},{4,0},{8,12},{12,8},{16,20},{20,16},{24,28},{28,24},{1,5},{5... | collective-permute-start | bytes 786440 | tf_op jit(solution)/shard_map/ppermute | solution.py:170
  32.7 15.6 %collective-permute-start.10 = (bf16[2064,128]{1,0:T(8,128)(2,1)}, bf16[2064,128]{1,0:T(8,128)(2,1)S(1)}, u32[]{:S(2)}, u32[]{:S(2)}) collective-permute-start(bf16[2064,128]{1,0:T(8,128)(2,1)} %copy-done.13), channel_id=1, source_target_pairs={{0,8},{4,12},{8,0},{12,4},{16,24},{20,28},{24,16},{28,20},{1,9},{5... | collective-permute-start | bytes 1585160 | tf_op jit(solution)/shard_map/ppermute | solution.py:170
  34.4 1.0 %copy-start.2 = (bf16[256,512]{1,0:T(8,128)(2,1)S(1)}, bf16[256,512]{1,0:T(8,128)(2,1)}, u32[]{:S(2)}) copy-start(bf16[256,512]{1,0:T(8,128)(2,1)} %refs_0_.1) | copy-start | bytes 786436
  35.4 0.9 %copy-start.4 = (bf16[256,512]{1,0:T(8,128)(2,1)S(1)}, bf16[256,512]{1,0:T(8,128)(2,1)}, u32[]{:S(2)}) copy-start(bf16[256,512]{1,0:T(8,128)(2,1)} %copy-done.3) | copy-start | bytes 786436
  36.3 0.9 %copy-start.6 = (bf16[256,512]{1,0:T(8,128)(2,1)S(1)}, bf16[256,512]{1,0:T(8,128)(2,1)}, u32[]{:S(2)}) copy-start(bf16[256,512]{1,0:T(8,128)(2,1)} %copy-done.5) | copy-start | bytes 786436
  37.3 0.9 %copy-start.8 = (bf16[256,512]{1,0:T(8,128)(2,1)S(1)}, bf16[256,512]{1,0:T(8,128)(2,1)}, u32[]{:S(2)}) copy-start(bf16[256,512]{1,0:T(8,128)(2,1)} %copy-done.7) | copy-start | bytes 786436
  38.2 0.9 %copy-start.10 = (bf16[256,512]{1,0:T(8,128)(2,1)S(1)}, bf16[256,512]{1,0:T(8,128)(2,1)}, u32[]{:S(2)}) copy-start(bf16[256,512]{1,0:T(8,128)(2,1)} %copy-done.9) | copy-start | bytes 786436
  52.1 2.0 %collective-permute-start.11 = (bf16[4,2,256,128]{3,2,1,0:T(8,128)(2,1)S(1)}, bf16[4,2,256,128]{3,2,1,0:T(8,128)(2,1)S(1)}, u32[]{:S(2)}, u32[]{:S(2)}) collective-permute-start(bf16[4,2,256,128]{3,2,1,0:T(8,128)(2,1)S(1)} %get-tuple-element.26), channel_id=1, source_target_pairs={{0,4},{4,0},{8,12},{12,8},{16,20},{20,16},{24,28},{28,24},{1,5},{5... | collective-permute-start | bytes 1572872 | tf_op jit(solution)/shard_map/ppermute | solution.py:170
  54.2 8.3 %collective-permute-start.12 = (bf16[2,256,128]{2,1,0:T(8,128)(2,1)S(1)}, bf16[2,256,128]{2,1,0:T(8,128)(2,1)S(1)}, u32[]{:S(2)}, u32[]{:S(2)}) collective-permute-start(bf16[2,256,128]{2,1,0:T(8,128)(2,1)S(1)} %get-tuple-element.28), channel_id=1, source_target_pairs={{0,3},{1,2},{2,1},{3,0},{4,7},{5,6},{6,5},{7,4},{8,11},{9,10},{10,... | collective-permute-start | bytes 393224 | tf_op jit(solution)/shard_map/ppermute | solution.py:173
  58.0 11.4 %collective-permute-start.13 = (bf16[2,256,128]{2,1,0:T(8,128)(2,1)S(1)}, bf16[2,256,128]{2,1,0:T(8,128)(2,1)S(1)}, u32[]{:S(2)}, u32[]{:S(2)}) collective-permute-start(bf16[2,256,128]{2,1,0:T(8,128)(2,1)S(1)} %get-tuple-element.29), channel_id=1, source_target_pairs={{0,2},{1,3},{2,0},{3,1},{4,6},{5,7},{6,4},{7,5},{8,10},{9,11},{10,... | collective-permute-start | bytes 393224 | tf_op jit(solution)/shard_map/ppermute | solution.py:173
  58.0 11.4 %collective-permute-start.14 = (bf16[2,256,128]{2,1,0:T(8,128)(2,1)S(1)}, bf16[2,256,128]{2,1,0:T(8,128)(2,1)S(1)}, u32[]{:S(2)}, u32[]{:S(2)}) collective-permute-start(bf16[2,256,128]{2,1,0:T(8,128)(2,1)S(1)} %get-tuple-element.30), channel_id=1, source_target_pairs={{0,1},{1,0},{2,3},{3,2},{4,5},{5,4},{6,7},{7,6},{8,9},{9,8},{10,11... | collective-permute-start | bytes 393224 | tf_op jit(solution)/shard_map/ppermute | solution.py:173
  69.5 1.4 %collective-permute-start.15 = (bf16[2,256,128]{2,1,0:T(8,128)(2,1)S(1)}, bf16[2,256,128]{2,1,0:T(8,128)(2,1)S(1)}, u32[]{:S(2)}, u32[]{:S(2)}) collective-permute-start(bf16[2,256,128]{2,1,0:T(8,128)(2,1)S(1)} %shard_map.51.own_ref), channel_id=1, source_target_pairs={{0,4},{4,0},{8,12},{12,8},{16,20},{20,16},{24,28},{28,24},{1,5},{5... | collective-permute-start | bytes 393224 | tf_op jit(solution)/shard_map/ppermute | solution.py:170
  (6 other events, 4.3 us)

commit v7 on v6

--- a/solution.py
+++ b/solution.py
@@ -65,19 +65,24 @@
 
 def add_products(grid_ref, acc_refs, tiles_ref, blocks_ref):
     empty = jnp.zeros((TILE, TILE), BF16)
+    rows = acc_refs[0].shape[1]
 
     @pl.loop(0, blocks_ref.shape[0] // 4, unroll=4)
     def _(t):
         to = [blocks_ref[4 * t + 2 * k] for k in range(2)]
         come = [blocks_ref[4 * t + 2 * k + 1] for k in range(2)]
         tiles = [tiles_ref[pl.ds(pl.multiple_of((2 * t + k) * TILE, TILE), TILE), :] for k in range(2)]
-        left = jnp.concatenate([grid_ref[come[0]], grid_ref[come[1]]], axis=1)
         right = jnp.concatenate(
             [jnp.concatenate([tiles[0], empty], axis=1), jnp.concatenate([empty, tiles[1]], axis=1)], axis=0
         )
-        products = jnp.dot(left, right, preferred_element_type=F32)
+        products = []
+        for side in range(2):
+            part = slice(side * rows, (side + 1) * rows)
+            left = jnp.concatenate([grid_ref[come[0], part], grid_ref[come[1], part]], axis=1)
+            products.append(jnp.dot(left, right, preferred_element_type=F32))
         for k in range(2):
-            acc_refs[k][to[k]] += products[:, k * TILE : (k + 1) * TILE]
+            for side in range(2):
+                acc_refs[side][to[k]] += products[side][:, k * TILE : (k + 1) * TILE]
 
 
 def first_kernel(n_vir, n_sets, *refs):
@@ -124,9 +129,9 @@
         for k in range(half):
             for out_ref, side in ((keep_ref, core), (send_ref, 1 - core)):
                 block = ((vir ^ shift) * 2 + side) * half + k
-                lower = acc_refs[0][block, :rows] + acc_refs[1][block, :rows]
-                upper = (acc_refs[0][block, rows:] + acc_refs[1][block, rows:]).astype(BF16)
-                out_ref[shift, k] = (lower + jnp.dot(upper, swap, preferred_element_type=F32)).astype(BF16)
+                upper = acc_refs[1][block].astype(BF16)
+                total = acc_refs[0][block] + jnp.dot(upper, swap, preferred_element_type=F32)
+                out_ref[shift, k] = total.astype(BF16)
 
 
 def join_kernel(keep_ref, come_ref, *outs):
@@ -203,7 +208,7 @@
     def ids(array):
         return array[:, length, : 2 * tile_dev].astype(jnp.int32)
 
-    sums = jax.ShapeDtypeStruct((n_blk, 2 * rows, TILE), F32)
+    sums = jax.ShapeDtypeStruct((n_blk, rows, TILE), F32)
     grid, *sums_so_far = call(
         functools.partial(first_kernel, n_vir, len(early)),
         [jax.ShapeDtypeStruct((n_blk, 2 * rows, TILE), BF16), sums, sums],

time: 72.6 us -> 71.6 us (0.986)
  Pallas kernels: 15.3 us -> 14.2 us
    pallas_call x1, Pallas kernels: 8.45 us -> 7.71 us  [local(): call(functools.partial(first_kernel, n_vir, len(early)), [jax.ShapeDtypeS...]
  transfers between devices with their start and end apart: 16 -> 16, of which waited for: 8 -> 8; matrix products, arithmetic and copies ran while one was open for 1% -> 1% of each run, Pallas kernels for 13% -> 12%
where the time goes in v7:
time: 71.6 us; the launch traced here: 71.2 us
  waiting for transfers between devices  28.7 us (40%)
  starting transfers between devices  17 us (24%)
  Pallas kernels  14.2 us (20%)
  local copies, waits for them, and re-layouts  10.4 us (15%)
    ppermute x6, waiting for transfers between devices, along(): return lax.ppermute(array, 'vir', [(i, i ^ bits) for i in range(n_vir)])  20.9 us
    unnamed x28, local copies, waits for them, and re-layouts  10.3 us
    ppermute x6, starting transfers between devices, along(): return lax.ppermute(array, 'vir', [(i, i ^ bits) for i in range(n_vir)])  9.64 us
    ppermute x10, waiting for transfers between devices, across(): return lax.ppermute(array, 'pair', [(i, i ^ bits) for i in range(n_pair)])  7.87 us
    pallas_call x1, Pallas kernels, local(): call(functools.partial(first_kernel, n_vir, len(early)), [jax.ShapeDtypeS...  7.71 us
    ppermute x10, starting transfers between devices, across(): return lax.ppermute(array, 'pair', [(i, i ^ bits) for i in range(n_pair)])  7.36 us
    pallas_call x1, Pallas kernels, local(): call(functools.partial(second_kernel, n_vir, len(late)), [piece, piece, s...  3.44 us
  transfers between devices with their start and end apart: 16, of which 8 were waited for; matrix products, arithmetic and copies ran while one was open for 1% of the time, Pallas kernels for 12%

profile of v7, /device:TPU:0, one launch (start us, length us, event | category | flops | bytes accessed | tf_op | source)
XLA Modules:
  0.0 71.2 jit_solution(6113236747321559133)
XLA Ops:
  0.0 1.2 %copy-done = bf16[2,16,128,128]{3,2,1,0:T(8,128)(2,1)S(1)} copy-done((bf16[2,16,128,128]{3,2,1,0:T(8,128)(2,1)S(1)}, bf16[2,16,128,128]{3,2,1,0:T(8,128)(2,1)}, u32[]{:S(2)}) %copy-start) | copy-done | bytes 1048600
  2.6 3.0 %collective-permute-start.8 = (bf16[2,2064,128]{2,1,0:T(8,128)(2,1)S(1)}, bf16[2,2064,128]{2,1,0:T(8,128)(2,1)S(1)}, u32[]{:S(2)}, u32[]{:S(2)}) collective-permute-start(bf16[2,2064,128]{2,1,0:T(8,128)(2,1)S(1)} %shard_map.46.refs_8_), channel_id=1, source_target_pairs={{0,16},{4,20},{8,24},{12,28},{16,0},{20,4},{24,8},{28,12},{1,17},{... | collective-permute-start | bytes 3170312 | tf_op jit(solution)/shard_map/ppermute | solution.py:175
  5.7 1.5 %collective-permute-start.7 = (bf16[2,2064,128]{2,1,0:T(8,128)(2,1)S(1)}, bf16[2,2064,128]{2,1,0:T(8,128)(2,1)S(1)}, u32[]{:S(2)}, u32[]{:S(2)}) collective-permute-start(bf16[2,2064,128]{2,1,0:T(8,128)(2,1)S(1)} %shard_map.46.refs_8_), channel_id=1, source_target_pairs={{0,8},{4,12},{8,0},{12,4},{16,24},{20,28},{24,16},{28,20},{1,9},{5... | collective-permute-start | bytes 3170312 | tf_op jit(solution)/shard_map/ppermute | solution.py:175
  7.1 2.6 %collective-permute-start.1 = (bf16[256,512]{1,0:T(8,128)(2,1)S(1)}, bf16[256,512]{1,0:T(8,128)(2,1)}, u32[]{:S(2)}, u32[]{:S(2)}) collective-permute-start(bf16[256,512]{1,0:T(8,128)(2,1)S(1)} %copy-done.1), channel_id=1, source_target_pairs={{0,2},{1,3},{2,0},{3,1},{4,6},{5,7},{6,4},{7,5},{8,10},{9,11},{10,... | collective-permute-start | bytes 786440 | tf_op jit(solution)/shard_map/ppermute | solution.py:178
  9.7 1.6 %collective-permute-start = (bf16[256,512]{1,0:T(8,128)(2,1)S(1)}, bf16[256,512]{1,0:T(8,128)(2,1)S(1)}, u32[]{:S(2)}, u32[]{:S(2)}) collective-permute-start(bf16[256,512]{1,0:T(8,128)(2,1)S(1)} %copy-done.1), channel_id=1, source_target_pairs={{0,1},{1,0},{2,3},{3,2},{4,5},{5,4},{6,7},{7,6},{8,9},{9,8},{10,11... | collective-permute-start | bytes 786440 | tf_op jit(solution)/shard_map/ppermute | solution.py:178
  11.3 10.0 %collective-permute-done.1.refs_2_ = bf16[256,512]{1,0:T(8,128)(2,1)} collective-permute-done((bf16[256,512]{1,0:T(8,128)(2,1)S(1)}, bf16[256,512]{1,0:T(8,128)(2,1)}, u32[]{:S(2)}, u32[]{:S(2)}) %collective-permute-start.1) | collective-permute-done | bytes 262176 | tf_op jit(solution)/shard_map/ppermute | solution.py:178
  23.3 1.0 %collective-permute-start.2 = (bf16[256,512]{1,0:T(8,128)(2,1)}, bf16[256,512]{1,0:T(8,128)(2,1)}, u32[]{:S(2)}, u32[]{:S(2)}) collective-permute-start(bf16[256,512]{1,0:T(8,128)(2,1)} %collective-permute-done.1.refs_2_), channel_id=1, source_target_pairs={{0,1},{1,0},{2,3},{3,2},{4,5},{5,4},{6,7},{7,6},{8,9},{9,8},{10,11... | collective-permute-start | bytes 786440 | tf_op jit(solution)/shard_map/ppermute | solution.py:178
  25.7 3.3 %collective-permute-done.8.refs_10_.y_ref = bf16[2,2064,128]{2,1,0:T(8,128)(2,1)S(1)} collective-permute-done((bf16[2,2064,128]{2,1,0:T(8,128)(2,1)S(1)}, bf16[2,2064,128]{2,1,0:T(8,128)(2,1)S(1)}, u32[]{:S(2)}, u32[]{:S(2)}) %collective-permute-start.8) | collective-permute-done | bytes 1056800 | tf_op jit(solution)/shard_map/ppermute | solution.py:175
  29.0 1.5 %collective-permute-done.7.refs_9_.x_ref = bf16[2,2064,128]{2,1,0:T(8,128)(2,1)S(1)} collective-permute-done((bf16[2,2064,128]{2,1,0:T(8,128)(2,1)S(1)}, bf16[2,2064,128]{2,1,0:T(8,128)(2,1)S(1)}, u32[]{:S(2)}, u32[]{:S(2)}) %collective-permute-start.7) | collective-permute-done | bytes 1056800 | tf_op jit(solution)/shard_map/ppermute | solution.py:175
  30.4 0.9 %shard_map.48 = (bf16[2064,128]{1,0:T(8,128)(2,1)}, bf16[2064,128]{1,0:T(8,128)(2,1)S(1)}) custom-call(bf16[2,2064,128]{2,1,0:T(8,128)(2,1)S(1)} %collective-permute-done.7.refs_9_.x_ref, bf16[2,2064,128]{2,1,0:T(8,128)(2,1)S(1)} %collective-permute-done.8.refs_10_.y_ref), custom_call_target="tpu_custom_call" | custom-call | tf_op jit(solution)/shard_map/pallas_call | solution.py:198
  32.7 1.7 %collective-permute-start.10 = (bf16[2064,128]{1,0:T(8,128)(2,1)}, bf16[2064,128]{1,0:T(8,128)(2,1)S(1)}, u32[]{:S(2)}, u32[]{:S(2)}) collective-permute-start(bf16[2064,128]{1,0:T(8,128)(2,1)} %copy-done.13), channel_id=1, source_target_pairs={{0,8},{4,12},{8,0},{12,4},{16,24},{20,28},{24,16},{28,20},{1,9},{5... | collective-permute-start | bytes 1585160 | tf_op jit(solution)/shard_map/ppermute | solution.py:175
  34.4 0.9 %copy-done.2 = bf16[256,512]{1,0:T(8,128)(2,1)S(1)} copy-done((bf16[256,512]{1,0:T(8,128)(2,1)S(1)}, bf16[256,512]{1,0:T(8,128)(2,1)}, u32[]{:S(2)}) %copy-start.2) | copy-done | bytes 262168
  35.4 0.9 %copy-done.4 = bf16[256,512]{1,0:T(8,128)(2,1)S(1)} copy-done((bf16[256,512]{1,0:T(8,128)(2,1)S(1)}, bf16[256,512]{1,0:T(8,128)(2,1)}, u32[]{:S(2)}) %copy-start.4) | copy-done | bytes 262168
  36.3 0.9 %copy-done.6 = bf16[256,512]{1,0:T(8,128)(2,1)S(1)} copy-done((bf16[256,512]{1,0:T(8,128)(2,1)S(1)}, bf16[256,512]{1,0:T(8,128)(2,1)}, u32[]{:S(2)}) %copy-start.6) | copy-done | bytes 262168
  37.3 0.9 %copy-done.8 = bf16[256,512]{1,0:T(8,128)(2,1)S(1)} copy-done((bf16[256,512]{1,0:T(8,128)(2,1)S(1)}, bf16[256,512]{1,0:T(8,128)(2,1)}, u32[]{:S(2)}) %copy-start.8) | copy-done | bytes 262168
  38.2 0.9 %copy-done.10 = bf16[256,512]{1,0:T(8,128)(2,1)S(1)} copy-done((bf16[256,512]{1,0:T(8,128)(2,1)S(1)}, bf16[256,512]{1,0:T(8,128)(2,1)}, u32[]{:S(2)}) %copy-start.10) | copy-done | bytes 262168
  39.2 7.7 %shard_map.47 = (bf16[16,512,128]{2,1,0:T(8,128)(2,1)S(1)}, f32[16,256,128]{2,1,0:T(8,128)S(1)}, f32[16,256,128]{2,1,0:T(8,128)S(1)}) custom-call(bf16[256,512]{1,0:T(8,128)(2,1)S(1)} %copy-done.2, bf16[256,512]{1,0:T(8,128)(2,1)S(1)} %copy-done.4, bf16[256,512]{1,0:T(8,128)(2,1)} %collective-permute-done.1.refs_2_, ...), custom_call_target="tpu_custom_call" | custom-call | tf_op jit(solution)/shard_map/pallas_call | solution.py:212
  47.6 3.4 %shard_map.49 = (bf16[4,2,256,128]{3,2,1,0:T(8,128)(2,1)S(1)}, bf16[4,2,256,128]{3,2,1,0:T(8,128)(2,1)S(1)}, f32[16,256,128]{2,1,0:T(8,128)S(1)}, f32[16,256,128]{2,1,0:T(8,128)S(1)}) custom-call(bf16[16,512,128]{2,1,0:T(8,128)(2,1)S(1)} %get-tuple-element.18.refs_0_, ...), custom_call_target="tpu_custom_call", output_to_operand_aliasing={{2}: (1, {}), {3}: (2, {})} | custom-call | tf_op jit(solution)/shard_map/pallas_call | solution.py:219
  51.2 1.8 %collective-permute-done.11.come_ref = bf16[4,2,256,128]{3,2,1,0:T(8,128)(2,1)S(1)} collective-permute-done((bf16[4,2,256,128]{3,2,1,0:T(8,128)(2,1)S(1)}, bf16[4,2,256,128]{3,2,1,0:T(8,128)(2,1)S(1)}, u32[]{:S(2)}, u32[]{:S(2)}) %collective-permute-start.11) | collective-permute-done | bytes 524320 | tf_op jit(solution)/shard_map/ppermute | solution.py:175
  53.1 3.8 %collective-permute-start.12 = (bf16[2,256,128]{2,1,0:T(8,128)(2,1)S(1)}, bf16[2,256,128]{2,1,0:T(8,128)(2,1)S(1)}, u32[]{:S(2)}, u32[]{:S(2)}) collective-permute-start(bf16[2,256,128]{2,1,0:T(8,128)(2,1)S(1)} %get-tuple-element.28), channel_id=1, source_target_pairs={{0,3},{1,2},{2,1},{3,0},{4,7},{5,6},{6,5},{7,4},{8,11},{9,10},{10,... | collective-permute-start | bytes 393224 | tf_op jit(solution)/shard_map/ppermute | solution.py:178
  57.6 3.8 %collective-permute-done.12.refs_1_ = bf16[2,256,128]{2,1,0:T(8,128)(2,1)S(1)} collective-permute-done((bf16[2,256,128]{2,1,0:T(8,128)(2,1)S(1)}, bf16[2,256,128]{2,1,0:T(8,128)(2,1)S(1)}, u32[]{:S(2)}, u32[]{:S(2)}) %collective-permute-start.12) | collective-permute-done | bytes 131104 | tf_op jit(solution)/shard_map/ppermute | solution.py:178
  61.4 6.9 %collective-permute-done.13.refs_2_ = bf16[2,256,128]{2,1,0:T(8,128)(2,1)S(1)} collective-permute-done((bf16[2,256,128]{2,1,0:T(8,128)(2,1)S(1)}, bf16[2,256,128]{2,1,0:T(8,128)(2,1)S(1)}, u32[]{:S(2)}, u32[]{:S(2)}) %collective-permute-start.13) | collective-permute-done | bytes 131104 | tf_op jit(solution)/shard_map/ppermute | solution.py:178
  68.5 1.3 %collective-permute-done.15.other_ref = bf16[2,256,128]{2,1,0:T(8,128)(2,1)S(1)} collective-permute-done((bf16[2,256,128]{2,1,0:T(8,128)(2,1)S(1)}, bf16[2,256,128]{2,1,0:T(8,128)(2,1)S(1)}, u32[]{:S(2)}, u32[]{:S(2)}) %collective-permute-start.15) | collective-permute-done | bytes 131104 | tf_op jit(solution)/shard_map/ppermute | solution.py:175
  69.8 1.3 %shard_map.52 = bf16[256,512]{1,0:T(8,128)(2,1)} custom-call(bf16[2,256,128]{2,1,0:T(8,128)(2,1)S(1)} %shard_map.51.own_ref, bf16[2,256,128]{2,1,0:T(8,128)(2,1)S(1)} %collective-permute-done.15.other_ref, s32[256,1]{1,0:T(8,128)S(1)} %copy.7.refs_15_.column_ref), custom_call_target="tpu_custom_call" | custom-call | tf_op jit(solution)/shard_map/pallas_call | solution.py:230
  (49 shorter events, 7.9 us)
Async XLA Ops:
  0.0 1.2 %copy-start = (bf16[2,16,128,128]{3,2,1,0:T(8,128)(2,1)S(1)}, bf16[2,16,128,128]{3,2,1,0:T(8,128)(2,1)}, u32[]{:S(2)}) copy-start(bf16[2,16,128,128]{3,2,1,0:T(8,128)(2,1)} %param.5) | copy-start | bytes 3145732
  1.9 5.2 %copy-start.1 = (bf16[256,512]{1,0:T(8,128)(2,1)S(1)}, bf16[256,512]{1,0:T(8,128)(2,1)}, u32[]{:S(2)}) copy-start(bf16[256,512]{1,0:T(8,128)(2,1)} %refs_0_.1) | copy-start | bytes 786436
  2.6 29.9 %copy-start.11 = (s32[256]{0:T(256)S(1)}, s32[256]{0:T(256)}, u32[]{:S(2)}) copy-start(s32[256]{0:T(256)} %param.7) | copy-start | bytes 3076
  2.6 26.4 %collective-permute-start.8 = (bf16[2,2064,128]{2,1,0:T(8,128)(2,1)S(1)}, bf16[2,2064,128]{2,1,0:T(8,128)(2,1)S(1)}, u32[]{:S(2)}, u32[]{:S(2)}) collective-permute-start(bf16[2,2064,128]{2,1,0:T(8,128)(2,1)S(1)} %shard_map.46.refs_8_), channel_id=1, source_target_pairs={{0,16},{4,20},{8,24},{12,28},{16,0},{20,4},{24,8},{28,12},{1,17},{... | collective-permute-start | bytes 3170312 | tf_op jit(solution)/shard_map/ppermute | solution.py:175
  5.7 24.8 %collective-permute-start.7 = (bf16[2,2064,128]{2,1,0:T(8,128)(2,1)S(1)}, bf16[2,2064,128]{2,1,0:T(8,128)(2,1)S(1)}, u32[]{:S(2)}, u32[]{:S(2)}) collective-permute-start(bf16[2,2064,128]{2,1,0:T(8,128)(2,1)S(1)} %shard_map.46.refs_8_), channel_id=1, source_target_pairs={{0,8},{4,12},{8,0},{12,4},{16,24},{20,28},{24,16},{28,20},{1,9},{5... | collective-permute-start | bytes 3170312 | tf_op jit(solution)/shard_map/ppermute | solution.py:175
  7.1 14.2 %collective-permute-start.1 = (bf16[256,512]{1,0:T(8,128)(2,1)S(1)}, bf16[256,512]{1,0:T(8,128)(2,1)}, u32[]{:S(2)}, u32[]{:S(2)}) collective-permute-start(bf16[256,512]{1,0:T(8,128)(2,1)S(1)} %copy-done.1), channel_id=1, source_target_pairs={{0,2},{1,3},{2,0},{3,1},{4,6},{5,7},{6,4},{7,5},{8,10},{9,11},{10,... | collective-permute-start | bytes 786440 | tf_op jit(solution)/shard_map/ppermute | solution.py:178
  9.7 11.7 %collective-permute-start = (bf16[256,512]{1,0:T(8,128)(2,1)S(1)}, bf16[256,512]{1,0:T(8,128)(2,1)S(1)}, u32[]{:S(2)}, u32[]{:S(2)}) collective-permute-start(bf16[256,512]{1,0:T(8,128)(2,1)S(1)} %copy-done.1), channel_id=1, source_target_pairs={{0,1},{1,0},{2,3},{3,2},{4,5},{5,4},{6,7},{7,6},{8,9},{9,8},{10,11... | collective-permute-start | bytes 786440 | tf_op jit(solution)/shard_map/ppermute | solution.py:178
  11.3 11.3 %collective-permute-start.3 = (bf16[256,512]{1,0:T(8,128)(2,1)S(1)}, bf16[256,512]{1,0:T(8,128)(2,1)S(1)}, u32[]{:S(2)}, u32[]{:S(2)}) collective-permute-start(bf16[256,512]{1,0:T(8,128)(2,1)S(1)} %copy-done.1), channel_id=1, source_target_pairs={{0,4},{4,0},{8,12},{12,8},{16,20},{20,16},{24,28},{28,24},{1,5},{5... | collective-permute-start | bytes 786440 | tf_op jit(solution)/shard_map/ppermute | solution.py:175
  21.4 2.9 %collective-permute-start.5 = (bf16[256,512]{1,0:T(8,128)(2,1)}, bf16[256,512]{1,0:T(8,128)(2,1)S(1)}, u32[]{:S(2)}, u32[]{:S(2)}) collective-permute-start(bf16[256,512]{1,0:T(8,128)(2,1)} %collective-permute-done.1.refs_2_), channel_id=1, source_target_pairs={{0,4},{4,0},{8,12},{12,8},{16,20},{20,16},{24,28},{28,24},{1,5},{5... | collective-permute-start | bytes 786440 | tf_op jit(solution)/shard_map/ppermute | solution.py:175
  21.4 3.6 %collective-permute-start.4 = (bf16[256,512]{1,0:T(8,128)(2,1)S(1)}, bf16[256,512]{1,0:T(8,128)(2,1)S(1)}, u32[]{:S(2)}, u32[]{:S(2)}) collective-permute-start(bf16[256,512]{1,0:T(8,128)(2,1)S(1)} %collective-permute-done.refs_1_), channel_id=1, source_target_pairs={{0,4},{4,0},{8,12},{12,8},{16,20},{20,16},{24,28},{28,24},{1,5},{5... | collective-permute-start | bytes 786440 | tf_op jit(solution)/shard_map/ppermute | solution.py:175
  23.3 9.3 %collective-permute-start.2 = (bf16[256,512]{1,0:T(8,128)(2,1)}, bf16[256,512]{1,0:T(8,128)(2,1)}, u32[]{:S(2)}, u32[]{:S(2)}) collective-permute-start(bf16[256,512]{1,0:T(8,128)(2,1)} %collective-permute-done.1.refs_2_), channel_id=1, source_target_pairs={{0,1},{1,0},{2,3},{3,2},{4,5},{5,4},{6,7},{7,6},{8,9},{9,8},{10,11... | collective-permute-start | bytes 786440 | tf_op jit(solution)/shard_map/ppermute | solution.py:178
  32.1 14.8 %collective-permute-start.9 = (bf16[2064,128]{1,0:T(8,128)(2,1)}, bf16[2064,128]{1,0:T(8,128)(2,1)}, u32[]{:S(2)}, u32[]{:S(2)}) collective-permute-start(bf16[2064,128]{1,0:T(8,128)(2,1)} %get-tuple-element.23), channel_id=1, source_target_pairs={{0,16},{4,20},{8,24},{12,28},{16,0},{20,4},{24,8},{28,12},{1,17},{... | collective-permute-start | bytes 1585160 | tf_op jit(solution)/shard_map/ppermute | solution.py:175
  32.6 1.8 %collective-permute-start.6 = (bf16[256,512]{1,0:T(8,128)(2,1)}, bf16[256,512]{1,0:T(8,128)(2,1)S(1)}, u32[]{:S(2)}, u32[]{:S(2)}) collective-permute-start(bf16[256,512]{1,0:T(8,128)(2,1)} %collective-permute-done.2.refs_3_), channel_id=1, source_target_pairs={{0,4},{4,0},{8,12},{12,8},{16,20},{20,16},{24,28},{28,24},{1,5},{5... | collective-permute-start | bytes 786440 | tf_op jit(solution)/shard_map/ppermute | solution.py:175
  32.7 14.9 %collective-permute-start.10 = (bf16[2064,128]{1,0:T(8,128)(2,1)}, bf16[2064,128]{1,0:T(8,128)(2,1)S(1)}, u32[]{:S(2)}, u32[]{:S(2)}) collective-permute-start(bf16[2064,128]{1,0:T(8,128)(2,1)} %copy-done.13), channel_id=1, source_target_pairs={{0,8},{4,12},{8,0},{12,4},{16,24},{20,28},{24,16},{28,20},{1,9},{5... | collective-permute-start | bytes 1585160 | tf_op jit(solution)/shard_map/ppermute | solution.py:175
  34.4 1.0 %copy-start.2 = (bf16[256,512]{1,0:T(8,128)(2,1)S(1)}, bf16[256,512]{1,0:T(8,128)(2,1)}, u32[]{:S(2)}) copy-start(bf16[256,512]{1,0:T(8,128)(2,1)} %refs_0_.1) | copy-start | bytes 786436
  35.4 0.9 %copy-start.4 = (bf16[256,512]{1,0:T(8,128)(2,1)S(1)}, bf16[256,512]{1,0:T(8,128)(2,1)}, u32[]{:S(2)}) copy-start(bf16[256,512]{1,0:T(8,128)(2,1)} %copy-done.3) | copy-start | bytes 786436
  36.3 0.9 %copy-start.6 = (bf16[256,512]{1,0:T(8,128)(2,1)S(1)}, bf16[256,512]{1,0:T(8,128)(2,1)}, u32[]{:S(2)}) copy-start(bf16[256,512]{1,0:T(8,128)(2,1)} %copy-done.5) | copy-start | bytes 786436
  37.3 0.9 %copy-start.8 = (bf16[256,512]{1,0:T(8,128)(2,1)S(1)}, bf16[256,512]{1,0:T(8,128)(2,1)}, u32[]{:S(2)}) copy-start(bf16[256,512]{1,0:T(8,128)(2,1)} %copy-done.7) | copy-start | bytes 786436
  38.2 0.9 %copy-start.10 = (bf16[256,512]{1,0:T(8,128)(2,1)S(1)}, bf16[256,512]{1,0:T(8,128)(2,1)}, u32[]{:S(2)}) copy-start(bf16[256,512]{1,0:T(8,128)(2,1)} %copy-done.9) | copy-start | bytes 786436
  51.0 2.0 %collective-permute-start.11 = (bf16[4,2,256,128]{3,2,1,0:T(8,128)(2,1)S(1)}, bf16[4,2,256,128]{3,2,1,0:T(8,128)(2,1)S(1)}, u32[]{:S(2)}, u32[]{:S(2)}) collective-permute-start(bf16[4,2,256,128]{3,2,1,0:T(8,128)(2,1)S(1)} %get-tuple-element.26), channel_id=1, source_target_pairs={{0,4},{4,0},{8,12},{12,8},{16,20},{20,16},{24,28},{28,24},{1,5},{5... | collective-permute-start | bytes 1572872 | tf_op jit(solution)/shard_map/ppermute | solution.py:175
  53.1 8.3 %collective-permute-start.12 = (bf16[2,256,128]{2,1,0:T(8,128)(2,1)S(1)}, bf16[2,256,128]{2,1,0:T(8,128)(2,1)S(1)}, u32[]{:S(2)}, u32[]{:S(2)}) collective-permute-start(bf16[2,256,128]{2,1,0:T(8,128)(2,1)S(1)} %get-tuple-element.28), channel_id=1, source_target_pairs={{0,3},{1,2},{2,1},{3,0},{4,7},{5,6},{6,5},{7,4},{8,11},{9,10},{10,... | collective-permute-start | bytes 393224 | tf_op jit(solution)/shard_map/ppermute | solution.py:178
  57.0 11.4 %collective-permute-start.13 = (bf16[2,256,128]{2,1,0:T(8,128)(2,1)S(1)}, bf16[2,256,128]{2,1,0:T(8,128)(2,1)S(1)}, u32[]{:S(2)}, u32[]{:S(2)}) collective-permute-start(bf16[2,256,128]{2,1,0:T(8,128)(2,1)S(1)} %get-tuple-element.29), channel_id=1, source_target_pairs={{0,2},{1,3},{2,0},{3,1},{4,6},{5,7},{6,4},{7,5},{8,10},{9,11},{10,... | collective-permute-start | bytes 393224 | tf_op jit(solution)/shard_map/ppermute | solution.py:178
  57.0 11.4 %collective-permute-start.14 = (bf16[2,256,128]{2,1,0:T(8,128)(2,1)S(1)}, bf16[2,256,128]{2,1,0:T(8,128)(2,1)S(1)}, u32[]{:S(2)}, u32[]{:S(2)}) collective-permute-start(bf16[2,256,128]{2,1,0:T(8,128)(2,1)S(1)} %get-tuple-element.30), channel_id=1, source_target_pairs={{0,1},{1,0},{2,3},{3,2},{4,5},{5,4},{6,7},{7,6},{8,9},{9,8},{10,11... | collective-permute-start | bytes 393224 | tf_op jit(solution)/shard_map/ppermute | solution.py:178
  68.4 1.4 %collective-permute-start.15 = (bf16[2,256,128]{2,1,0:T(8,128)(2,1)S(1)}, bf16[2,256,128]{2,1,0:T(8,128)(2,1)S(1)}, u32[]{:S(2)}, u32[]{:S(2)}) collective-permute-start(bf16[2,256,128]{2,1,0:T(8,128)(2,1)S(1)} %shard_map.51.own_ref), channel_id=1, source_target_pairs={{0,4},{4,0},{8,12},{12,8},{16,20},{20,16},{24,28},{28,24},{1,5},{5... | collective-permute-start | bytes 393224 | tf_op jit(solution)/shard_map/ppermute | solution.py:175
  (6 other events, 4.3 us)

commit v8 on v7

--- a/solution.py
+++ b/solution.py
@@ -40,26 +40,8 @@
     return iota((TILE, TILE), 0) == (1 - h) * SUB * SUB + b * SUB + a
 
 
-def pack_kernel(integrals_ref, blocks_ref, out_ref, sems):
-    slabs, length = integrals_ref.shape[:2]
-    copies = [
-        pltpu.make_async_copy(integrals_ref.at[s], out_ref.at[s, pl.ds(0, length)], sems.at[s]) for s in range(slabs)
-    ]
-    for copy in copies:
-        copy.start()
-    lane = iota((EXTRA, TILE), 1)
-    for s in range(slabs):
-        ids = jnp.zeros((EXTRA, TILE), jnp.int32)
-        for t in range(length // TILE):
-            for which in range(2):
-                ids = jnp.where(lane == 2 * t + which, blocks_ref[s, which, t], ids)
-        out_ref[s, length:, :] = ids.astype(F32).astype(BF16)
-    for copy in copies:
-        copy.wait()
-
-
-def cut_kernel(x_ref, y_ref, *outs):
-    for s, out_ref in enumerate(outs):
+def cut_kernel(slabs, x_ref, y_ref, *refs):
+    for s, out_ref in enumerate(refs[-slabs:]):
         out_ref[...] = (x_ref if s % 2 == 0 else y_ref)[s]
 
 
@@ -67,10 +49,9 @@
     empty = jnp.zeros((TILE, TILE), BF16)
     rows = acc_refs[0].shape[1]
 
-    @pl.loop(0, blocks_ref.shape[0] // 4, unroll=4)
+    @pl.loop(0, blocks_ref.shape[1] // 2, unroll=4)
     def _(t):
-        to = [blocks_ref[4 * t + 2 * k] for k in range(2)]
-        come = [blocks_ref[4 * t + 2 * k + 1] for k in range(2)]
+        to, come = [[blocks_ref[which, 2 * t + k] for k in range(2)] for which in range(2)]
         tiles = [tiles_ref[pl.ds(pl.multiple_of((2 * t + k) * TILE, TILE), TILE), :] for k in range(2)]
         right = jnp.concatenate(
             [jnp.concatenate([tiles[0], empty], axis=1), jnp.concatenate([empty, tiles[1]], axis=1)], axis=0
@@ -135,15 +116,9 @@
 
 
 def join_kernel(keep_ref, come_ref, *outs):
-    for shift, out_ref in enumerate(outs):
-        out_ref[...] = (keep_ref[shift].astype(F32) + come_ref[shift].astype(F32)).astype(BF16)
-
-
-def total_kernel(*refs):
-    total = refs[0][...].astype(F32)
-    for ref in refs[1:-1]:
-        total += ref[...].astype(F32)
-    refs[-1][...] = total.astype(BF16)
+    for place in range(keep_ref.shape[0]):
+        total = keep_ref[place].astype(F32) + come_ref[place].astype(F32)
+        outs[place % 2][place // 2] = total.astype(BF16)
 
 
 def finish_kernel(own_ref, other_ref, column_ref, out_ref):
@@ -177,13 +152,9 @@
     def along(array, bits):
         return lax.ppermute(array, "vir", [(i, i ^ bits) for i in range(n_vir)])
 
-    packed = call(
-        pack_kernel,
-        jax.ShapeDtypeStruct((slabs, length + EXTRA, TILE), BF16),
-        [pl.BlockSpec(memory_space=pltpu.HBM), SMEM],
-        [pltpu.SemaphoreType.DMA((slabs,))],
-        megabytes=8,
-    )(integrals.reshape(slabs, length, TILE), tile_blocks.transpose(0, 2, 1))
+    ids = tile_blocks.transpose(0, 2, 1).astype(BF16)
+    ids = jnp.pad(ids, ((0, 0), (0, EXTRA - 2), (0, TILE - tile_dev)))
+    packed = jnp.concatenate([integrals.reshape(slabs, length, TILE), ids], axis=1)
     early = [packed, across(packed, 2), across(packed, 4)]
 
     pieces = {0: amplitudes}
@@ -193,9 +164,14 @@
         reach //= 2
     mine = [pieces[shift] for shift in range(n_vir)]
     others = [across(piece, 1) for piece in mine]
-    tiles_x, tiles_y, *_ = lax.optimization_barrier((*early[1:], *others[:-1], *mine[:-1]))
+    first = [*others[:-1], *mine[1:-1]]
     slab = jax.ShapeDtypeStruct((length + EXTRA, TILE), BF16)
-    halves = call(cut_kernel, [slab] * slabs, [VMEM, VMEM], megabytes=4)(tiles_x, tiles_y)
+    halves = call(
+        functools.partial(cut_kernel, slabs),
+        [slab] * slabs,
+        [VMEM, VMEM] + [pl.BlockSpec(memory_space=pl.ANY)] * len(first),
+        megabytes=4,
+    )(early[1], early[2], *first)
     late = [across(half, 4 if s % 2 == 0 else 2) for s, half in enumerate(halves)]
     reach = 4
     while reach < chips:
@@ -206,7 +182,7 @@
     row, column = mirror_row.reshape(1, rows), mirror_row.reshape(rows, 1)
 
     def ids(array):
-        return array[:, length, : 2 * tile_dev].astype(jnp.int32)
+        return array[:, length : length + 2, :tile_dev].astype(jnp.int32)
 
     sums = jax.ShapeDtypeStruct((n_blk, rows, TILE), F32)
     grid, *sums_so_far = call(
@@ -223,10 +199,14 @@
         megabytes=24,
         aliases={1: 2, 2: 3},
     )(grid, *sums_so_far, *late, *[ids(array) for array in late])
-    one = jax.ShapeDtypeStruct((per // 2, rows, TILE), BF16)
-    parts = call(join_kernel, [one] * n_vir, [VMEM, VMEM], megabytes=4)(keep, across(send, 1))
-    arrived = [along(parts[shift], shift) for shift in range(n_vir - 1, 0, -1)]
-    total = call(total_kernel, one, [VMEM] * n_vir, megabytes=4)(parts[0], *arrived)
+    come, left, reach = across(send, 1), n_vir, 1
+    while left > 1:
+        left //= 2
+        part = jax.ShapeDtypeStruct((left, per // 2, rows, TILE), BF16)
+        keep, send = call(join_kernel, [part, part], [VMEM, VMEM], megabytes=4)(keep, come)
+        come = along(send, reach)
+        reach *= 2
+    total = call(join_kernel, [part], [VMEM, VMEM], megabytes=4)(keep, come)[0][0]
     return call(
         finish_kernel, jax.ShapeDtypeStruct((rows, width), BF16), [VMEM] * 3, megabytes=8
     )(total, across(total, 1), column)

time: 71.6 us -> 72.9 us (1.018)
  local copies, waits for them, and re-layouts: 10.4 us -> 5.7 us
  waiting for transfers between devices: 28.7 us -> 33.2 us
  other arithmetic: 0.69 us -> 2.7 us
    unnamed x28 -> x24, local copies, waits for them, and re-layouts: 10.3 us -> 5.57 us
    ppermute x10, waiting for transfers between devices: 7.87 us -> 10.6 us  [across(): return lax.ppermute(array, 'pair', [(i, i ^ bits) for i in range(n_pair)])]
    ppermute x6 -> x5, waiting for transfers between devices: 20.9 us -> 22.6 us  [along(): return lax.ppermute(array, 'vir', [(i, i ^ bits) for i in range(n_vir)])]
    concatenate x0 -> x1, other arithmetic: none -> 1.29 us  [local(): jnp.concatenate([integrals.reshape(slabs, length, TILE), ids], axis=1)]
    ppermute x6 -> x5, starting transfers between devices: 9.64 us -> 9.8 us  [along(): return lax.ppermute(array, 'vir', [(i, i ^ bits) for i in range(n_vir)])]
  transfers between devices with their start and end apart: 16 -> 15, of which waited for: 8 -> 10; matrix products, arithmetic and copies ran while one was open for 1% -> 1% of each run, Pallas kernels for 12% -> 12%
where the time goes in v8:
time: 72.9 us; the launch traced here: 72.5 us
  waiting for transfers between devices  33.2 us (46%)
  starting transfers between devices  17.2 us (24%)
  Pallas kernels  13.6 us (19%)
  local copies, waits for them, and re-layouts  5.7 us (8%)
  other arithmetic  2.7 us (4%)
    ppermute x5, waiting for transfers between devices, along(): return lax.ppermute(array, 'vir', [(i, i ^ bits) for i in range(n_vir)])  22.6 us
    ppermute x10, waiting for transfers between devices, across(): return lax.ppermute(array, 'pair', [(i, i ^ bits) for i in range(n_pair)])  10.6 us
    ppermute x5, starting transfers between devices, along(): return lax.ppermute(array, 'vir', [(i, i ^ bits) for i in range(n_vir)])  9.8 us
    pallas_call x1, Pallas kernels, local(): call(functools.partial(first_kernel, n_vir, len(early)), [jax.ShapeDtypeS...  7.7 us
    ppermute x10, starting transfers between devices, across(): return lax.ppermute(array, 'pair', [(i, i ^ bits) for i in range(n_pair)])  7.38 us
    unnamed x24, local copies, waits for them, and re-layouts  5.57 us
    pallas_call x1, Pallas kernels, local(): call(functools.partial(second_kernel, n_vir, len(late)), [piece, piece, s...  3.44 us
  transfers between devices with their start and end apart: 15, of which 10 were waited for; matrix products, arithmetic and copies ran while one was open for 1% of the time, Pallas kernels for 12%

profile of v8, /device:TPU:0, one launch (start us, length us, event | category | flops | bytes accessed | tf_op | source)
XLA Modules:
  0.0 72.5 jit_solution(4237690525680092023)
XLA Ops:
  0.7 1.3 %fusion.1.refs_8_ = bf16[2,2064,128]{2,1,0:T(8,128)(2,1)S(1)} fusion(bf16[2,2,16]{2,1,0:T(2,128)(2,1)S(1)} %get-tuple-element.28, bf16[2,2048,128]{2,1,0:T(8,128)(2,1)} %bitcast.15), kind=kLoop, calls=%fused_computation.2 | loop fusion | flops 3170304 | bytes 2105472 | tf_op jit(solution)/shard_map/concatenate | solution.py:157
  2.0 3.0 %collective-permute-start.8 = (bf16[2,2064,128]{2,1,0:T(8,128)(2,1)S(1)}, bf16[2,2064,128]{2,1,0:T(8,128)(2,1)S(1)}, u32[]{:S(2)}, u32[]{:S(2)}) collective-permute-start(bf16[2,2064,128]{2,1,0:T(8,128)(2,1)S(1)} %fusion.1.refs_8_), channel_id=1, source_target_pairs={{0,16},{4,20},{8,24},{12,28},{16,0},{20,4},{24,8},{28,12},{1,17},{... | collective-permute-start | bytes 3170312 | tf_op jit(solution)/shard_map/ppermute | solution.py:150
  5.1 1.5 %collective-permute-start.7 = (bf16[2,2064,128]{2,1,0:T(8,128)(2,1)S(1)}, bf16[2,2064,128]{2,1,0:T(8,128)(2,1)S(1)}, u32[]{:S(2)}, u32[]{:S(2)}) collective-permute-start(bf16[2,2064,128]{2,1,0:T(8,128)(2,1)S(1)} %fusion.1.refs_8_), channel_id=1, source_target_pairs={{0,8},{4,12},{8,0},{12,4},{16,24},{20,28},{24,16},{28,20},{1,9},{5... | collective-permute-start | bytes 3170312 | tf_op jit(solution)/shard_map/ppermute | solution.py:150
  6.6 2.6 %collective-permute-start.1 = (bf16[256,512]{1,0:T(8,128)(2,1)S(1)}, bf16[256,512]{1,0:T(8,128)(2,1)}, u32[]{:S(2)}, u32[]{:S(2)}) collective-permute-start(bf16[256,512]{1,0:T(8,128)(2,1)S(1)} %copy-done.8), channel_id=1, source_target_pairs={{0,2},{1,3},{2,0},{3,1},{4,6},{5,7},{6,4},{7,5},{8,10},{9,11},{10,... | collective-permute-start | bytes 786440 | tf_op jit(solution)/shard_map/ppermute | solution.py:153
  9.2 1.6 %collective-permute-start = (bf16[256,512]{1,0:T(8,128)(2,1)S(1)}, bf16[256,512]{1,0:T(8,128)(2,1)S(1)}, u32[]{:S(2)}, u32[]{:S(2)}) collective-permute-start(bf16[256,512]{1,0:T(8,128)(2,1)S(1)} %copy-done.8), channel_id=1, source_target_pairs={{0,1},{1,0},{2,3},{3,2},{4,5},{5,4},{6,7},{7,6},{8,9},{9,8},{10,11... | collective-permute-start | bytes 786440 | tf_op jit(solution)/shard_map/ppermute | solution.py:153
  10.7 10.0 %collective-permute-done.1.refs_2_.refs_4_ = bf16[256,512]{1,0:T(8,128)(2,1)} collective-permute-done((bf16[256,512]{1,0:T(8,128)(2,1)S(1)}, bf16[256,512]{1,0:T(8,128)(2,1)}, u32[]{:S(2)}, u32[]{:S(2)}) %collective-permute-start.1) | collective-permute-done | bytes 262176 | tf_op jit(solution)/shard_map/ppermute | solution.py:153
  21.3 1.1 %collective-permute-start.2 = (bf16[256,512]{1,0:T(8,128)(2,1)}, bf16[256,512]{1,0:T(8,128)(2,1)}, u32[]{:S(2)}, u32[]{:S(2)}) collective-permute-start(bf16[256,512]{1,0:T(8,128)(2,1)} %collective-permute-done.1.refs_2_.refs_4_), channel_id=1, source_target_pairs={{0,1},{1,0},{2,3},{3,2},{4,5},{5,4},{6,7},{7,6},{8,9},{9,8},{10,11... | collective-permute-start | bytes 786440 | tf_op jit(solution)/shard_map/ppermute | solution.py:153
  22.7 5.7 %collective-permute-done.8.refs_10_.y_ref = bf16[2,2064,128]{2,1,0:T(8,128)(2,1)S(1)} collective-permute-done((bf16[2,2064,128]{2,1,0:T(8,128)(2,1)S(1)}, bf16[2,2064,128]{2,1,0:T(8,128)(2,1)S(1)}, u32[]{:S(2)}, u32[]{:S(2)}) %collective-permute-start.8) | collective-permute-done | bytes 1056800 | tf_op jit(solution)/shard_map/ppermute | solution.py:150
  28.4 1.5 %collective-permute-done.7.refs_9_.x_ref = bf16[2,2064,128]{2,1,0:T(8,128)(2,1)S(1)} collective-permute-done((bf16[2,2064,128]{2,1,0:T(8,128)(2,1)S(1)}, bf16[2,2064,128]{2,1,0:T(8,128)(2,1)S(1)}, u32[]{:S(2)}, u32[]{:S(2)}) %collective-permute-start.7) | collective-permute-done | bytes 1056800 | tf_op jit(solution)/shard_map/ppermute | solution.py:150
  32.2 1.7 %collective-permute-start.10 = (bf16[2064,128]{1,0:T(8,128)(2,1)}, bf16[2064,128]{1,0:T(8,128)(2,1)S(1)}, u32[]{:S(2)}, u32[]{:S(2)}) collective-permute-start(bf16[2064,128]{1,0:T(8,128)(2,1)} %copy-done.11), channel_id=1, source_target_pairs={{0,8},{4,12},{8,0},{12,4},{16,24},{20,28},{24,16},{28,20},{1,9},{5... | collective-permute-start | bytes 1585160 | tf_op jit(solution)/shard_map/ppermute | solution.py:150
  33.9 0.9 %copy-done.1 = bf16[256,512]{1,0:T(8,128)(2,1)S(1)} copy-done((bf16[256,512]{1,0:T(8,128)(2,1)S(1)}, bf16[256,512]{1,0:T(8,128)(2,1)}, u32[]{:S(2)}) %copy-start.1) | copy-done | bytes 262168
  34.8 0.9 %copy-done.3 = bf16[256,512]{1,0:T(8,128)(2,1)S(1)} copy-done((bf16[256,512]{1,0:T(8,128)(2,1)S(1)}, bf16[256,512]{1,0:T(8,128)(2,1)}, u32[]{:S(2)}) %copy-start.3) | copy-done | bytes 262168
  35.8 0.9 %copy-done.5 = bf16[256,512]{1,0:T(8,128)(2,1)S(1)} copy-done((bf16[256,512]{1,0:T(8,128)(2,1)S(1)}, bf16[256,512]{1,0:T(8,128)(2,1)}, u32[]{:S(2)}) %copy-start.5) | copy-done | bytes 262168
  36.7 0.9 %copy-done.7 = bf16[256,512]{1,0:T(8,128)(2,1)S(1)} copy-done((bf16[256,512]{1,0:T(8,128)(2,1)S(1)}, bf16[256,512]{1,0:T(8,128)(2,1)}, u32[]{:S(2)}) %copy-start.7) | copy-done | bytes 262168
  37.7 0.9 %copy-done.9 = bf16[256,512]{1,0:T(8,128)(2,1)S(1)} copy-done((bf16[256,512]{1,0:T(8,128)(2,1)S(1)}, bf16[256,512]{1,0:T(8,128)(2,1)}, u32[]{:S(2)}) %copy-start.9) | copy-done | bytes 262168
  38.6 7.7 %shard_map.46 = (bf16[16,512,128]{2,1,0:T(8,128)(2,1)S(1)}, f32[16,256,128]{2,1,0:T(8,128)S(1)}, f32[16,256,128]{2,1,0:T(8,128)S(1)}) custom-call(bf16[256,512]{1,0:T(8,128)(2,1)S(1)} %copy-done.9, bf16[256,512]{1,0:T(8,128)(2,1)S(1)} %copy-done.1, bf16[256,512]{1,0:T(8,128)(2,1)} %collective-permute-done.1.refs_2_.refs_4_, ...), custom_call_target="tpu_custom_call" | custom-call | tf_op jit(solution)/shard_map/pallas_call | solution.py:188
  47.0 3.4 %shard_map.48 = (bf16[4,2,256,128]{3,2,1,0:T(8,128)(2,1)S(1)}, bf16[4,2,256,128]{3,2,1,0:T(8,128)(2,1)S(1)}, f32[16,256,128]{2,1,0:T(8,128)S(1)}, f32[16,256,128]{2,1,0:T(8,128)S(1)}) custom-call(bf16[16,512,128]{2,1,0:T(8,128)(2,1)S(1)} %get-tuple-element.16.refs_0_, ...), custom_call_target="tpu_custom_call", output_to_operand_aliasing={{2}: (1, {}), {3}: (2, {})} | custom-call | tf_op jit(solution)/shard_map/pallas_call | solution.py:195
  50.7 1.8 %collective-permute-done.11.come_ref = bf16[4,2,256,128]{3,2,1,0:T(8,128)(2,1)S(1)} collective-permute-done((bf16[4,2,256,128]{3,2,1,0:T(8,128)(2,1)S(1)}, bf16[4,2,256,128]{3,2,1,0:T(8,128)(2,1)S(1)}, u32[]{:S(2)}, u32[]{:S(2)}) %collective-permute-start.11) | collective-permute-done | bytes 524320 | tf_op jit(solution)/shard_map/ppermute | solution.py:150
  52.6 1.8 %collective-permute-start.12 = (bf16[2,2,256,128]{3,2,1,0:T(8,128)(2,1)S(1)}, bf16[2,2,256,128]{3,2,1,0:T(8,128)(2,1)S(1)}, u32[]{:S(2)}, u32[]{:S(2)}) collective-permute-start(bf16[2,2,256,128]{3,2,1,0:T(8,128)(2,1)S(1)} %get-tuple-element.24), channel_id=1, source_target_pairs={{0,1},{1,0},{2,3},{3,2},{4,5},{5,4},{6,7},{7,6},{8,9},{9,8},{10,11... | collective-permute-start | bytes 786440 | tf_op jit(solution)/shard_map/ppermute | solution.py:153
  54.3 6.7 %collective-permute-done.12.come_ref = bf16[2,2,256,128]{3,2,1,0:T(8,128)(2,1)S(1)} collective-permute-done((bf16[2,2,256,128]{3,2,1,0:T(8,128)(2,1)S(1)}, bf16[2,2,256,128]{3,2,1,0:T(8,128)(2,1)S(1)}, u32[]{:S(2)}, u32[]{:S(2)}) %collective-permute-start.12) | collective-permute-done | bytes 262176 | tf_op jit(solution)/shard_map/ppermute | solution.py:153
  61.1 2.8 %collective-permute-start.13 = (bf16[1,2,256,128]{3,2,1,0:T(8,128)(2,1)S(1)}, bf16[1,2,256,128]{3,2,1,0:T(8,128)(2,1)S(1)}, u32[]{:S(2)}, u32[]{:S(2)}) collective-permute-start(bf16[1,2,256,128]{3,2,1,0:T(8,128)(2,1)S(1)} %get-tuple-element.26), channel_id=1, source_target_pairs={{0,2},{1,3},{2,0},{3,1},{4,6},{5,7},{6,4},{7,5},{8,10},{9,11},{10,... | collective-permute-start | bytes 393224 | tf_op jit(solution)/shard_map/ppermute | solution.py:153
  63.9 5.8 %collective-permute-done.13.come_ref = bf16[1,2,256,128]{3,2,1,0:T(8,128)(2,1)S(1)} collective-permute-done((bf16[1,2,256,128]{3,2,1,0:T(8,128)(2,1)S(1)}, bf16[1,2,256,128]{3,2,1,0:T(8,128)(2,1)S(1)}, u32[]{:S(2)}, u32[]{:S(2)}) %collective-permute-start.13) | collective-permute-done | bytes 131104 | tf_op jit(solution)/shard_map/ppermute | solution.py:153
  69.8 1.3 %collective-permute-done.14.other_ref = bf16[2,256,128]{2,1,0:T(8,128)(2,1)S(1)} collective-permute-done((bf16[2,256,128]{2,1,0:T(8,128)(2,1)S(1)}, bf16[2,256,128]{2,1,0:T(8,128)(2,1)S(1)}, u32[]{:S(2)}, u32[]{:S(2)}) %collective-permute-start.14) | collective-permute-done | bytes 131104 | tf_op jit(solution)/shard_map/ppermute | solution.py:150
  71.1 1.3 %shard_map.52 = bf16[256,512]{1,0:T(8,128)(2,1)} custom-call(bf16[2,256,128]{2,1,0:T(8,128)(2,1)S(1)} %bitcast.12, bf16[2,256,128]{2,1,0:T(8,128)(2,1)S(1)} %collective-permute-done.14.other_ref, s32[256,1]{1,0:T(8,128)S(1)} %copy.7.refs_15_.column_ref), custom_call_target="tpu_custom_call" | custom-call | tf_op jit(solution)/shard_map/pallas_call | solution.py:210
  (44 shorter events, 5.0 us)
Async XLA Ops:
  0.0 6.6 %copy-start.8 = (bf16[256,512]{1,0:T(8,128)(2,1)S(1)}, bf16[256,512]{1,0:T(8,128)(2,1)}, u32[]{:S(2)}) copy-start(bf16[256,512]{1,0:T(8,128)(2,1)} %refs_0_.1) | copy-start | bytes 786436
  2.0 29.9 %copy-start.10 = (s32[256]{0:T(256)S(1)}, s32[256]{0:T(256)}, u32[]{:S(2)}) copy-start(s32[256]{0:T(256)} %param.7) | copy-start | bytes 3076
  2.0 26.4 %collective-permute-start.8 = (bf16[2,2064,128]{2,1,0:T(8,128)(2,1)S(1)}, bf16[2,2064,128]{2,1,0:T(8,128)(2,1)S(1)}, u32[]{:S(2)}, u32[]{:S(2)}) collective-permute-start(bf16[2,2064,128]{2,1,0:T(8,128)(2,1)S(1)} %fusion.1.refs_8_), channel_id=1, source_target_pairs={{0,16},{4,20},{8,24},{12,28},{16,0},{20,4},{24,8},{28,12},{1,17},{... | collective-permute-start | bytes 3170312 | tf_op jit(solution)/shard_map/ppermute | solution.py:150
  5.1 24.8 %collective-permute-start.7 = (bf16[2,2064,128]{2,1,0:T(8,128)(2,1)S(1)}, bf16[2,2064,128]{2,1,0:T(8,128)(2,1)S(1)}, u32[]{:S(2)}, u32[]{:S(2)}) collective-permute-start(bf16[2,2064,128]{2,1,0:T(8,128)(2,1)S(1)} %fusion.1.refs_8_), channel_id=1, source_target_pairs={{0,8},{4,12},{8,0},{12,4},{16,24},{20,28},{24,16},{28,20},{1,9},{5... | collective-permute-start | bytes 3170312 | tf_op jit(solution)/shard_map/ppermute | solution.py:150
  6.6 14.2 %collective-permute-start.1 = (bf16[256,512]{1,0:T(8,128)(2,1)S(1)}, bf16[256,512]{1,0:T(8,128)(2,1)}, u32[]{:S(2)}, u32[]{:S(2)}) collective-permute-start(bf16[256,512]{1,0:T(8,128)(2,1)S(1)} %copy-done.8), channel_id=1, source_target_pairs={{0,2},{1,3},{2,0},{3,1},{4,6},{5,7},{6,4},{7,5},{8,10},{9,11},{10,... | collective-permute-start | bytes 786440 | tf_op jit(solution)/shard_map/ppermute | solution.py:153
  9.2 11.7 %collective-permute-start = (bf16[256,512]{1,0:T(8,128)(2,1)S(1)}, bf16[256,512]{1,0:T(8,128)(2,1)S(1)}, u32[]{:S(2)}, u32[]{:S(2)}) collective-permute-start(bf16[256,512]{1,0:T(8,128)(2,1)S(1)} %copy-done.8), channel_id=1, source_target_pairs={{0,1},{1,0},{2,3},{3,2},{4,5},{5,4},{6,7},{7,6},{8,9},{9,8},{10,11... | collective-permute-start | bytes 786440 | tf_op jit(solution)/shard_map/ppermute | solution.py:153
  10.7 10.6 %collective-permute-start.3 = (bf16[256,512]{1,0:T(8,128)(2,1)S(1)}, bf16[256,512]{1,0:T(8,128)(2,1)S(1)}, u32[]{:S(2)}, u32[]{:S(2)}) collective-permute-start(bf16[256,512]{1,0:T(8,128)(2,1)S(1)} %copy-done.8), channel_id=1, source_target_pairs={{0,4},{4,0},{8,12},{12,8},{16,20},{20,16},{24,28},{28,24},{1,5},{5... | collective-permute-start | bytes 786440 | tf_op jit(solution)/shard_map/ppermute | solution.py:150
  20.8 1.7 %collective-permute-start.5 = (bf16[256,512]{1,0:T(8,128)(2,1)}, bf16[256,512]{1,0:T(8,128)(2,1)S(1)}, u32[]{:S(2)}, u32[]{:S(2)}) collective-permute-start(bf16[256,512]{1,0:T(8,128)(2,1)} %collective-permute-done.1.refs_2_.refs_4_), channel_id=1, source_target_pairs={{0,4},{4,0},{8,12},{12,8},{16,20},{20,16},{24,28},{28,24},{1,5},{5... | collective-permute-start | bytes 786440 | tf_op jit(solution)/shard_map/ppermute | solution.py:150
  20.9 11.0 %copy-start = (bf16[256,512]{1,0:T(8,128)(2,1)}, bf16[256,512]{1,0:T(8,128)(2,1)S(1)}, u32[]{:S(2)}) copy-start(bf16[256,512]{1,0:T(8,128)(2,1)S(1)} %collective-permute-done.refs_1_.refs_3_) | copy-start | bytes 786436
  20.9 1.8 %collective-permute-start.4 = (bf16[256,512]{1,0:T(8,128)(2,1)S(1)}, bf16[256,512]{1,0:T(8,128)(2,1)S(1)}, u32[]{:S(2)}, u32[]{:S(2)}) collective-permute-start(bf16[256,512]{1,0:T(8,128)(2,1)S(1)} %collective-permute-done.refs_1_.refs_3_), channel_id=1, source_target_pairs={{0,4},{4,0},{8,12},{12,8},{16,20},{20,16},{24,28},{28,24},{1,5},{5... | collective-permute-start | bytes 786440 | tf_op jit(solution)/shard_map/ppermute | solution.py:150
  21.3 10.6 %copy-start.2 = (bf16[256,512]{1,0:T(8,128)(2,1)}, bf16[256,512]{1,0:T(8,128)(2,1)S(1)}, u32[]{:S(2)}) copy-start(bf16[256,512]{1,0:T(8,128)(2,1)S(1)} %collective-permute-done.3.refs_4_.refs_0_) | copy-start | bytes 786436
  21.3 10.8 %collective-permute-start.2 = (bf16[256,512]{1,0:T(8,128)(2,1)}, bf16[256,512]{1,0:T(8,128)(2,1)}, u32[]{:S(2)}, u32[]{:S(2)}) collective-permute-start(bf16[256,512]{1,0:T(8,128)(2,1)} %collective-permute-done.1.refs_2_.refs_4_), channel_id=1, source_target_pairs={{0,1},{1,0},{2,3},{3,2},{4,5},{5,4},{6,7},{7,6},{8,9},{9,8},{10,11... | collective-permute-start | bytes 786440 | tf_op jit(solution)/shard_map/ppermute | solution.py:153
  22.5 9.4 %copy-start.4 = (bf16[256,512]{1,0:T(8,128)(2,1)}, bf16[256,512]{1,0:T(8,128)(2,1)S(1)}, u32[]{:S(2)}) copy-start(bf16[256,512]{1,0:T(8,128)(2,1)S(1)} %collective-permute-done.5.refs_6_.refs_2_) | copy-start | bytes 786436
  22.7 9.2 %copy-start.6 = (bf16[256,512]{1,0:T(8,128)(2,1)}, bf16[256,512]{1,0:T(8,128)(2,1)S(1)}, u32[]{:S(2)}) copy-start(bf16[256,512]{1,0:T(8,128)(2,1)S(1)} %collective-permute-done.4.refs_5_.refs_1_) | copy-start | bytes 786436
  31.5 14.8 %collective-permute-start.9 = (bf16[2064,128]{1,0:T(8,128)(2,1)}, bf16[2064,128]{1,0:T(8,128)(2,1)}, u32[]{:S(2)}, u32[]{:S(2)}) collective-permute-start(bf16[2064,128]{1,0:T(8,128)(2,1)} %get-tuple-element.19), channel_id=1, source_target_pairs={{0,16},{4,20},{8,24},{12,28},{16,0},{20,4},{24,8},{28,12},{1,17},{... | collective-permute-start | bytes 1585160 | tf_op jit(solution)/shard_map/ppermute | solution.py:150
  32.1 1.8 %collective-permute-start.6 = (bf16[256,512]{1,0:T(8,128)(2,1)}, bf16[256,512]{1,0:T(8,128)(2,1)S(1)}, u32[]{:S(2)}, u32[]{:S(2)}) collective-permute-start(bf16[256,512]{1,0:T(8,128)(2,1)} %collective-permute-done.2.refs_3_), channel_id=1, source_target_pairs={{0,4},{4,0},{8,12},{12,8},{16,20},{20,16},{24,28},{28,24},{1,5},{5... | collective-permute-start | bytes 786440 | tf_op jit(solution)/shard_map/ppermute | solution.py:150
  32.2 14.9 %collective-permute-start.10 = (bf16[2064,128]{1,0:T(8,128)(2,1)}, bf16[2064,128]{1,0:T(8,128)(2,1)S(1)}, u32[]{:S(2)}, u32[]{:S(2)}) collective-permute-start(bf16[2064,128]{1,0:T(8,128)(2,1)} %copy-done.11), channel_id=1, source_target_pairs={{0,8},{4,12},{8,0},{12,4},{16,24},{20,28},{24,16},{28,20},{1,9},{5... | collective-permute-start | bytes 1585160 | tf_op jit(solution)/shard_map/ppermute | solution.py:150
  33.9 1.0 %copy-start.1 = (bf16[256,512]{1,0:T(8,128)(2,1)S(1)}, bf16[256,512]{1,0:T(8,128)(2,1)}, u32[]{:S(2)}) copy-start(bf16[256,512]{1,0:T(8,128)(2,1)} %copy-done) | copy-start | bytes 786436
  34.8 0.9 %copy-start.3 = (bf16[256,512]{1,0:T(8,128)(2,1)S(1)}, bf16[256,512]{1,0:T(8,128)(2,1)}, u32[]{:S(2)}) copy-start(bf16[256,512]{1,0:T(8,128)(2,1)} %copy-done.2) | copy-start | bytes 786436
  35.8 0.9 %copy-start.5 = (bf16[256,512]{1,0:T(8,128)(2,1)S(1)}, bf16[256,512]{1,0:T(8,128)(2,1)}, u32[]{:S(2)}) copy-start(bf16[256,512]{1,0:T(8,128)(2,1)} %copy-done.4) | copy-start | bytes 786436
  50.5 2.0 %collective-permute-start.11 = (bf16[4,2,256,128]{3,2,1,0:T(8,128)(2,1)S(1)}, bf16[4,2,256,128]{3,2,1,0:T(8,128)(2,1)S(1)}, u32[]{:S(2)}, u32[]{:S(2)}) collective-permute-start(bf16[4,2,256,128]{3,2,1,0:T(8,128)(2,1)S(1)} %get-tuple-element.22), channel_id=1, source_target_pairs={{0,4},{4,0},{8,12},{12,8},{16,20},{20,16},{24,28},{28,24},{1,5},{5... | collective-permute-start | bytes 1572872 | tf_op jit(solution)/shard_map/ppermute | solution.py:150
  52.6 8.4 %collective-permute-start.12 = (bf16[2,2,256,128]{3,2,1,0:T(8,128)(2,1)S(1)}, bf16[2,2,256,128]{3,2,1,0:T(8,128)(2,1)S(1)}, u32[]{:S(2)}, u32[]{:S(2)}) collective-permute-start(bf16[2,2,256,128]{3,2,1,0:T(8,128)(2,1)S(1)} %get-tuple-element.24), channel_id=1, source_target_pairs={{0,1},{1,0},{2,3},{3,2},{4,5},{5,4},{6,7},{7,6},{8,9},{9,8},{10,11... | collective-permute-start | bytes 786440 | tf_op jit(solution)/shard_map/ppermute | solution.py:153
  61.1 8.6 %collective-permute-start.13 = (bf16[1,2,256,128]{3,2,1,0:T(8,128)(2,1)S(1)}, bf16[1,2,256,128]{3,2,1,0:T(8,128)(2,1)S(1)}, u32[]{:S(2)}, u32[]{:S(2)}) collective-permute-start(bf16[1,2,256,128]{3,2,1,0:T(8,128)(2,1)S(1)} %get-tuple-element.26), channel_id=1, source_target_pairs={{0,2},{1,3},{2,0},{3,1},{4,6},{5,7},{6,4},{7,5},{8,10},{9,11},{10,... | collective-permute-start | bytes 393224 | tf_op jit(solution)/shard_map/ppermute | solution.py:153
  69.7 1.4 %collective-permute-start.14 = (bf16[2,256,128]{2,1,0:T(8,128)(2,1)S(1)}, bf16[2,256,128]{2,1,0:T(8,128)(2,1)S(1)}, u32[]{:S(2)}, u32[]{:S(2)}) collective-permute-start(bf16[2,256,128]{2,1,0:T(8,128)(2,1)S(1)} %bitcast.11), channel_id=1, source_target_pairs={{0,4},{4,0},{8,12},{12,8},{16,20},{20,16},{24,28},{28,24},{1,5},{5... | collective-permute-start | bytes 393224 | tf_op jit(solution)/shard_map/ppermute | solution.py:150
  (3 other events, 2.7 us)

commit v9 on v8

--- a/solution.py
+++ b/solution.py
@@ -70,15 +70,14 @@
     own, other = refs[:n_vir], refs[n_vir : 2 * n_vir]
     tiles = refs[2 * n_vir : 2 * n_vir + n_sets]
     blocks = refs[2 * n_vir + n_sets : 2 * n_vir + 2 * n_sets]
-    row_ref, column_ref, grid_ref, *acc_refs = refs[2 * n_vir + 2 * n_sets :]
+    row_ref, grid_ref, *acc_refs = refs[2 * n_vir + 2 * n_sets :]
     rows, width = own[0].shape
     per = width // TILE
     pair = lax.axis_index("pair")
     vir = lax.axis_index("vir")
     upper = pair % 2 == 1
-    base = (pair ^ 1) * rows
-    wanted = jnp.where(upper, row_ref[...] - base - iota((rows, rows), 0), column_ref[...] - base - iota((rows, rows), 1))
-    hot = jnp.where(wanted == 0, 1.0, 0.0).astype(BF16)
+    mirrors = (row_ref[...] - (pair ^ 1) * rows == iota((rows, rows), 0)).astype(F32)
+    hot = jnp.where(upper, mirrors, mirrors.T).astype(BF16)
     for shift in range(n_vir):
         first = (vir ^ shift) * per
         mine, others = own[shift][...], other[shift][...]
@@ -116,17 +115,23 @@
 
 
 def join_kernel(keep_ref, come_ref, *outs):
-    for place in range(keep_ref.shape[0]):
-        total = keep_ref[place].astype(F32) + come_ref[place].astype(F32)
-        outs[place % 2][place // 2] = total.astype(BF16)
-
-
-def finish_kernel(own_ref, other_ref, column_ref, out_ref):
+    for shift, out_ref in enumerate(outs):
+        out_ref[...] = (keep_ref[shift].astype(F32) + come_ref[shift].astype(F32)).astype(BF16)
+
+
+def total_kernel(*refs):
+    total = refs[0][...].astype(F32)
+    for ref in refs[1:-1]:
+        total += ref[...].astype(F32)
+    refs[-1][...] = total.astype(BF16)
+
+
+def finish_kernel(own_ref, other_ref, row_ref, out_ref):
     half, rows, _ = own_ref.shape
     pair = lax.axis_index("pair")
     upper = pair % 2 == 1
-    place = jnp.where(upper, column_ref[...] - (pair ^ 1) * rows, iota((rows, 1), 0))
-    hot = (iota((rows, rows), 1) == place).astype(BF16)
+    place = jnp.where(upper, row_ref[...] - (pair ^ 1) * rows, iota((1, rows), 1))
+    hot = (iota((rows, rows), 0) == place).astype(F32).T.astype(BF16)
     same = (iota((TILE, TILE), 0) == iota((TILE, TILE), 1)).astype(F32)
     swap = jnp.where(upper, swap_matrix().astype(F32), same).astype(BF16)
     for which in range(2):
@@ -179,7 +184,7 @@
         late = late + [across(array, 2 * reach) for array in farther]
         reach *= 2
     late = [array.reshape(-1, length + EXTRA, TILE) for array in late]
-    row, column = mirror_row.reshape(1, rows), mirror_row.reshape(rows, 1)
+    row = mirror_row.reshape(1, rows)
 
     def ids(array):
         return array[:, length : length + 2, :tile_dev].astype(jnp.int32)
@@ -188,9 +193,9 @@
     grid, *sums_so_far = call(
         functools.partial(first_kernel, n_vir, len(early)),
         [jax.ShapeDtypeStruct((n_blk, 2 * rows, TILE), BF16), sums, sums],
-        [VMEM] * (2 * n_vir + len(early)) + [SMEM] * len(early) + [VMEM, VMEM],
+        [VMEM] * (2 * n_vir + len(early)) + [SMEM] * len(early) + [VMEM],
         megabytes=20,
-    )(*mine, *others, *early, *[ids(array) for array in early], row, column)
+    )(*mine, *others, *early, *[ids(array) for array in early], row)
     piece = jax.ShapeDtypeStruct((n_vir, per // 2, rows, TILE), BF16)
     keep, send, *_ = call(
         functools.partial(second_kernel, n_vir, len(late)),
@@ -199,17 +204,13 @@
         megabytes=24,
         aliases={1: 2, 2: 3},
     )(grid, *sums_so_far, *late, *[ids(array) for array in late])
-    come, left, reach = across(send, 1), n_vir, 1
-    while left > 1:
-        left //= 2
-        part = jax.ShapeDtypeStruct((left, per // 2, rows, TILE), BF16)
-        keep, send = call(join_kernel, [part, part], [VMEM, VMEM], megabytes=4)(keep, come)
-        come = along(send, reach)
-        reach *= 2
-    total = call(join_kernel, [part], [VMEM, VMEM], megabytes=4)(keep, come)[0][0]
+    one = jax.ShapeDtypeStruct((per // 2, rows, TILE), BF16)
+    parts = call(join_kernel, [one] * n_vir, [VMEM, VMEM], megabytes=4)(keep, across(send, 1))
+    arrived = [along(parts[shift], shift) for shift in range(n_vir - 1, 0, -1)]
+    total = call(total_kernel, one, [VMEM] * n_vir, megabytes=4)(parts[0], *arrived)
     return call(
         finish_kernel, jax.ShapeDtypeStruct((rows, width), BF16), [VMEM] * 3, megabytes=8
-    )(total, across(total, 1), column)
+    )(total, across(total, 1), row)
 
 
 def solution(mesh):

time: 72.9 us -> 68 us (0.933)
  local copies, waits for them, and re-layouts: 5.7 us -> 0.01 us
  waiting for transfers between devices: 33.2 us -> 37 us
  Pallas kernels: 13.6 us -> 12 us
    unnamed x24 -> x4, local copies, waits for them, and re-layouts: 5.57 us -> 0.01 us
    ppermute x10, waiting for transfers between devices: 10.6 us -> 16.1 us  [across(): return lax.ppermute(array, 'pair', [(i, i ^ bits) for i in range(n_pair)])]
    ppermute x5 -> x6, waiting for transfers between devices: 22.6 us -> 20.9 us  [along(): return lax.ppermute(array, 'vir', [(i, i ^ bits) for i in range(n_vir)])]
    pallas_call x1, Pallas kernels: 0.88 us -> 0.07 us  [local(): call(functools.partial(cut_kernel, slabs), [slab] * slabs, [VMEM, VMEM] +...]
    ppermute x5 -> x6, starting transfers between devices: 9.8 us -> 9.74 us  [along(): return lax.ppermute(array, 'vir', [(i, i ^ bits) for i in range(n_vir)])]
  transfers between devices with their start and end apart: 15 -> 16, of which waited for: 10 -> 11; matrix products, arithmetic and copies ran while one was open for 1% -> 0% of each run, Pallas kernels for 12% -> 11%
where the time goes in v9:
time: 68 us; the launch traced here: 67.9 us
  waiting for transfers between devices  37 us (54%)
  starting transfers between devices  16.8 us (25%)
  Pallas kernels  12 us (18%)
  other arithmetic  2.04 us (3%)
    ppermute x6, waiting for transfers between devices, along(): return lax.ppermute(array, 'vir', [(i, i ^ bits) for i in range(n_vir)])  20.9 us
    ppermute x10, waiting for transfers between devices, across(): return lax.ppermute(array, 'pair', [(i, i ^ bits) for i in range(n_pair)])  16.1 us
    ppermute x6, starting transfers between devices, along(): return lax.ppermute(array, 'vir', [(i, i ^ bits) for i in range(n_vir)])  9.74 us
    pallas_call x1, Pallas kernels, local(): call(functools.partial(first_kernel, n_vir, len(early)), [jax.ShapeDtypeS...  7.43 us
    ppermute x10, starting transfers between devices, across(): return lax.ppermute(array, 'pair', [(i, i ^ bits) for i in range(n_pair)])  7.06 us
    pallas_call x1, Pallas kernels, local(): call(functools.partial(second_kernel, n_vir, len(late)), [piece, piece, s...  2.97 us
  transfers between devices with their start and end apart: 16, of which 11 were waited for; matrix products, arithmetic and copies ran while one was open for 0% of the time, Pallas kernels for 11%

profile of v9, /device:TPU:0, one launch (start us, length us, event | category | flops | bytes accessed | tf_op | source)
XLA Modules:
  0.0 67.9 jit_solution(5941961593702081402)
XLA Ops:
  0.0 0.7 %fusion.2 = (s32[2,2,16]{2,1,0:T(2,128)S(1)}, bf16[2,2,16]{2,1,0:T(2,128)(2,1)S(1)}) fusion(s32[2,16,2]{1,2,0:T(2,128)} %param.6), kind=kLoop, calls=%fused_computation.8 | loop fusion | flops 128 | bytes 640 | tf_op jit(solution)/shard_map/convert_element_type | solution.py:190
  0.7 1.3 %fusion.1.refs_8_ = bf16[2,2064,128]{2,1,0:T(8,128)(2,1)S(1)} fusion(bf16[2,2,16]{2,1,0:T(2,128)(2,1)S(1)} %get-tuple-element.28, bf16[2,2048,128]{2,1,0:T(8,128)(2,1)} %bitcast.13), kind=kLoop, calls=%fused_computation.2 | loop fusion | flops 3170304 | bytes 2105472 | tf_op jit(solution)/shard_map/concatenate | solution.py:162
  2.0 3.0 %collective-permute-start.8 = (bf16[2,2064,128]{2,1,0:T(8,128)(2,1)S(1)}, bf16[2,2064,128]{2,1,0:T(8,128)(2,1)S(1)}, u32[]{:S(2)}, u32[]{:S(2)}) collective-permute-start(bf16[2,2064,128]{2,1,0:T(8,128)(2,1)S(1)} %fusion.1.refs_8_), channel_id=1, source_target_pairs={{0,16},{4,20},{8,24},{12,28},{16,0},{20,4},{24,8},{28,12},{1,17},{... | collective-permute-start | bytes 3170312 | tf_op jit(solution)/shard_map/ppermute | solution.py:155
  5.1 1.5 %collective-permute-start.7 = (bf16[2,2064,128]{2,1,0:T(8,128)(2,1)S(1)}, bf16[2,2064,128]{2,1,0:T(8,128)(2,1)S(1)}, u32[]{:S(2)}, u32[]{:S(2)}) collective-permute-start(bf16[2,2064,128]{2,1,0:T(8,128)(2,1)S(1)} %fusion.1.refs_8_), channel_id=1, source_target_pairs={{0,8},{4,12},{8,0},{12,4},{16,24},{20,28},{24,16},{28,20},{1,9},{5... | collective-permute-start | bytes 3170312 | tf_op jit(solution)/shard_map/ppermute | solution.py:155
  6.6 2.6 %collective-permute-start.1 = (bf16[256,512]{1,0:T(8,128)(2,1)S(1)}, bf16[256,512]{1,0:T(8,128)(2,1)S(1)}, u32[]{:S(2)}, u32[]{:S(2)}) collective-permute-start(bf16[256,512]{1,0:T(8,128)(2,1)S(1)} %copy-done), channel_id=1, source_target_pairs={{0,2},{1,3},{2,0},{3,1},{4,6},{5,7},{6,4},{7,5},{8,10},{9,11},{10,... | collective-permute-start | bytes 786440 | tf_op jit(solution)/shard_map/ppermute | solution.py:158
  9.2 1.6 %collective-permute-start = (bf16[256,512]{1,0:T(8,128)(2,1)S(1)}, bf16[256,512]{1,0:T(8,128)(2,1)S(1)}, u32[]{:S(2)}, u32[]{:S(2)}) collective-permute-start(bf16[256,512]{1,0:T(8,128)(2,1)S(1)} %copy-done), channel_id=1, source_target_pairs={{0,1},{1,0},{2,3},{3,2},{4,5},{5,4},{6,7},{7,6},{8,9},{9,8},{10,11... | collective-permute-start | bytes 786440 | tf_op jit(solution)/shard_map/ppermute | solution.py:158
  10.7 9.9 %collective-permute-done.1.refs_2_.refs_4_ = bf16[256,512]{1,0:T(8,128)(2,1)S(1)} collective-permute-done((bf16[256,512]{1,0:T(8,128)(2,1)S(1)}, bf16[256,512]{1,0:T(8,128)(2,1)S(1)}, u32[]{:S(2)}, u32[]{:S(2)}) %collective-permute-start.1) | collective-permute-done | bytes 262176 | tf_op jit(solution)/shard_map/ppermute | solution.py:158
  20.9 0.3 collective-permute-start.4
  21.2 1.1 %collective-permute-start.2 = (bf16[256,512]{1,0:T(8,128)(2,1)S(1)}, bf16[256,512]{1,0:T(8,128)(2,1)S(1)}, u32[]{:S(2)}, u32[]{:S(2)}) collective-permute-start(bf16[256,512]{1,0:T(8,128)(2,1)S(1)} %collective-permute-done.1.refs_2_.refs_4_), channel_id=1, source_target_pairs={{0,1},{1,0},{2,3},{3,2},{4,5},{5,4},{6,7},{7,6},{8,9},{9,8},{10,11... | collective-permute-start | bytes 786440 | tf_op jit(solution)/shard_map/ppermute | solution.py:158
  22.6 5.8 %collective-permute-done.8.refs_10_.y_ref = bf16[2,2064,128]{2,1,0:T(8,128)(2,1)S(1)} collective-permute-done((bf16[2,2064,128]{2,1,0:T(8,128)(2,1)S(1)}, bf16[2,2064,128]{2,1,0:T(8,128)(2,1)S(1)}, u32[]{:S(2)}, u32[]{:S(2)}) %collective-permute-start.8) | collective-permute-done | bytes 1056800 | tf_op jit(solution)/shard_map/ppermute | solution.py:155
  28.4 1.5 %collective-permute-done.7.refs_9_.x_ref = bf16[2,2064,128]{2,1,0:T(8,128)(2,1)S(1)} collective-permute-done((bf16[2,2064,128]{2,1,0:T(8,128)(2,1)S(1)}, bf16[2,2064,128]{2,1,0:T(8,128)(2,1)S(1)}, u32[]{:S(2)}, u32[]{:S(2)}) %collective-permute-start.7) | collective-permute-done | bytes 1056800 | tf_op jit(solution)/shard_map/ppermute | solution.py:155
  29.9 0.4 collective-permute-start.9
  30.4 1.6 %collective-permute-start.10 = (bf16[2064,128]{1,0:T(8,128)(2,1)S(1)}, bf16[2064,128]{1,0:T(8,128)(2,1)S(1)}, u32[]{:S(2)}, u32[]{:S(2)}) collective-permute-start(bf16[2064,128]{1,0:T(8,128)(2,1)S(1)} %get-tuple-element.20), channel_id=1, source_target_pairs={{0,8},{4,12},{8,0},{12,4},{16,24},{20,28},{24,16},{28,20},{1,9},{5... | collective-permute-start | bytes 1585160 | tf_op jit(solution)/shard_map/ppermute | solution.py:155
  32.0 7.4 %shard_map.46 = (bf16[16,512,128]{2,1,0:T(8,128)(2,1)S(1)}, f32[16,256,128]{2,1,0:T(8,128)S(1)}, f32[16,256,128]{2,1,0:T(8,128)S(1)}) custom-call(bf16[256,512]{1,0:T(8,128)(2,1)S(1)} %copy-done, bf16[256,512]{1,0:T(8,128)(2,1)S(1)} %collective-permute-done.refs_1_.refs_3_, bf16[256,512]{1,0:T(8,128)(2,1)S(1)} %collective-permute-done.1.refs_2_.refs_4_, ...), custom_call_target="tpu_custom_call" | custom-call | tf_op jit(solution)/shard_map/pallas_call | solution.py:193
  39.5 3.1 %collective-permute-done.9 = bf16[2064,128]{1,0:T(8,128)(2,1)S(1)} collective-permute-done((bf16[2064,128]{1,0:T(8,128)(2,1)S(1)}, bf16[2064,128]{1,0:T(8,128)(2,1)S(1)}, u32[]{:S(2)}, u32[]{:S(2)}) %collective-permute-start.9) | collective-permute-done | bytes 528416 | tf_op jit(solution)/shard_map/ppermute | solution.py:155
  42.6 2.2 %collective-permute-done.10 = bf16[2064,128]{1,0:T(8,128)(2,1)S(1)} collective-permute-done((bf16[2064,128]{1,0:T(8,128)(2,1)S(1)}, bf16[2064,128]{1,0:T(8,128)(2,1)S(1)}, u32[]{:S(2)}, u32[]{:S(2)}) %collective-permute-start.10) | collective-permute-done | bytes 528416 | tf_op jit(solution)/shard_map/ppermute | solution.py:155
  44.8 3.0 %shard_map.48 = (bf16[4,2,256,128]{3,2,1,0:T(8,128)(2,1)S(1)}, bf16[4,2,256,128]{3,2,1,0:T(8,128)(2,1)S(1)}, f32[16,256,128]{2,1,0:T(8,128)S(1)}, f32[16,256,128]{2,1,0:T(8,128)S(1)}) custom-call(bf16[16,512,128]{2,1,0:T(8,128)(2,1)S(1)} %get-tuple-element.16.refs_0_, ...), custom_call_target="tpu_custom_call", output_to_operand_aliasing={{2}: (1, {}), {3}: (2, {})} | custom-call | tf_op jit(solution)/shard_map/pallas_call | solution.py:200
  47.9 1.9 %collective-permute-done.11.come_ref = bf16[4,2,256,128]{3,2,1,0:T(8,128)(2,1)S(1)} collective-permute-done((bf16[4,2,256,128]{3,2,1,0:T(8,128)(2,1)S(1)}, bf16[4,2,256,128]{3,2,1,0:T(8,128)(2,1)S(1)}, u32[]{:S(2)}, u32[]{:S(2)}) %collective-permute-start.11) | collective-permute-done | bytes 524320 | tf_op jit(solution)/shard_map/ppermute | solution.py:155
  49.9 3.8 %collective-permute-start.12 = (bf16[2,256,128]{2,1,0:T(8,128)(2,1)S(1)}, bf16[2,256,128]{2,1,0:T(8,128)(2,1)S(1)}, u32[]{:S(2)}, u32[]{:S(2)}) collective-permute-start(bf16[2,256,128]{2,1,0:T(8,128)(2,1)S(1)} %get-tuple-element.24), channel_id=1, source_target_pairs={{0,3},{1,2},{2,1},{3,0},{4,7},{5,6},{6,5},{7,4},{8,11},{9,10},{10,... | collective-permute-start | bytes 393224 | tf_op jit(solution)/shard_map/ppermute | solution.py:158
  53.7 0.6 collective-permute-start.14
  54.3 3.8 %collective-permute-done.12.refs_1_ = bf16[2,256,128]{2,1,0:T(8,128)(2,1)S(1)} collective-permute-done((bf16[2,256,128]{2,1,0:T(8,128)(2,1)S(1)}, bf16[2,256,128]{2,1,0:T(8,128)(2,1)S(1)}, u32[]{:S(2)}, u32[]{:S(2)}) %collective-permute-start.12) | collective-permute-done | bytes 131104 | tf_op jit(solution)/shard_map/ppermute | solution.py:158
  58.2 6.9 %collective-permute-done.13.refs_2_ = bf16[2,256,128]{2,1,0:T(8,128)(2,1)S(1)} collective-permute-done((bf16[2,256,128]{2,1,0:T(8,128)(2,1)S(1)}, bf16[2,256,128]{2,1,0:T(8,128)(2,1)S(1)}, u32[]{:S(2)}, u32[]{:S(2)}) %collective-permute-start.13) | collective-permute-done | bytes 131104 | tf_op jit(solution)/shard_map/ppermute | solution.py:158
  65.2 1.3 %collective-permute-done.15.other_ref = bf16[2,256,128]{2,1,0:T(8,128)(2,1)S(1)} collective-permute-done((bf16[2,256,128]{2,1,0:T(8,128)(2,1)S(1)}, bf16[2,256,128]{2,1,0:T(8,128)(2,1)S(1)}, u32[]{:S(2)}, u32[]{:S(2)}) %collective-permute-start.15) | collective-permute-done | bytes 131104 | tf_op jit(solution)/shard_map/ppermute | solution.py:155
  66.6 1.3 %shard_map.51 = bf16[256,512]{1,0:T(8,128)(2,1)} custom-call(bf16[2,256,128]{2,1,0:T(8,128)(2,1)S(1)} %shard_map.50.own_ref, bf16[2,256,128]{2,1,0:T(8,128)(2,1)S(1)} %collective-permute-done.15.other_ref, s32[1,256]{1,0:T(1,128)S(1)} %bitcast.12), custom_call_target="tpu_custom_call" | custom-call | tf_op jit(solution)/shard_map/pallas_call | solution.py:211
  (24 shorter events, 0.9 us)
Async XLA Ops:
  0.0 6.6 %copy-start = (bf16[256,512]{1,0:T(8,128)(2,1)S(1)}, bf16[256,512]{1,0:T(8,128)(2,1)}, u32[]{:S(2)}) copy-start(bf16[256,512]{1,0:T(8,128)(2,1)} %refs_0_.1) | copy-start | bytes 786436
  2.0 30.0 %copy-start.1 = (s32[256]{0:T(256)S(1)}, s32[256]{0:T(256)}, u32[]{:S(2)}) copy-start(s32[256]{0:T(256)} %param.7) | copy-start | bytes 3076
  2.0 26.4 %collective-permute-start.8 = (bf16[2,2064,128]{2,1,0:T(8,128)(2,1)S(1)}, bf16[2,2064,128]{2,1,0:T(8,128)(2,1)S(1)}, u32[]{:S(2)}, u32[]{:S(2)}) collective-permute-start(bf16[2,2064,128]{2,1,0:T(8,128)(2,1)S(1)} %fusion.1.refs_8_), channel_id=1, source_target_pairs={{0,16},{4,20},{8,24},{12,28},{16,0},{20,4},{24,8},{28,12},{1,17},{... | collective-permute-start | bytes 3170312 | tf_op jit(solution)/shard_map/ppermute | solution.py:155
  5.1 24.8 %collective-permute-start.7 = (bf16[2,2064,128]{2,1,0:T(8,128)(2,1)S(1)}, bf16[2,2064,128]{2,1,0:T(8,128)(2,1)S(1)}, u32[]{:S(2)}, u32[]{:S(2)}) collective-permute-start(bf16[2,2064,128]{2,1,0:T(8,128)(2,1)S(1)} %fusion.1.refs_8_), channel_id=1, source_target_pairs={{0,8},{4,12},{8,0},{12,4},{16,24},{20,28},{24,16},{28,20},{1,9},{5... | collective-permute-start | bytes 3170312 | tf_op jit(solution)/shard_map/ppermute | solution.py:155
  6.6 14.1 %collective-permute-start.1 = (bf16[256,512]{1,0:T(8,128)(2,1)S(1)}, bf16[256,512]{1,0:T(8,128)(2,1)S(1)}, u32[]{:S(2)}, u32[]{:S(2)}) collective-permute-start(bf16[256,512]{1,0:T(8,128)(2,1)S(1)} %copy-done), channel_id=1, source_target_pairs={{0,2},{1,3},{2,0},{3,1},{4,6},{5,7},{6,4},{7,5},{8,10},{9,11},{10,... | collective-permute-start | bytes 786440 | tf_op jit(solution)/shard_map/ppermute | solution.py:158
  9.2 11.7 %collective-permute-start = (bf16[256,512]{1,0:T(8,128)(2,1)S(1)}, bf16[256,512]{1,0:T(8,128)(2,1)S(1)}, u32[]{:S(2)}, u32[]{:S(2)}) collective-permute-start(bf16[256,512]{1,0:T(8,128)(2,1)S(1)} %copy-done), channel_id=1, source_target_pairs={{0,1},{1,0},{2,3},{3,2},{4,5},{5,4},{6,7},{7,6},{8,9},{9,8},{10,11... | collective-permute-start | bytes 786440 | tf_op jit(solution)/shard_map/ppermute | solution.py:158
  10.7 10.5 %collective-permute-start.3 = (bf16[256,512]{1,0:T(8,128)(2,1)S(1)}, bf16[256,512]{1,0:T(8,128)(2,1)S(1)}, u32[]{:S(2)}, u32[]{:S(2)}) collective-permute-start(bf16[256,512]{1,0:T(8,128)(2,1)S(1)} %copy-done), channel_id=1, source_target_pairs={{0,4},{4,0},{8,12},{12,8},{16,20},{20,16},{24,28},{28,24},{1,5},{5... | collective-permute-start | bytes 786440 | tf_op jit(solution)/shard_map/ppermute | solution.py:155
  20.7 1.6 %collective-permute-start.5 = (bf16[256,512]{1,0:T(8,128)(2,1)S(1)}, bf16[256,512]{1,0:T(8,128)(2,1)S(1)}, u32[]{:S(2)}, u32[]{:S(2)}) collective-permute-start(bf16[256,512]{1,0:T(8,128)(2,1)S(1)} %collective-permute-done.1.refs_2_.refs_4_), channel_id=1, source_target_pairs={{0,4},{4,0},{8,12},{12,8},{16,20},{20,16},{24,28},{28,24},{1,5},{5... | collective-permute-start | bytes 786440 | tf_op jit(solution)/shard_map/ppermute | solution.py:155
  20.9 1.7 %collective-permute-start.4 = (bf16[256,512]{1,0:T(8,128)(2,1)S(1)}, bf16[256,512]{1,0:T(8,128)(2,1)S(1)}, u32[]{:S(2)}, u32[]{:S(2)}) collective-permute-start(bf16[256,512]{1,0:T(8,128)(2,1)S(1)} %collective-permute-done.refs_1_.refs_3_), channel_id=1, source_target_pairs={{0,4},{4,0},{8,12},{12,8},{16,20},{20,16},{24,28},{28,24},{1,5},{5... | collective-permute-start | bytes 786440 | tf_op jit(solution)/shard_map/ppermute | solution.py:155
  21.2 9.2 %collective-permute-start.2 = (bf16[256,512]{1,0:T(8,128)(2,1)S(1)}, bf16[256,512]{1,0:T(8,128)(2,1)S(1)}, u32[]{:S(2)}, u32[]{:S(2)}) collective-permute-start(bf16[256,512]{1,0:T(8,128)(2,1)S(1)} %collective-permute-done.1.refs_2_.refs_4_), channel_id=1, source_target_pairs={{0,1},{1,0},{2,3},{3,2},{4,5},{5,4},{6,7},{7,6},{8,9},{9,8},{10,11... | collective-permute-start | bytes 786440 | tf_op jit(solution)/shard_map/ppermute | solution.py:158
  29.9 12.6 %collective-permute-start.9 = (bf16[2064,128]{1,0:T(8,128)(2,1)S(1)}, bf16[2064,128]{1,0:T(8,128)(2,1)S(1)}, u32[]{:S(2)}, u32[]{:S(2)}) collective-permute-start(bf16[2064,128]{1,0:T(8,128)(2,1)S(1)} %get-tuple-element.19), channel_id=1, source_target_pairs={{0,16},{4,20},{8,24},{12,28},{16,0},{20,4},{24,8},{28,12},{1,17},{... | collective-permute-start | bytes 1585160 | tf_op jit(solution)/shard_map/ppermute | solution.py:155
  30.4 1.7 %collective-permute-start.6 = (bf16[256,512]{1,0:T(8,128)(2,1)S(1)}, bf16[256,512]{1,0:T(8,128)(2,1)S(1)}, u32[]{:S(2)}, u32[]{:S(2)}) collective-permute-start(bf16[256,512]{1,0:T(8,128)(2,1)S(1)} %collective-permute-done.2.refs_3_), channel_id=1, source_target_pairs={{0,4},{4,0},{8,12},{12,8},{16,20},{20,16},{24,28},{28,24},{1,5},{5... | collective-permute-start | bytes 786440 | tf_op jit(solution)/shard_map/ppermute | solution.py:155
  30.4 14.4 %collective-permute-start.10 = (bf16[2064,128]{1,0:T(8,128)(2,1)S(1)}, bf16[2064,128]{1,0:T(8,128)(2,1)S(1)}, u32[]{:S(2)}, u32[]{:S(2)}) collective-permute-start(bf16[2064,128]{1,0:T(8,128)(2,1)S(1)} %get-tuple-element.20), channel_id=1, source_target_pairs={{0,8},{4,12},{8,0},{12,4},{16,24},{20,28},{24,16},{28,20},{1,9},{5... | collective-permute-start | bytes 1585160 | tf_op jit(solution)/shard_map/ppermute | solution.py:155
  47.8 2.0 %collective-permute-start.11 = (bf16[4,2,256,128]{3,2,1,0:T(8,128)(2,1)S(1)}, bf16[4,2,256,128]{3,2,1,0:T(8,128)(2,1)S(1)}, u32[]{:S(2)}, u32[]{:S(2)}) collective-permute-start(bf16[4,2,256,128]{3,2,1,0:T(8,128)(2,1)S(1)} %get-tuple-element.22), channel_id=1, source_target_pairs={{0,4},{4,0},{8,12},{12,8},{16,20},{20,16},{24,28},{28,24},{1,5},{5... | collective-permute-start | bytes 1572872 | tf_op jit(solution)/shard_map/ppermute | solution.py:155
  49.9 8.3 %collective-permute-start.12 = (bf16[2,256,128]{2,1,0:T(8,128)(2,1)S(1)}, bf16[2,256,128]{2,1,0:T(8,128)(2,1)S(1)}, u32[]{:S(2)}, u32[]{:S(2)}) collective-permute-start(bf16[2,256,128]{2,1,0:T(8,128)(2,1)S(1)} %get-tuple-element.24), channel_id=1, source_target_pairs={{0,3},{1,2},{2,1},{3,0},{4,7},{5,6},{6,5},{7,4},{8,11},{9,10},{10,... | collective-permute-start | bytes 393224 | tf_op jit(solution)/shard_map/ppermute | solution.py:158
  53.7 11.4 %collective-permute-start.13 = (bf16[2,256,128]{2,1,0:T(8,128)(2,1)S(1)}, bf16[2,256,128]{2,1,0:T(8,128)(2,1)S(1)}, u32[]{:S(2)}, u32[]{:S(2)}) collective-permute-start(bf16[2,256,128]{2,1,0:T(8,128)(2,1)S(1)} %get-tuple-element.25), channel_id=1, source_target_pairs={{0,2},{1,3},{2,0},{3,1},{4,6},{5,7},{6,4},{7,5},{8,10},{9,11},{10,... | collective-permute-start | bytes 393224 | tf_op jit(solution)/shard_map/ppermute | solution.py:158
  53.7 11.4 %collective-permute-start.14 = (bf16[2,256,128]{2,1,0:T(8,128)(2,1)S(1)}, bf16[2,256,128]{2,1,0:T(8,128)(2,1)S(1)}, u32[]{:S(2)}, u32[]{:S(2)}) collective-permute-start(bf16[2,256,128]{2,1,0:T(8,128)(2,1)S(1)} %get-tuple-element.26), channel_id=1, source_target_pairs={{0,1},{1,0},{2,3},{3,2},{4,5},{5,4},{6,7},{7,6},{8,9},{9,8},{10,11... | collective-permute-start | bytes 393224 | tf_op jit(solution)/shard_map/ppermute | solution.py:158
  65.1 1.4 %collective-permute-start.15 = (bf16[2,256,128]{2,1,0:T(8,128)(2,1)S(1)}, bf16[2,256,128]{2,1,0:T(8,128)(2,1)S(1)}, u32[]{:S(2)}, u32[]{:S(2)}) collective-permute-start(bf16[2,256,128]{2,1,0:T(8,128)(2,1)S(1)} %shard_map.50.own_ref), channel_id=1, source_target_pairs={{0,4},{4,0},{8,12},{12,8},{16,20},{20,16},{24,28},{28,24},{1,5},{5... | collective-permute-start | bytes 393224 | tf_op jit(solution)/shard_map/ppermute | solution.py:155

commit v10 on v9

--- a/solution.py
+++ b/solution.py
@@ -16,17 +16,17 @@
 SMEM = pl.BlockSpec(memory_space=pltpu.SMEM)
 
 
-def call(body, out_shape, in_specs, scratch=(), megabytes=32, aliases=None, out_specs=None):
+def call(body, out_shape, in_specs, scratch=(), megabytes=32, aliases=None, flops=0, moved=0):
     many = isinstance(out_shape, (list, tuple))
     return pl.pallas_call(
         body,
         out_shape=out_shape,
         in_specs=in_specs,
-        out_specs=out_specs or ([VMEM] * len(out_shape) if many else VMEM),
+        out_specs=[VMEM] * len(out_shape) if many else VMEM,
         scratch_shapes=list(scratch),
         compiler_params=pltpu.CompilerParams(vmem_limit_bytes=megabytes << 20),
         input_output_aliases=aliases or {},
-        cost_estimate=pl.CostEstimate(flops=0, bytes_accessed=0, transcendentals=0),
+        cost_estimate=pl.CostEstimate(flops=flops, bytes_accessed=moved, transcendentals=0),
     )
 
 
@@ -94,16 +94,21 @@
             add_products(grid_ref, acc_refs, tiles_ref.at[s], blocks_ref.at[s])
 
 
-def second_kernel(n_vir, n_sets, *refs):
+def more_kernel(n_sets, *refs):
     grid_ref = refs[0]
     tiles, blocks = refs[3 : 3 + n_sets], refs[3 + n_sets : 3 + 2 * n_sets]
-    keep_ref, send_ref, *acc_refs = refs[3 + 2 * n_sets :]
-    half, rows = keep_ref.shape[1:3]
-    core = lax.axis_index("pair") % 2
-    vir = lax.axis_index("vir")
+    acc_refs = refs[3 + 2 * n_sets :]
     for tiles_ref, blocks_ref in zip(tiles, blocks):
         for s in range(tiles_ref.shape[0]):
             add_products(grid_ref, acc_refs, tiles_ref.at[s], blocks_ref.at[s])
+
+
+def last_kernel(n_vir, n_sets, *refs):
+    keep_ref, send_ref, *acc_refs = refs[3 + 2 * n_sets :]
+    more_kernel(n_sets, *refs[: 3 + 2 * n_sets], *acc_refs)
+    half = keep_ref.shape[1]
+    core = lax.axis_index("pair") % 2
+    vir = lax.axis_index("vir")
     swap = swap_matrix().astype(BF16)
     for shift in range(n_vir):
         for k in range(half):
@@ -157,8 +162,9 @@
     def along(array, bits):
         return lax.ppermute(array, "vir", [(i, i ^ bits) for i in range(n_vir)])
 
-    ids = tile_blocks.transpose(0, 2, 1).astype(BF16)
-    ids = jnp.pad(ids, ((0, 0), (0, EXTRA - 2), (0, TILE - tile_dev)))
+    ids = tile_blocks.transpose(0, 2, 1).reshape(1, 2 * slabs, tile_dev).astype(BF16)
+    ids = jnp.pad(ids, ((0, 0), (0, EXTRA - 2 * slabs), (0, TILE - tile_dev)))
+    ids = jnp.broadcast_to(ids, (slabs, EXTRA, TILE))
     packed = jnp.concatenate([integrals.reshape(slabs, length, TILE), ids], axis=1)
     early = [packed, across(packed, 2), across(packed, 4)]
 
@@ -169,7 +175,7 @@
         reach //= 2
     mine = [pieces[shift] for shift in range(n_vir)]
     others = [across(piece, 1) for piece in mine]
-    first = [*others[:-1], *mine[1:-1]]
+    first = [*others, *mine[1:]]
     slab = jax.ShapeDtypeStruct((length + EXTRA, TILE), BF16)
     halves = call(
         functools.partial(cut_kernel, slabs),
@@ -186,24 +192,35 @@
     late = [array.reshape(-1, length + EXTRA, TILE) for array in late]
     row = mirror_row.reshape(1, rows)
 
-    def ids(array):
-        return array[:, length : length + 2, :tile_dev].astype(jnp.int32)
-
+    def ids_in(array):
+        return array[0, length : length + 2 * slabs, :tile_dev].astype(jnp.int32).reshape(slabs, 2, tile_dev)
+
+    diagonal = ids_in(late[0])
+    late_ids = [diagonal[s : s + 1] for s in range(slabs)] + [ids_in(array) for array in late[slabs:]]
     sums = jax.ShapeDtypeStruct((n_blk, rows, TILE), F32)
     grid, *sums_so_far = call(
         functools.partial(first_kernel, n_vir, len(early)),
         [jax.ShapeDtypeStruct((n_blk, 2 * rows, TILE), BF16), sums, sums],
         [VMEM] * (2 * n_vir + len(early)) + [SMEM] * len(early) + [VMEM],
         megabytes=20,
-    )(*mine, *others, *early, *[ids(array) for array in early], row)
+    )(*mine, *others, *early, *[ids_in(array) for array in early], row)
+    sums_so_far = call(
+        functools.partial(more_kernel, 1),
+        [sums, sums],
+        [VMEM] * 4 + [SMEM],
+        megabytes=20,
+        aliases={1: 0, 2: 1},
+        flops=2 * tile_dev * 2 * rows * 2 * TILE * TILE,
+        moved=8 << 20,
+    )(grid, *sums_so_far, late[0], late_ids[0])
     piece = jax.ShapeDtypeStruct((n_vir, per // 2, rows, TILE), BF16)
     keep, send, *_ = call(
-        functools.partial(second_kernel, n_vir, len(late)),
+        functools.partial(last_kernel, n_vir, len(late) - 1),
         [piece, piece, sums, sums],
-        [VMEM] * (3 + len(late)) + [SMEM] * len(late),
+        [VMEM] * (2 + len(late)) + [SMEM] * (len(late) - 1),
         megabytes=24,
         aliases={1: 2, 2: 3},
-    )(grid, *sums_so_far, *late, *[ids(array) for array in late])
+    )(grid, *sums_so_far, *late[1:], *late_ids[1:])
     one = jax.ShapeDtypeStruct((per // 2, rows, TILE), BF16)
     parts = call(join_kernel, [one] * n_vir, [VMEM, VMEM], megabytes=4)(keep, across(send, 1))
     arrived = [along(parts[shift], shift) for shift in range(n_vir - 1, 0, -1)]

time: 68 us -> 67.7 us (level)
  waiting for transfers between devices: 37 us -> 35.7 us
    ppermute x10, waiting for transfers between devices: 16.1 us -> 9.38 us  [across(): return lax.ppermute(array, 'pair', [(i, i ^ bits) for i in range(n_pair)])]
    ppermute x6, waiting for transfers between devices: 20.9 us -> 26.3 us  [along(): return lax.ppermute(array, 'vir', [(i, i ^ bits) for i in range(n_vir)])]
    pallas_call x1 -> x2, Pallas kernels: 2.97 us -> 3.47 us  [the longest x1 1.95 us: local(): call(functools.partial(last_kernel, n_vir, len(late) - 1), [piece, piece,...]
  transfers between devices with their start and end apart: 16 -> 16, of which waited for: 11 -> 9; matrix products, arithmetic and copies ran while one was open for 0% -> 0% of each run, Pallas kernels for 11% -> 13%
where the time goes in v10:
time: 67.7 us; the launch traced here: 67.6 us
  waiting for transfers between devices  35.7 us (53%)
  starting transfers between devices  17.3 us (26%)
  Pallas kernels  12.4 us (18%)
  other arithmetic  2.05 us (3%)
    ppermute x6, waiting for transfers between devices, along(): return lax.ppermute(array, 'vir', [(i, i ^ bits) for i in range(n_vir)])  26.3 us
    ppermute x6, starting transfers between devices, along(): return lax.ppermute(array, 'vir', [(i, i ^ bits) for i in range(n_vir)])  9.97 us
    ppermute x10, waiting for transfers between devices, across(): return lax.ppermute(array, 'pair', [(i, i ^ bits) for i in range(n_pair)])  9.38 us
    pallas_call x1, Pallas kernels, local(): call(functools.partial(first_kernel, n_vir, len(early)), [jax.ShapeDtypeS...  7.33 us
    ppermute x10, starting transfers between devices, across(): return lax.ppermute(array, 'pair', [(i, i ^ bits) for i in range(n_pair)])  7.3 us
    pallas_call x1, Pallas kernels, local(): call(functools.partial(last_kernel, n_vir, len(late) - 1), [piece, piece,...  1.95 us
    pallas_call x1, Pallas kernels, local(): call(functools.partial(more_kernel, 1), [sums, sums], [VMEM] * 4 + [SMEM]...  1.52 us
  transfers between devices with their start and end apart: 16, of which 9 were waited for; matrix products, arithmetic and copies ran while one was open for 0% of the time, Pallas kernels for 13%

profile of v10, /device:TPU:0, one launch (start us, length us, event | category | flops | bytes accessed | tf_op | source)
XLA Modules:
  0.0 67.6 jit_solution(9717292373893073107)
XLA Ops:
  0.0 0.7 %convert_element_type.44 = bf16[2,16,2]{1,2,0:T(2,128)(2,1)S(1)} convert(s32[2,16,2]{1,2,0:T(2,128)} %param.6) | non-fusion elementwise | flops 64 | bytes 384 | tf_op jit(solution)/shard_map/convert_element_type | solution.py:165
  0.7 1.3 %pad_maximum_fusion.refs_8_ = bf16[2,2064,128]{2,1,0:T(8,128)(2,1)S(1)} fusion(bf16[2,16,128]{2,1,0:T(8,128)(2,1)S(1)} %broadcast_in_dim.8, bf16[2,2048,128]{2,1,0:T(8,128)(2,1)} %bitcast.20), kind=kLoop, calls=%fused_computation | loop fusion | flops 2113536 | bytes 2113536 | tf_op jit(solution)/shard_map/concatenate | solution.py:168
  2.1 3.0 %collective-permute-start.7 = (bf16[2,2064,128]{2,1,0:T(8,128)(2,1)S(1)}, bf16[2,2064,128]{2,1,0:T(8,128)(2,1)S(1)}, u32[]{:S(2)}, u32[]{:S(2)}) collective-permute-start(bf16[2,2064,128]{2,1,0:T(8,128)(2,1)S(1)} %pad_maximum_fusion.refs_8_), channel_id=1, source_target_pairs={{0,8},{4,12},{8,0},{12,4},{16,24},{20,28},{24,16},{28,20},{1,9},{5... | collective-permute-start | bytes 3170312 | tf_op jit(solution)/shard_map/ppermute | solution.py:160
  5.1 1.5 %collective-permute-start.8 = (bf16[2,2064,128]{2,1,0:T(8,128)(2,1)S(1)}, bf16[2,2064,128]{2,1,0:T(8,128)(2,1)S(1)}, u32[]{:S(2)}, u32[]{:S(2)}) collective-permute-start(bf16[2,2064,128]{2,1,0:T(8,128)(2,1)S(1)} %pad_maximum_fusion.refs_8_), channel_id=1, source_target_pairs={{0,16},{4,20},{8,24},{12,28},{16,0},{20,4},{24,8},{28,12},{1,17},{... | collective-permute-start | bytes 3170312 | tf_op jit(solution)/shard_map/ppermute | solution.py:160
  6.6 2.6 %collective-permute-start.1 = (bf16[256,512]{1,0:T(8,128)(2,1)S(1)}, bf16[256,512]{1,0:T(8,128)(2,1)S(1)}, u32[]{:S(2)}, u32[]{:S(2)}) collective-permute-start(bf16[256,512]{1,0:T(8,128)(2,1)S(1)} %copy-done), channel_id=1, source_target_pairs={{0,2},{1,3},{2,0},{3,1},{4,6},{5,7},{6,4},{7,5},{8,10},{9,11},{10,... | collective-permute-start | bytes 786440 | tf_op jit(solution)/shard_map/ppermute | solution.py:163
  9.2 1.6 %collective-permute-start = (bf16[256,512]{1,0:T(8,128)(2,1)S(1)}, bf16[256,512]{1,0:T(8,128)(2,1)S(1)}, u32[]{:S(2)}, u32[]{:S(2)}) collective-permute-start(bf16[256,512]{1,0:T(8,128)(2,1)S(1)} %copy-done), channel_id=1, source_target_pairs={{0,1},{1,0},{2,3},{3,2},{4,5},{5,4},{6,7},{7,6},{8,9},{9,8},{10,11... | collective-permute-start | bytes 786440 | tf_op jit(solution)/shard_map/ppermute | solution.py:163
  10.8 9.9 %collective-permute-done.1.refs_2_.refs_5_ = bf16[256,512]{1,0:T(8,128)(2,1)S(1)} collective-permute-done((bf16[256,512]{1,0:T(8,128)(2,1)S(1)}, bf16[256,512]{1,0:T(8,128)(2,1)S(1)}, u32[]{:S(2)}, u32[]{:S(2)}) %collective-permute-start.1) | collective-permute-done | bytes 262176 | tf_op jit(solution)/shard_map/ppermute | solution.py:163
  20.7 0.6 collective-permute-start.2
  21.8 6.0 %collective-permute-done.2.refs_3_.refs_6_ = bf16[256,512]{1,0:T(8,128)(2,1)S(1)} collective-permute-done((bf16[256,512]{1,0:T(8,128)(2,1)S(1)}, bf16[256,512]{1,0:T(8,128)(2,1)S(1)}, u32[]{:S(2)}, u32[]{:S(2)}) %collective-permute-start.2) | collective-permute-done | bytes 262176 | tf_op jit(solution)/shard_map/ppermute | solution.py:163
  27.8 1.5 %collective-permute-done.6.refs_7_.refs_3_ = bf16[256,512]{1,0:T(8,128)(2,1)S(1)} collective-permute-done((bf16[256,512]{1,0:T(8,128)(2,1)S(1)}, bf16[256,512]{1,0:T(8,128)(2,1)S(1)}, u32[]{:S(2)}, u32[]{:S(2)}) %collective-permute-start.6) | collective-permute-done | bytes 262176 | tf_op jit(solution)/shard_map/ppermute | solution.py:160
  29.3 0.5 collective-permute-done.8.refs_10_.y_ref
  29.9 1.6 %collective-permute-start.9 = (bf16[2064,128]{1,0:T(8,128)(2,1)S(1)}, bf16[2064,128]{1,0:T(8,128)(2,1)S(1)}, u32[]{:S(2)}, u32[]{:S(2)}) collective-permute-start(bf16[2064,128]{1,0:T(8,128)(2,1)S(1)} %get-tuple-element.21), channel_id=1, source_target_pairs={{0,16},{4,20},{8,24},{12,28},{16,0},{20,4},{24,8},{28,12},{1,17},{... | collective-permute-start | bytes 1585160 | tf_op jit(solution)/shard_map/ppermute | solution.py:160
  31.5 0.5 collective-permute-start.10
  32.1 7.3 %shard_map.46 = (bf16[16,512,128]{2,1,0:T(8,128)(2,1)S(1)}, f32[16,256,128]{2,1,0:T(8,128)S(1)}, f32[16,256,128]{2,1,0:T(8,128)S(1)}) custom-call(bf16[256,512]{1,0:T(8,128)(2,1)S(1)} %copy-done, bf16[256,512]{1,0:T(8,128)(2,1)S(1)} %collective-permute-done.refs_1_.refs_4_, bf16[256,512]{1,0:T(8,128)(2,1)S(1)} %collective-permute-done.1.refs_2_.refs_5_, ...), custom_call_target="tpu_custom_call" | custom-call | tf_op jit(solution)/shard_map/pallas_call | solution.py:201
  39.4 4.1 %collective-permute-done.9 = bf16[2064,128]{1,0:T(8,128)(2,1)S(1)} collective-permute-done((bf16[2064,128]{1,0:T(8,128)(2,1)S(1)}, bf16[2064,128]{1,0:T(8,128)(2,1)S(1)}, u32[]{:S(2)}, u32[]{:S(2)}) %collective-permute-start.9) | collective-permute-done | bytes 528416 | tf_op jit(solution)/shard_map/ppermute | solution.py:160
  43.5 1.5 %shard_map.48 = (f32[16,256,128]{2,1,0:T(8,128)S(1)}, f32[16,256,128]{2,1,0:T(8,128)S(1)}) custom-call(bf16[16,512,128]{2,1,0:T(8,128)(2,1)S(1)} %get-tuple-element.18.refs_0_, f32[16,256,128]{2,1,0:T(8,128)S(1)} %get-tuple-element.19.refs_1_, f32[16,256,128]{2,1,0:T(8,128)S(1)} %get-tuple-element.20.refs_2_, ...), custom_call_target="tpu_custom_call", output_to_operand_aliasing={{0}: (1, {}), {1}: (2, {})} | custom-call | flops 536870912 | bytes 8388608 | tf_op jit(solution)/shard_map/pallas_call | solution.py:207
  45.1 1.9 %shard_map.49 = (bf16[4,2,256,128]{3,2,1,0:T(8,128)(2,1)S(1)}, bf16[4,2,256,128]{3,2,1,0:T(8,128)(2,1)S(1)}, f32[16,256,128]{2,1,0:T(8,128)S(1)}, f32[16,256,128]{2,1,0:T(8,128)S(1)}) custom-call(bf16[16,512,128]{2,1,0:T(8,128)(2,1)S(1)} %get-tuple-element.18.refs_0_, ...), custom_call_target="tpu_custom_call", output_to_operand_aliasing={{2}: (1, {}), {3}: (2, {})} | custom-call | tf_op jit(solution)/shard_map/pallas_call | solution.py:217
  47.1 1.9 %collective-permute-done.11.come_ref = bf16[4,2,256,128]{3,2,1,0:T(8,128)(2,1)S(1)} collective-permute-done((bf16[4,2,256,128]{3,2,1,0:T(8,128)(2,1)S(1)}, bf16[4,2,256,128]{3,2,1,0:T(8,128)(2,1)S(1)}, u32[]{:S(2)}, u32[]{:S(2)}) %collective-permute-start.11) | collective-permute-done | bytes 524320 | tf_op jit(solution)/shard_map/ppermute | solution.py:160
  49.1 4.6 %collective-permute-start.12 = (bf16[2,256,128]{2,1,0:T(8,128)(2,1)S(1)}, bf16[2,256,128]{2,1,0:T(8,128)(2,1)S(1)}, u32[]{:S(2)}, u32[]{:S(2)}) collective-permute-start(bf16[2,256,128]{2,1,0:T(8,128)(2,1)S(1)} %get-tuple-element.28), channel_id=1, source_target_pairs={{0,3},{1,2},{2,1},{3,0},{4,7},{5,6},{6,5},{7,4},{8,11},{9,10},{10,... | collective-permute-start | bytes 393224 | tf_op jit(solution)/shard_map/ppermute | solution.py:163
  53.7 0.6 collective-permute-start.14
  54.4 3.7 %collective-permute-done.12.refs_1_ = bf16[2,256,128]{2,1,0:T(8,128)(2,1)S(1)} collective-permute-done((bf16[2,256,128]{2,1,0:T(8,128)(2,1)S(1)}, bf16[2,256,128]{2,1,0:T(8,128)(2,1)S(1)}, u32[]{:S(2)}, u32[]{:S(2)}) %collective-permute-start.12) | collective-permute-done | bytes 131104 | tf_op jit(solution)/shard_map/ppermute | solution.py:163
  58.1 6.7 %collective-permute-done.13.refs_2_ = bf16[2,256,128]{2,1,0:T(8,128)(2,1)S(1)} collective-permute-done((bf16[2,256,128]{2,1,0:T(8,128)(2,1)S(1)}, bf16[2,256,128]{2,1,0:T(8,128)(2,1)S(1)}, u32[]{:S(2)}, u32[]{:S(2)}) %collective-permute-start.13) | collective-permute-done | bytes 131104 | tf_op jit(solution)/shard_map/ppermute | solution.py:163
  64.9 1.3 %collective-permute-done.15.other_ref = bf16[2,256,128]{2,1,0:T(8,128)(2,1)S(1)} collective-permute-done((bf16[2,256,128]{2,1,0:T(8,128)(2,1)S(1)}, bf16[2,256,128]{2,1,0:T(8,128)(2,1)S(1)}, u32[]{:S(2)}, u32[]{:S(2)}) %collective-permute-start.15) | collective-permute-done | bytes 131104 | tf_op jit(solution)/shard_map/ppermute | solution.py:160
  66.2 1.3 %shard_map.52 = bf16[256,512]{1,0:T(8,128)(2,1)} custom-call(bf16[2,256,128]{2,1,0:T(8,128)(2,1)S(1)} %shard_map.51.own_ref, bf16[2,256,128]{2,1,0:T(8,128)(2,1)S(1)} %collective-permute-done.15.other_ref, s32[1,256]{1,0:T(1,128)S(1)} %bitcast.19), custom_call_target="tpu_custom_call" | custom-call | tf_op jit(solution)/shard_map/pallas_call | solution.py:228
  (31 shorter events, 1.0 us)
Async XLA Ops:
  0.0 6.6 %copy-start = (bf16[256,512]{1,0:T(8,128)(2,1)S(1)}, bf16[256,512]{1,0:T(8,128)(2,1)}, u32[]{:S(2)}) copy-start(bf16[256,512]{1,0:T(8,128)(2,1)} %refs_0_.1) | copy-start | bytes 786436
  2.0 30.0 %copy-start.1 = (s32[256]{0:T(256)S(1)}, s32[256]{0:T(256)}, u32[]{:S(2)}) copy-start(s32[256]{0:T(256)} %param.7) | copy-start | bytes 3076
  2.1 27.3 %collective-permute-start.7 = (bf16[2,2064,128]{2,1,0:T(8,128)(2,1)S(1)}, bf16[2,2064,128]{2,1,0:T(8,128)(2,1)S(1)}, u32[]{:S(2)}, u32[]{:S(2)}) collective-permute-start(bf16[2,2064,128]{2,1,0:T(8,128)(2,1)S(1)} %pad_maximum_fusion.refs_8_), channel_id=1, source_target_pairs={{0,8},{4,12},{8,0},{12,4},{16,24},{20,28},{24,16},{28,20},{1,9},{5... | collective-permute-start | bytes 3170312 | tf_op jit(solution)/shard_map/ppermute | solution.py:160
  5.1 24.8 %collective-permute-start.8 = (bf16[2,2064,128]{2,1,0:T(8,128)(2,1)S(1)}, bf16[2,2064,128]{2,1,0:T(8,128)(2,1)S(1)}, u32[]{:S(2)}, u32[]{:S(2)}) collective-permute-start(bf16[2,2064,128]{2,1,0:T(8,128)(2,1)S(1)} %pad_maximum_fusion.refs_8_), channel_id=1, source_target_pairs={{0,16},{4,20},{8,24},{12,28},{16,0},{20,4},{24,8},{28,12},{1,17},{... | collective-permute-start | bytes 3170312 | tf_op jit(solution)/shard_map/ppermute | solution.py:160
  6.6 14.1 %collective-permute-start.1 = (bf16[256,512]{1,0:T(8,128)(2,1)S(1)}, bf16[256,512]{1,0:T(8,128)(2,1)S(1)}, u32[]{:S(2)}, u32[]{:S(2)}) collective-permute-start(bf16[256,512]{1,0:T(8,128)(2,1)S(1)} %copy-done), channel_id=1, source_target_pairs={{0,2},{1,3},{2,0},{3,1},{4,6},{5,7},{6,4},{7,5},{8,10},{9,11},{10,... | collective-permute-start | bytes 786440 | tf_op jit(solution)/shard_map/ppermute | solution.py:163
  9.2 12.1 %collective-permute-start = (bf16[256,512]{1,0:T(8,128)(2,1)S(1)}, bf16[256,512]{1,0:T(8,128)(2,1)S(1)}, u32[]{:S(2)}, u32[]{:S(2)}) collective-permute-start(bf16[256,512]{1,0:T(8,128)(2,1)S(1)} %copy-done), channel_id=1, source_target_pairs={{0,1},{1,0},{2,3},{3,2},{4,5},{5,4},{6,7},{7,6},{8,9},{9,8},{10,11... | collective-permute-start | bytes 786440 | tf_op jit(solution)/shard_map/ppermute | solution.py:163
  10.7 10.5 %collective-permute-start.3 = (bf16[256,512]{1,0:T(8,128)(2,1)S(1)}, bf16[256,512]{1,0:T(8,128)(2,1)S(1)}, u32[]{:S(2)}, u32[]{:S(2)}) collective-permute-start(bf16[256,512]{1,0:T(8,128)(2,1)S(1)} %copy-done), channel_id=1, source_target_pairs={{0,4},{4,0},{8,12},{12,8},{16,20},{20,16},{24,28},{28,24},{1,5},{5... | collective-permute-start | bytes 786440 | tf_op jit(solution)/shard_map/ppermute | solution.py:160
  20.7 7.1 %collective-permute-start.2 = (bf16[256,512]{1,0:T(8,128)(2,1)S(1)}, bf16[256,512]{1,0:T(8,128)(2,1)S(1)}, u32[]{:S(2)}, u32[]{:S(2)}) collective-permute-start(bf16[256,512]{1,0:T(8,128)(2,1)S(1)} %collective-permute-done.1.refs_2_.refs_5_), channel_id=1, source_target_pairs={{0,1},{1,0},{2,3},{3,2},{4,5},{5,4},{6,7},{7,6},{8,9},{9,8},{10,11... | collective-permute-start | bytes 786440 | tf_op jit(solution)/shard_map/ppermute | solution.py:163
  21.3 6.5 %collective-permute-start.5 = (bf16[256,512]{1,0:T(8,128)(2,1)S(1)}, bf16[256,512]{1,0:T(8,128)(2,1)S(1)}, u32[]{:S(2)}, u32[]{:S(2)}) collective-permute-start(bf16[256,512]{1,0:T(8,128)(2,1)S(1)} %collective-permute-done.1.refs_2_.refs_5_), channel_id=1, source_target_pairs={{0,4},{4,0},{8,12},{12,8},{16,20},{20,16},{24,28},{28,24},{1,5},{5... | collective-permute-start | bytes 786440 | tf_op jit(solution)/shard_map/ppermute | solution.py:160
  21.3 6.5 %collective-permute-start.4 = (bf16[256,512]{1,0:T(8,128)(2,1)S(1)}, bf16[256,512]{1,0:T(8,128)(2,1)S(1)}, u32[]{:S(2)}, u32[]{:S(2)}) collective-permute-start(bf16[256,512]{1,0:T(8,128)(2,1)S(1)} %collective-permute-done.refs_1_.refs_4_), channel_id=1, source_target_pairs={{0,4},{4,0},{8,12},{12,8},{16,20},{20,16},{24,28},{28,24},{1,5},{5... | collective-permute-start | bytes 786440 | tf_op jit(solution)/shard_map/ppermute | solution.py:160
  27.8 1.5 %collective-permute-start.6 = (bf16[256,512]{1,0:T(8,128)(2,1)S(1)}, bf16[256,512]{1,0:T(8,128)(2,1)S(1)}, u32[]{:S(2)}, u32[]{:S(2)}) collective-permute-start(bf16[256,512]{1,0:T(8,128)(2,1)S(1)} %collective-permute-done.2.refs_3_.refs_6_), channel_id=1, source_target_pairs={{0,4},{4,0},{8,12},{12,8},{16,20},{20,16},{24,28},{28,24},{1,5},{5... | collective-permute-start | bytes 786440 | tf_op jit(solution)/shard_map/ppermute | solution.py:160
  29.9 13.6 %collective-permute-start.9 = (bf16[2064,128]{1,0:T(8,128)(2,1)S(1)}, bf16[2064,128]{1,0:T(8,128)(2,1)S(1)}, u32[]{:S(2)}, u32[]{:S(2)}) collective-permute-start(bf16[2064,128]{1,0:T(8,128)(2,1)S(1)} %get-tuple-element.21), channel_id=1, source_target_pairs={{0,16},{4,20},{8,24},{12,28},{16,0},{20,4},{24,8},{28,12},{1,17},{... | collective-permute-start | bytes 1585160 | tf_op jit(solution)/shard_map/ppermute | solution.py:160
  31.5 13.5 %collective-permute-start.10 = (bf16[2064,128]{1,0:T(8,128)(2,1)S(1)}, bf16[2064,128]{1,0:T(8,128)(2,1)S(1)}, u32[]{:S(2)}, u32[]{:S(2)}) collective-permute-start(bf16[2064,128]{1,0:T(8,128)(2,1)S(1)} %get-tuple-element.24), channel_id=1, source_target_pairs={{0,8},{4,12},{8,0},{12,4},{16,24},{20,28},{24,16},{28,20},{1,9},{5... | collective-permute-start | bytes 1585160 | tf_op jit(solution)/shard_map/ppermute | solution.py:160
  47.0 2.0 %collective-permute-start.11 = (bf16[4,2,256,128]{3,2,1,0:T(8,128)(2,1)S(1)}, bf16[4,2,256,128]{3,2,1,0:T(8,128)(2,1)S(1)}, u32[]{:S(2)}, u32[]{:S(2)}) collective-permute-start(bf16[4,2,256,128]{3,2,1,0:T(8,128)(2,1)S(1)} %get-tuple-element.26), channel_id=1, source_target_pairs={{0,4},{4,0},{8,12},{12,8},{16,20},{20,16},{24,28},{28,24},{1,5},{5... | collective-permute-start | bytes 1572872 | tf_op jit(solution)/shard_map/ppermute | solution.py:160
  49.1 9.0 %collective-permute-start.12 = (bf16[2,256,128]{2,1,0:T(8,128)(2,1)S(1)}, bf16[2,256,128]{2,1,0:T(8,128)(2,1)S(1)}, u32[]{:S(2)}, u32[]{:S(2)}) collective-permute-start(bf16[2,256,128]{2,1,0:T(8,128)(2,1)S(1)} %get-tuple-element.28), channel_id=1, source_target_pairs={{0,3},{1,2},{2,1},{3,0},{4,7},{5,6},{6,5},{7,4},{8,11},{9,10},{10,... | collective-permute-start | bytes 393224 | tf_op jit(solution)/shard_map/ppermute | solution.py:163
  53.7 11.0 %collective-permute-start.13 = (bf16[2,256,128]{2,1,0:T(8,128)(2,1)S(1)}, bf16[2,256,128]{2,1,0:T(8,128)(2,1)S(1)}, u32[]{:S(2)}, u32[]{:S(2)}) collective-permute-start(bf16[2,256,128]{2,1,0:T(8,128)(2,1)S(1)} %get-tuple-element.29), channel_id=1, source_target_pairs={{0,2},{1,3},{2,0},{3,1},{4,6},{5,7},{6,4},{7,5},{8,10},{9,11},{10,... | collective-permute-start | bytes 393224 | tf_op jit(solution)/shard_map/ppermute | solution.py:163
  53.7 11.0 %collective-permute-start.14 = (bf16[2,256,128]{2,1,0:T(8,128)(2,1)S(1)}, bf16[2,256,128]{2,1,0:T(8,128)(2,1)S(1)}, u32[]{:S(2)}, u32[]{:S(2)}) collective-permute-start(bf16[2,256,128]{2,1,0:T(8,128)(2,1)S(1)} %get-tuple-element.30), channel_id=1, source_target_pairs={{0,1},{1,0},{2,3},{3,2},{4,5},{5,4},{6,7},{7,6},{8,9},{9,8},{10,11... | collective-permute-start | bytes 393224 | tf_op jit(solution)/shard_map/ppermute | solution.py:163
  64.8 1.4 %collective-permute-start.15 = (bf16[2,256,128]{2,1,0:T(8,128)(2,1)S(1)}, bf16[2,256,128]{2,1,0:T(8,128)(2,1)S(1)}, u32[]{:S(2)}, u32[]{:S(2)}) collective-permute-start(bf16[2,256,128]{2,1,0:T(8,128)(2,1)S(1)} %shard_map.51.own_ref), channel_id=1, source_target_pairs={{0,4},{4,0},{8,12},{12,8},{16,20},{20,16},{24,28},{28,24},{1,5},{5... | collective-permute-start | bytes 393224 | tf_op jit(solution)/shard_map/ppermute | solution.py:160

commit v11 on v10

--- a/solution.py
+++ b/solution.py
@@ -16,7 +16,7 @@
 SMEM = pl.BlockSpec(memory_space=pltpu.SMEM)
 
 
-def call(body, out_shape, in_specs, scratch=(), megabytes=32, aliases=None, flops=0, moved=0):
+def call(body, out_shape, in_specs, scratch=(), megabytes=32, aliases=None):
     many = isinstance(out_shape, (list, tuple))
     return pl.pallas_call(
         body,
@@ -26,7 +26,7 @@
         scratch_shapes=list(scratch),
         compiler_params=pltpu.CompilerParams(vmem_limit_bytes=megabytes << 20),
         input_output_aliases=aliases or {},
-        cost_estimate=pl.CostEstimate(flops=flops, bytes_accessed=moved, transcendentals=0),
+        cost_estimate=pl.CostEstimate(flops=0, bytes_accessed=0, transcendentals=0),
     )
 
 
@@ -70,14 +70,17 @@
     own, other = refs[:n_vir], refs[n_vir : 2 * n_vir]
     tiles = refs[2 * n_vir : 2 * n_vir + n_sets]
     blocks = refs[2 * n_vir + n_sets : 2 * n_vir + 2 * n_sets]
-    row_ref, grid_ref, *acc_refs = refs[2 * n_vir + 2 * n_sets :]
+    row_ref, grid_ref, last_hot_ref, *acc_refs = refs[2 * n_vir + 2 * n_sets :]
     rows, width = own[0].shape
     per = width // TILE
     pair = lax.axis_index("pair")
     vir = lax.axis_index("vir")
     upper = pair % 2 == 1
     mirrors = (row_ref[...] - (pair ^ 1) * rows == iota((rows, rows), 0)).astype(F32)
-    hot = jnp.where(upper, mirrors, mirrors.T).astype(BF16)
+    turned = mirrors.T
+    hot = jnp.where(upper, mirrors, turned).astype(BF16)
+    same = (iota((rows, rows), 0) == iota((rows, rows), 1)).astype(F32)
+    last_hot_ref[...] = jnp.where(upper, turned, same).astype(BF16)
     for shift in range(n_vir):
         first = (vir ^ shift) * per
         mine, others = own[shift][...], other[shift][...]
@@ -103,20 +106,18 @@
             add_products(grid_ref, acc_refs, tiles_ref.at[s], blocks_ref.at[s])
 
 
-def last_kernel(n_vir, n_sets, *refs):
-    keep_ref, send_ref, *acc_refs = refs[3 + 2 * n_sets :]
-    more_kernel(n_sets, *refs[: 3 + 2 * n_sets], *acc_refs)
+def fold_kernel(shifts, own_ref, mirror_ref, keep_ref, send_ref):
     half = keep_ref.shape[1]
     core = lax.axis_index("pair") % 2
     vir = lax.axis_index("vir")
     swap = swap_matrix().astype(BF16)
-    for shift in range(n_vir):
+    for place, shift in enumerate(shifts):
         for k in range(half):
             for out_ref, side in ((keep_ref, core), (send_ref, 1 - core)):
                 block = ((vir ^ shift) * 2 + side) * half + k
-                upper = acc_refs[1][block].astype(BF16)
-                total = acc_refs[0][block] + jnp.dot(upper, swap, preferred_element_type=F32)
-                out_ref[shift, k] = total.astype(BF16)
+                upper = mirror_ref[block].astype(BF16)
+                total = own_ref[block] + jnp.dot(upper, swap, preferred_element_type=F32)
+                out_ref[place, k] = total.astype(BF16)
 
 
 def join_kernel(keep_ref, come_ref, *outs):
@@ -131,12 +132,10 @@
     refs[-1][...] = total.astype(BF16)
 
 
-def finish_kernel(own_ref, other_ref, row_ref, out_ref):
-    half, rows, _ = own_ref.shape
-    pair = lax.axis_index("pair")
-    upper = pair % 2 == 1
-    place = jnp.where(upper, row_ref[...] - (pair ^ 1) * rows, iota((1, rows), 1))
-    hot = (iota((rows, rows), 0) == place).astype(F32).T.astype(BF16)
+def finish_kernel(own_ref, other_ref, hot_ref, out_ref):
+    half = own_ref.shape[0]
+    upper = lax.axis_index("pair") % 2 == 1
+    hot = hot_ref[...]
     same = (iota((TILE, TILE), 0) == iota((TILE, TILE), 1)).astype(F32)
     swap = jnp.where(upper, swap_matrix().astype(F32), same).astype(BF16)
     for which in range(2):
@@ -198,36 +197,38 @@
     diagonal = ids_in(late[0])
     late_ids = [diagonal[s : s + 1] for s in range(slabs)] + [ids_in(array) for array in late[slabs:]]
     sums = jax.ShapeDtypeStruct((n_blk, rows, TILE), F32)
-    grid, *sums_so_far = call(
+    grid, last_hot, *sums_so_far = call(
         functools.partial(first_kernel, n_vir, len(early)),
-        [jax.ShapeDtypeStruct((n_blk, 2 * rows, TILE), BF16), sums, sums],
+        [
+            jax.ShapeDtypeStruct((n_blk, 2 * rows, TILE), BF16),
+            jax.ShapeDtypeStruct((rows, rows), BF16),
+            sums,
+            sums,
+        ],
         [VMEM] * (2 * n_vir + len(early)) + [SMEM] * len(early) + [VMEM],
         megabytes=20,
     )(*mine, *others, *early, *[ids_in(array) for array in early], row)
     sums_so_far = call(
-        functools.partial(more_kernel, 1),
+        functools.partial(more_kernel, len(late)),
         [sums, sums],
-        [VMEM] * 4 + [SMEM],
-        megabytes=20,
+        [VMEM] * (3 + len(late)) + [SMEM] * len(late),
+        megabytes=24,
         aliases={1: 0, 2: 1},
-        flops=2 * tile_dev * 2 * rows * 2 * TILE * TILE,
-        moved=8 << 20,
-    )(grid, *sums_so_far, late[0], late_ids[0])
-    piece = jax.ShapeDtypeStruct((n_vir, per // 2, rows, TILE), BF16)
-    keep, send, *_ = call(
-        functools.partial(last_kernel, n_vir, len(late) - 1),
-        [piece, piece, sums, sums],
-        [VMEM] * (2 + len(late)) + [SMEM] * (len(late) - 1),
-        megabytes=24,
-        aliases={1: 2, 2: 3},
-    )(grid, *sums_so_far, *late[1:], *late_ids[1:])
-    one = jax.ShapeDtypeStruct((per // 2, rows, TILE), BF16)
-    parts = call(join_kernel, [one] * n_vir, [VMEM, VMEM], megabytes=4)(keep, across(send, 1))
-    arrived = [along(parts[shift], shift) for shift in range(n_vir - 1, 0, -1)]
-    total = call(total_kernel, one, [VMEM] * n_vir, megabytes=4)(parts[0], *arrived)
+    )(grid, *sums_so_far, *late, *late_ids)
+
+    parts = {}
+    for shifts in (range(n_vir - 1, n_vir // 2 - 1, -1), range(n_vir // 2 - 1, -1, -1)):
+        piece = jax.ShapeDtypeStruct((len(shifts), per // 2, rows, TILE), BF16)
+        keep, send = call(
+            functools.partial(fold_kernel, shifts), [piece, piece], [VMEM, VMEM], megabytes=8
+        )(*sums_so_far)
+        one = jax.ShapeDtypeStruct((per // 2, rows, TILE), BF16)
+        joined = call(join_kernel, [one] * len(shifts), [VMEM, VMEM], megabytes=4)(keep, across(send, 1))
+        parts |= {shift: along(part, shift) if shift else part for shift, part in zip(shifts, joined)}
+    total = call(total_kernel, one, [VMEM] * n_vir, megabytes=4)(*[parts[shift] for shift in range(n_vir)])
     return call(
         finish_kernel, jax.ShapeDtypeStruct((rows, width), BF16), [VMEM] * 3, megabytes=8
-    )(total, across(total, 1), row)
+    )(total, across(total, 1), last_hot)
 
 
 def solution(mesh):

time: 67.7 us -> 65.8 us (0.972)
  waiting for transfers between devices: 35.7 us -> 33.4 us
    ppermute x6, waiting for transfers between devices: 26.3 us -> 25 us  [along(): return lax.ppermute(array, 'vir', [(i, i ^ bits) for i in range(n_vir)])]
    ppermute x10 -> x11, waiting for transfers between devices: 9.38 us -> 8.41 us  [across(): return lax.ppermute(array, 'pair', [(i, i ^ bits) for i in range(n_pair)])]
    ppermute x10 -> x11, starting transfers between devices: 7.3 us -> 7.87 us  [across(): return lax.ppermute(array, 'pair', [(i, i ^ bits) for i in range(n_pair)])]
    pallas_call x4 -> x6, Pallas kernels: 3.66 us -> 3.29 us  [the longest x1 2.5 us: local(): call(functools.partial(more_kernel, len(late)), [sums, sums], [VMEM] * (3...]
  transfers between devices with their start and end apart: 16 -> 17, of which waited for: 9 -> 10; matrix products, arithmetic and copies ran while one was open for 0% -> 0% of each run, Pallas kernels for 13% -> 12%
where the time goes in v11:
time: 65.8 us; the launch traced here: 65.4 us
  waiting for transfers between devices  33.4 us (51%)
  starting transfers between devices  17.8 us (27%)
  Pallas kernels  12 us (18%)
  other arithmetic  2.05 us (3%)
    ppermute x6, waiting for transfers between devices, along(): return lax.ppermute(array, 'vir', [(i, i ^ bits) for i in range(n_vir)])  25 us
    ppermute x6, starting transfers between devices, along(): return lax.ppermute(array, 'vir', [(i, i ^ bits) for i in range(n_vir)])  9.91 us
    ppermute x11, waiting for transfers between devices, across(): return lax.ppermute(array, 'pair', [(i, i ^ bits) for i in range(n_pair)])  8.41 us
    ppermute x11, starting transfers between devices, across(): return lax.ppermute(array, 'pair', [(i, i ^ bits) for i in range(n_pair)])  7.87 us
    pallas_call x1, Pallas kernels, local(): call(functools.partial(first_kernel, n_vir, len(early)), [jax.ShapeDtypeS...  7.33 us
    pallas_call x1, Pallas kernels, local(): call(functools.partial(more_kernel, len(late)), [sums, sums], [VMEM] * (3...  2.5 us
    pallas_call x1, Pallas kernels, local(): call(finish_kernel, jax.ShapeDtypeStruct((rows, width), BF16), [VMEM] * 3...  1.32 us
  transfers between devices with their start and end apart: 17, of which 10 were waited for; matrix products, arithmetic and copies ran while one was open for 0% of the time, Pallas kernels for 12%

profile of v11, /device:TPU:0, one launch (start us, length us, event | category | flops | bytes accessed | tf_op | source)
XLA Modules:
  0.0 65.4 jit_solution(14397987278195811874)
XLA Ops:
  0.0 0.7 %convert_element_type.44 = bf16[2,16,2]{1,2,0:T(2,128)(2,1)S(1)} convert(s32[2,16,2]{1,2,0:T(2,128)} %param.6) | non-fusion elementwise | flops 64 | bytes 384 | tf_op jit(solution)/shard_map/convert_element_type | solution.py:164
  0.7 1.3 %pad_maximum_fusion.refs_8_ = bf16[2,2064,128]{2,1,0:T(8,128)(2,1)S(1)} fusion(bf16[2,16,128]{2,1,0:T(8,128)(2,1)S(1)} %broadcast_in_dim.8, bf16[2,2048,128]{2,1,0:T(8,128)(2,1)} %bitcast.19), kind=kLoop, calls=%fused_computation | loop fusion | flops 2113536 | bytes 2113536 | tf_op jit(solution)/shard_map/concatenate | solution.py:167
  2.1 3.0 %collective-permute-start.7 = (bf16[2,2064,128]{2,1,0:T(8,128)(2,1)S(1)}, bf16[2,2064,128]{2,1,0:T(8,128)(2,1)S(1)}, u32[]{:S(2)}, u32[]{:S(2)}) collective-permute-start(bf16[2,2064,128]{2,1,0:T(8,128)(2,1)S(1)} %pad_maximum_fusion.refs_8_), channel_id=1, source_target_pairs={{0,8},{4,12},{8,0},{12,4},{16,24},{20,28},{24,16},{28,20},{1,9},{5... | collective-permute-start | bytes 3170312 | tf_op jit(solution)/shard_map/ppermute | solution.py:159
  5.1 1.5 %collective-permute-start.8 = (bf16[2,2064,128]{2,1,0:T(8,128)(2,1)S(1)}, bf16[2,2064,128]{2,1,0:T(8,128)(2,1)S(1)}, u32[]{:S(2)}, u32[]{:S(2)}) collective-permute-start(bf16[2,2064,128]{2,1,0:T(8,128)(2,1)S(1)} %pad_maximum_fusion.refs_8_), channel_id=1, source_target_pairs={{0,16},{4,20},{8,24},{12,28},{16,0},{20,4},{24,8},{28,12},{1,17},{... | collective-permute-start | bytes 3170312 | tf_op jit(solution)/shard_map/ppermute | solution.py:159
  6.6 2.6 %collective-permute-start.1 = (bf16[256,512]{1,0:T(8,128)(2,1)S(1)}, bf16[256,512]{1,0:T(8,128)(2,1)S(1)}, u32[]{:S(2)}, u32[]{:S(2)}) collective-permute-start(bf16[256,512]{1,0:T(8,128)(2,1)S(1)} %copy-done), channel_id=1, source_target_pairs={{0,2},{1,3},{2,0},{3,1},{4,6},{5,7},{6,4},{7,5},{8,10},{9,11},{10,... | collective-permute-start | bytes 786440 | tf_op jit(solution)/shard_map/ppermute | solution.py:162
  9.2 1.6 %collective-permute-start = (bf16[256,512]{1,0:T(8,128)(2,1)S(1)}, bf16[256,512]{1,0:T(8,128)(2,1)S(1)}, u32[]{:S(2)}, u32[]{:S(2)}) collective-permute-start(bf16[256,512]{1,0:T(8,128)(2,1)S(1)} %copy-done), channel_id=1, source_target_pairs={{0,1},{1,0},{2,3},{3,2},{4,5},{5,4},{6,7},{7,6},{8,9},{9,8},{10,11... | collective-permute-start | bytes 786440 | tf_op jit(solution)/shard_map/ppermute | solution.py:162
  10.8 9.9 %collective-permute-done.1.refs_2_.refs_5_ = bf16[256,512]{1,0:T(8,128)(2,1)S(1)} collective-permute-done((bf16[256,512]{1,0:T(8,128)(2,1)S(1)}, bf16[256,512]{1,0:T(8,128)(2,1)S(1)}, u32[]{:S(2)}, u32[]{:S(2)}) %collective-permute-start.1) | collective-permute-done | bytes 262176 | tf_op jit(solution)/shard_map/ppermute | solution.py:162
  20.7 0.6 collective-permute-start.2
  21.8 6.0 %collective-permute-done.2.refs_3_.refs_6_ = bf16[256,512]{1,0:T(8,128)(2,1)S(1)} collective-permute-done((bf16[256,512]{1,0:T(8,128)(2,1)S(1)}, bf16[256,512]{1,0:T(8,128)(2,1)S(1)}, u32[]{:S(2)}, u32[]{:S(2)}) %collective-permute-start.2) | collective-permute-done | bytes 262176 | tf_op jit(solution)/shard_map/ppermute | solution.py:162
  27.8 1.5 %collective-permute-done.6.refs_7_.refs_3_ = bf16[256,512]{1,0:T(8,128)(2,1)S(1)} collective-permute-done((bf16[256,512]{1,0:T(8,128)(2,1)S(1)}, bf16[256,512]{1,0:T(8,128)(2,1)S(1)}, u32[]{:S(2)}, u32[]{:S(2)}) %collective-permute-start.6) | collective-permute-done | bytes 262176 | tf_op jit(solution)/shard_map/ppermute | solution.py:159
  29.3 0.5 collective-permute-done.8.refs_10_.y_ref
  29.9 1.6 %collective-permute-start.9 = (bf16[2064,128]{1,0:T(8,128)(2,1)S(1)}, bf16[2064,128]{1,0:T(8,128)(2,1)S(1)}, u32[]{:S(2)}, u32[]{:S(2)}) collective-permute-start(bf16[2064,128]{1,0:T(8,128)(2,1)S(1)} %get-tuple-element.24), channel_id=1, source_target_pairs={{0,16},{4,20},{8,24},{12,28},{16,0},{20,4},{24,8},{28,12},{1,17},{... | collective-permute-start | bytes 1585160 | tf_op jit(solution)/shard_map/ppermute | solution.py:159
  32.1 7.3 %shard_map.46 = (bf16[16,512,128]{2,1,0:T(8,128)(2,1)S(1)}, bf16[256,256]{1,0:T(8,128)(2,1)S(1)}, f32[16,256,128]{2,1,0:T(8,128)S(1)}, f32[16,256,128]{2,1,0:T(8,128)S(1)}) custom-call(bf16[256,512]{1,0:T(8,128)(2,1)S(1)} %copy-done, bf16[256,512]{1,0:T(8,128)(2,1)S(1)} %collective-permute-done.refs_1_.refs_4_, ...), custom_call_target="tpu_custom_call" | custom-call | tf_op jit(solution)/shard_map/pallas_call | solution.py:200
  39.4 4.1 %collective-permute-done.9 = bf16[2064,128]{1,0:T(8,128)(2,1)S(1)} collective-permute-done((bf16[2064,128]{1,0:T(8,128)(2,1)S(1)}, bf16[2064,128]{1,0:T(8,128)(2,1)S(1)}, u32[]{:S(2)}, u32[]{:S(2)}) %collective-permute-start.9) | collective-permute-done | bytes 528416 | tf_op jit(solution)/shard_map/ppermute | solution.py:159
  43.8 2.5 %shard_map.48 = (f32[16,256,128]{2,1,0:T(8,128)S(1)}, f32[16,256,128]{2,1,0:T(8,128)S(1)}) custom-call(bf16[16,512,128]{2,1,0:T(8,128)(2,1)S(1)} %get-tuple-element.21.refs_0_, f32[16,256,128]{2,1,0:T(8,128)S(1)} %get-tuple-element.22.refs_1_, f32[16,256,128]{2,1,0:T(8,128)S(1)} %get-tuple-element.23.refs_2_, ...), custom_call_target="tpu_custom_call", output_to_operand_aliasing={{0}: (1, {}), {1}: (2, {})} | custom-call | tf_op jit(solution)/shard_map/pallas_call | solution.py:211
  47.0 0.6 collective-permute-start.11
  47.6 0.6 collective-permute-done.13.come_ref
  48.3 3.4 %collective-permute-start.14 = (bf16[2,256,128]{2,1,0:T(8,128)(2,1)S(1)}, bf16[2,256,128]{2,1,0:T(8,128)(2,1)S(1)}, u32[]{:S(2)}, u32[]{:S(2)}) collective-permute-start(bf16[2,256,128]{2,1,0:T(8,128)(2,1)S(1)} %get-tuple-element.34), channel_id=1, source_target_pairs={{0,2},{1,3},{2,0},{3,1},{4,6},{5,7},{6,4},{7,5},{8,10},{9,11},{10,... | collective-permute-start | bytes 393224 | tf_op jit(solution)/shard_map/ppermute | solution.py:162
  51.6 1.3 %collective-permute-start.15 = (bf16[2,256,128]{2,1,0:T(8,128)(2,1)S(1)}, bf16[2,256,128]{2,1,0:T(8,128)(2,1)S(1)}, u32[]{:S(2)}, u32[]{:S(2)}) collective-permute-start(bf16[2,256,128]{2,1,0:T(8,128)(2,1)S(1)} %get-tuple-element.35), channel_id=1, source_target_pairs={{0,3},{1,2},{2,1},{3,0},{4,7},{5,6},{6,5},{7,4},{8,11},{9,10},{10,... | collective-permute-start | bytes 393224 | tf_op jit(solution)/shard_map/ppermute | solution.py:162
  53.0 0.6 collective-permute-start.12
  53.5 8.1 %collective-permute-done.14.refs_2_ = bf16[2,256,128]{2,1,0:T(8,128)(2,1)S(1)} collective-permute-done((bf16[2,256,128]{2,1,0:T(8,128)(2,1)S(1)}, bf16[2,256,128]{2,1,0:T(8,128)(2,1)S(1)}, u32[]{:S(2)}, u32[]{:S(2)}) %collective-permute-start.14) | collective-permute-done | bytes 131104 | tf_op jit(solution)/shard_map/ppermute | solution.py:162
  61.6 1.0 %collective-permute-done.12.refs_1_ = bf16[2,256,128]{2,1,0:T(8,128)(2,1)S(1)} collective-permute-done((bf16[2,256,128]{2,1,0:T(8,128)(2,1)S(1)}, bf16[2,256,128]{2,1,0:T(8,128)(2,1)S(1)}, u32[]{:S(2)}, u32[]{:S(2)}) %collective-permute-start.12) | collective-permute-done | bytes 131104 | tf_op jit(solution)/shard_map/ppermute | solution.py:162
  62.8 1.3 %collective-permute-done.16.other_ref = bf16[2,256,128]{2,1,0:T(8,128)(2,1)S(1)} collective-permute-done((bf16[2,256,128]{2,1,0:T(8,128)(2,1)S(1)}, bf16[2,256,128]{2,1,0:T(8,128)(2,1)S(1)}, u32[]{:S(2)}, u32[]{:S(2)}) %collective-permute-start.16) | collective-permute-done | bytes 131104 | tf_op jit(solution)/shard_map/ppermute | solution.py:159
  64.1 1.3 %shard_map.54 = bf16[256,512]{1,0:T(8,128)(2,1)} custom-call(bf16[2,256,128]{2,1,0:T(8,128)(2,1)S(1)} %shard_map.53.own_ref, bf16[2,256,128]{2,1,0:T(8,128)(2,1)S(1)} %collective-permute-done.16.other_ref, bf16[256,256]{1,0:T(8,128)(2,1)S(1)} %get-tuple-element.36.hot_ref), custom_call_target="tpu_custom_call" | custom-call | tf_op jit(solution)/shard_map/pallas_call | solution.py:229
  (35 shorter events, 2.4 us)
Async XLA Ops:
  0.0 6.6 %copy-start = (bf16[256,512]{1,0:T(8,128)(2,1)S(1)}, bf16[256,512]{1,0:T(8,128)(2,1)}, u32[]{:S(2)}) copy-start(bf16[256,512]{1,0:T(8,128)(2,1)} %refs_0_.1) | copy-start | bytes 786436
  2.0 30.0 %copy-start.1 = (s32[256]{0:T(256)S(1)}, s32[256]{0:T(256)}, u32[]{:S(2)}) copy-start(s32[256]{0:T(256)} %param.7) | copy-start | bytes 3076
  2.1 27.3 %collective-permute-start.7 = (bf16[2,2064,128]{2,1,0:T(8,128)(2,1)S(1)}, bf16[2,2064,128]{2,1,0:T(8,128)(2,1)S(1)}, u32[]{:S(2)}, u32[]{:S(2)}) collective-permute-start(bf16[2,2064,128]{2,1,0:T(8,128)(2,1)S(1)} %pad_maximum_fusion.refs_8_), channel_id=1, source_target_pairs={{0,8},{4,12},{8,0},{12,4},{16,24},{20,28},{24,16},{28,20},{1,9},{5... | collective-permute-start | bytes 3170312 | tf_op jit(solution)/shard_map/ppermute | solution.py:159
  5.1 24.8 %collective-permute-start.8 = (bf16[2,2064,128]{2,1,0:T(8,128)(2,1)S(1)}, bf16[2,2064,128]{2,1,0:T(8,128)(2,1)S(1)}, u32[]{:S(2)}, u32[]{:S(2)}) collective-permute-start(bf16[2,2064,128]{2,1,0:T(8,128)(2,1)S(1)} %pad_maximum_fusion.refs_8_), channel_id=1, source_target_pairs={{0,16},{4,20},{8,24},{12,28},{16,0},{20,4},{24,8},{28,12},{1,17},{... | collective-permute-start | bytes 3170312 | tf_op jit(solution)/shard_map/ppermute | solution.py:159
  6.6 14.1 %collective-permute-start.1 = (bf16[256,512]{1,0:T(8,128)(2,1)S(1)}, bf16[256,512]{1,0:T(8,128)(2,1)S(1)}, u32[]{:S(2)}, u32[]{:S(2)}) collective-permute-start(bf16[256,512]{1,0:T(8,128)(2,1)S(1)} %copy-done), channel_id=1, source_target_pairs={{0,2},{1,3},{2,0},{3,1},{4,6},{5,7},{6,4},{7,5},{8,10},{9,11},{10,... | collective-permute-start | bytes 786440 | tf_op jit(solution)/shard_map/ppermute | solution.py:162
  9.2 12.1 %collective-permute-start = (bf16[256,512]{1,0:T(8,128)(2,1)S(1)}, bf16[256,512]{1,0:T(8,128)(2,1)S(1)}, u32[]{:S(2)}, u32[]{:S(2)}) collective-permute-start(bf16[256,512]{1,0:T(8,128)(2,1)S(1)} %copy-done), channel_id=1, source_target_pairs={{0,1},{1,0},{2,3},{3,2},{4,5},{5,4},{6,7},{7,6},{8,9},{9,8},{10,11... | collective-permute-start | bytes 786440 | tf_op jit(solution)/shard_map/ppermute | solution.py:162
  10.7 10.5 %collective-permute-start.3 = (bf16[256,512]{1,0:T(8,128)(2,1)S(1)}, bf16[256,512]{1,0:T(8,128)(2,1)S(1)}, u32[]{:S(2)}, u32[]{:S(2)}) collective-permute-start(bf16[256,512]{1,0:T(8,128)(2,1)S(1)} %copy-done), channel_id=1, source_target_pairs={{0,4},{4,0},{8,12},{12,8},{16,20},{20,16},{24,28},{28,24},{1,5},{5... | collective-permute-start | bytes 786440 | tf_op jit(solution)/shard_map/ppermute | solution.py:159
  20.7 7.1 %collective-permute-start.2 = (bf16[256,512]{1,0:T(8,128)(2,1)S(1)}, bf16[256,512]{1,0:T(8,128)(2,1)S(1)}, u32[]{:S(2)}, u32[]{:S(2)}) collective-permute-start(bf16[256,512]{1,0:T(8,128)(2,1)S(1)} %collective-permute-done.1.refs_2_.refs_5_), channel_id=1, source_target_pairs={{0,1},{1,0},{2,3},{3,2},{4,5},{5,4},{6,7},{7,6},{8,9},{9,8},{10,11... | collective-permute-start | bytes 786440 | tf_op jit(solution)/shard_map/ppermute | solution.py:162
  21.3 6.5 %collective-permute-start.5 = (bf16[256,512]{1,0:T(8,128)(2,1)S(1)}, bf16[256,512]{1,0:T(8,128)(2,1)S(1)}, u32[]{:S(2)}, u32[]{:S(2)}) collective-permute-start(bf16[256,512]{1,0:T(8,128)(2,1)S(1)} %collective-permute-done.1.refs_2_.refs_5_), channel_id=1, source_target_pairs={{0,4},{4,0},{8,12},{12,8},{16,20},{20,16},{24,28},{28,24},{1,5},{5... | collective-permute-start | bytes 786440 | tf_op jit(solution)/shard_map/ppermute | solution.py:159
  21.3 6.5 %collective-permute-start.4 = (bf16[256,512]{1,0:T(8,128)(2,1)S(1)}, bf16[256,512]{1,0:T(8,128)(2,1)S(1)}, u32[]{:S(2)}, u32[]{:S(2)}) collective-permute-start(bf16[256,512]{1,0:T(8,128)(2,1)S(1)} %collective-permute-done.refs_1_.refs_4_), channel_id=1, source_target_pairs={{0,4},{4,0},{8,12},{12,8},{16,20},{20,16},{24,28},{28,24},{1,5},{5... | collective-permute-start | bytes 786440 | tf_op jit(solution)/shard_map/ppermute | solution.py:159
  27.8 1.5 %collective-permute-start.6 = (bf16[256,512]{1,0:T(8,128)(2,1)S(1)}, bf16[256,512]{1,0:T(8,128)(2,1)S(1)}, u32[]{:S(2)}, u32[]{:S(2)}) collective-permute-start(bf16[256,512]{1,0:T(8,128)(2,1)S(1)} %collective-permute-done.2.refs_3_.refs_6_), channel_id=1, source_target_pairs={{0,4},{4,0},{8,12},{12,8},{16,20},{20,16},{24,28},{28,24},{1,5},{5... | collective-permute-start | bytes 786440 | tf_op jit(solution)/shard_map/ppermute | solution.py:159
  29.9 13.6 %collective-permute-start.9 = (bf16[2064,128]{1,0:T(8,128)(2,1)S(1)}, bf16[2064,128]{1,0:T(8,128)(2,1)S(1)}, u32[]{:S(2)}, u32[]{:S(2)}) collective-permute-start(bf16[2064,128]{1,0:T(8,128)(2,1)S(1)} %get-tuple-element.24), channel_id=1, source_target_pairs={{0,16},{4,20},{8,24},{12,28},{16,0},{20,4},{24,8},{28,12},{1,17},{... | collective-permute-start | bytes 1585160 | tf_op jit(solution)/shard_map/ppermute | solution.py:159
  31.5 12.3 %collective-permute-start.10 = (bf16[2064,128]{1,0:T(8,128)(2,1)S(1)}, bf16[2064,128]{1,0:T(8,128)(2,1)S(1)}, u32[]{:S(2)}, u32[]{:S(2)}) collective-permute-start(bf16[2064,128]{1,0:T(8,128)(2,1)S(1)} %get-tuple-element.25), channel_id=1, source_target_pairs={{0,8},{4,12},{8,0},{12,4},{16,24},{20,28},{24,16},{28,20},{1,9},{5... | collective-permute-start | bytes 1585160 | tf_op jit(solution)/shard_map/ppermute | solution.py:159
  46.6 1.6 %collective-permute-start.13 = (bf16[2,2,256,128]{3,2,1,0:T(8,128)(2,1)S(1)}, bf16[2,2,256,128]{3,2,1,0:T(8,128)(2,1)S(1)}, u32[]{:S(2)}, u32[]{:S(2)}) collective-permute-start(bf16[2,2,256,128]{3,2,1,0:T(8,128)(2,1)S(1)} %get-tuple-element.33), channel_id=1, source_target_pairs={{0,4},{4,0},{8,12},{12,8},{16,20},{20,16},{24,28},{28,24},{1,5},{5... | collective-permute-start | bytes 786440 | tf_op jit(solution)/shard_map/ppermute | solution.py:159
  47.0 5.9 %collective-permute-start.11 = (bf16[2,2,256,128]{3,2,1,0:T(8,128)(2,1)S(1)}, bf16[2,2,256,128]{3,2,1,0:T(8,128)(2,1)S(1)}, u32[]{:S(2)}, u32[]{:S(2)}) collective-permute-start(bf16[2,2,256,128]{3,2,1,0:T(8,128)(2,1)S(1)} %get-tuple-element.29), channel_id=1, source_target_pairs={{0,4},{4,0},{8,12},{12,8},{16,20},{20,16},{24,28},{28,24},{1,5},{5... | collective-permute-start | bytes 786440 | tf_op jit(solution)/shard_map/ppermute | solution.py:159
  48.3 13.3 %collective-permute-start.14 = (bf16[2,256,128]{2,1,0:T(8,128)(2,1)S(1)}, bf16[2,256,128]{2,1,0:T(8,128)(2,1)S(1)}, u32[]{:S(2)}, u32[]{:S(2)}) collective-permute-start(bf16[2,256,128]{2,1,0:T(8,128)(2,1)S(1)} %get-tuple-element.34), channel_id=1, source_target_pairs={{0,2},{1,3},{2,0},{3,1},{4,6},{5,7},{6,4},{7,5},{8,10},{9,11},{10,... | collective-permute-start | bytes 393224 | tf_op jit(solution)/shard_map/ppermute | solution.py:162
  51.6 9.9 %collective-permute-start.15 = (bf16[2,256,128]{2,1,0:T(8,128)(2,1)S(1)}, bf16[2,256,128]{2,1,0:T(8,128)(2,1)S(1)}, u32[]{:S(2)}, u32[]{:S(2)}) collective-permute-start(bf16[2,256,128]{2,1,0:T(8,128)(2,1)S(1)} %get-tuple-element.35), channel_id=1, source_target_pairs={{0,3},{1,2},{2,1},{3,0},{4,7},{5,6},{6,5},{7,4},{8,11},{9,10},{10,... | collective-permute-start | bytes 393224 | tf_op jit(solution)/shard_map/ppermute | solution.py:162
  53.0 9.6 %collective-permute-start.12 = (bf16[2,256,128]{2,1,0:T(8,128)(2,1)S(1)}, bf16[2,256,128]{2,1,0:T(8,128)(2,1)S(1)}, u32[]{:S(2)}, u32[]{:S(2)}) collective-permute-start(bf16[2,256,128]{2,1,0:T(8,128)(2,1)S(1)} %get-tuple-element.31), channel_id=1, source_target_pairs={{0,1},{1,0},{2,3},{3,2},{4,5},{5,4},{6,7},{7,6},{8,9},{9,8},{10,11... | collective-permute-start | bytes 393224 | tf_op jit(solution)/shard_map/ppermute | solution.py:162
  62.7 1.4 %collective-permute-start.16 = (bf16[2,256,128]{2,1,0:T(8,128)(2,1)S(1)}, bf16[2,256,128]{2,1,0:T(8,128)(2,1)S(1)}, u32[]{:S(2)}, u32[]{:S(2)}) collective-permute-start(bf16[2,256,128]{2,1,0:T(8,128)(2,1)S(1)} %shard_map.53.own_ref), channel_id=1, source_target_pairs={{0,4},{4,0},{8,12},{12,8},{16,20},{20,16},{24,28},{28,24},{1,5},{5... | collective-permute-start | bytes 393224 | tf_op jit(solution)/shard_map/ppermute | solution.py:159

commit v12 on v11

--- a/solution.py
+++ b/solution.py
@@ -16,13 +16,13 @@
 SMEM = pl.BlockSpec(memory_space=pltpu.SMEM)
 
 
-def call(body, out_shape, in_specs, scratch=(), megabytes=32, aliases=None):
+def call(body, out_shape, in_specs, scratch=(), megabytes=32, aliases=None, out_specs=None):
     many = isinstance(out_shape, (list, tuple))
     return pl.pallas_call(
         body,
         out_shape=out_shape,
         in_specs=in_specs,
-        out_specs=[VMEM] * len(out_shape) if many else VMEM,
+        out_specs=out_specs or ([VMEM] * len(out_shape) if many else VMEM),
         scratch_shapes=list(scratch),
         compiler_params=pltpu.CompilerParams(vmem_limit_bytes=megabytes << 20),
         input_output_aliases=aliases or {},
@@ -41,18 +41,22 @@
 
 
 def cut_kernel(slabs, x_ref, y_ref, *refs):
-    for s, out_ref in enumerate(refs[-slabs:]):
-        out_ref[...] = (x_ref if s % 2 == 0 else y_ref)[s]
-
-
-def add_products(grid_ref, acc_refs, tiles_ref, blocks_ref):
+    for s in range(slabs):
+        slab_ref = (x_ref if s % 2 == 0 else y_ref).at[s]
+        upper_ref, lower_ref = refs[2 * (s - slabs)], refs[2 * (s - slabs) + 1]
+        middle = upper_ref.shape[0]
+        upper_ref[...] = slab_ref[:middle]
+        lower_ref[...] = slab_ref[middle:]
+
+
+def add_products(grid_ref, acc_refs, tiles_ref, blocks_ref, first=EXTRA):
     empty = jnp.zeros((TILE, TILE), BF16)
     rows = acc_refs[0].shape[1]
 
     @pl.loop(0, blocks_ref.shape[1] // 2, unroll=4)
     def _(t):
         to, come = [[blocks_ref[which, 2 * t + k] for k in range(2)] for which in range(2)]
-        tiles = [tiles_ref[pl.ds(pl.multiple_of((2 * t + k) * TILE, TILE), TILE), :] for k in range(2)]
+        tiles = [tiles_ref[pl.ds(pl.multiple_of((2 * t + k) * TILE + first, EXTRA), TILE), :] for k in range(2)]
         right = jnp.concatenate(
             [jnp.concatenate([tiles[0], empty], axis=1), jnp.concatenate([empty, tiles[1]], axis=1)], axis=0
         )
@@ -103,7 +107,8 @@
     acc_refs = refs[3 + 2 * n_sets :]
     for tiles_ref, blocks_ref in zip(tiles, blocks):
         for s in range(tiles_ref.shape[0]):
-            add_products(grid_ref, acc_refs, tiles_ref.at[s], blocks_ref.at[s])
+            first = tiles_ref.shape[1] % TILE
+            add_products(grid_ref, acc_refs, tiles_ref.at[s], blocks_ref.at[s], first)
 
 
 def fold_kernel(shifts, own_ref, mirror_ref, keep_ref, send_ref):
@@ -132,18 +137,24 @@
     refs[-1][...] = total.astype(BF16)
 
 
-def finish_kernel(own_ref, other_ref, hot_ref, out_ref):
+def finish_kernel(own_ref, other_ref, hot_ref, out_ref, made_ref, sems):
     half = own_ref.shape[0]
     upper = lax.axis_index("pair") % 2 == 1
     hot = hot_ref[...]
     same = (iota((TILE, TILE), 0) == iota((TILE, TILE), 1)).astype(F32)
     swap = jnp.where(upper, swap_matrix().astype(F32), same).astype(BF16)
+    copies = []
     for which in range(2):
         for k in range(half):
             values = jnp.where(upper == (which == 1), own_ref[k], other_ref[k])
             values = jnp.dot(values, swap, preferred_element_type=F32).astype(BF16)
-            column = (which * half + k) * TILE
-            out_ref[:, column : column + TILE] = jnp.dot(hot, values, preferred_element_type=F32).astype(BF16)
+            block = which * half + k
+            columns = pl.ds(block * TILE, TILE)
+            made_ref[:, columns] = jnp.dot(hot, values, preferred_element_type=F32).astype(BF16)
+            copies.append(pltpu.make_async_copy(made_ref.at[:, columns], out_ref.at[:, columns], sems.at[block]))
+            copies[-1].start()
+    for copy in copies:
+        copy.wait()
 
 
 def local(amplitudes, integrals, tile_blocks, mirror_row):
@@ -164,7 +175,7 @@
     ids = tile_blocks.transpose(0, 2, 1).reshape(1, 2 * slabs, tile_dev).astype(BF16)
     ids = jnp.pad(ids, ((0, 0), (0, EXTRA - 2 * slabs), (0, TILE - tile_dev)))
     ids = jnp.broadcast_to(ids, (slabs, EXTRA, TILE))
-    packed = jnp.concatenate([integrals.reshape(slabs, length, TILE), ids], axis=1)
+    packed = jnp.concatenate([ids, integrals.reshape(slabs, length, TILE)], axis=1)
     early = [packed, across(packed, 2), across(packed, 4)]
 
     pieces = {0: amplitudes}
@@ -175,27 +186,27 @@
     mine = [pieces[shift] for shift in range(n_vir)]
     others = [across(piece, 1) for piece in mine]
     first = [*others, *mine[1:]]
-    slab = jax.ShapeDtypeStruct((length + EXTRA, TILE), BF16)
+    middle = EXTRA + length // 2
     halves = call(
         functools.partial(cut_kernel, slabs),
-        [slab] * slabs,
+        [jax.ShapeDtypeStruct((size, TILE), BF16) for _ in range(slabs) for size in (middle, length // 2)],
         [VMEM, VMEM] + [pl.BlockSpec(memory_space=pl.ANY)] * len(first),
         megabytes=4,
     )(early[1], early[2], *first)
-    late = [across(half, 4 if s % 2 == 0 else 2) for s, half in enumerate(halves)]
-    reach = 4
+    late = [[across(half, 4 if s % 2 == 0 else 2) for s, half in enumerate(halves[part::2])] for part in range(2)]
+    farther, reach = [], 4
     while reach < chips:
-        farther = early + late if reach == 4 else late
-        late = late + [across(array, 2 * reach) for array in farther]
+        if reach == 4:
+            diagonal = jnp.stack([jnp.concatenate([late[part][s] for part in range(2)]) for s in range(slabs)])
+            farther = [across(array, 2 * reach) for array in (*early, diagonal)]
+        else:
+            farther += [across(array, 2 * reach) for array in (*early, diagonal, *farther)]
         reach *= 2
-    late = [array.reshape(-1, length + EXTRA, TILE) for array in late]
     row = mirror_row.reshape(1, rows)
 
     def ids_in(array):
-        return array[0, length : length + 2 * slabs, :tile_dev].astype(jnp.int32).reshape(slabs, 2, tile_dev)
-
-    diagonal = ids_in(late[0])
-    late_ids = [diagonal[s : s + 1] for s in range(slabs)] + [ids_in(array) for array in late[slabs:]]
+        return array[: 2 * slabs, :tile_dev].astype(jnp.int32).reshape(slabs, 2, tile_dev)
+
     sums = jax.ShapeDtypeStruct((n_blk, rows, TILE), F32)
     grid, last_hot, *sums_so_far = call(
         functools.partial(first_kernel, n_vir, len(early)),
@@ -207,14 +218,19 @@
         ],
         [VMEM] * (2 * n_vir + len(early)) + [SMEM] * len(early) + [VMEM],
         megabytes=20,
-    )(*mine, *others, *early, *[ids_in(array) for array in early], row)
-    sums_so_far = call(
-        functools.partial(more_kernel, len(late)),
-        [sums, sums],
-        [VMEM] * (3 + len(late)) + [SMEM] * len(late),
-        megabytes=24,
-        aliases={1: 0, 2: 1},
-    )(grid, *sums_so_far, *late, *late_ids)
+    )(*mine, *others, *early, *[ids_in(array[0]) for array in early], row)
+    diagonal_ids = ids_in(late[0][0]).reshape(slabs, 2, 2, tile_dev // 2)
+    for part in range(2):
+        more = [half[None] for half in late[part]] + (farther if part else [])
+        more_ids = [diagonal_ids[s : s + 1, :, part] for s in range(slabs)]
+        more_ids += [ids_in(array[0]) for array in farther] if part else []
+        sums_so_far = call(
+            functools.partial(more_kernel, len(more)),
+            [sums, sums],
+            [VMEM] * (3 + len(more)) + [SMEM] * len(more),
+            megabytes=24,
+            aliases={1: 0, 2: 1},
+        )(grid, *sums_so_far, *more, *more_ids)
 
     parts = {}
     for shifts in (range(n_vir - 1, n_vir // 2 - 1, -1), range(n_vir // 2 - 1, -1, -1)):
@@ -227,7 +243,12 @@
         parts |= {shift: along(part, shift) if shift else part for shift, part in zip(shifts, joined)}
     total = call(total_kernel, one, [VMEM] * n_vir, megabytes=4)(*[parts[shift] for shift in range(n_vir)])
     return call(
-        finish_kernel, jax.ShapeDtypeStruct((rows, width), BF16), [VMEM] * 3, megabytes=8
+        finish_kernel,
+        jax.ShapeDtypeStruct((rows, width), BF16),
+        [VMEM] * 3,
+        [pltpu.VMEM((rows, width), BF16), pltpu.SemaphoreType.DMA((per,))],
+        megabytes=8,
+        out_specs=pl.BlockSpec(memory_space=pl.ANY),
     )(total, across(total, 1), last_hot)
 
 

time: 65.8 us -> 71.5 us (1.087)
  local copies, waits for them, and re-layouts: 0.04 us -> 6.72 us
  waiting for transfers between devices: 33.4 us -> 29.1 us
  starting transfers between devices: 17.8 us -> 19.3 us
  Pallas kernels: 12 us -> 13 us
    unnamed x4 -> x14, local copies, waits for them, and re-layouts: 0.01 us -> 5.86 us
    ppermute x11 -> x13, waiting for transfers between devices: 8.41 us -> 4 us  [across(): return lax.ppermute(array, 'pair', [(i, i ^ bits) for i in range(n_pair)])]
    ppermute x11 -> x13, starting transfers between devices: 7.87 us -> 9.85 us  [across(): return lax.ppermute(array, 'pair', [(i, i ^ bits) for i in range(n_pair)])]
    pallas_call x2 -> x3, Pallas kernels: 2.57 us -> 3.61 us  [the longest x2 2.76 us: local(): call(functools.partial(more_kernel, len(more)), [sums, sums], [VMEM] * (3...]
    another operation x0 -> x1, local copies, waits for them, and re-layouts: none -> 0.75 us  [local(): diagonal_ids = ids_in(late[0][0]).reshape(slabs, 2, 2, tile_dev // 2)]
  transfers between devices with their start and end apart: 17 -> 19, of which waited for: 10 -> 8; matrix products, arithmetic and copies ran while one was open for 0% -> 2% of each run, Pallas kernels for 12% -> 13%
where the time goes in v12:
time: 71.5 us; the launch traced here: 71 us
  waiting for transfers between devices  29.1 us (41%)
  starting transfers between devices  19.3 us (27%)
  Pallas kernels  13 us (18%)
  local copies, waits for them, and re-layouts  6.72 us (9%)
  other arithmetic  2.73 us (4%)
    ppermute x6, waiting for transfers between devices, along(): return lax.ppermute(array, 'vir', [(i, i ^ bits) for i in range(n_vir)])  25.1 us
    ppermute x13, starting transfers between devices, across(): return lax.ppermute(array, 'pair', [(i, i ^ bits) for i in range(n_pair)])  9.85 us
    ppermute x6, starting transfers between devices, along(): return lax.ppermute(array, 'vir', [(i, i ^ bits) for i in range(n_vir)])  9.42 us
    pallas_call x1, Pallas kernels, local(): call(functools.partial(first_kernel, n_vir, len(early)), [jax.ShapeDtypeS...  7.31 us
    unnamed x14, local copies, waits for them, and re-layouts  5.86 us
    ppermute x13, waiting for transfers between devices, across(): return lax.ppermute(array, 'pair', [(i, i ^ bits) for i in range(n_pair)])  4 us
    pallas_call x2, Pallas kernels, local(): call(functools.partial(more_kernel, len(more)), [sums, sums], [VMEM] * (3...  2.76 us
  transfers between devices with their start and end apart: 19, of which 8 were waited for; matrix products, arithmetic and copies ran while one was open for 2% of the time, Pallas kernels for 13%

profile of v12, /device:TPU:0, one launch (start us, length us, event | category | flops | bytes accessed | tf_op | source)
XLA Modules:
  0.0 71.0 jit_solution(4737564851137122216)
XLA Ops:
  0.7 1.4 %pad_maximum_fusion.refs_8_ = bf16[2,2064,128]{2,1,0:T(8,128)(2,1)S(1)} fusion(bf16[2,16,128]{2,1,0:T(8,128)(2,1)S(1)} %broadcast_in_dim.20, bf16[2,2048,128]{2,1,0:T(8,128)(2,1)} %bitcast.36), kind=kLoop, calls=%fused_computation.1 | loop fusion | flops 2113536 | bytes 2113536 | tf_op jit(solution)/shard_map/concatenate | solution.py:178
  2.1 3.0 %collective-permute-start.7 = (bf16[2,2064,128]{2,1,0:T(8,128)(2,1)S(1)}, bf16[2,2064,128]{2,1,0:T(8,128)(2,1)S(1)}, u32[]{:S(2)}, u32[]{:S(2)}) collective-permute-start(bf16[2,2064,128]{2,1,0:T(8,128)(2,1)S(1)} %pad_maximum_fusion.refs_8_), channel_id=1, source_target_pairs={{0,8},{4,12},{8,0},{12,4},{16,24},{20,28},{24,16},{28,20},{1,9},{5... | collective-permute-start | bytes 3170312 | tf_op jit(solution)/shard_map/ppermute | solution.py:170
  5.1 1.5 %collective-permute-start.8 = (bf16[2,2064,128]{2,1,0:T(8,128)(2,1)S(1)}, bf16[2,2064,128]{2,1,0:T(8,128)(2,1)S(1)}, u32[]{:S(2)}, u32[]{:S(2)}) collective-permute-start(bf16[2,2064,128]{2,1,0:T(8,128)(2,1)S(1)} %pad_maximum_fusion.refs_8_), channel_id=1, source_target_pairs={{0,16},{4,20},{8,24},{12,28},{16,0},{20,4},{24,8},{28,12},{1,17},{... | collective-permute-start | bytes 3170312 | tf_op jit(solution)/shard_map/ppermute | solution.py:170
  6.6 2.6 %collective-permute-start.1 = (bf16[256,512]{1,0:T(8,128)(2,1)S(1)}, bf16[256,512]{1,0:T(8,128)(2,1)S(1)}, u32[]{:S(2)}, u32[]{:S(2)}) collective-permute-start(bf16[256,512]{1,0:T(8,128)(2,1)S(1)} %copy-done.4), channel_id=1, source_target_pairs={{0,2},{1,3},{2,0},{3,1},{4,6},{5,7},{6,4},{7,5},{8,10},{9,11},{10,... | collective-permute-start | bytes 786440 | tf_op jit(solution)/shard_map/ppermute | solution.py:173
  9.2 1.6 %collective-permute-start = (bf16[256,512]{1,0:T(8,128)(2,1)S(1)}, bf16[256,512]{1,0:T(8,128)(2,1)S(1)}, u32[]{:S(2)}, u32[]{:S(2)}) collective-permute-start(bf16[256,512]{1,0:T(8,128)(2,1)S(1)} %copy-done.4), channel_id=1, source_target_pairs={{0,1},{1,0},{2,3},{3,2},{4,5},{5,4},{6,7},{7,6},{8,9},{9,8},{10,11... | collective-permute-start | bytes 786440 | tf_op jit(solution)/shard_map/ppermute | solution.py:173
  10.8 9.9 %collective-permute-done.1.refs_2_.refs_5_ = bf16[256,512]{1,0:T(8,128)(2,1)S(1)} collective-permute-done((bf16[256,512]{1,0:T(8,128)(2,1)S(1)}, bf16[256,512]{1,0:T(8,128)(2,1)S(1)}, u32[]{:S(2)}, u32[]{:S(2)}) %collective-permute-start.1) | collective-permute-done | bytes 262176 | tf_op jit(solution)/shard_map/ppermute | solution.py:173
  21.8 6.0 %collective-permute-done.2.refs_3_.refs_6_ = bf16[256,512]{1,0:T(8,128)(2,1)S(1)} collective-permute-done((bf16[256,512]{1,0:T(8,128)(2,1)S(1)}, bf16[256,512]{1,0:T(8,128)(2,1)S(1)}, u32[]{:S(2)}, u32[]{:S(2)}) %collective-permute-start.2) | collective-permute-done | bytes 262176 | tf_op jit(solution)/shard_map/ppermute | solution.py:173
  27.9 1.4 %collective-permute-done.6.refs_7_.refs_3_ = bf16[256,512]{1,0:T(8,128)(2,1)S(1)} collective-permute-done((bf16[256,512]{1,0:T(8,128)(2,1)S(1)}, bf16[256,512]{1,0:T(8,128)(2,1)S(1)}, u32[]{:S(2)}, u32[]{:S(2)}) %collective-permute-start.6) | collective-permute-done | bytes 262176 | tf_op jit(solution)/shard_map/ppermute | solution.py:170
  29.9 0.8 %shard_map.47 = (bf16[1040,128]{1,0:T(8,128)(2,1)S(1)}, bf16[1024,128]{1,0:T(8,128)(2,1)}, bf16[1040,128]{1,0:T(8,128)(2,1)S(1)}, bf16[1024,128]{1,0:T(8,128)(2,1)}) custom-call(bf16[2,2064,128]{2,1,0:T(8,128)(2,1)S(1)} %collective-permute-done.7.refs_9_.x_ref, bf16[2,2064,128]{2,1,0:T(8,128)(2,1)S(1)} %collective-permute-done.8.refs_10_.y_ref, ...), custom_call_target="tpu_custom_call" | custom-call | tf_op jit(solution)/shard_map/pallas_call | solution.py:190
  30.8 1.5 %collective-permute-start.9 = (bf16[1040,128]{1,0:T(8,128)(2,1)S(1)}, bf16[1040,128]{1,0:T(8,128)(2,1)S(1)}, u32[]{:S(2)}, u32[]{:S(2)}) collective-permute-start(bf16[1040,128]{1,0:T(8,128)(2,1)S(1)} %get-tuple-element.28), channel_id=1, source_target_pairs={{0,16},{4,20},{8,24},{12,28},{16,0},{20,4},{24,8},{28,12},{1,17},{... | collective-permute-start | bytes 798728 | tf_op jit(solution)/shard_map/ppermute | solution.py:170
  33.4 1.7 %collective-permute-start.12 = (bf16[1024,128]{1,0:T(8,128)(2,1)}, bf16[1024,128]{1,0:T(8,128)(2,1)S(1)}, u32[]{:S(2)}, u32[]{:S(2)}) collective-permute-start(bf16[1024,128]{1,0:T(8,128)(2,1)} %get-tuple-element.33), channel_id=1, source_target_pairs={{0,8},{4,12},{8,0},{12,4},{16,24},{20,28},{24,16},{28,20},{1,9},{5... | collective-permute-start | bytes 786440 | tf_op jit(solution)/shard_map/ppermute | solution.py:170
  35.0 7.3 %shard_map.46 = (bf16[16,512,128]{2,1,0:T(8,128)(2,1)S(1)}, bf16[256,256]{1,0:T(8,128)(2,1)S(1)}, f32[16,256,128]{2,1,0:T(8,128)S(1)}, f32[16,256,128]{2,1,0:T(8,128)S(1)}) custom-call(bf16[256,512]{1,0:T(8,128)(2,1)S(1)} %copy-done.4, bf16[256,512]{1,0:T(8,128)(2,1)S(1)} %collective-permute-done.refs_1_.refs_4_, ...), custom_call_target="tpu_custom_call" | custom-call | tf_op jit(solution)/shard_map/pallas_call | solution.py:211
  42.4 1.3 %copy-done = f32[16,256,128]{2,1,0:T(8,128)} copy-done((f32[16,256,128]{2,1,0:T(8,128)}, f32[16,256,128]{2,1,0:T(8,128)S(1)}, u32[]{:S(2)}) %copy-start) | copy-done | bytes 2097176
  43.7 1.3 %copy-done.2 = bf16[16,512,128]{2,1,0:T(8,128)(2,1)} copy-done((bf16[16,512,128]{2,1,0:T(8,128)(2,1)}, bf16[16,512,128]{2,1,0:T(8,128)(2,1)S(1)}, u32[]{:S(2)}) %copy-start.2) | copy-done | bytes 2097176
  46.4 1.6 %copy-done.1 = f32[16,256,128]{2,1,0:T(8,128)S(1)} copy-done((f32[16,256,128]{2,1,0:T(8,128)S(1)}, f32[16,256,128]{2,1,0:T(8,128)}, u32[]{:S(2)}) %copy-start.1) | copy-done | bytes 2097176
  48.0 1.6 %copy-done.3 = bf16[16,512,128]{2,1,0:T(8,128)(2,1)S(1)} copy-done((bf16[16,512,128]{2,1,0:T(8,128)(2,1)S(1)}, bf16[16,512,128]{2,1,0:T(8,128)(2,1)}, u32[]{:S(2)}) %copy-start.3) | copy-done | bytes 2097176
  49.6 1.4 %shard_map.48 = (f32[16,256,128]{2,1,0:T(8,128)S(1)}, f32[16,256,128]{2,1,0:T(8,128)S(1)}) custom-call(bf16[16,512,128]{2,1,0:T(8,128)(2,1)S(1)} %copy-done.3, f32[16,256,128]{2,1,0:T(8,128)S(1)} %get-tuple-element.26.refs_1_, f32[16,256,128]{2,1,0:T(8,128)S(1)} %copy-done.1, ...), custom_call_target="tpu_custom_call", output_to_operand_aliasing={{0}: (1, {}), {1}: (2, {})} | custom-call | tf_op jit(solution)/shard_map/pallas_call | solution.py:227
  51.0 1.4 %shard_map.49 = (f32[16,256,128]{2,1,0:T(8,128)S(1)}, f32[16,256,128]{2,1,0:T(8,128)S(1)}) custom-call(bf16[16,512,128]{2,1,0:T(8,128)(2,1)S(1)} %copy-done.3, f32[16,256,128]{2,1,0:T(8,128)S(1)} %get-tuple-element.30.refs_1_, f32[16,256,128]{2,1,0:T(8,128)S(1)} %get-tuple-element.31.refs_2_, ...), custom_call_target="tpu_custom_call", output_to_operand_aliasing={{0}: (1, {}), {1}: (2, {})} | custom-call | tf_op jit(solution)/shard_map/pallas_call | solution.py:227
  54.3 2.9 %collective-permute-start.16 = (bf16[2,256,128]{2,1,0:T(8,128)(2,1)S(1)}, bf16[2,256,128]{2,1,0:T(8,128)(2,1)S(1)}, u32[]{:S(2)}, u32[]{:S(2)}) collective-permute-start(bf16[2,256,128]{2,1,0:T(8,128)(2,1)S(1)} %get-tuple-element.42), channel_id=1, source_target_pairs={{0,2},{1,3},{2,0},{3,1},{4,6},{5,7},{6,4},{7,5},{8,10},{9,11},{10,... | collective-permute-start | bytes 393224 | tf_op jit(solution)/shard_map/ppermute | solution.py:173
  57.2 1.3 %collective-permute-start.17 = (bf16[2,256,128]{2,1,0:T(8,128)(2,1)S(1)}, bf16[2,256,128]{2,1,0:T(8,128)(2,1)S(1)}, u32[]{:S(2)}, u32[]{:S(2)}) collective-permute-start(bf16[2,256,128]{2,1,0:T(8,128)(2,1)S(1)} %get-tuple-element.43), channel_id=1, source_target_pairs={{0,3},{1,2},{2,1},{3,0},{4,7},{5,6},{6,5},{7,4},{8,11},{9,10},{10,... | collective-permute-start | bytes 393224 | tf_op jit(solution)/shard_map/ppermute | solution.py:173
  59.1 8.2 %collective-permute-done.16.refs_2_ = bf16[2,256,128]{2,1,0:T(8,128)(2,1)S(1)} collective-permute-done((bf16[2,256,128]{2,1,0:T(8,128)(2,1)S(1)}, bf16[2,256,128]{2,1,0:T(8,128)(2,1)S(1)}, u32[]{:S(2)}, u32[]{:S(2)}) %collective-permute-start.16) | collective-permute-done | bytes 131104 | tf_op jit(solution)/shard_map/ppermute | solution.py:173
  67.3 0.9 %collective-permute-done.14.refs_1_ = bf16[2,256,128]{2,1,0:T(8,128)(2,1)S(1)} collective-permute-done((bf16[2,256,128]{2,1,0:T(8,128)(2,1)S(1)}, bf16[2,256,128]{2,1,0:T(8,128)(2,1)S(1)}, u32[]{:S(2)}, u32[]{:S(2)}) %collective-permute-start.14) | collective-permute-done | bytes 131104 | tf_op jit(solution)/shard_map/ppermute | solution.py:173
  68.4 1.3 %collective-permute-done.18.other_ref = bf16[2,256,128]{2,1,0:T(8,128)(2,1)S(1)} collective-permute-done((bf16[2,256,128]{2,1,0:T(8,128)(2,1)S(1)}, bf16[2,256,128]{2,1,0:T(8,128)(2,1)S(1)}, u32[]{:S(2)}, u32[]{:S(2)}) %collective-permute-start.18) | collective-permute-done | bytes 131104 | tf_op jit(solution)/shard_map/ppermute | solution.py:170
  69.7 1.3 %shard_map.55 = bf16[256,512]{1,0:T(8,128)(2,1)} custom-call(bf16[2,256,128]{2,1,0:T(8,128)(2,1)S(1)} %shard_map.54.own_ref, bf16[2,256,128]{2,1,0:T(8,128)(2,1)S(1)} %collective-permute-done.18.other_ref, bf16[256,256]{1,0:T(8,128)(2,1)S(1)} %get-tuple-element.44.hot_ref), custom_call_target="tpu_custom_call" | custom-call | tf_op jit(solution)/shard_map/pallas_call | solution.py:245
  (54 shorter events, 7.5 us)
Async XLA Ops:
  0.7 5.9 %copy-start.4 = (bf16[256,512]{1,0:T(8,128)(2,1)S(1)}, bf16[256,512]{1,0:T(8,128)(2,1)}, u32[]{:S(2)}) copy-start(bf16[256,512]{1,0:T(8,128)(2,1)} %refs_0_.1) | copy-start | bytes 786436
  0.7 27.1 %copy-start.6 = (bf16[2,16,128,128]{3,2,1,0:T(8,128)(2,1)S(1)}, bf16[2,16,128,128]{3,2,1,0:T(8,128)(2,1)}, u32[]{:S(2)}) copy-start(bf16[2,16,128,128]{3,2,1,0:T(8,128)(2,1)} %param.5) | copy-start | bytes 3145732
  2.1 27.3 %collective-permute-start.7 = (bf16[2,2064,128]{2,1,0:T(8,128)(2,1)S(1)}, bf16[2,2064,128]{2,1,0:T(8,128)(2,1)S(1)}, u32[]{:S(2)}, u32[]{:S(2)}) collective-permute-start(bf16[2,2064,128]{2,1,0:T(8,128)(2,1)S(1)} %pad_maximum_fusion.refs_8_), channel_id=1, source_target_pairs={{0,8},{4,12},{8,0},{12,4},{16,24},{20,28},{24,16},{28,20},{1,9},{5... | collective-permute-start | bytes 3170312 | tf_op jit(solution)/shard_map/ppermute | solution.py:170
  5.1 24.8 %collective-permute-start.8 = (bf16[2,2064,128]{2,1,0:T(8,128)(2,1)S(1)}, bf16[2,2064,128]{2,1,0:T(8,128)(2,1)S(1)}, u32[]{:S(2)}, u32[]{:S(2)}) collective-permute-start(bf16[2,2064,128]{2,1,0:T(8,128)(2,1)S(1)} %pad_maximum_fusion.refs_8_), channel_id=1, source_target_pairs={{0,16},{4,20},{8,24},{12,28},{16,0},{20,4},{24,8},{28,12},{1,17},{... | collective-permute-start | bytes 3170312 | tf_op jit(solution)/shard_map/ppermute | solution.py:170
  6.6 14.1 %collective-permute-start.1 = (bf16[256,512]{1,0:T(8,128)(2,1)S(1)}, bf16[256,512]{1,0:T(8,128)(2,1)S(1)}, u32[]{:S(2)}, u32[]{:S(2)}) collective-permute-start(bf16[256,512]{1,0:T(8,128)(2,1)S(1)} %copy-done.4), channel_id=1, source_target_pairs={{0,2},{1,3},{2,0},{3,1},{4,6},{5,7},{6,4},{7,5},{8,10},{9,11},{10,... | collective-permute-start | bytes 786440 | tf_op jit(solution)/shard_map/ppermute | solution.py:173
  9.2 12.1 %collective-permute-start = (bf16[256,512]{1,0:T(8,128)(2,1)S(1)}, bf16[256,512]{1,0:T(8,128)(2,1)S(1)}, u32[]{:S(2)}, u32[]{:S(2)}) collective-permute-start(bf16[256,512]{1,0:T(8,128)(2,1)S(1)} %copy-done.4), channel_id=1, source_target_pairs={{0,1},{1,0},{2,3},{3,2},{4,5},{5,4},{6,7},{7,6},{8,9},{9,8},{10,11... | collective-permute-start | bytes 786440 | tf_op jit(solution)/shard_map/ppermute | solution.py:173
  10.8 10.5 %collective-permute-start.3 = (bf16[256,512]{1,0:T(8,128)(2,1)S(1)}, bf16[256,512]{1,0:T(8,128)(2,1)S(1)}, u32[]{:S(2)}, u32[]{:S(2)}) collective-permute-start(bf16[256,512]{1,0:T(8,128)(2,1)S(1)} %copy-done.4), channel_id=1, source_target_pairs={{0,4},{4,0},{8,12},{12,8},{16,20},{20,16},{24,28},{28,24},{1,5},{5... | collective-permute-start | bytes 786440 | tf_op jit(solution)/shard_map/ppermute | solution.py:170
  20.8 7.1 %collective-permute-start.2 = (bf16[256,512]{1,0:T(8,128)(2,1)S(1)}, bf16[256,512]{1,0:T(8,128)(2,1)S(1)}, u32[]{:S(2)}, u32[]{:S(2)}) collective-permute-start(bf16[256,512]{1,0:T(8,128)(2,1)S(1)} %collective-permute-done.1.refs_2_.refs_5_), channel_id=1, source_target_pairs={{0,1},{1,0},{2,3},{3,2},{4,5},{5,4},{6,7},{7,6},{8,9},{9,8},{10,11... | collective-permute-start | bytes 786440 | tf_op jit(solution)/shard_map/ppermute | solution.py:173
  21.3 6.6 %collective-permute-start.5 = (bf16[256,512]{1,0:T(8,128)(2,1)S(1)}, bf16[256,512]{1,0:T(8,128)(2,1)S(1)}, u32[]{:S(2)}, u32[]{:S(2)}) collective-permute-start(bf16[256,512]{1,0:T(8,128)(2,1)S(1)} %collective-permute-done.1.refs_2_.refs_5_), channel_id=1, source_target_pairs={{0,4},{4,0},{8,12},{12,8},{16,20},{20,16},{24,28},{28,24},{1,5},{5... | collective-permute-start | bytes 786440 | tf_op jit(solution)/shard_map/ppermute | solution.py:170
  21.3 6.6 %collective-permute-start.4 = (bf16[256,512]{1,0:T(8,128)(2,1)S(1)}, bf16[256,512]{1,0:T(8,128)(2,1)S(1)}, u32[]{:S(2)}, u32[]{:S(2)}) collective-permute-start(bf16[256,512]{1,0:T(8,128)(2,1)S(1)} %collective-permute-done.refs_1_.refs_4_), channel_id=1, source_target_pairs={{0,4},{4,0},{8,12},{12,8},{16,20},{20,16},{24,28},{28,24},{1,5},{5... | collective-permute-start | bytes 786440 | tf_op jit(solution)/shard_map/ppermute | solution.py:170
  27.8 1.5 %collective-permute-start.6 = (bf16[256,512]{1,0:T(8,128)(2,1)S(1)}, bf16[256,512]{1,0:T(8,128)(2,1)S(1)}, u32[]{:S(2)}, u32[]{:S(2)}) collective-permute-start(bf16[256,512]{1,0:T(8,128)(2,1)S(1)} %collective-permute-done.2.refs_3_.refs_6_), channel_id=1, source_target_pairs={{0,4},{4,0},{8,12},{12,8},{16,20},{20,16},{24,28},{28,24},{1,5},{5... | collective-permute-start | bytes 786440 | tf_op jit(solution)/shard_map/ppermute | solution.py:170
  30.8 4.3 %copy-start.5 = (s32[256]{0:T(256)S(1)}, s32[256]{0:T(256)}, u32[]{:S(2)}) copy-start(s32[256]{0:T(256)} %param.7) | copy-start | bytes 3076
  30.8 14.3 %collective-permute-start.9 = (bf16[1040,128]{1,0:T(8,128)(2,1)S(1)}, bf16[1040,128]{1,0:T(8,128)(2,1)S(1)}, u32[]{:S(2)}, u32[]{:S(2)}) collective-permute-start(bf16[1040,128]{1,0:T(8,128)(2,1)S(1)} %get-tuple-element.28), channel_id=1, source_target_pairs={{0,16},{4,20},{8,24},{12,28},{16,0},{20,4},{24,8},{28,12},{1,17},{... | collective-permute-start | bytes 798728 | tf_op jit(solution)/shard_map/ppermute | solution.py:170
  32.4 14.0 %collective-permute-start.10 = (bf16[1040,128]{1,0:T(8,128)(2,1)S(1)}, bf16[1040,128]{1,0:T(8,128)(2,1)S(1)}, u32[]{:S(2)}, u32[]{:S(2)}) collective-permute-start(bf16[1040,128]{1,0:T(8,128)(2,1)S(1)} %get-tuple-element.29), channel_id=1, source_target_pairs={{0,8},{4,12},{8,0},{12,4},{16,24},{20,28},{24,16},{28,20},{1,9},{5... | collective-permute-start | bytes 798728 | tf_op jit(solution)/shard_map/ppermute | solution.py:170
  33.0 17.9 %collective-permute-start.11 = (bf16[1024,128]{1,0:T(8,128)(2,1)}, bf16[1024,128]{1,0:T(8,128)(2,1)S(1)}, u32[]{:S(2)}, u32[]{:S(2)}) collective-permute-start(bf16[1024,128]{1,0:T(8,128)(2,1)} %get-tuple-element.32), channel_id=1, source_target_pairs={{0,16},{4,20},{8,24},{12,28},{16,0},{20,4},{24,8},{28,12},{1,17},{... | collective-permute-start | bytes 786440 | tf_op jit(solution)/shard_map/ppermute | solution.py:170
  33.4 17.6 %collective-permute-start.12 = (bf16[1024,128]{1,0:T(8,128)(2,1)}, bf16[1024,128]{1,0:T(8,128)(2,1)S(1)}, u32[]{:S(2)}, u32[]{:S(2)}) collective-permute-start(bf16[1024,128]{1,0:T(8,128)(2,1)} %get-tuple-element.33), channel_id=1, source_target_pairs={{0,8},{4,12},{8,0},{12,4},{16,24},{20,28},{24,16},{28,20},{1,9},{5... | collective-permute-start | bytes 786440 | tf_op jit(solution)/shard_map/ppermute | solution.py:170
  46.4 1.6 %copy-start.1 = (f32[16,256,128]{2,1,0:T(8,128)S(1)}, f32[16,256,128]{2,1,0:T(8,128)}, u32[]{:S(2)}) copy-start(f32[16,256,128]{2,1,0:T(8,128)} %copy-done) | copy-start | bytes 6291460
  48.0 1.6 %copy-start.3 = (bf16[16,512,128]{2,1,0:T(8,128)(2,1)S(1)}, bf16[16,512,128]{2,1,0:T(8,128)(2,1)}, u32[]{:S(2)}) copy-start(bf16[16,512,128]{2,1,0:T(8,128)(2,1)} %copy-done.2) | copy-start | bytes 6291460
  52.7 1.6 %collective-permute-start.15 = (bf16[2,2,256,128]{3,2,1,0:T(8,128)(2,1)S(1)}, bf16[2,2,256,128]{3,2,1,0:T(8,128)(2,1)S(1)}, u32[]{:S(2)}, u32[]{:S(2)}) collective-permute-start(bf16[2,2,256,128]{3,2,1,0:T(8,128)(2,1)S(1)} %get-tuple-element.41), channel_id=1, source_target_pairs={{0,4},{4,0},{8,12},{12,8},{16,20},{20,16},{24,28},{28,24},{1,5},{5... | collective-permute-start | bytes 786440 | tf_op jit(solution)/shard_map/ppermute | solution.py:170
  53.1 5.4 %collective-permute-start.13 = (bf16[2,2,256,128]{3,2,1,0:T(8,128)(2,1)S(1)}, bf16[2,2,256,128]{3,2,1,0:T(8,128)(2,1)S(1)}, u32[]{:S(2)}, u32[]{:S(2)}) collective-permute-start(bf16[2,2,256,128]{3,2,1,0:T(8,128)(2,1)S(1)} %get-tuple-element.37), channel_id=1, source_target_pairs={{0,4},{4,0},{8,12},{12,8},{16,20},{20,16},{24,28},{28,24},{1,5},{5... | collective-permute-start | bytes 786440 | tf_op jit(solution)/shard_map/ppermute | solution.py:170
  54.3 12.9 %collective-permute-start.16 = (bf16[2,256,128]{2,1,0:T(8,128)(2,1)S(1)}, bf16[2,256,128]{2,1,0:T(8,128)(2,1)S(1)}, u32[]{:S(2)}, u32[]{:S(2)}) collective-permute-start(bf16[2,256,128]{2,1,0:T(8,128)(2,1)S(1)} %get-tuple-element.42), channel_id=1, source_target_pairs={{0,2},{1,3},{2,0},{3,1},{4,6},{5,7},{6,4},{7,5},{8,10},{9,11},{10,... | collective-permute-start | bytes 393224 | tf_op jit(solution)/shard_map/ppermute | solution.py:173
  57.2 10.1 %collective-permute-start.17 = (bf16[2,256,128]{2,1,0:T(8,128)(2,1)S(1)}, bf16[2,256,128]{2,1,0:T(8,128)(2,1)S(1)}, u32[]{:S(2)}, u32[]{:S(2)}) collective-permute-start(bf16[2,256,128]{2,1,0:T(8,128)(2,1)S(1)} %get-tuple-element.43), channel_id=1, source_target_pairs={{0,3},{1,2},{2,1},{3,0},{4,7},{5,6},{6,5},{7,4},{8,11},{9,10},{10,... | collective-permute-start | bytes 393224 | tf_op jit(solution)/shard_map/ppermute | solution.py:173
  58.5 9.7 %collective-permute-start.14 = (bf16[2,256,128]{2,1,0:T(8,128)(2,1)S(1)}, bf16[2,256,128]{2,1,0:T(8,128)(2,1)S(1)}, u32[]{:S(2)}, u32[]{:S(2)}) collective-permute-start(bf16[2,256,128]{2,1,0:T(8,128)(2,1)S(1)} %get-tuple-element.39), channel_id=1, source_target_pairs={{0,1},{1,0},{2,3},{3,2},{4,5},{5,4},{6,7},{7,6},{8,9},{9,8},{10,11... | collective-permute-start | bytes 393224 | tf_op jit(solution)/shard_map/ppermute | solution.py:173
  68.3 1.4 %collective-permute-start.18 = (bf16[2,256,128]{2,1,0:T(8,128)(2,1)S(1)}, bf16[2,256,128]{2,1,0:T(8,128)(2,1)S(1)}, u32[]{:S(2)}, u32[]{:S(2)}) collective-permute-start(bf16[2,256,128]{2,1,0:T(8,128)(2,1)S(1)} %shard_map.54.own_ref), channel_id=1, source_target_pairs={{0,4},{4,0},{8,12},{12,8},{16,20},{20,16},{24,28},{28,24},{1,5},{5... | collective-permute-start | bytes 393224 | tf_op jit(solution)/shard_map/ppermute | solution.py:170
  (2 other events, 2.7 us)

commit v13 on v12

--- a/solution.py
+++ b/solution.py
@@ -49,13 +49,13 @@
         lower_ref[...] = slab_ref[middle:]
 
 
-def add_products(grid_ref, acc_refs, tiles_ref, blocks_ref, first=EXTRA):
+def add_products(grid_ref, acc_refs, tiles_ref, blocks_ref, first=EXTRA, start=0):
     empty = jnp.zeros((TILE, TILE), BF16)
     rows = acc_refs[0].shape[1]
 
-    @pl.loop(0, blocks_ref.shape[1] // 2, unroll=4)
+    @pl.loop(0, tiles_ref.shape[0] // TILE // 2, unroll=4)
     def _(t):
-        to, come = [[blocks_ref[which, 2 * t + k] for k in range(2)] for which in range(2)]
+        to, come = [[blocks_ref[which, start + 2 * t + k] for k in range(2)] for which in range(2)]
         tiles = [tiles_ref[pl.ds(pl.multiple_of((2 * t + k) * TILE + first, EXTRA), TILE), :] for k in range(2)]
         right = jnp.concatenate(
             [jnp.concatenate([tiles[0], empty], axis=1), jnp.concatenate([empty, tiles[1]], axis=1)], axis=0
@@ -101,14 +101,15 @@
             add_products(grid_ref, acc_refs, tiles_ref.at[s], blocks_ref.at[s])
 
 
-def more_kernel(n_sets, *refs):
+def more_kernel(starts, *refs):
+    n_sets = len(starts)
     grid_ref = refs[0]
     tiles, blocks = refs[3 : 3 + n_sets], refs[3 + n_sets : 3 + 2 * n_sets]
     acc_refs = refs[3 + 2 * n_sets :]
-    for tiles_ref, blocks_ref in zip(tiles, blocks):
+    for tiles_ref, blocks_ref, start in zip(tiles, blocks, starts):
         for s in range(tiles_ref.shape[0]):
             first = tiles_ref.shape[1] % TILE
-            add_products(grid_ref, acc_refs, tiles_ref.at[s], blocks_ref.at[s], first)
+            add_products(grid_ref, acc_refs, tiles_ref.at[s], blocks_ref.at[s], first, start)
 
 
 def fold_kernel(shifts, own_ref, mirror_ref, keep_ref, send_ref):
@@ -218,14 +219,15 @@
         ],
         [VMEM] * (2 * n_vir + len(early)) + [SMEM] * len(early) + [VMEM],
         megabytes=20,
-    )(*mine, *others, *early, *[ids_in(array[0]) for array in early], row)
-    diagonal_ids = ids_in(late[0][0]).reshape(slabs, 2, 2, tile_dev // 2)
+    )(*mine, *others, *early, tile_blocks.transpose(0, 2, 1), *[ids_in(array[0]) for array in early[1:]], row)
+    diagonal_ids = ids_in(late[0][0])
     for part in range(2):
         more = [half[None] for half in late[part]] + (farther if part else [])
-        more_ids = [diagonal_ids[s : s + 1, :, part] for s in range(slabs)]
+        more_ids = [diagonal_ids[s : s + 1] for s in range(slabs)]
         more_ids += [ids_in(array[0]) for array in farther] if part else []
+        starts = [part * tile_dev // 2] * slabs + [0] * (len(more) - slabs)
         sums_so_far = call(
-            functools.partial(more_kernel, len(more)),
+            functools.partial(more_kernel, starts),
             [sums, sums],
             [VMEM] * (3 + len(more)) + [SMEM] * len(more),
             megabytes=24,

time: 71.5 us -> 64.8 us (0.906)
  local copies, waits for them, and re-layouts: 6.72 us -> 0.11 us
  waiting for transfers between devices: 29.1 us -> 30.1 us
  Pallas kernels: 13 us -> 12.2 us
    unnamed x14 -> x6, local copies, waits for them, and re-layouts: 5.86 us -> 0.02 us
    ppermute x13, waiting for transfers between devices: 4 us -> 5.04 us  [across(): return lax.ppermute(array, 'pair', [(i, i ^ bits) for i in range(n_pair)])]
    pallas_call x1, Pallas kernels: 0.85 us -> 0.07 us  [local(): call(functools.partial(cut_kernel, slabs), [jax.ShapeDtypeStruct((size, T...]
    another operation x1 -> x0, local copies, waits for them, and re-layouts: 0.75 us -> none  [local(): diagonal_ids = ids_in(late[0][0]).reshape(slabs, 2, 2, tile_dev // 2)]
  transfers between devices with their start and end apart: 19 -> 19, of which waited for: 8 -> 10; matrix products, arithmetic and copies ran while one was open for 2% -> 0% of each run, Pallas kernels for 13% -> 14%
where the time goes in v13:
time: 64.8 us; the launch traced here: 64.5 us
  waiting for transfers between devices  30.1 us (46%)
  starting transfers between devices  19.8 us (31%)
  Pallas kernels  12.2 us (19%)
  other arithmetic  2.04 us (3%)
    ppermute x6, waiting for transfers between devices, along(): return lax.ppermute(array, 'vir', [(i, i ^ bits) for i in range(n_vir)])  25 us
    ppermute x13, starting transfers between devices, across(): return lax.ppermute(array, 'pair', [(i, i ^ bits) for i in range(n_pair)])  9.92 us
    ppermute x6, starting transfers between devices, along(): return lax.ppermute(array, 'vir', [(i, i ^ bits) for i in range(n_vir)])  9.91 us
    pallas_call x1, Pallas kernels, local(): call(functools.partial(first_kernel, n_vir, len(early)), [jax.ShapeDtypeS...  7.35 us
    ppermute x13, waiting for transfers between devices, across(): return lax.ppermute(array, 'pair', [(i, i ^ bits) for i in range(n_pair)])  5.04 us
    pallas_call x2, Pallas kernels, local(): call(functools.partial(more_kernel, starts), [sums, sums], [VMEM] * (3 +...  2.74 us
    pallas_call x1, Pallas kernels, local(): call(finish_kernel, jax.ShapeDtypeStruct((rows, width), BF16), [VMEM] * 3...  1.3 us
  transfers between devices with their start and end apart: 19, of which 10 were waited for; matrix products, arithmetic and copies ran while one was open for 0% of the time, Pallas kernels for 14%

profile of v13, /device:TPU:0, one launch (start us, length us, event | category | flops | bytes accessed | tf_op | source)
XLA Modules:
  0.0 64.5 jit_solution(16612456547421351514)
XLA Ops:
  0.0 0.7 %bitcast_convert_fusion = bf16[2,2,16]{2,1,0:T(2,128)(2,1)S(1)} fusion(s32[2,16,2]{1,2,0:T(2,128)} %param.6), kind=kLoop, calls=%fused_computation.7 | loop fusion | flops 64 | bytes 384 | tf_op jit(solution)/shard_map/convert_element_type | solution.py:176
  0.7 1.3 %pad_maximum_fusion.refs_8_ = bf16[2,2064,128]{2,1,0:T(8,128)(2,1)S(1)} fusion(bf16[2,2048,128]{2,1,0:T(8,128)(2,1)} %bitcast.29, bf16[2,16,128]{2,1,0:T(8,128)(2,1)S(1)} %broadcast_in_dim.20), kind=kLoop, calls=%fused_computation | loop fusion | flops 2113536 | bytes 2113536 | tf_op jit(solution)/shard_map/concatenate | solution.py:179
  2.1 3.0 %collective-permute-start.7 = (bf16[2,2064,128]{2,1,0:T(8,128)(2,1)S(1)}, bf16[2,2064,128]{2,1,0:T(8,128)(2,1)S(1)}, u32[]{:S(2)}, u32[]{:S(2)}) collective-permute-start(bf16[2,2064,128]{2,1,0:T(8,128)(2,1)S(1)} %pad_maximum_fusion.refs_8_), channel_id=1, source_target_pairs={{0,8},{4,12},{8,0},{12,4},{16,24},{20,28},{24,16},{28,20},{1,9},{5... | collective-permute-start | bytes 3170312 | tf_op jit(solution)/shard_map/ppermute | solution.py:171
  5.1 1.5 %collective-permute-start.8 = (bf16[2,2064,128]{2,1,0:T(8,128)(2,1)S(1)}, bf16[2,2064,128]{2,1,0:T(8,128)(2,1)S(1)}, u32[]{:S(2)}, u32[]{:S(2)}) collective-permute-start(bf16[2,2064,128]{2,1,0:T(8,128)(2,1)S(1)} %pad_maximum_fusion.refs_8_), channel_id=1, source_target_pairs={{0,16},{4,20},{8,24},{12,28},{16,0},{20,4},{24,8},{28,12},{1,17},{... | collective-permute-start | bytes 3170312 | tf_op jit(solution)/shard_map/ppermute | solution.py:171
  6.6 2.6 %collective-permute-start.1 = (bf16[256,512]{1,0:T(8,128)(2,1)S(1)}, bf16[256,512]{1,0:T(8,128)(2,1)S(1)}, u32[]{:S(2)}, u32[]{:S(2)}) collective-permute-start(bf16[256,512]{1,0:T(8,128)(2,1)S(1)} %copy-done), channel_id=1, source_target_pairs={{0,2},{1,3},{2,0},{3,1},{4,6},{5,7},{6,4},{7,5},{8,10},{9,11},{10,... | collective-permute-start | bytes 786440 | tf_op jit(solution)/shard_map/ppermute | solution.py:174
  9.2 1.6 %collective-permute-start = (bf16[256,512]{1,0:T(8,128)(2,1)S(1)}, bf16[256,512]{1,0:T(8,128)(2,1)S(1)}, u32[]{:S(2)}, u32[]{:S(2)}) collective-permute-start(bf16[256,512]{1,0:T(8,128)(2,1)S(1)} %copy-done), channel_id=1, source_target_pairs={{0,1},{1,0},{2,3},{3,2},{4,5},{5,4},{6,7},{7,6},{8,9},{9,8},{10,11... | collective-permute-start | bytes 786440 | tf_op jit(solution)/shard_map/ppermute | solution.py:174
  10.8 9.9 %collective-permute-done.1.refs_2_.refs_5_ = bf16[256,512]{1,0:T(8,128)(2,1)S(1)} collective-permute-done((bf16[256,512]{1,0:T(8,128)(2,1)S(1)}, bf16[256,512]{1,0:T(8,128)(2,1)S(1)}, u32[]{:S(2)}, u32[]{:S(2)}) %collective-permute-start.1) | collective-permute-done | bytes 262176 | tf_op jit(solution)/shard_map/ppermute | solution.py:174
  20.7 0.6 collective-permute-start.2
  21.8 6.0 %collective-permute-done.2.refs_3_.refs_6_ = bf16[256,512]{1,0:T(8,128)(2,1)S(1)} collective-permute-done((bf16[256,512]{1,0:T(8,128)(2,1)S(1)}, bf16[256,512]{1,0:T(8,128)(2,1)S(1)}, u32[]{:S(2)}, u32[]{:S(2)}) %collective-permute-start.2) | collective-permute-done | bytes 262176 | tf_op jit(solution)/shard_map/ppermute | solution.py:174
  27.8 1.5 %collective-permute-done.6.refs_7_.refs_3_ = bf16[256,512]{1,0:T(8,128)(2,1)S(1)} collective-permute-done((bf16[256,512]{1,0:T(8,128)(2,1)S(1)}, bf16[256,512]{1,0:T(8,128)(2,1)S(1)}, u32[]{:S(2)}, u32[]{:S(2)}) %collective-permute-start.6) | collective-permute-done | bytes 262176 | tf_op jit(solution)/shard_map/ppermute | solution.py:171
  29.9 1.6 %collective-permute-start.9 = (bf16[1040,128]{1,0:T(8,128)(2,1)S(1)}, bf16[1040,128]{1,0:T(8,128)(2,1)S(1)}, u32[]{:S(2)}, u32[]{:S(2)}) collective-permute-start(bf16[1040,128]{1,0:T(8,128)(2,1)S(1)} %get-tuple-element.28), channel_id=1, source_target_pairs={{0,16},{4,20},{8,24},{12,28},{16,0},{20,4},{24,8},{28,12},{1,17},{... | collective-permute-start | bytes 798728 | tf_op jit(solution)/shard_map/ppermute | solution.py:171
  31.7 0.6 collective-permute-start.10
  32.6 1.7 %collective-permute-start.12 = (bf16[1024,128]{1,0:T(8,128)(2,1)S(1)}, bf16[1024,128]{1,0:T(8,128)(2,1)S(1)}, u32[]{:S(2)}, u32[]{:S(2)}) collective-permute-start(bf16[1024,128]{1,0:T(8,128)(2,1)S(1)} %get-tuple-element.33), channel_id=1, source_target_pairs={{0,8},{4,12},{8,0},{12,4},{16,24},{20,28},{24,16},{28,20},{1,9},{5... | collective-permute-start | bytes 786440 | tf_op jit(solution)/shard_map/ppermute | solution.py:171
  34.3 7.3 %shard_map.46 = (bf16[16,512,128]{2,1,0:T(8,128)(2,1)S(1)}, bf16[256,256]{1,0:T(8,128)(2,1)S(1)}, f32[16,256,128]{2,1,0:T(8,128)S(1)}, f32[16,256,128]{2,1,0:T(8,128)S(1)}) custom-call(bf16[256,512]{1,0:T(8,128)(2,1)S(1)} %copy-done, bf16[256,512]{1,0:T(8,128)(2,1)S(1)} %collective-permute-done.refs_1_.refs_4_, ...), custom_call_target="tpu_custom_call" | custom-call | tf_op jit(solution)/shard_map/pallas_call | solution.py:212
  41.7 1.4 %shard_map.48 = (f32[16,256,128]{2,1,0:T(8,128)S(1)}, f32[16,256,128]{2,1,0:T(8,128)S(1)}) custom-call(bf16[16,512,128]{2,1,0:T(8,128)(2,1)S(1)} %get-tuple-element.25.refs_0_, f32[16,256,128]{2,1,0:T(8,128)S(1)} %get-tuple-element.26.refs_1_, f32[16,256,128]{2,1,0:T(8,128)S(1)} %get-tuple-element.27.refs_2_, ...), custom_call_target="tpu_custom_call", output_to_operand_aliasing={{0}: (1, {}), {1}: (2, {})} | custom-call | tf_op jit(solution)/shard_map/pallas_call | solution.py:229
  44.0 1.4 %shard_map.49 = (f32[16,256,128]{2,1,0:T(8,128)S(1)}, f32[16,256,128]{2,1,0:T(8,128)S(1)}) custom-call(bf16[16,512,128]{2,1,0:T(8,128)(2,1)S(1)} %get-tuple-element.25.refs_0_, f32[16,256,128]{2,1,0:T(8,128)S(1)} %get-tuple-element.30.refs_1_, f32[16,256,128]{2,1,0:T(8,128)S(1)} %get-tuple-element.31.refs_2_, ...), custom_call_target="tpu_custom_call", output_to_operand_aliasing={{0}: (1, {}), {1}: (2, {})} | custom-call | tf_op jit(solution)/shard_map/pallas_call | solution.py:229
  46.1 0.6 collective-permute-start.13
  46.6 0.7 %collective-permute-done.15.come_ref = bf16[2,2,256,128]{3,2,1,0:T(8,128)(2,1)S(1)} collective-permute-done((bf16[2,2,256,128]{3,2,1,0:T(8,128)(2,1)S(1)}, bf16[2,2,256,128]{3,2,1,0:T(8,128)(2,1)S(1)}, u32[]{:S(2)}, u32[]{:S(2)}) %collective-permute-start.15) | collective-permute-done | bytes 262176 | tf_op jit(solution)/shard_map/ppermute | solution.py:171
  47.4 3.3 %collective-permute-start.16 = (bf16[2,256,128]{2,1,0:T(8,128)(2,1)S(1)}, bf16[2,256,128]{2,1,0:T(8,128)(2,1)S(1)}, u32[]{:S(2)}, u32[]{:S(2)}) collective-permute-start(bf16[2,256,128]{2,1,0:T(8,128)(2,1)S(1)} %get-tuple-element.42), channel_id=1, source_target_pairs={{0,2},{1,3},{2,0},{3,1},{4,6},{5,7},{6,4},{7,5},{8,10},{9,11},{10,... | collective-permute-start | bytes 393224 | tf_op jit(solution)/shard_map/ppermute | solution.py:174
  50.7 1.3 %collective-permute-start.17 = (bf16[2,256,128]{2,1,0:T(8,128)(2,1)S(1)}, bf16[2,256,128]{2,1,0:T(8,128)(2,1)S(1)}, u32[]{:S(2)}, u32[]{:S(2)}) collective-permute-start(bf16[2,256,128]{2,1,0:T(8,128)(2,1)S(1)} %get-tuple-element.43), channel_id=1, source_target_pairs={{0,3},{1,2},{2,1},{3,0},{4,7},{5,6},{6,5},{7,4},{8,11},{9,10},{10,... | collective-permute-start | bytes 393224 | tf_op jit(solution)/shard_map/ppermute | solution.py:174
  52.6 8.0 %collective-permute-done.16.refs_2_ = bf16[2,256,128]{2,1,0:T(8,128)(2,1)S(1)} collective-permute-done((bf16[2,256,128]{2,1,0:T(8,128)(2,1)S(1)}, bf16[2,256,128]{2,1,0:T(8,128)(2,1)S(1)}, u32[]{:S(2)}, u32[]{:S(2)}) %collective-permute-start.16) | collective-permute-done | bytes 131104 | tf_op jit(solution)/shard_map/ppermute | solution.py:174
  60.7 1.0 %collective-permute-done.14.refs_1_ = bf16[2,256,128]{2,1,0:T(8,128)(2,1)S(1)} collective-permute-done((bf16[2,256,128]{2,1,0:T(8,128)(2,1)S(1)}, bf16[2,256,128]{2,1,0:T(8,128)(2,1)S(1)}, u32[]{:S(2)}, u32[]{:S(2)}) %collective-permute-start.14) | collective-permute-done | bytes 131104 | tf_op jit(solution)/shard_map/ppermute | solution.py:174
  61.8 1.3 %collective-permute-done.18.other_ref = bf16[2,256,128]{2,1,0:T(8,128)(2,1)S(1)} collective-permute-done((bf16[2,256,128]{2,1,0:T(8,128)(2,1)S(1)}, bf16[2,256,128]{2,1,0:T(8,128)(2,1)S(1)}, u32[]{:S(2)}, u32[]{:S(2)}) %collective-permute-start.18) | collective-permute-done | bytes 131104 | tf_op jit(solution)/shard_map/ppermute | solution.py:171
  63.2 1.3 %shard_map.55 = bf16[256,512]{1,0:T(8,128)(2,1)} custom-call(bf16[2,256,128]{2,1,0:T(8,128)(2,1)S(1)} %shard_map.54.own_ref, bf16[2,256,128]{2,1,0:T(8,128)(2,1)S(1)} %collective-permute-done.18.other_ref, bf16[256,256]{1,0:T(8,128)(2,1)S(1)} %get-tuple-element.44.hot_ref), custom_call_target="tpu_custom_call" | custom-call | tf_op jit(solution)/shard_map/pallas_call | solution.py:247
  (42 shorter events, 4.1 us)
Async XLA Ops:
  0.0 6.6 %copy-start = (bf16[256,512]{1,0:T(8,128)(2,1)S(1)}, bf16[256,512]{1,0:T(8,128)(2,1)}, u32[]{:S(2)}) copy-start(bf16[256,512]{1,0:T(8,128)(2,1)} %refs_0_.1) | copy-start | bytes 786436
  2.0 32.2 %copy-start.1 = (s32[2,16,2]{1,2,0:T(2,128)S(1)}, s32[2,16,2]{1,2,0:T(2,128)}, u32[]{:S(2)}) copy-start(s32[2,16,2]{1,2,0:T(2,128)} %param.6) | copy-start | bytes 772
  2.1 32.2 %copy-start.2 = (s32[256]{0:T(256)S(1)}, s32[256]{0:T(256)}, u32[]{:S(2)}) copy-start(s32[256]{0:T(256)} %param.7) | copy-start | bytes 3076
  2.1 27.3 %collective-permute-start.7 = (bf16[2,2064,128]{2,1,0:T(8,128)(2,1)S(1)}, bf16[2,2064,128]{2,1,0:T(8,128)(2,1)S(1)}, u32[]{:S(2)}, u32[]{:S(2)}) collective-permute-start(bf16[2,2064,128]{2,1,0:T(8,128)(2,1)S(1)} %pad_maximum_fusion.refs_8_), channel_id=1, source_target_pairs={{0,8},{4,12},{8,0},{12,4},{16,24},{20,28},{24,16},{28,20},{1,9},{5... | collective-permute-start | bytes 3170312 | tf_op jit(solution)/shard_map/ppermute | solution.py:171
  5.1 24.8 %collective-permute-start.8 = (bf16[2,2064,128]{2,1,0:T(8,128)(2,1)S(1)}, bf16[2,2064,128]{2,1,0:T(8,128)(2,1)S(1)}, u32[]{:S(2)}, u32[]{:S(2)}) collective-permute-start(bf16[2,2064,128]{2,1,0:T(8,128)(2,1)S(1)} %pad_maximum_fusion.refs_8_), channel_id=1, source_target_pairs={{0,16},{4,20},{8,24},{12,28},{16,0},{20,4},{24,8},{28,12},{1,17},{... | collective-permute-start | bytes 3170312 | tf_op jit(solution)/shard_map/ppermute | solution.py:171
  6.6 14.1 %collective-permute-start.1 = (bf16[256,512]{1,0:T(8,128)(2,1)S(1)}, bf16[256,512]{1,0:T(8,128)(2,1)S(1)}, u32[]{:S(2)}, u32[]{:S(2)}) collective-permute-start(bf16[256,512]{1,0:T(8,128)(2,1)S(1)} %copy-done), channel_id=1, source_target_pairs={{0,2},{1,3},{2,0},{3,1},{4,6},{5,7},{6,4},{7,5},{8,10},{9,11},{10,... | collective-permute-start | bytes 786440 | tf_op jit(solution)/shard_map/ppermute | solution.py:174
  9.2 12.1 %collective-permute-start = (bf16[256,512]{1,0:T(8,128)(2,1)S(1)}, bf16[256,512]{1,0:T(8,128)(2,1)S(1)}, u32[]{:S(2)}, u32[]{:S(2)}) collective-permute-start(bf16[256,512]{1,0:T(8,128)(2,1)S(1)} %copy-done), channel_id=1, source_target_pairs={{0,1},{1,0},{2,3},{3,2},{4,5},{5,4},{6,7},{7,6},{8,9},{9,8},{10,11... | collective-permute-start | bytes 786440 | tf_op jit(solution)/shard_map/ppermute | solution.py:174
  10.8 10.5 %collective-permute-start.3 = (bf16[256,512]{1,0:T(8,128)(2,1)S(1)}, bf16[256,512]{1,0:T(8,128)(2,1)S(1)}, u32[]{:S(2)}, u32[]{:S(2)}) collective-permute-start(bf16[256,512]{1,0:T(8,128)(2,1)S(1)} %copy-done), channel_id=1, source_target_pairs={{0,4},{4,0},{8,12},{12,8},{16,20},{20,16},{24,28},{28,24},{1,5},{5... | collective-permute-start | bytes 786440 | tf_op jit(solution)/shard_map/ppermute | solution.py:171
  20.7 7.1 %collective-permute-start.2 = (bf16[256,512]{1,0:T(8,128)(2,1)S(1)}, bf16[256,512]{1,0:T(8,128)(2,1)S(1)}, u32[]{:S(2)}, u32[]{:S(2)}) collective-permute-start(bf16[256,512]{1,0:T(8,128)(2,1)S(1)} %collective-permute-done.1.refs_2_.refs_5_), channel_id=1, source_target_pairs={{0,1},{1,0},{2,3},{3,2},{4,5},{5,4},{6,7},{7,6},{8,9},{9,8},{10,11... | collective-permute-start | bytes 786440 | tf_op jit(solution)/shard_map/ppermute | solution.py:174
  21.3 6.5 %collective-permute-start.5 = (bf16[256,512]{1,0:T(8,128)(2,1)S(1)}, bf16[256,512]{1,0:T(8,128)(2,1)S(1)}, u32[]{:S(2)}, u32[]{:S(2)}) collective-permute-start(bf16[256,512]{1,0:T(8,128)(2,1)S(1)} %collective-permute-done.1.refs_2_.refs_5_), channel_id=1, source_target_pairs={{0,4},{4,0},{8,12},{12,8},{16,20},{20,16},{24,28},{28,24},{1,5},{5... | collective-permute-start | bytes 786440 | tf_op jit(solution)/shard_map/ppermute | solution.py:171
  21.3 6.5 %collective-permute-start.4 = (bf16[256,512]{1,0:T(8,128)(2,1)S(1)}, bf16[256,512]{1,0:T(8,128)(2,1)S(1)}, u32[]{:S(2)}, u32[]{:S(2)}) collective-permute-start(bf16[256,512]{1,0:T(8,128)(2,1)S(1)} %collective-permute-done.refs_1_.refs_4_), channel_id=1, source_target_pairs={{0,4},{4,0},{8,12},{12,8},{16,20},{20,16},{24,28},{28,24},{1,5},{5... | collective-permute-start | bytes 786440 | tf_op jit(solution)/shard_map/ppermute | solution.py:171
  27.8 1.5 %collective-permute-start.6 = (bf16[256,512]{1,0:T(8,128)(2,1)S(1)}, bf16[256,512]{1,0:T(8,128)(2,1)S(1)}, u32[]{:S(2)}, u32[]{:S(2)}) collective-permute-start(bf16[256,512]{1,0:T(8,128)(2,1)S(1)} %collective-permute-done.2.refs_3_.refs_6_), channel_id=1, source_target_pairs={{0,4},{4,0},{8,12},{12,8},{16,20},{20,16},{24,28},{28,24},{1,5},{5... | collective-permute-start | bytes 786440 | tf_op jit(solution)/shard_map/ppermute | solution.py:171
  29.9 11.7 %collective-permute-start.9 = (bf16[1040,128]{1,0:T(8,128)(2,1)S(1)}, bf16[1040,128]{1,0:T(8,128)(2,1)S(1)}, u32[]{:S(2)}, u32[]{:S(2)}) collective-permute-start(bf16[1040,128]{1,0:T(8,128)(2,1)S(1)} %get-tuple-element.28), channel_id=1, source_target_pairs={{0,16},{4,20},{8,24},{12,28},{16,0},{20,4},{24,8},{28,12},{1,17},{... | collective-permute-start | bytes 798728 | tf_op jit(solution)/shard_map/ppermute | solution.py:171
  31.7 10.0 %collective-permute-start.10 = (bf16[1040,128]{1,0:T(8,128)(2,1)S(1)}, bf16[1040,128]{1,0:T(8,128)(2,1)S(1)}, u32[]{:S(2)}, u32[]{:S(2)}) collective-permute-start(bf16[1040,128]{1,0:T(8,128)(2,1)S(1)} %get-tuple-element.29), channel_id=1, source_target_pairs={{0,8},{4,12},{8,0},{12,4},{16,24},{20,28},{24,16},{28,20},{1,9},{5... | collective-permute-start | bytes 798728 | tf_op jit(solution)/shard_map/ppermute | solution.py:171
  32.3 11.3 %collective-permute-start.11 = (bf16[1024,128]{1,0:T(8,128)(2,1)S(1)}, bf16[1024,128]{1,0:T(8,128)(2,1)S(1)}, u32[]{:S(2)}, u32[]{:S(2)}) collective-permute-start(bf16[1024,128]{1,0:T(8,128)(2,1)S(1)} %get-tuple-element.32), channel_id=1, source_target_pairs={{0,16},{4,20},{8,24},{12,28},{16,0},{20,4},{24,8},{28,12},{1,17},{... | collective-permute-start | bytes 786440 | tf_op jit(solution)/shard_map/ppermute | solution.py:171
  32.6 11.4 %collective-permute-start.12 = (bf16[1024,128]{1,0:T(8,128)(2,1)S(1)}, bf16[1024,128]{1,0:T(8,128)(2,1)S(1)}, u32[]{:S(2)}, u32[]{:S(2)}) collective-permute-start(bf16[1024,128]{1,0:T(8,128)(2,1)S(1)} %get-tuple-element.33), channel_id=1, source_target_pairs={{0,8},{4,12},{8,0},{12,4},{16,24},{20,28},{24,16},{28,20},{1,9},{5... | collective-permute-start | bytes 786440 | tf_op jit(solution)/shard_map/ppermute | solution.py:171
  45.7 1.6 %collective-permute-start.15 = (bf16[2,2,256,128]{3,2,1,0:T(8,128)(2,1)S(1)}, bf16[2,2,256,128]{3,2,1,0:T(8,128)(2,1)S(1)}, u32[]{:S(2)}, u32[]{:S(2)}) collective-permute-start(bf16[2,2,256,128]{3,2,1,0:T(8,128)(2,1)S(1)} %get-tuple-element.41), channel_id=1, source_target_pairs={{0,4},{4,0},{8,12},{12,8},{16,20},{20,16},{24,28},{28,24},{1,5},{5... | collective-permute-start | bytes 786440 | tf_op jit(solution)/shard_map/ppermute | solution.py:171
  46.1 5.9 %collective-permute-start.13 = (bf16[2,2,256,128]{3,2,1,0:T(8,128)(2,1)S(1)}, bf16[2,2,256,128]{3,2,1,0:T(8,128)(2,1)S(1)}, u32[]{:S(2)}, u32[]{:S(2)}) collective-permute-start(bf16[2,2,256,128]{3,2,1,0:T(8,128)(2,1)S(1)} %get-tuple-element.37), channel_id=1, source_target_pairs={{0,4},{4,0},{8,12},{12,8},{16,20},{20,16},{24,28},{28,24},{1,5},{5... | collective-permute-start | bytes 786440 | tf_op jit(solution)/shard_map/ppermute | solution.py:171
  47.4 13.3 %collective-permute-start.16 = (bf16[2,256,128]{2,1,0:T(8,128)(2,1)S(1)}, bf16[2,256,128]{2,1,0:T(8,128)(2,1)S(1)}, u32[]{:S(2)}, u32[]{:S(2)}) collective-permute-start(bf16[2,256,128]{2,1,0:T(8,128)(2,1)S(1)} %get-tuple-element.42), channel_id=1, source_target_pairs={{0,2},{1,3},{2,0},{3,1},{4,6},{5,7},{6,4},{7,5},{8,10},{9,11},{10,... | collective-permute-start | bytes 393224 | tf_op jit(solution)/shard_map/ppermute | solution.py:174
  50.7 9.9 %collective-permute-start.17 = (bf16[2,256,128]{2,1,0:T(8,128)(2,1)S(1)}, bf16[2,256,128]{2,1,0:T(8,128)(2,1)S(1)}, u32[]{:S(2)}, u32[]{:S(2)}) collective-permute-start(bf16[2,256,128]{2,1,0:T(8,128)(2,1)S(1)} %get-tuple-element.43), channel_id=1, source_target_pairs={{0,3},{1,2},{2,1},{3,0},{4,7},{5,6},{6,5},{7,4},{8,11},{9,10},{10,... | collective-permute-start | bytes 393224 | tf_op jit(solution)/shard_map/ppermute | solution.py:174
  52.0 9.6 %collective-permute-start.14 = (bf16[2,256,128]{2,1,0:T(8,128)(2,1)S(1)}, bf16[2,256,128]{2,1,0:T(8,128)(2,1)S(1)}, u32[]{:S(2)}, u32[]{:S(2)}) collective-permute-start(bf16[2,256,128]{2,1,0:T(8,128)(2,1)S(1)} %get-tuple-element.39), channel_id=1, source_target_pairs={{0,1},{1,0},{2,3},{3,2},{4,5},{5,4},{6,7},{7,6},{8,9},{9,8},{10,11... | collective-permute-start | bytes 393224 | tf_op jit(solution)/shard_map/ppermute | solution.py:174
  61.8 1.4 %collective-permute-start.18 = (bf16[2,256,128]{2,1,0:T(8,128)(2,1)S(1)}, bf16[2,256,128]{2,1,0:T(8,128)(2,1)S(1)}, u32[]{:S(2)}, u32[]{:S(2)}) collective-permute-start(bf16[2,256,128]{2,1,0:T(8,128)(2,1)S(1)} %shard_map.54.own_ref), channel_id=1, source_target_pairs={{0,4},{4,0},{8,12},{12,8},{16,20},{20,16},{24,28},{28,24},{1,5},{5... | collective-permute-start | bytes 393224 | tf_op jit(solution)/shard_map/ppermute | solution.py:171

commit v14 on v13

--- a/solution.py
+++ b/solution.py
@@ -9,7 +9,6 @@
 
 TILE = 128
 SUB = 8
-EXTRA = 16
 F32 = jnp.float32
 BF16 = jnp.bfloat16
 VMEM = pl.BlockSpec(memory_space=pltpu.VMEM)
@@ -40,6 +39,10 @@
     return iota((TILE, TILE), 0) == (1 - h) * SUB * SUB + b * SUB + a
 
 
+def copy_kernel(in_ref, *refs):
+    refs[-1][...] = in_ref[...]
+
+
 def cut_kernel(slabs, x_ref, y_ref, *refs):
     for s in range(slabs):
         slab_ref = (x_ref if s % 2 == 0 else y_ref).at[s]
@@ -49,14 +52,14 @@
         lower_ref[...] = slab_ref[middle:]
 
 
-def add_products(grid_ref, acc_refs, tiles_ref, blocks_ref, first=EXTRA, start=0):
+def add_products(grid_ref, acc_refs, tiles_ref, blocks_ref, start=0):
     empty = jnp.zeros((TILE, TILE), BF16)
     rows = acc_refs[0].shape[1]
 
     @pl.loop(0, tiles_ref.shape[0] // TILE // 2, unroll=4)
     def _(t):
         to, come = [[blocks_ref[which, start + 2 * t + k] for k in range(2)] for which in range(2)]
-        tiles = [tiles_ref[pl.ds(pl.multiple_of((2 * t + k) * TILE + first, EXTRA), TILE), :] for k in range(2)]
+        tiles = [tiles_ref[pl.ds(pl.multiple_of((2 * t + k) * TILE, TILE), TILE), :] for k in range(2)]
         right = jnp.concatenate(
             [jnp.concatenate([tiles[0], empty], axis=1), jnp.concatenate([empty, tiles[1]], axis=1)], axis=0
         )
@@ -108,8 +111,7 @@
     acc_refs = refs[3 + 2 * n_sets :]
     for tiles_ref, blocks_ref, start in zip(tiles, blocks, starts):
         for s in range(tiles_ref.shape[0]):
-            first = tiles_ref.shape[1] % TILE
-            add_products(grid_ref, acc_refs, tiles_ref.at[s], blocks_ref.at[s], first, start)
+            add_products(grid_ref, acc_refs, tiles_ref.at[s], blocks_ref.at[s], start)
 
 
 def fold_kernel(shifts, own_ref, mirror_ref, keep_ref, send_ref):
@@ -173,11 +175,8 @@
     def along(array, bits):
         return lax.ppermute(array, "vir", [(i, i ^ bits) for i in range(n_vir)])
 
-    ids = tile_blocks.transpose(0, 2, 1).reshape(1, 2 * slabs, tile_dev).astype(BF16)
-    ids = jnp.pad(ids, ((0, 0), (0, EXTRA - 2 * slabs), (0, TILE - tile_dev)))
-    ids = jnp.broadcast_to(ids, (slabs, EXTRA, TILE))
-    packed = jnp.concatenate([ids, integrals.reshape(slabs, length, TILE)], axis=1)
-    early = [packed, across(packed, 2), across(packed, 4)]
+    tiles = integrals.reshape(slabs, length, TILE)
+    early = [tiles, across(tiles, 2), across(tiles, 4)]
 
     pieces = {0: amplitudes}
     reach = n_vir // 2
@@ -186,12 +185,18 @@
         reach //= 2
     mine = [pieces[shift] for shift in range(n_vir)]
     others = [across(piece, 1) for piece in mine]
-    first = [*others, *mine[1:]]
-    middle = EXTRA + length // 2
+    ids = tile_blocks.transpose(0, 2, 1)
+    anywhere = pl.BlockSpec(memory_space=pl.ANY)
+    first = [others[n_vir // 2], others[1]]
+    held = call(
+        copy_kernel, jax.ShapeDtypeStruct(ids.shape, ids.dtype), [VMEM, anywhere, anywhere], megabytes=4
+    )(ids, *first)
+    blocks = [ids] + [across(held, 2 * d) for d in range(1, chips)]
+    first = [*others, *mine[1:], *blocks[1:]]
     halves = call(
         functools.partial(cut_kernel, slabs),
-        [jax.ShapeDtypeStruct((size, TILE), BF16) for _ in range(slabs) for size in (middle, length // 2)],
-        [VMEM, VMEM] + [pl.BlockSpec(memory_space=pl.ANY)] * len(first),
+        [jax.ShapeDtypeStruct((length // 2, TILE), BF16)] * (2 * slabs),
+        [VMEM, VMEM] + [anywhere] * len(first),
         megabytes=4,
     )(early[1], early[2], *first)
     late = [[across(half, 4 if s % 2 == 0 else 2) for s, half in enumerate(halves[part::2])] for part in range(2)]
@@ -205,9 +210,6 @@
         reach *= 2
     row = mirror_row.reshape(1, rows)
 
-    def ids_in(array):
-        return array[: 2 * slabs, :tile_dev].astype(jnp.int32).reshape(slabs, 2, tile_dev)
-
     sums = jax.ShapeDtypeStruct((n_blk, rows, TILE), F32)
     grid, last_hot, *sums_so_far = call(
         functools.partial(first_kernel, n_vir, len(early)),
@@ -219,12 +221,10 @@
         ],
         [VMEM] * (2 * n_vir + len(early)) + [SMEM] * len(early) + [VMEM],
         megabytes=20,
-    )(*mine, *others, *early, tile_blocks.transpose(0, 2, 1), *[ids_in(array[0]) for array in early[1:]], row)
-    diagonal_ids = ids_in(late[0][0])
+    )(*mine, *others, *early, *blocks[:3], row)
     for part in range(2):
         more = [half[None] for half in late[part]] + (farther if part else [])
-        more_ids = [diagonal_ids[s : s + 1] for s in range(slabs)]
-        more_ids += [ids_in(array[0]) for array in farther] if part else []
+        more_ids = [blocks[3][s : s + 1] for s in range(slabs)] + (blocks[4:] if part else [])
         starts = [part * tile_dev // 2] * slabs + [0] * (len(more) - slabs)
         sums_so_far = call(
             functools.partial(more_kernel, starts),

time: 64.8 us -> 69.2 us (1.068)
  waiting for transfers between devices: 30.1 us -> 34.9 us
  other arithmetic: 2.04 us -> 0 us
  starting transfers between devices: 19.8 us -> 21.2 us
    ppermute x13 -> x16, waiting for transfers between devices: 5.04 us -> 8.17 us  [across(): return lax.ppermute(array, 'pair', [(i, i ^ bits) for i in range(n_pair)])]
    ppermute x13 -> x16, starting transfers between devices: 9.92 us -> 12.2 us  [across(): return lax.ppermute(array, 'pair', [(i, i ^ bits) for i in range(n_pair)])]
    ppermute x6, waiting for transfers between devices: 25 us -> 26.7 us  [along(): return lax.ppermute(array, 'vir', [(i, i ^ bits) for i in range(n_vir)])]
    concatenate x1 -> x0, other arithmetic: 1.29 us -> none  [local(): jnp.concatenate([ids, integrals.reshape(slabs, length, TILE)], axis=1)]
    ppermute x6, starting transfers between devices: 9.91 us -> 8.93 us  [along(): return lax.ppermute(array, 'vir', [(i, i ^ bits) for i in range(n_vir)])]
    convert_element_type x2 -> x0, other arithmetic: 0.73 us -> none  [the longest x1 0.73 us: local(): tile_blocks.transpose(0, 2, 1).reshape(1, 2 * slabs, tile_dev).astype(BF16)]
  transfers between devices with their start and end apart: 19 -> 22, of which waited for: 10 -> 9; matrix products, arithmetic and copies ran while one was open for 0% -> 0% of each run, Pallas kernels for 14% -> 13%
where the time goes in v14:
time: 69.2 us; the launch traced here: 69 us
  waiting for transfers between devices  34.9 us (50%)
  starting transfers between devices  21.2 us (31%)
  Pallas kernels  12.1 us (17%)
  local copies, waits for them, and re-layouts  0.7 us (1%)
    ppermute x6, waiting for transfers between devices, along(): return lax.ppermute(array, 'vir', [(i, i ^ bits) for i in range(n_vir)])  26.7 us
    ppermute x16, starting transfers between devices, across(): return lax.ppermute(array, 'pair', [(i, i ^ bits) for i in range(n_pair)])  12.2 us
    ppermute x6, starting transfers between devices, along(): return lax.ppermute(array, 'vir', [(i, i ^ bits) for i in range(n_vir)])  8.93 us
    ppermute x16, waiting for transfers between devices, across(): return lax.ppermute(array, 'pair', [(i, i ^ bits) for i in range(n_pair)])  8.17 us
    pallas_call x1, Pallas kernels, local(): call(functools.partial(first_kernel, n_vir, len(early)), [jax.ShapeDtypeS...  7.25 us
    pallas_call x2, Pallas kernels, local(): call(functools.partial(more_kernel, starts), [sums, sums], [VMEM] * (3 +...  2.69 us
  transfers between devices with their start and end apart: 22, of which 9 were waited for; matrix products, arithmetic and copies ran while one was open for 0% of the time, Pallas kernels for 13%

profile of v14, /device:TPU:0, one launch (start us, length us, event | category | flops | bytes accessed | tf_op | source)
XLA Modules:
  0.0 69.0 jit_solution(15448533853997381098)
XLA Ops:
  0.0 3.0 %collective-permute-start.8 = (bf16[2,2048,128]{2,1,0:T(8,128)(2,1)}, bf16[2,2048,128]{2,1,0:T(8,128)(2,1)S(1)}, u32[]{:S(2)}, u32[]{:S(2)}) collective-permute-start(bf16[2,2048,128]{2,1,0:T(8,128)(2,1)} %bitcast.7), channel_id=1, source_target_pairs={{0,16},{4,20},{8,24},{12,28},{16,0},{20,4},{24,8},{28,12},{1,17},{... | collective-permute-start | bytes 3145736 | tf_op jit(solution)/shard_map/ppermute | solution.py:173
  3.0 1.5 %collective-permute-start.7 = (bf16[2,2048,128]{2,1,0:T(8,128)(2,1)}, bf16[2,2048,128]{2,1,0:T(8,128)(2,1)S(1)}, u32[]{:S(2)}, u32[]{:S(2)}) collective-permute-start(bf16[2,2048,128]{2,1,0:T(8,128)(2,1)} %bitcast.8), channel_id=1, source_target_pairs={{0,8},{4,12},{8,0},{12,4},{16,24},{20,28},{24,16},{28,20},{1,9},{5... | collective-permute-start | bytes 3145736 | tf_op jit(solution)/shard_map/ppermute | solution.py:173
  4.5 2.6 %collective-permute-start.1 = (bf16[256,512]{1,0:T(8,128)(2,1)}, bf16[256,512]{1,0:T(8,128)(2,1)S(1)}, u32[]{:S(2)}, u32[]{:S(2)}) collective-permute-start(bf16[256,512]{1,0:T(8,128)(2,1)} %refs_0_.1), channel_id=1, source_target_pairs={{0,2},{1,3},{2,0},{3,1},{4,6},{5,7},{6,4},{7,5},{8,10},{9,11},{10,... | collective-permute-start | bytes 786440 | tf_op jit(solution)/shard_map/ppermute | solution.py:176
  7.0 1.6 %collective-permute-start = (bf16[256,512]{1,0:T(8,128)(2,1)}, bf16[256,512]{1,0:T(8,128)(2,1)S(1)}, u32[]{:S(2)}, u32[]{:S(2)}) collective-permute-start(bf16[256,512]{1,0:T(8,128)(2,1)} %refs_0_.1), channel_id=1, source_target_pairs={{0,1},{1,0},{2,3},{3,2},{4,5},{5,4},{6,7},{7,6},{8,9},{9,8},{10,11... | collective-permute-start | bytes 786440 | tf_op jit(solution)/shard_map/ppermute | solution.py:176
  8.6 10.2 %collective-permute-done.1.refs_2_.refs_5_ = bf16[256,512]{1,0:T(8,128)(2,1)S(1)} collective-permute-done((bf16[256,512]{1,0:T(8,128)(2,1)}, bf16[256,512]{1,0:T(8,128)(2,1)S(1)}, u32[]{:S(2)}, u32[]{:S(2)}) %collective-permute-start.1) | collective-permute-done | bytes 262176 | tf_op jit(solution)/shard_map/ppermute | solution.py:176
  18.8 0.7 collective-permute-start.2
  19.7 0.6 collective-permute-done.5.refs_0_.refs_6_.refs_2_
  20.5 7.0 %collective-permute-done.2.refs_3_.refs_6_ = bf16[256,512]{1,0:T(8,128)(2,1)S(1)} collective-permute-done((bf16[256,512]{1,0:T(8,128)(2,1)S(1)}, bf16[256,512]{1,0:T(8,128)(2,1)S(1)}, u32[]{:S(2)}, u32[]{:S(2)}) %collective-permute-start.2) | collective-permute-done | bytes 262176 | tf_op jit(solution)/shard_map/ppermute | solution.py:176
  27.5 0.7 copy-done.2
  28.7 1.6 %collective-permute-start.10 = (s32[2,2,16]{2,1,0:T(2,128)S(1)}, s32[2,2,16]{2,1,0:T(2,128)S(1)}, u32[]{:S(2)}, u32[]{:S(2)}) collective-permute-start(s32[2,2,16]{2,1,0:T(2,128)S(1)} %shard_map.46), channel_id=1, source_target_pairs={{0,16},{4,20},{8,24},{12,28},{16,0},{20,4},{24,8},{28,12},{1,17},{... | collective-permute-start | bytes 776 | tf_op jit(solution)/shard_map/ppermute | solution.py:173
  30.3 2.5 %collective-permute-done.11.refs_9_ = s32[2,2,16]{2,1,0:T(2,128)S(1)} collective-permute-done((s32[2,2,16]{2,1,0:T(2,128)S(1)}, s32[2,2,16]{2,1,0:T(2,128)S(1)}, u32[]{:S(2)}, u32[]{:S(2)}) %collective-permute-start.11) | collective-permute-done | bytes 288 | tf_op jit(solution)/shard_map/ppermute | solution.py:173
  33.3 3.0 %collective-permute-done.9.refs_12_.refs_7_ = s32[2,2,16]{2,1,0:T(2,128)S(1)} collective-permute-done((s32[2,2,16]{2,1,0:T(2,128)S(1)}, s32[2,2,16]{2,1,0:T(2,128)S(1)}, u32[]{:S(2)}, u32[]{:S(2)}) %collective-permute-start.9) | collective-permute-done | bytes 288 | tf_op jit(solution)/shard_map/ppermute | solution.py:173
  37.5 1.6 %collective-permute-start.14 = (bf16[1024,128]{1,0:T(8,128)(2,1)S(1)}, bf16[1024,128]{1,0:T(8,128)(2,1)S(1)}, u32[]{:S(2)}, u32[]{:S(2)}) collective-permute-start(bf16[1024,128]{1,0:T(8,128)(2,1)S(1)} %get-tuple-element.32), channel_id=1, source_target_pairs={{0,16},{4,20},{8,24},{12,28},{16,0},{20,4},{24,8},{28,12},{1,17},{... | collective-permute-start | bytes 786440 | tf_op jit(solution)/shard_map/ppermute | solution.py:173
  39.1 1.5 %collective-permute-start.15 = (bf16[1024,128]{1,0:T(8,128)(2,1)S(1)}, bf16[1024,128]{1,0:T(8,128)(2,1)S(1)}, u32[]{:S(2)}, u32[]{:S(2)}) collective-permute-start(bf16[1024,128]{1,0:T(8,128)(2,1)S(1)} %get-tuple-element.33), channel_id=1, source_target_pairs={{0,8},{4,12},{8,0},{12,4},{16,24},{20,28},{24,16},{28,20},{1,9},{5... | collective-permute-start | bytes 786440 | tf_op jit(solution)/shard_map/ppermute | solution.py:173
  40.6 7.3 %shard_map.47 = (bf16[16,512,128]{2,1,0:T(8,128)(2,1)S(1)}, bf16[256,256]{1,0:T(8,128)(2,1)S(1)}, f32[16,256,128]{2,1,0:T(8,128)S(1)}, f32[16,256,128]{2,1,0:T(8,128)S(1)}) custom-call(bf16[256,512]{1,0:T(8,128)(2,1)S(1)} %copy-done.1, bf16[256,512]{1,0:T(8,128)(2,1)S(1)} %collective-permute-done.refs_1_.refs_4_, ...), custom_call_target="tpu_custom_call" | custom-call | tf_op jit(solution)/shard_map/pallas_call | solution.py:214
  47.9 1.3 %shard_map.49 = (f32[16,256,128]{2,1,0:T(8,128)S(1)}, f32[16,256,128]{2,1,0:T(8,128)S(1)}) custom-call(bf16[16,512,128]{2,1,0:T(8,128)(2,1)S(1)} %get-tuple-element.25.refs_0_, f32[16,256,128]{2,1,0:T(8,128)S(1)} %get-tuple-element.26.refs_1_, f32[16,256,128]{2,1,0:T(8,128)S(1)} %get-tuple-element.27.refs_2_, ...), custom_call_target="tpu_custom_call", output_to_operand_aliasing={{0}: (1, {}), {1}: (2, {})} | custom-call | tf_op jit(solution)/shard_map/pallas_call | solution.py:229
  49.2 1.3 %shard_map.50 = (f32[16,256,128]{2,1,0:T(8,128)S(1)}, f32[16,256,128]{2,1,0:T(8,128)S(1)}) custom-call(bf16[16,512,128]{2,1,0:T(8,128)(2,1)S(1)} %get-tuple-element.25.refs_0_, f32[16,256,128]{2,1,0:T(8,128)S(1)} %get-tuple-element.30.refs_1_, f32[16,256,128]{2,1,0:T(8,128)S(1)} %get-tuple-element.31.refs_2_, ...), custom_call_target="tpu_custom_call", output_to_operand_aliasing={{0}: (1, {}), {1}: (2, {})} | custom-call | tf_op jit(solution)/shard_map/pallas_call | solution.py:229
  51.8 0.6 collective-permute-done.18.come_ref
  52.6 2.3 %collective-permute-start.19 = (bf16[2,256,128]{2,1,0:T(8,128)(2,1)S(1)}, bf16[2,256,128]{2,1,0:T(8,128)(2,1)S(1)}, u32[]{:S(2)}, u32[]{:S(2)}) collective-permute-start(bf16[2,256,128]{2,1,0:T(8,128)(2,1)S(1)} %get-tuple-element.42), channel_id=1, source_target_pairs={{0,2},{1,3},{2,0},{3,1},{4,6},{5,7},{6,4},{7,5},{8,10},{9,11},{10,... | collective-permute-start | bytes 393224 | tf_op jit(solution)/shard_map/ppermute | solution.py:176
  54.8 1.3 %collective-permute-start.20 = (bf16[2,256,128]{2,1,0:T(8,128)(2,1)S(1)}, bf16[2,256,128]{2,1,0:T(8,128)(2,1)S(1)}, u32[]{:S(2)}, u32[]{:S(2)}) collective-permute-start(bf16[2,256,128]{2,1,0:T(8,128)(2,1)S(1)} %get-tuple-element.43), channel_id=1, source_target_pairs={{0,3},{1,2},{2,1},{3,0},{4,7},{5,6},{6,5},{7,4},{8,11},{9,10},{10,... | collective-permute-start | bytes 393224 | tf_op jit(solution)/shard_map/ppermute | solution.py:176
  56.7 8.8 %collective-permute-done.19.refs_2_ = bf16[2,256,128]{2,1,0:T(8,128)(2,1)S(1)} collective-permute-done((bf16[2,256,128]{2,1,0:T(8,128)(2,1)S(1)}, bf16[2,256,128]{2,1,0:T(8,128)(2,1)S(1)}, u32[]{:S(2)}, u32[]{:S(2)}) %collective-permute-start.19) | collective-permute-done | bytes 131104 | tf_op jit(solution)/shard_map/ppermute | solution.py:176
  65.5 0.7 %collective-permute-done.17.refs_1_ = bf16[2,256,128]{2,1,0:T(8,128)(2,1)S(1)} collective-permute-done((bf16[2,256,128]{2,1,0:T(8,128)(2,1)S(1)}, bf16[2,256,128]{2,1,0:T(8,128)(2,1)S(1)}, u32[]{:S(2)}, u32[]{:S(2)}) %collective-permute-start.17) | collective-permute-done | bytes 131104 | tf_op jit(solution)/shard_map/ppermute | solution.py:176
  66.4 1.3 %collective-permute-done.21.other_ref = bf16[2,256,128]{2,1,0:T(8,128)(2,1)S(1)} collective-permute-done((bf16[2,256,128]{2,1,0:T(8,128)(2,1)S(1)}, bf16[2,256,128]{2,1,0:T(8,128)(2,1)S(1)}, u32[]{:S(2)}, u32[]{:S(2)}) %collective-permute-start.21) | collective-permute-done | bytes 131104 | tf_op jit(solution)/shard_map/ppermute | solution.py:173
  67.7 1.3 %shard_map.56 = bf16[256,512]{1,0:T(8,128)(2,1)} custom-call(bf16[2,256,128]{2,1,0:T(8,128)(2,1)S(1)} %shard_map.55.own_ref, bf16[2,256,128]{2,1,0:T(8,128)(2,1)S(1)} %collective-permute-done.21.other_ref, bf16[256,256]{1,0:T(8,128)(2,1)S(1)} %get-tuple-element.44.hot_ref), custom_call_target="tpu_custom_call" | custom-call | tf_op jit(solution)/shard_map/pallas_call | solution.py:247
  (42 shorter events, 4.6 us)
Async XLA Ops:
  0.0 36.4 %collective-permute-start.8 = (bf16[2,2048,128]{2,1,0:T(8,128)(2,1)}, bf16[2,2048,128]{2,1,0:T(8,128)(2,1)S(1)}, u32[]{:S(2)}, u32[]{:S(2)}) collective-permute-start(bf16[2,2048,128]{2,1,0:T(8,128)(2,1)} %bitcast.7), channel_id=1, source_target_pairs={{0,16},{4,20},{8,24},{12,28},{16,0},{20,4},{24,8},{28,12},{1,17},{... | collective-permute-start | bytes 3145736 | tf_op jit(solution)/shard_map/ppermute | solution.py:173
  3.0 33.4 %collective-permute-start.7 = (bf16[2,2048,128]{2,1,0:T(8,128)(2,1)}, bf16[2,2048,128]{2,1,0:T(8,128)(2,1)S(1)}, u32[]{:S(2)}, u32[]{:S(2)}) collective-permute-start(bf16[2,2048,128]{2,1,0:T(8,128)(2,1)} %bitcast.8), channel_id=1, source_target_pairs={{0,8},{4,12},{8,0},{12,4},{16,24},{20,28},{24,16},{28,20},{1,9},{5... | collective-permute-start | bytes 3145736 | tf_op jit(solution)/shard_map/ppermute | solution.py:173
  4.5 14.3 %collective-permute-start.1 = (bf16[256,512]{1,0:T(8,128)(2,1)}, bf16[256,512]{1,0:T(8,128)(2,1)S(1)}, u32[]{:S(2)}, u32[]{:S(2)}) collective-permute-start(bf16[256,512]{1,0:T(8,128)(2,1)} %refs_0_.1), channel_id=1, source_target_pairs={{0,2},{1,3},{2,0},{3,1},{4,6},{5,7},{6,4},{7,5},{8,10},{9,11},{10,... | collective-permute-start | bytes 786440 | tf_op jit(solution)/shard_map/ppermute | solution.py:176
  7.0 12.4 %collective-permute-start = (bf16[256,512]{1,0:T(8,128)(2,1)}, bf16[256,512]{1,0:T(8,128)(2,1)S(1)}, u32[]{:S(2)}, u32[]{:S(2)}) collective-permute-start(bf16[256,512]{1,0:T(8,128)(2,1)} %refs_0_.1), channel_id=1, source_target_pairs={{0,1},{1,0},{2,3},{3,2},{4,5},{5,4},{6,7},{7,6},{8,9},{9,8},{10,11... | collective-permute-start | bytes 786440 | tf_op jit(solution)/shard_map/ppermute | solution.py:176
  18.8 1.5 %collective-permute-start.5 = (bf16[256,512]{1,0:T(8,128)(2,1)S(1)}, bf16[256,512]{1,0:T(8,128)(2,1)S(1)}, u32[]{:S(2)}, u32[]{:S(2)}) collective-permute-start(bf16[256,512]{1,0:T(8,128)(2,1)S(1)} %collective-permute-done.1.refs_2_.refs_5_), channel_id=1, source_target_pairs={{0,4},{4,0},{8,12},{12,8},{16,20},{20,16},{24,28},{28,24},{1,5},{5... | collective-permute-start | bytes 786440 | tf_op jit(solution)/shard_map/ppermute | solution.py:173
  18.8 8.7 %collective-permute-start.2 = (bf16[256,512]{1,0:T(8,128)(2,1)S(1)}, bf16[256,512]{1,0:T(8,128)(2,1)S(1)}, u32[]{:S(2)}, u32[]{:S(2)}) collective-permute-start(bf16[256,512]{1,0:T(8,128)(2,1)S(1)} %collective-permute-done.1.refs_2_.refs_5_), channel_id=1, source_target_pairs={{0,1},{1,0},{2,3},{3,2},{4,5},{5,4},{6,7},{7,6},{8,9},{9,8},{10,11... | collective-permute-start | bytes 786440 | tf_op jit(solution)/shard_map/ppermute | solution.py:176
  19.5 8.0 %collective-permute-start.4 = (bf16[256,512]{1,0:T(8,128)(2,1)S(1)}, bf16[256,512]{1,0:T(8,128)(2,1)S(1)}, u32[]{:S(2)}, u32[]{:S(2)}) collective-permute-start(bf16[256,512]{1,0:T(8,128)(2,1)S(1)} %collective-permute-done.refs_1_.refs_4_), channel_id=1, source_target_pairs={{0,4},{4,0},{8,12},{12,8},{16,20},{20,16},{24,28},{28,24},{1,5},{5... | collective-permute-start | bytes 786440 | tf_op jit(solution)/shard_map/ppermute | solution.py:173
  20.3 8.4 %collective-permute-start.3 = (bf16[256,512]{1,0:T(8,128)(2,1)}, bf16[256,512]{1,0:T(8,128)(2,1)S(1)}, u32[]{:S(2)}, u32[]{:S(2)}) collective-permute-start(bf16[256,512]{1,0:T(8,128)(2,1)} %refs_0_.1), channel_id=1, source_target_pairs={{0,4},{4,0},{8,12},{12,8},{16,20},{20,16},{24,28},{28,24},{1,5},{5... | collective-permute-start | bytes 786440 | tf_op jit(solution)/shard_map/ppermute | solution.py:173
  27.5 8.9 %collective-permute-start.6 = (bf16[256,512]{1,0:T(8,128)(2,1)S(1)}, bf16[256,512]{1,0:T(8,128)(2,1)S(1)}, u32[]{:S(2)}, u32[]{:S(2)}) collective-permute-start(bf16[256,512]{1,0:T(8,128)(2,1)S(1)} %collective-permute-done.2.refs_3_.refs_6_), channel_id=1, source_target_pairs={{0,4},{4,0},{8,12},{12,8},{16,20},{20,16},{24,28},{28,24},{1,5},{5... | collective-permute-start | bytes 786440 | tf_op jit(solution)/shard_map/ppermute | solution.py:173
  28.2 12.4 %copy-start.3 = (s32[2,16,2]{1,2,0:T(2,128)S(1)}, s32[2,16,2]{1,2,0:T(2,128)}, u32[]{:S(2)}) copy-start(s32[2,16,2]{1,2,0:T(2,128)} %param.6) | copy-start | bytes 772
  28.2 12.4 %copy-start.4 = (s32[256]{0:T(256)S(1)}, s32[256]{0:T(256)}, u32[]{:S(2)}) copy-start(s32[256]{0:T(256)} %param.7) | copy-start | bytes 3076
  28.2 4.5 %collective-permute-start.11 = (s32[2,2,16]{2,1,0:T(2,128)S(1)}, s32[2,2,16]{2,1,0:T(2,128)S(1)}, u32[]{:S(2)}, u32[]{:S(2)}) collective-permute-start(s32[2,2,16]{2,1,0:T(2,128)S(1)} %shard_map.46), channel_id=1, source_target_pairs={{0,24},{4,28},{8,16},{12,20},{16,8},{20,12},{24,0},{28,4},{1,25},{... | collective-permute-start | bytes 776 | tf_op jit(solution)/shard_map/ppermute | solution.py:173
  28.7 4.6 %collective-permute-start.10 = (s32[2,2,16]{2,1,0:T(2,128)S(1)}, s32[2,2,16]{2,1,0:T(2,128)S(1)}, u32[]{:S(2)}, u32[]{:S(2)}) collective-permute-start(s32[2,2,16]{2,1,0:T(2,128)S(1)} %shard_map.46), channel_id=1, source_target_pairs={{0,16},{4,20},{8,24},{12,28},{16,0},{20,4},{24,8},{28,12},{1,17},{... | collective-permute-start | bytes 776 | tf_op jit(solution)/shard_map/ppermute | solution.py:173
  32.8 3.6 %collective-permute-start.9 = (s32[2,2,16]{2,1,0:T(2,128)S(1)}, s32[2,2,16]{2,1,0:T(2,128)S(1)}, u32[]{:S(2)}, u32[]{:S(2)}) collective-permute-start(s32[2,2,16]{2,1,0:T(2,128)S(1)} %shard_map.46), channel_id=1, source_target_pairs={{0,8},{4,12},{8,0},{12,4},{16,24},{20,28},{24,16},{28,20},{1,9},{5... | collective-permute-start | bytes 776 | tf_op jit(solution)/shard_map/ppermute | solution.py:173
  36.4 11.4 %collective-permute-start.12 = (bf16[1024,128]{1,0:T(8,128)(2,1)S(1)}, bf16[1024,128]{1,0:T(8,128)(2,1)S(1)}, u32[]{:S(2)}, u32[]{:S(2)}) collective-permute-start(bf16[1024,128]{1,0:T(8,128)(2,1)S(1)} %get-tuple-element.28), channel_id=1, source_target_pairs={{0,16},{4,20},{8,24},{12,28},{16,0},{20,4},{24,8},{28,12},{1,17},{... | collective-permute-start | bytes 786440 | tf_op jit(solution)/shard_map/ppermute | solution.py:173
  37.0 10.8 %collective-permute-start.13 = (bf16[1024,128]{1,0:T(8,128)(2,1)S(1)}, bf16[1024,128]{1,0:T(8,128)(2,1)S(1)}, u32[]{:S(2)}, u32[]{:S(2)}) collective-permute-start(bf16[1024,128]{1,0:T(8,128)(2,1)S(1)} %get-tuple-element.29), channel_id=1, source_target_pairs={{0,8},{4,12},{8,0},{12,4},{16,24},{20,28},{24,16},{28,20},{1,9},{5... | collective-permute-start | bytes 786440 | tf_op jit(solution)/shard_map/ppermute | solution.py:173
  37.5 11.7 %collective-permute-start.14 = (bf16[1024,128]{1,0:T(8,128)(2,1)S(1)}, bf16[1024,128]{1,0:T(8,128)(2,1)S(1)}, u32[]{:S(2)}, u32[]{:S(2)}) collective-permute-start(bf16[1024,128]{1,0:T(8,128)(2,1)S(1)} %get-tuple-element.32), channel_id=1, source_target_pairs={{0,16},{4,20},{8,24},{12,28},{16,0},{20,4},{24,8},{28,12},{1,17},{... | collective-permute-start | bytes 786440 | tf_op jit(solution)/shard_map/ppermute | solution.py:173
  39.1 10.2 %collective-permute-start.15 = (bf16[1024,128]{1,0:T(8,128)(2,1)S(1)}, bf16[1024,128]{1,0:T(8,128)(2,1)S(1)}, u32[]{:S(2)}, u32[]{:S(2)}) collective-permute-start(bf16[1024,128]{1,0:T(8,128)(2,1)S(1)} %get-tuple-element.33), channel_id=1, source_target_pairs={{0,8},{4,12},{8,0},{12,4},{16,24},{20,28},{24,16},{28,20},{1,9},{5... | collective-permute-start | bytes 786440 | tf_op jit(solution)/shard_map/ppermute | solution.py:173
  50.9 1.6 %collective-permute-start.18 = (bf16[2,2,256,128]{3,2,1,0:T(8,128)(2,1)S(1)}, bf16[2,2,256,128]{3,2,1,0:T(8,128)(2,1)S(1)}, u32[]{:S(2)}, u32[]{:S(2)}) collective-permute-start(bf16[2,2,256,128]{3,2,1,0:T(8,128)(2,1)S(1)} %get-tuple-element.41), channel_id=1, source_target_pairs={{0,4},{4,0},{8,12},{12,8},{16,20},{20,16},{24,28},{28,24},{1,5},{5... | collective-permute-start | bytes 786440 | tf_op jit(solution)/shard_map/ppermute | solution.py:173
  51.3 4.8 %collective-permute-start.16 = (bf16[2,2,256,128]{3,2,1,0:T(8,128)(2,1)S(1)}, bf16[2,2,256,128]{3,2,1,0:T(8,128)(2,1)S(1)}, u32[]{:S(2)}, u32[]{:S(2)}) collective-permute-start(bf16[2,2,256,128]{3,2,1,0:T(8,128)(2,1)S(1)} %get-tuple-element.37), channel_id=1, source_target_pairs={{0,4},{4,0},{8,12},{12,8},{16,20},{20,16},{24,28},{28,24},{1,5},{5... | collective-permute-start | bytes 786440 | tf_op jit(solution)/shard_map/ppermute | solution.py:173
  52.6 13.0 %collective-permute-start.19 = (bf16[2,256,128]{2,1,0:T(8,128)(2,1)S(1)}, bf16[2,256,128]{2,1,0:T(8,128)(2,1)S(1)}, u32[]{:S(2)}, u32[]{:S(2)}) collective-permute-start(bf16[2,256,128]{2,1,0:T(8,128)(2,1)S(1)} %get-tuple-element.42), channel_id=1, source_target_pairs={{0,2},{1,3},{2,0},{3,1},{4,6},{5,7},{6,4},{7,5},{8,10},{9,11},{10,... | collective-permute-start | bytes 393224 | tf_op jit(solution)/shard_map/ppermute | solution.py:176
  54.8 10.7 %collective-permute-start.20 = (bf16[2,256,128]{2,1,0:T(8,128)(2,1)S(1)}, bf16[2,256,128]{2,1,0:T(8,128)(2,1)S(1)}, u32[]{:S(2)}, u32[]{:S(2)}) collective-permute-start(bf16[2,256,128]{2,1,0:T(8,128)(2,1)S(1)} %get-tuple-element.43), channel_id=1, source_target_pairs={{0,3},{1,2},{2,1},{3,0},{4,7},{5,6},{6,5},{7,4},{8,11},{9,10},{10,... | collective-permute-start | bytes 393224 | tf_op jit(solution)/shard_map/ppermute | solution.py:176
  56.1 10.1 %collective-permute-start.17 = (bf16[2,256,128]{2,1,0:T(8,128)(2,1)S(1)}, bf16[2,256,128]{2,1,0:T(8,128)(2,1)S(1)}, u32[]{:S(2)}, u32[]{:S(2)}) collective-permute-start(bf16[2,256,128]{2,1,0:T(8,128)(2,1)S(1)} %get-tuple-element.39), channel_id=1, source_target_pairs={{0,1},{1,0},{2,3},{3,2},{4,5},{5,4},{6,7},{7,6},{8,9},{9,8},{10,11... | collective-permute-start | bytes 393224 | tf_op jit(solution)/shard_map/ppermute | solution.py:176
  66.3 1.4 %collective-permute-start.21 = (bf16[2,256,128]{2,1,0:T(8,128)(2,1)S(1)}, bf16[2,256,128]{2,1,0:T(8,128)(2,1)S(1)}, u32[]{:S(2)}, u32[]{:S(2)}) collective-permute-start(bf16[2,256,128]{2,1,0:T(8,128)(2,1)S(1)} %shard_map.55.own_ref), channel_id=1, source_target_pairs={{0,4},{4,0},{8,12},{12,8},{16,20},{20,16},{24,28},{28,24},{1,5},{5... | collective-permute-start | bytes 393224 | tf_op jit(solution)/shard_map/ppermute | solution.py:173
  (3 other events, 25.4 us)

commit v15 on v14

--- a/solution.py
+++ b/solution.py
@@ -187,9 +187,9 @@
     others = [across(piece, 1) for piece in mine]
     ids = tile_blocks.transpose(0, 2, 1)
     anywhere = pl.BlockSpec(memory_space=pl.ANY)
-    first = [others[n_vir // 2], others[1]]
+    first = [pieces[n_vir // 2]]
     held = call(
-        copy_kernel, jax.ShapeDtypeStruct(ids.shape, ids.dtype), [VMEM, anywhere, anywhere], megabytes=4
+        copy_kernel, jax.ShapeDtypeStruct(ids.shape, ids.dtype), [VMEM, anywhere], megabytes=4
     )(ids, *first)
     blocks = [ids] + [across(held, 2 * d) for d in range(1, chips)]
     first = [*others, *mine[1:], *blocks[1:]]

time: 69.2 us -> 68.8 us (level)
  waiting for transfers between devices: 34.9 us -> 32.7 us
  starting transfers between devices: 21.2 us -> 22.7 us
    ppermute x6, waiting for transfers between devices: 26.7 us -> 19.4 us  [along(): return lax.ppermute(array, 'vir', [(i, i ^ bits) for i in range(n_vir)])]
    ppermute x16, waiting for transfers between devices: 8.17 us -> 13.3 us  [across(): return lax.ppermute(array, 'pair', [(i, i ^ bits) for i in range(n_pair)])]
    ppermute x16, starting transfers between devices: 12.2 us -> 13.6 us  [across(): return lax.ppermute(array, 'pair', [(i, i ^ bits) for i in range(n_pair)])]
  transfers between devices with their start and end apart: 22 -> 22, of which waited for: 9 -> 11; matrix products, arithmetic and copies ran while one was open for 0% -> 0% of each run, Pallas kernels for 13% -> 13%
where the time goes in v15:
time: 68.8 us; the launch traced here: 68.4 us
  waiting for transfers between devices  32.7 us (48%)
  starting transfers between devices  22.7 us (33%)
  Pallas kernels  12.1 us (18%)
  local copies, waits for them, and re-layouts  0.7 us (1%)
    ppermute x6, waiting for transfers between devices, along(): return lax.ppermute(array, 'vir', [(i, i ^ bits) for i in range(n_vir)])  19.4 us
    ppermute x16, starting transfers between devices, across(): return lax.ppermute(array, 'pair', [(i, i ^ bits) for i in range(n_pair)])  13.6 us
    ppermute x16, waiting for transfers between devices, across(): return lax.ppermute(array, 'pair', [(i, i ^ bits) for i in range(n_pair)])  13.3 us
    ppermute x6, starting transfers between devices, along(): return lax.ppermute(array, 'vir', [(i, i ^ bits) for i in range(n_vir)])  9.13 us
    pallas_call x1, Pallas kernels, local(): call(functools.partial(first_kernel, n_vir, len(early)), [jax.ShapeDtypeS...  7.25 us
    pallas_call x2, Pallas kernels, local(): call(functools.partial(more_kernel, starts), [sums, sums], [VMEM] * (3 +...  2.68 us
  transfers between devices with their start and end apart: 22, of which 11 were waited for; matrix products, arithmetic and copies ran while one was open for 0% of the time, Pallas kernels for 13%

profile of v15, /device:TPU:0, one launch (start us, length us, event | category | flops | bytes accessed | tf_op | source)
XLA Modules:
  0.0 68.4 jit_solution(16980687976874457360)
XLA Ops:
  0.0 3.0 %collective-permute-start.8 = (bf16[2,2048,128]{2,1,0:T(8,128)(2,1)}, bf16[2,2048,128]{2,1,0:T(8,128)(2,1)S(1)}, u32[]{:S(2)}, u32[]{:S(2)}) collective-permute-start(bf16[2,2048,128]{2,1,0:T(8,128)(2,1)} %bitcast.7), channel_id=1, source_target_pairs={{0,16},{4,20},{8,24},{12,28},{16,0},{20,4},{24,8},{28,12},{1,17},{... | collective-permute-start | bytes 3145736 | tf_op jit(solution)/shard_map/ppermute | solution.py:173
  3.0 1.5 %collective-permute-start.7 = (bf16[2,2048,128]{2,1,0:T(8,128)(2,1)}, bf16[2,2048,128]{2,1,0:T(8,128)(2,1)S(1)}, u32[]{:S(2)}, u32[]{:S(2)}) collective-permute-start(bf16[2,2048,128]{2,1,0:T(8,128)(2,1)} %bitcast.8), channel_id=1, source_target_pairs={{0,8},{4,12},{8,0},{12,4},{16,24},{20,28},{24,16},{28,20},{1,9},{5... | collective-permute-start | bytes 3145736 | tf_op jit(solution)/shard_map/ppermute | solution.py:173
  4.5 2.6 %collective-permute-start.1 = (bf16[256,512]{1,0:T(8,128)(2,1)}, bf16[256,512]{1,0:T(8,128)(2,1)S(1)}, u32[]{:S(2)}, u32[]{:S(2)}) collective-permute-start(bf16[256,512]{1,0:T(8,128)(2,1)} %refs_0_.1), channel_id=1, source_target_pairs={{0,2},{1,3},{2,0},{3,1},{4,6},{5,7},{6,4},{7,5},{8,10},{9,11},{10,... | collective-permute-start | bytes 786440 | tf_op jit(solution)/shard_map/ppermute | solution.py:176
  7.0 1.6 %collective-permute-start = (bf16[256,512]{1,0:T(8,128)(2,1)}, bf16[256,512]{1,0:T(8,128)(2,1)S(1)}, u32[]{:S(2)}, u32[]{:S(2)}) collective-permute-start(bf16[256,512]{1,0:T(8,128)(2,1)} %refs_0_.1), channel_id=1, source_target_pairs={{0,1},{1,0},{2,3},{3,2},{4,5},{5,4},{6,7},{7,6},{8,9},{9,8},{10,11... | collective-permute-start | bytes 786440 | tf_op jit(solution)/shard_map/ppermute | solution.py:176
  8.6 10.1 %collective-permute-done.1.refs_0_.refs_2_.refs_5_ = bf16[256,512]{1,0:T(8,128)(2,1)S(1)} collective-permute-done((bf16[256,512]{1,0:T(8,128)(2,1)}, bf16[256,512]{1,0:T(8,128)(2,1)S(1)}, u32[]{:S(2)}, u32[]{:S(2)}) %collective-permute-start.1) | collective-permute-done | bytes 262176 | tf_op jit(solution)/shard_map/ppermute | solution.py:176
  18.8 0.7 collective-permute-start.2
  19.5 0.7 copy-done.2
  20.7 1.5 %collective-permute-start.10 = (s32[2,2,16]{2,1,0:T(2,128)S(1)}, s32[2,2,16]{2,1,0:T(2,128)S(1)}, u32[]{:S(2)}, u32[]{:S(2)}) collective-permute-start(s32[2,2,16]{2,1,0:T(2,128)S(1)} %shard_map.46), channel_id=1, source_target_pairs={{0,16},{4,20},{8,24},{12,28},{16,0},{20,4},{24,8},{28,12},{1,17},{... | collective-permute-start | bytes 776 | tf_op jit(solution)/shard_map/ppermute | solution.py:173
  22.2 5.3 %collective-permute-done.11.refs_9_ = s32[2,2,16]{2,1,0:T(2,128)S(1)} collective-permute-done((s32[2,2,16]{2,1,0:T(2,128)S(1)}, s32[2,2,16]{2,1,0:T(2,128)S(1)}, u32[]{:S(2)}, u32[]{:S(2)}) %collective-permute-start.11) | collective-permute-done | bytes 288 | tf_op jit(solution)/shard_map/ppermute | solution.py:173
  27.6 1.7 %collective-permute-start.9 = (s32[2,2,16]{2,1,0:T(2,128)S(1)}, s32[2,2,16]{2,1,0:T(2,128)S(1)}, u32[]{:S(2)}, u32[]{:S(2)}) collective-permute-start(s32[2,2,16]{2,1,0:T(2,128)S(1)} %shard_map.46), channel_id=1, source_target_pairs={{0,8},{4,12},{8,0},{12,4},{16,24},{20,28},{24,16},{28,20},{1,9},{5... | collective-permute-start | bytes 776 | tf_op jit(solution)/shard_map/ppermute | solution.py:173
  29.3 1.9 %collective-permute-done.9.refs_12_.refs_7_ = s32[2,2,16]{2,1,0:T(2,128)S(1)} collective-permute-done((s32[2,2,16]{2,1,0:T(2,128)S(1)}, s32[2,2,16]{2,1,0:T(2,128)S(1)}, u32[]{:S(2)}, u32[]{:S(2)}) %collective-permute-start.9) | collective-permute-done | bytes 288 | tf_op jit(solution)/shard_map/ppermute | solution.py:173
  31.7 1.0 %collective-permute-done.4.refs_5_.refs_1_ = bf16[256,512]{1,0:T(8,128)(2,1)S(1)} collective-permute-done((bf16[256,512]{1,0:T(8,128)(2,1)S(1)}, bf16[256,512]{1,0:T(8,128)(2,1)S(1)}, u32[]{:S(2)}, u32[]{:S(2)}) %collective-permute-start.4) | collective-permute-done | bytes 262176 | tf_op jit(solution)/shard_map/ppermute | solution.py:173
  33.1 1.8 %collective-permute-start.12 = (bf16[1024,128]{1,0:T(8,128)(2,1)S(1)}, bf16[1024,128]{1,0:T(8,128)(2,1)S(1)}, u32[]{:S(2)}, u32[]{:S(2)}) collective-permute-start(bf16[1024,128]{1,0:T(8,128)(2,1)S(1)} %get-tuple-element.28), channel_id=1, source_target_pairs={{0,16},{4,20},{8,24},{12,28},{16,0},{20,4},{24,8},{28,12},{1,17},{... | collective-permute-start | bytes 786440 | tf_op jit(solution)/shard_map/ppermute | solution.py:173
  34.9 1.5 %collective-permute-start.13 = (bf16[1024,128]{1,0:T(8,128)(2,1)S(1)}, bf16[1024,128]{1,0:T(8,128)(2,1)S(1)}, u32[]{:S(2)}, u32[]{:S(2)}) collective-permute-start(bf16[1024,128]{1,0:T(8,128)(2,1)S(1)} %get-tuple-element.29), channel_id=1, source_target_pairs={{0,8},{4,12},{8,0},{12,4},{16,24},{20,28},{24,16},{28,20},{1,9},{5... | collective-permute-start | bytes 786440 | tf_op jit(solution)/shard_map/ppermute | solution.py:173
  37.3 7.3 %shard_map.47 = (bf16[16,512,128]{2,1,0:T(8,128)(2,1)S(1)}, bf16[256,256]{1,0:T(8,128)(2,1)S(1)}, f32[16,256,128]{2,1,0:T(8,128)S(1)}, f32[16,256,128]{2,1,0:T(8,128)S(1)}) custom-call(bf16[256,512]{1,0:T(8,128)(2,1)S(1)} %copy-done.1, bf16[256,512]{1,0:T(8,128)(2,1)S(1)} %collective-permute-done.refs_1_.refs_4_, ...), custom_call_target="tpu_custom_call" | custom-call | tf_op jit(solution)/shard_map/pallas_call | solution.py:214
  44.6 1.3 %shard_map.49 = (f32[16,256,128]{2,1,0:T(8,128)S(1)}, f32[16,256,128]{2,1,0:T(8,128)S(1)}) custom-call(bf16[16,512,128]{2,1,0:T(8,128)(2,1)S(1)} %get-tuple-element.25.refs_0_, f32[16,256,128]{2,1,0:T(8,128)S(1)} %get-tuple-element.26.refs_1_, f32[16,256,128]{2,1,0:T(8,128)S(1)} %get-tuple-element.27.refs_2_, ...), custom_call_target="tpu_custom_call", output_to_operand_aliasing={{0}: (1, {}), {1}: (2, {})} | custom-call | tf_op jit(solution)/shard_map/pallas_call | solution.py:229
  45.9 1.3 %collective-permute-done.14 = bf16[1024,128]{1,0:T(8,128)(2,1)S(1)} collective-permute-done((bf16[1024,128]{1,0:T(8,128)(2,1)S(1)}, bf16[1024,128]{1,0:T(8,128)(2,1)S(1)}, u32[]{:S(2)}, u32[]{:S(2)}) %collective-permute-start.14) | collective-permute-done | bytes 262176 | tf_op jit(solution)/shard_map/ppermute | solution.py:173
  47.2 1.5 %collective-permute-done.15 = bf16[1024,128]{1,0:T(8,128)(2,1)S(1)} collective-permute-done((bf16[1024,128]{1,0:T(8,128)(2,1)S(1)}, bf16[1024,128]{1,0:T(8,128)(2,1)S(1)}, u32[]{:S(2)}, u32[]{:S(2)}) %collective-permute-start.15) | collective-permute-done | bytes 262176 | tf_op jit(solution)/shard_map/ppermute | solution.py:173
  48.6 1.3 %shard_map.50 = (f32[16,256,128]{2,1,0:T(8,128)S(1)}, f32[16,256,128]{2,1,0:T(8,128)S(1)}) custom-call(bf16[16,512,128]{2,1,0:T(8,128)(2,1)S(1)} %get-tuple-element.25.refs_0_, f32[16,256,128]{2,1,0:T(8,128)S(1)} %get-tuple-element.30.refs_1_, f32[16,256,128]{2,1,0:T(8,128)S(1)} %get-tuple-element.31.refs_2_, ...), custom_call_target="tpu_custom_call", output_to_operand_aliasing={{0}: (1, {}), {1}: (2, {})} | custom-call | tf_op jit(solution)/shard_map/pallas_call | solution.py:229
  52.0 2.6 %collective-permute-start.19 = (bf16[2,256,128]{2,1,0:T(8,128)(2,1)S(1)}, bf16[2,256,128]{2,1,0:T(8,128)(2,1)S(1)}, u32[]{:S(2)}, u32[]{:S(2)}) collective-permute-start(bf16[2,256,128]{2,1,0:T(8,128)(2,1)S(1)} %get-tuple-element.42), channel_id=1, source_target_pairs={{0,2},{1,3},{2,0},{3,1},{4,6},{5,7},{6,4},{7,5},{8,10},{9,11},{10,... | collective-permute-start | bytes 393224 | tf_op jit(solution)/shard_map/ppermute | solution.py:176
  54.6 1.4 %collective-permute-start.20 = (bf16[2,256,128]{2,1,0:T(8,128)(2,1)S(1)}, bf16[2,256,128]{2,1,0:T(8,128)(2,1)S(1)}, u32[]{:S(2)}, u32[]{:S(2)}) collective-permute-start(bf16[2,256,128]{2,1,0:T(8,128)(2,1)S(1)} %get-tuple-element.43), channel_id=1, source_target_pairs={{0,3},{1,2},{2,1},{3,0},{4,7},{5,6},{6,5},{7,4},{8,11},{9,10},{10,... | collective-permute-start | bytes 393224 | tf_op jit(solution)/shard_map/ppermute | solution.py:176
  56.3 8.6 %collective-permute-done.19.refs_2_ = bf16[2,256,128]{2,1,0:T(8,128)(2,1)S(1)} collective-permute-done((bf16[2,256,128]{2,1,0:T(8,128)(2,1)S(1)}, bf16[2,256,128]{2,1,0:T(8,128)(2,1)S(1)}, u32[]{:S(2)}, u32[]{:S(2)}) %collective-permute-start.19) | collective-permute-done | bytes 131104 | tf_op jit(solution)/shard_map/ppermute | solution.py:176
  65.7 1.3 %collective-permute-done.21.other_ref = bf16[2,256,128]{2,1,0:T(8,128)(2,1)S(1)} collective-permute-done((bf16[2,256,128]{2,1,0:T(8,128)(2,1)S(1)}, bf16[2,256,128]{2,1,0:T(8,128)(2,1)S(1)}, u32[]{:S(2)}, u32[]{:S(2)}) %collective-permute-start.21) | collective-permute-done | bytes 131104 | tf_op jit(solution)/shard_map/ppermute | solution.py:173
  67.1 1.3 %shard_map.56 = bf16[256,512]{1,0:T(8,128)(2,1)} custom-call(bf16[2,256,128]{2,1,0:T(8,128)(2,1)S(1)} %shard_map.55.own_ref, bf16[2,256,128]{2,1,0:T(8,128)(2,1)S(1)} %collective-permute-done.21.other_ref, bf16[256,256]{1,0:T(8,128)(2,1)S(1)} %get-tuple-element.44.hot_ref), custom_call_target="tpu_custom_call" | custom-call | tf_op jit(solution)/shard_map/pallas_call | solution.py:247
  (42 shorter events, 5.4 us)
Async XLA Ops:
  0.0 33.1 %collective-permute-start.8 = (bf16[2,2048,128]{2,1,0:T(8,128)(2,1)}, bf16[2,2048,128]{2,1,0:T(8,128)(2,1)S(1)}, u32[]{:S(2)}, u32[]{:S(2)}) collective-permute-start(bf16[2,2048,128]{2,1,0:T(8,128)(2,1)} %bitcast.7), channel_id=1, source_target_pairs={{0,16},{4,20},{8,24},{12,28},{16,0},{20,4},{24,8},{28,12},{1,17},{... | collective-permute-start | bytes 3145736 | tf_op jit(solution)/shard_map/ppermute | solution.py:173
  3.0 30.1 %collective-permute-start.7 = (bf16[2,2048,128]{2,1,0:T(8,128)(2,1)}, bf16[2,2048,128]{2,1,0:T(8,128)(2,1)S(1)}, u32[]{:S(2)}, u32[]{:S(2)}) collective-permute-start(bf16[2,2048,128]{2,1,0:T(8,128)(2,1)} %bitcast.8), channel_id=1, source_target_pairs={{0,8},{4,12},{8,0},{12,4},{16,24},{20,28},{24,16},{28,20},{1,9},{5... | collective-permute-start | bytes 3145736 | tf_op jit(solution)/shard_map/ppermute | solution.py:173
  4.5 14.3 %collective-permute-start.1 = (bf16[256,512]{1,0:T(8,128)(2,1)}, bf16[256,512]{1,0:T(8,128)(2,1)S(1)}, u32[]{:S(2)}, u32[]{:S(2)}) collective-permute-start(bf16[256,512]{1,0:T(8,128)(2,1)} %refs_0_.1), channel_id=1, source_target_pairs={{0,2},{1,3},{2,0},{3,1},{4,6},{5,7},{6,4},{7,5},{8,10},{9,11},{10,... | collective-permute-start | bytes 786440 | tf_op jit(solution)/shard_map/ppermute | solution.py:176
  7.0 13.1 %collective-permute-start = (bf16[256,512]{1,0:T(8,128)(2,1)}, bf16[256,512]{1,0:T(8,128)(2,1)S(1)}, u32[]{:S(2)}, u32[]{:S(2)}) collective-permute-start(bf16[256,512]{1,0:T(8,128)(2,1)} %refs_0_.1), channel_id=1, source_target_pairs={{0,1},{1,0},{2,3},{3,2},{4,5},{5,4},{6,7},{7,6},{8,9},{9,8},{10,11... | collective-permute-start | bytes 786440 | tf_op jit(solution)/shard_map/ppermute | solution.py:176
  8.6 12.1 %collective-permute-start.3 = (bf16[256,512]{1,0:T(8,128)(2,1)}, bf16[256,512]{1,0:T(8,128)(2,1)S(1)}, u32[]{:S(2)}, u32[]{:S(2)}) collective-permute-start(bf16[256,512]{1,0:T(8,128)(2,1)} %refs_0_.1), channel_id=1, source_target_pairs={{0,4},{4,0},{8,12},{12,8},{16,20},{20,16},{24,28},{28,24},{1,5},{5... | collective-permute-start | bytes 786440 | tf_op jit(solution)/shard_map/ppermute | solution.py:173
  18.8 12.4 %collective-permute-start.2 = (bf16[256,512]{1,0:T(8,128)(2,1)S(1)}, bf16[256,512]{1,0:T(8,128)(2,1)S(1)}, u32[]{:S(2)}, u32[]{:S(2)}) collective-permute-start(bf16[256,512]{1,0:T(8,128)(2,1)S(1)} %collective-permute-done.1.refs_0_.refs_2_.refs_5_), channel_id=1, source_target_pairs={{0,1},{1,0},{2,3},{3,2},{4,5},{5,4},{6,7},{7,6},{8,9},{9,8},{10,11... | collective-permute-start | bytes 786440 | tf_op jit(solution)/shard_map/ppermute | solution.py:176
  20.1 17.1 %copy-start.3 = (s32[2,16,2]{1,2,0:T(2,128)S(1)}, s32[2,16,2]{1,2,0:T(2,128)}, u32[]{:S(2)}) copy-start(s32[2,16,2]{1,2,0:T(2,128)} %param.6) | copy-start | bytes 772
  20.1 17.1 %copy-start.4 = (s32[256]{0:T(256)S(1)}, s32[256]{0:T(256)}, u32[]{:S(2)}) copy-start(s32[256]{0:T(256)} %param.7) | copy-start | bytes 3076
  20.2 7.4 %collective-permute-start.11 = (s32[2,2,16]{2,1,0:T(2,128)S(1)}, s32[2,2,16]{2,1,0:T(2,128)S(1)}, u32[]{:S(2)}, u32[]{:S(2)}) collective-permute-start(s32[2,2,16]{2,1,0:T(2,128)S(1)} %shard_map.46), channel_id=1, source_target_pairs={{0,24},{4,28},{8,16},{12,20},{16,8},{20,12},{24,0},{28,4},{1,25},{... | collective-permute-start | bytes 776 | tf_op jit(solution)/shard_map/ppermute | solution.py:173
  20.7 8.6 %collective-permute-start.10 = (s32[2,2,16]{2,1,0:T(2,128)S(1)}, s32[2,2,16]{2,1,0:T(2,128)S(1)}, u32[]{:S(2)}, u32[]{:S(2)}) collective-permute-start(s32[2,2,16]{2,1,0:T(2,128)S(1)} %shard_map.46), channel_id=1, source_target_pairs={{0,16},{4,20},{8,24},{12,28},{16,0},{20,4},{24,8},{28,12},{1,17},{... | collective-permute-start | bytes 776 | tf_op jit(solution)/shard_map/ppermute | solution.py:173
  27.6 3.6 %collective-permute-start.9 = (s32[2,2,16]{2,1,0:T(2,128)S(1)}, s32[2,2,16]{2,1,0:T(2,128)S(1)}, u32[]{:S(2)}, u32[]{:S(2)}) collective-permute-start(s32[2,2,16]{2,1,0:T(2,128)S(1)} %shard_map.46), channel_id=1, source_target_pairs={{0,8},{4,12},{8,0},{12,4},{16,24},{20,28},{24,16},{28,20},{1,9},{5... | collective-permute-start | bytes 776 | tf_op jit(solution)/shard_map/ppermute | solution.py:173
  29.3 2.4 %collective-permute-start.5 = (bf16[256,512]{1,0:T(8,128)(2,1)S(1)}, bf16[256,512]{1,0:T(8,128)(2,1)S(1)}, u32[]{:S(2)}, u32[]{:S(2)}) collective-permute-start(bf16[256,512]{1,0:T(8,128)(2,1)S(1)} %collective-permute-done.1.refs_0_.refs_2_.refs_5_), channel_id=1, source_target_pairs={{0,4},{4,0},{8,12},{12,8},{16,20},{20,16},{24,28},{28,24},{1,5},{5... | collective-permute-start | bytes 786440 | tf_op jit(solution)/shard_map/ppermute | solution.py:173
  31.2 1.5 %collective-permute-start.4 = (bf16[256,512]{1,0:T(8,128)(2,1)S(1)}, bf16[256,512]{1,0:T(8,128)(2,1)S(1)}, u32[]{:S(2)}, u32[]{:S(2)}) collective-permute-start(bf16[256,512]{1,0:T(8,128)(2,1)S(1)} %collective-permute-done.refs_1_.refs_4_), channel_id=1, source_target_pairs={{0,4},{4,0},{8,12},{12,8},{16,20},{20,16},{24,28},{28,24},{1,5},{5... | collective-permute-start | bytes 786440 | tf_op jit(solution)/shard_map/ppermute | solution.py:173
  31.2 1.9 %collective-permute-start.6 = (bf16[256,512]{1,0:T(8,128)(2,1)S(1)}, bf16[256,512]{1,0:T(8,128)(2,1)S(1)}, u32[]{:S(2)}, u32[]{:S(2)}) collective-permute-start(bf16[256,512]{1,0:T(8,128)(2,1)S(1)} %collective-permute-done.2.refs_3_.refs_6_), channel_id=1, source_target_pairs={{0,4},{4,0},{8,12},{12,8},{16,20},{20,16},{24,28},{28,24},{1,5},{5... | collective-permute-start | bytes 786440 | tf_op jit(solution)/shard_map/ppermute | solution.py:173
  33.1 11.4 %collective-permute-start.12 = (bf16[1024,128]{1,0:T(8,128)(2,1)S(1)}, bf16[1024,128]{1,0:T(8,128)(2,1)S(1)}, u32[]{:S(2)}, u32[]{:S(2)}) collective-permute-start(bf16[1024,128]{1,0:T(8,128)(2,1)S(1)} %get-tuple-element.28), channel_id=1, source_target_pairs={{0,16},{4,20},{8,24},{12,28},{16,0},{20,4},{24,8},{28,12},{1,17},{... | collective-permute-start | bytes 786440 | tf_op jit(solution)/shard_map/ppermute | solution.py:173
  34.9 9.6 %collective-permute-start.13 = (bf16[1024,128]{1,0:T(8,128)(2,1)S(1)}, bf16[1024,128]{1,0:T(8,128)(2,1)S(1)}, u32[]{:S(2)}, u32[]{:S(2)}) collective-permute-start(bf16[1024,128]{1,0:T(8,128)(2,1)S(1)} %get-tuple-element.29), channel_id=1, source_target_pairs={{0,8},{4,12},{8,0},{12,4},{16,24},{20,28},{24,16},{28,20},{1,9},{5... | collective-permute-start | bytes 786440 | tf_op jit(solution)/shard_map/ppermute | solution.py:173
  36.4 10.7 %collective-permute-start.14 = (bf16[1024,128]{1,0:T(8,128)(2,1)S(1)}, bf16[1024,128]{1,0:T(8,128)(2,1)S(1)}, u32[]{:S(2)}, u32[]{:S(2)}) collective-permute-start(bf16[1024,128]{1,0:T(8,128)(2,1)S(1)} %get-tuple-element.32), channel_id=1, source_target_pairs={{0,16},{4,20},{8,24},{12,28},{16,0},{20,4},{24,8},{28,12},{1,17},{... | collective-permute-start | bytes 786440 | tf_op jit(solution)/shard_map/ppermute | solution.py:173
  36.9 11.7 %collective-permute-start.15 = (bf16[1024,128]{1,0:T(8,128)(2,1)S(1)}, bf16[1024,128]{1,0:T(8,128)(2,1)S(1)}, u32[]{:S(2)}, u32[]{:S(2)}) collective-permute-start(bf16[1024,128]{1,0:T(8,128)(2,1)S(1)} %get-tuple-element.33), channel_id=1, source_target_pairs={{0,8},{4,12},{8,0},{12,4},{16,24},{20,28},{24,16},{28,20},{1,9},{5... | collective-permute-start | bytes 786440 | tf_op jit(solution)/shard_map/ppermute | solution.py:173
  50.3 1.6 %collective-permute-start.18 = (bf16[2,2,256,128]{3,2,1,0:T(8,128)(2,1)S(1)}, bf16[2,2,256,128]{3,2,1,0:T(8,128)(2,1)S(1)}, u32[]{:S(2)}, u32[]{:S(2)}) collective-permute-start(bf16[2,2,256,128]{3,2,1,0:T(8,128)(2,1)S(1)} %get-tuple-element.41), channel_id=1, source_target_pairs={{0,4},{4,0},{8,12},{12,8},{16,20},{20,16},{24,28},{28,24},{1,5},{5... | collective-permute-start | bytes 786440 | tf_op jit(solution)/shard_map/ppermute | solution.py:173
  50.7 5.3 %collective-permute-start.16 = (bf16[2,2,256,128]{3,2,1,0:T(8,128)(2,1)S(1)}, bf16[2,2,256,128]{3,2,1,0:T(8,128)(2,1)S(1)}, u32[]{:S(2)}, u32[]{:S(2)}) collective-permute-start(bf16[2,2,256,128]{3,2,1,0:T(8,128)(2,1)S(1)} %get-tuple-element.37), channel_id=1, source_target_pairs={{0,4},{4,0},{8,12},{12,8},{16,20},{20,16},{24,28},{28,24},{1,5},{5... | collective-permute-start | bytes 786440 | tf_op jit(solution)/shard_map/ppermute | solution.py:173
  52.0 13.0 %collective-permute-start.19 = (bf16[2,256,128]{2,1,0:T(8,128)(2,1)S(1)}, bf16[2,256,128]{2,1,0:T(8,128)(2,1)S(1)}, u32[]{:S(2)}, u32[]{:S(2)}) collective-permute-start(bf16[2,256,128]{2,1,0:T(8,128)(2,1)S(1)} %get-tuple-element.42), channel_id=1, source_target_pairs={{0,2},{1,3},{2,0},{3,1},{4,6},{5,7},{6,4},{7,5},{8,10},{9,11},{10,... | collective-permute-start | bytes 393224 | tf_op jit(solution)/shard_map/ppermute | solution.py:176
  54.6 10.3 %collective-permute-start.20 = (bf16[2,256,128]{2,1,0:T(8,128)(2,1)S(1)}, bf16[2,256,128]{2,1,0:T(8,128)(2,1)S(1)}, u32[]{:S(2)}, u32[]{:S(2)}) collective-permute-start(bf16[2,256,128]{2,1,0:T(8,128)(2,1)S(1)} %get-tuple-element.43), channel_id=1, source_target_pairs={{0,3},{1,2},{2,1},{3,0},{4,7},{5,6},{6,5},{7,4},{8,11},{9,10},{10,... | collective-permute-start | bytes 393224 | tf_op jit(solution)/shard_map/ppermute | solution.py:176
  56.1 9.5 %collective-permute-start.17 = (bf16[2,256,128]{2,1,0:T(8,128)(2,1)S(1)}, bf16[2,256,128]{2,1,0:T(8,128)(2,1)S(1)}, u32[]{:S(2)}, u32[]{:S(2)}) collective-permute-start(bf16[2,256,128]{2,1,0:T(8,128)(2,1)S(1)} %get-tuple-element.39), channel_id=1, source_target_pairs={{0,1},{1,0},{2,3},{3,2},{4,5},{5,4},{6,7},{7,6},{8,9},{9,8},{10,11... | collective-permute-start | bytes 393224 | tf_op jit(solution)/shard_map/ppermute | solution.py:176
  65.6 1.4 %collective-permute-start.21 = (bf16[2,256,128]{2,1,0:T(8,128)(2,1)S(1)}, bf16[2,256,128]{2,1,0:T(8,128)(2,1)S(1)}, u32[]{:S(2)}, u32[]{:S(2)}) collective-permute-start(bf16[2,256,128]{2,1,0:T(8,128)(2,1)S(1)} %shard_map.55.own_ref), channel_id=1, source_target_pairs={{0,4},{4,0},{8,12},{12,8},{16,20},{20,16},{24,28},{28,24},{1,5},{5... | collective-permute-start | bytes 393224 | tf_op jit(solution)/shard_map/ppermute | solution.py:173
  (3 other events, 34.9 us)

commit v16 on v13

--- a/solution.py
+++ b/solution.py
@@ -138,24 +138,33 @@
     refs[-1][...] = total.astype(BF16)
 
 
-def finish_kernel(own_ref, other_ref, hot_ref, out_ref, made_ref, sems):
-    half = own_ref.shape[0]
+def order_half(hot, half_ref, place):
     upper = lax.axis_index("pair") % 2 == 1
-    hot = hot_ref[...]
     same = (iota((TILE, TILE), 0) == iota((TILE, TILE), 1)).astype(F32)
     swap = jnp.where(upper, swap_matrix().astype(F32), same).astype(BF16)
-    copies = []
-    for which in range(2):
-        for k in range(half):
-            values = jnp.where(upper == (which == 1), own_ref[k], other_ref[k])
-            values = jnp.dot(values, swap, preferred_element_type=F32).astype(BF16)
-            block = which * half + k
-            columns = pl.ds(block * TILE, TILE)
-            made_ref[:, columns] = jnp.dot(hot, values, preferred_element_type=F32).astype(BF16)
-            copies.append(pltpu.make_async_copy(made_ref.at[:, columns], out_ref.at[:, columns], sems.at[block]))
-            copies[-1].start()
-    for copy in copies:
-        copy.wait()
+    for k in range(half_ref.shape[0]):
+        values = jnp.dot(half_ref[k], swap, preferred_element_type=F32).astype(BF16)
+        place(k, jnp.dot(hot, values, preferred_element_type=F32).astype(BF16))
+
+
+def own_half_kernel(half_ref, hot_ref, out_ref):
+    def place(k, values):
+        out_ref[k] = values
+
+    order_half(hot_ref[...], half_ref, place)
+
+
+def finish_kernel(ordered_ref, other_ref, hot_ref, out_ref):
+    half = other_ref.shape[0]
+    upper = lax.axis_index("pair") % 2 == 1
+
+    def place(k, values):
+        ordered = ordered_ref[k]
+        low, high = slice(k * TILE, (k + 1) * TILE), slice((half + k) * TILE, (half + k + 1) * TILE)
+        out_ref[:, low] = jnp.where(upper, values, ordered)
+        out_ref[:, high] = jnp.where(upper, ordered, values)
+
+    order_half(hot_ref[...], other_ref, place)
 
 
 def local(amplitudes, integrals, tile_blocks, mirror_row):
@@ -244,14 +253,10 @@
         joined = call(join_kernel, [one] * len(shifts), [VMEM, VMEM], megabytes=4)(keep, across(send, 1))
         parts |= {shift: along(part, shift) if shift else part for shift, part in zip(shifts, joined)}
     total = call(total_kernel, one, [VMEM] * n_vir, megabytes=4)(*[parts[shift] for shift in range(n_vir)])
+    ordered = call(own_half_kernel, one, [VMEM, VMEM], megabytes=4)(total, last_hot)
     return call(
-        finish_kernel,
-        jax.ShapeDtypeStruct((rows, width), BF16),
-        [VMEM] * 3,
-        [pltpu.VMEM((rows, width), BF16), pltpu.SemaphoreType.DMA((per,))],
-        megabytes=8,
-        out_specs=pl.BlockSpec(memory_space=pl.ANY),
-    )(total, across(total, 1), last_hot)
+        finish_kernel, jax.ShapeDtypeStruct((rows, width), BF16), [VMEM] * 3, megabytes=8
+    )(ordered, across(total, 1), last_hot)
 
 
 def solution(mesh):

time: 64.8 us -> 64.6 us (level)
  transfers between devices with their start and end apart: 19 -> 19, of which waited for: 10 -> 10; matrix products, arithmetic and copies ran while one was open for 0% -> 0% of each run, Pallas kernels for 14% -> 15%
where the time goes in v16:
time: 64.6 us; the launch traced here: 64.3 us
  waiting for transfers between devices  29.7 us (46%)
  starting transfers between devices  19.8 us (31%)
  Pallas kernels  12.4 us (19%)
  other arithmetic  2.04 us (3%)
    ppermute x6, waiting for transfers between devices, along(): return lax.ppermute(array, 'vir', [(i, i ^ bits) for i in range(n_vir)])  25 us
    ppermute x13, starting transfers between devices, across(): return lax.ppermute(array, 'pair', [(i, i ^ bits) for i in range(n_pair)])  9.92 us
    ppermute x6, starting transfers between devices, along(): return lax.ppermute(array, 'vir', [(i, i ^ bits) for i in range(n_vir)])  9.91 us
    pallas_call x1, Pallas kernels, local(): call(functools.partial(first_kernel, n_vir, len(early)), [jax.ShapeDtypeS...  7.35 us
    ppermute x13, waiting for transfers between devices, across(): return lax.ppermute(array, 'pair', [(i, i ^ bits) for i in range(n_pair)])  4.65 us
    pallas_call x2, Pallas kernels, local(): call(functools.partial(more_kernel, starts), [sums, sums], [VMEM] * (3 +...  2.74 us
    concatenate x1, other arithmetic, local(): jnp.concatenate([ids, integrals.reshape(slabs, length, TILE)], axis=1)  1.29 us
  transfers between devices with their start and end apart: 19, of which 10 were waited for; matrix products, arithmetic and copies ran while one was open for 0% of the time, Pallas kernels for 15%

profile of v16, /device:TPU:0, one launch (start us, length us, event | category | flops | bytes accessed | tf_op | source)
XLA Modules:
  0.0 64.3 jit_solution(9954419801796063842)
XLA Ops:
  0.0 0.7 %bitcast_convert_fusion = bf16[2,2,16]{2,1,0:T(2,128)(2,1)S(1)} fusion(s32[2,16,2]{1,2,0:T(2,128)} %param.6), kind=kLoop, calls=%fused_computation.7 | loop fusion | flops 64 | bytes 384 | tf_op jit(solution)/shard_map/convert_element_type | solution.py:185
  0.7 1.3 %pad_maximum_fusion.refs_8_ = bf16[2,2064,128]{2,1,0:T(8,128)(2,1)S(1)} fusion(bf16[2,2048,128]{2,1,0:T(8,128)(2,1)} %bitcast.29, bf16[2,16,128]{2,1,0:T(8,128)(2,1)S(1)} %broadcast_in_dim.20), kind=kLoop, calls=%fused_computation | loop fusion | flops 2113536 | bytes 2113536 | tf_op jit(solution)/shard_map/concatenate | solution.py:188
  2.1 3.0 %collective-permute-start.7 = (bf16[2,2064,128]{2,1,0:T(8,128)(2,1)S(1)}, bf16[2,2064,128]{2,1,0:T(8,128)(2,1)S(1)}, u32[]{:S(2)}, u32[]{:S(2)}) collective-permute-start(bf16[2,2064,128]{2,1,0:T(8,128)(2,1)S(1)} %pad_maximum_fusion.refs_8_), channel_id=1, source_target_pairs={{0,8},{4,12},{8,0},{12,4},{16,24},{20,28},{24,16},{28,20},{1,9},{5... | collective-permute-start | bytes 3170312 | tf_op jit(solution)/shard_map/ppermute | solution.py:180
  5.1 1.5 %collective-permute-start.8 = (bf16[2,2064,128]{2,1,0:T(8,128)(2,1)S(1)}, bf16[2,2064,128]{2,1,0:T(8,128)(2,1)S(1)}, u32[]{:S(2)}, u32[]{:S(2)}) collective-permute-start(bf16[2,2064,128]{2,1,0:T(8,128)(2,1)S(1)} %pad_maximum_fusion.refs_8_), channel_id=1, source_target_pairs={{0,16},{4,20},{8,24},{12,28},{16,0},{20,4},{24,8},{28,12},{1,17},{... | collective-permute-start | bytes 3170312 | tf_op jit(solution)/shard_map/ppermute | solution.py:180
  6.6 2.6 %collective-permute-start.1 = (bf16[256,512]{1,0:T(8,128)(2,1)S(1)}, bf16[256,512]{1,0:T(8,128)(2,1)S(1)}, u32[]{:S(2)}, u32[]{:S(2)}) collective-permute-start(bf16[256,512]{1,0:T(8,128)(2,1)S(1)} %copy-done), channel_id=1, source_target_pairs={{0,2},{1,3},{2,0},{3,1},{4,6},{5,7},{6,4},{7,5},{8,10},{9,11},{10,... | collective-permute-start | bytes 786440 | tf_op jit(solution)/shard_map/ppermute | solution.py:183
  9.2 1.6 %collective-permute-start = (bf16[256,512]{1,0:T(8,128)(2,1)S(1)}, bf16[256,512]{1,0:T(8,128)(2,1)S(1)}, u32[]{:S(2)}, u32[]{:S(2)}) collective-permute-start(bf16[256,512]{1,0:T(8,128)(2,1)S(1)} %copy-done), channel_id=1, source_target_pairs={{0,1},{1,0},{2,3},{3,2},{4,5},{5,4},{6,7},{7,6},{8,9},{9,8},{10,11... | collective-permute-start | bytes 786440 | tf_op jit(solution)/shard_map/ppermute | solution.py:183
  10.8 9.9 %collective-permute-done.1.refs_2_.refs_5_ = bf16[256,512]{1,0:T(8,128)(2,1)S(1)} collective-permute-done((bf16[256,512]{1,0:T(8,128)(2,1)S(1)}, bf16[256,512]{1,0:T(8,128)(2,1)S(1)}, u32[]{:S(2)}, u32[]{:S(2)}) %collective-permute-start.1) | collective-permute-done | bytes 262176 | tf_op jit(solution)/shard_map/ppermute | solution.py:183
  20.7 0.6 collective-permute-start.2
  21.8 6.0 %collective-permute-done.2.refs_3_.refs_6_ = bf16[256,512]{1,0:T(8,128)(2,1)S(1)} collective-permute-done((bf16[256,512]{1,0:T(8,128)(2,1)S(1)}, bf16[256,512]{1,0:T(8,128)(2,1)S(1)}, u32[]{:S(2)}, u32[]{:S(2)}) %collective-permute-start.2) | collective-permute-done | bytes 262176 | tf_op jit(solution)/shard_map/ppermute | solution.py:183
  27.8 1.5 %collective-permute-done.6.refs_7_.refs_3_ = bf16[256,512]{1,0:T(8,128)(2,1)S(1)} collective-permute-done((bf16[256,512]{1,0:T(8,128)(2,1)S(1)}, bf16[256,512]{1,0:T(8,128)(2,1)S(1)}, u32[]{:S(2)}, u32[]{:S(2)}) %collective-permute-start.6) | collective-permute-done | bytes 262176 | tf_op jit(solution)/shard_map/ppermute | solution.py:180
  29.9 1.6 %collective-permute-start.9 = (bf16[1040,128]{1,0:T(8,128)(2,1)S(1)}, bf16[1040,128]{1,0:T(8,128)(2,1)S(1)}, u32[]{:S(2)}, u32[]{:S(2)}) collective-permute-start(bf16[1040,128]{1,0:T(8,128)(2,1)S(1)} %get-tuple-element.28), channel_id=1, source_target_pairs={{0,16},{4,20},{8,24},{12,28},{16,0},{20,4},{24,8},{28,12},{1,17},{... | collective-permute-start | bytes 798728 | tf_op jit(solution)/shard_map/ppermute | solution.py:180
  31.7 0.6 collective-permute-start.10
  32.6 1.7 %collective-permute-start.12 = (bf16[1024,128]{1,0:T(8,128)(2,1)S(1)}, bf16[1024,128]{1,0:T(8,128)(2,1)S(1)}, u32[]{:S(2)}, u32[]{:S(2)}) collective-permute-start(bf16[1024,128]{1,0:T(8,128)(2,1)S(1)} %get-tuple-element.33), channel_id=1, source_target_pairs={{0,8},{4,12},{8,0},{12,4},{16,24},{20,28},{24,16},{28,20},{1,9},{5... | collective-permute-start | bytes 786440 | tf_op jit(solution)/shard_map/ppermute | solution.py:180
  34.3 7.3 %shard_map.46 = (bf16[16,512,128]{2,1,0:T(8,128)(2,1)S(1)}, bf16[256,256]{1,0:T(8,128)(2,1)S(1)}, f32[16,256,128]{2,1,0:T(8,128)S(1)}, f32[16,256,128]{2,1,0:T(8,128)S(1)}) custom-call(bf16[256,512]{1,0:T(8,128)(2,1)S(1)} %copy-done, bf16[256,512]{1,0:T(8,128)(2,1)S(1)} %collective-permute-done.refs_1_.refs_4_, ...), custom_call_target="tpu_custom_call" | custom-call | tf_op jit(solution)/shard_map/pallas_call | solution.py:221
  41.7 1.4 %shard_map.48 = (f32[16,256,128]{2,1,0:T(8,128)S(1)}, f32[16,256,128]{2,1,0:T(8,128)S(1)}) custom-call(bf16[16,512,128]{2,1,0:T(8,128)(2,1)S(1)} %get-tuple-element.25.refs_0_, f32[16,256,128]{2,1,0:T(8,128)S(1)} %get-tuple-element.26.refs_1_, f32[16,256,128]{2,1,0:T(8,128)S(1)} %get-tuple-element.27.refs_2_, ...), custom_call_target="tpu_custom_call", output_to_operand_aliasing={{0}: (1, {}), {1}: (2, {})} | custom-call | tf_op jit(solution)/shard_map/pallas_call | solution.py:238
  44.0 1.4 %shard_map.49 = (f32[16,256,128]{2,1,0:T(8,128)S(1)}, f32[16,256,128]{2,1,0:T(8,128)S(1)}) custom-call(bf16[16,512,128]{2,1,0:T(8,128)(2,1)S(1)} %get-tuple-element.25.refs_0_, f32[16,256,128]{2,1,0:T(8,128)S(1)} %get-tuple-element.30.refs_1_, f32[16,256,128]{2,1,0:T(8,128)S(1)} %get-tuple-element.31.refs_2_, ...), custom_call_target="tpu_custom_call", output_to_operand_aliasing={{0}: (1, {}), {1}: (2, {})} | custom-call | tf_op jit(solution)/shard_map/pallas_call | solution.py:238
  46.1 0.6 collective-permute-start.13
  46.6 0.7 %collective-permute-done.15.come_ref = bf16[2,2,256,128]{3,2,1,0:T(8,128)(2,1)S(1)} collective-permute-done((bf16[2,2,256,128]{3,2,1,0:T(8,128)(2,1)S(1)}, bf16[2,2,256,128]{3,2,1,0:T(8,128)(2,1)S(1)}, u32[]{:S(2)}, u32[]{:S(2)}) %collective-permute-start.15) | collective-permute-done | bytes 262176 | tf_op jit(solution)/shard_map/ppermute | solution.py:180
  47.4 3.3 %collective-permute-start.16 = (bf16[2,256,128]{2,1,0:T(8,128)(2,1)S(1)}, bf16[2,256,128]{2,1,0:T(8,128)(2,1)S(1)}, u32[]{:S(2)}, u32[]{:S(2)}) collective-permute-start(bf16[2,256,128]{2,1,0:T(8,128)(2,1)S(1)} %get-tuple-element.42), channel_id=1, source_target_pairs={{0,2},{1,3},{2,0},{3,1},{4,6},{5,7},{6,4},{7,5},{8,10},{9,11},{10,... | collective-permute-start | bytes 393224 | tf_op jit(solution)/shard_map/ppermute | solution.py:183
  50.7 1.3 %collective-permute-start.17 = (bf16[2,256,128]{2,1,0:T(8,128)(2,1)S(1)}, bf16[2,256,128]{2,1,0:T(8,128)(2,1)S(1)}, u32[]{:S(2)}, u32[]{:S(2)}) collective-permute-start(bf16[2,256,128]{2,1,0:T(8,128)(2,1)S(1)} %get-tuple-element.43), channel_id=1, source_target_pairs={{0,3},{1,2},{2,1},{3,0},{4,7},{5,6},{6,5},{7,4},{8,11},{9,10},{10,... | collective-permute-start | bytes 393224 | tf_op jit(solution)/shard_map/ppermute | solution.py:183
  52.6 8.0 %collective-permute-done.16.refs_2_ = bf16[2,256,128]{2,1,0:T(8,128)(2,1)S(1)} collective-permute-done((bf16[2,256,128]{2,1,0:T(8,128)(2,1)S(1)}, bf16[2,256,128]{2,1,0:T(8,128)(2,1)S(1)}, u32[]{:S(2)}, u32[]{:S(2)}) %collective-permute-start.16) | collective-permute-done | bytes 131104 | tf_op jit(solution)/shard_map/ppermute | solution.py:183
  60.7 1.0 %collective-permute-done.14.refs_1_ = bf16[2,256,128]{2,1,0:T(8,128)(2,1)S(1)} collective-permute-done((bf16[2,256,128]{2,1,0:T(8,128)(2,1)S(1)}, bf16[2,256,128]{2,1,0:T(8,128)(2,1)S(1)}, u32[]{:S(2)}, u32[]{:S(2)}) %collective-permute-start.14) | collective-permute-done | bytes 131104 | tf_op jit(solution)/shard_map/ppermute | solution.py:183
  62.2 0.9 %collective-permute-done.18.other_ref = bf16[2,256,128]{2,1,0:T(8,128)(2,1)S(1)} collective-permute-done((bf16[2,256,128]{2,1,0:T(8,128)(2,1)S(1)}, bf16[2,256,128]{2,1,0:T(8,128)(2,1)S(1)}, u32[]{:S(2)}, u32[]{:S(2)}) %collective-permute-start.18) | collective-permute-done | bytes 131104 | tf_op jit(solution)/shard_map/ppermute | solution.py:180
  63.2 1.1 %shard_map.56 = bf16[256,512]{1,0:T(8,128)(2,1)} custom-call(bf16[2,256,128]{2,1,0:T(8,128)(2,1)S(1)} %shard_map.55.ordered_ref, bf16[2,256,128]{2,1,0:T(8,128)(2,1)S(1)} %collective-permute-done.18.other_ref, bf16[256,256]{1,0:T(8,128)(2,1)S(1)} %get-tuple-element.44.hot_ref), custom_call_target="tpu_custom_call" | custom-call | tf_op jit(solution)/shard_map/pallas_call | solution.py:257
  (43 shorter events, 4.4 us)
Async XLA Ops:
  0.0 6.6 %copy-start = (bf16[256,512]{1,0:T(8,128)(2,1)S(1)}, bf16[256,512]{1,0:T(8,128)(2,1)}, u32[]{:S(2)}) copy-start(bf16[256,512]{1,0:T(8,128)(2,1)} %refs_0_.1) | copy-start | bytes 786436
  2.0 32.2 %copy-start.1 = (s32[2,16,2]{1,2,0:T(2,128)S(1)}, s32[2,16,2]{1,2,0:T(2,128)}, u32[]{:S(2)}) copy-start(s32[2,16,2]{1,2,0:T(2,128)} %param.6) | copy-start | bytes 772
  2.1 32.2 %copy-start.2 = (s32[256]{0:T(256)S(1)}, s32[256]{0:T(256)}, u32[]{:S(2)}) copy-start(s32[256]{0:T(256)} %param.7) | copy-start | bytes 3076
  2.1 27.3 %collective-permute-start.7 = (bf16[2,2064,128]{2,1,0:T(8,128)(2,1)S(1)}, bf16[2,2064,128]{2,1,0:T(8,128)(2,1)S(1)}, u32[]{:S(2)}, u32[]{:S(2)}) collective-permute-start(bf16[2,2064,128]{2,1,0:T(8,128)(2,1)S(1)} %pad_maximum_fusion.refs_8_), channel_id=1, source_target_pairs={{0,8},{4,12},{8,0},{12,4},{16,24},{20,28},{24,16},{28,20},{1,9},{5... | collective-permute-start | bytes 3170312 | tf_op jit(solution)/shard_map/ppermute | solution.py:180
  5.1 24.8 %collective-permute-start.8 = (bf16[2,2064,128]{2,1,0:T(8,128)(2,1)S(1)}, bf16[2,2064,128]{2,1,0:T(8,128)(2,1)S(1)}, u32[]{:S(2)}, u32[]{:S(2)}) collective-permute-start(bf16[2,2064,128]{2,1,0:T(8,128)(2,1)S(1)} %pad_maximum_fusion.refs_8_), channel_id=1, source_target_pairs={{0,16},{4,20},{8,24},{12,28},{16,0},{20,4},{24,8},{28,12},{1,17},{... | collective-permute-start | bytes 3170312 | tf_op jit(solution)/shard_map/ppermute | solution.py:180
  6.6 14.1 %collective-permute-start.1 = (bf16[256,512]{1,0:T(8,128)(2,1)S(1)}, bf16[256,512]{1,0:T(8,128)(2,1)S(1)}, u32[]{:S(2)}, u32[]{:S(2)}) collective-permute-start(bf16[256,512]{1,0:T(8,128)(2,1)S(1)} %copy-done), channel_id=1, source_target_pairs={{0,2},{1,3},{2,0},{3,1},{4,6},{5,7},{6,4},{7,5},{8,10},{9,11},{10,... | collective-permute-start | bytes 786440 | tf_op jit(solution)/shard_map/ppermute | solution.py:183
  9.2 12.1 %collective-permute-start = (bf16[256,512]{1,0:T(8,128)(2,1)S(1)}, bf16[256,512]{1,0:T(8,128)(2,1)S(1)}, u32[]{:S(2)}, u32[]{:S(2)}) collective-permute-start(bf16[256,512]{1,0:T(8,128)(2,1)S(1)} %copy-done), channel_id=1, source_target_pairs={{0,1},{1,0},{2,3},{3,2},{4,5},{5,4},{6,7},{7,6},{8,9},{9,8},{10,11... | collective-permute-start | bytes 786440 | tf_op jit(solution)/shard_map/ppermute | solution.py:183
  10.8 10.5 %collective-permute-start.3 = (bf16[256,512]{1,0:T(8,128)(2,1)S(1)}, bf16[256,512]{1,0:T(8,128)(2,1)S(1)}, u32[]{:S(2)}, u32[]{:S(2)}) collective-permute-start(bf16[256,512]{1,0:T(8,128)(2,1)S(1)} %copy-done), channel_id=1, source_target_pairs={{0,4},{4,0},{8,12},{12,8},{16,20},{20,16},{24,28},{28,24},{1,5},{5... | collective-permute-start | bytes 786440 | tf_op jit(solution)/shard_map/ppermute | solution.py:180
  20.7 7.1 %collective-permute-start.2 = (bf16[256,512]{1,0:T(8,128)(2,1)S(1)}, bf16[256,512]{1,0:T(8,128)(2,1)S(1)}, u32[]{:S(2)}, u32[]{:S(2)}) collective-permute-start(bf16[256,512]{1,0:T(8,128)(2,1)S(1)} %collective-permute-done.1.refs_2_.refs_5_), channel_id=1, source_target_pairs={{0,1},{1,0},{2,3},{3,2},{4,5},{5,4},{6,7},{7,6},{8,9},{9,8},{10,11... | collective-permute-start | bytes 786440 | tf_op jit(solution)/shard_map/ppermute | solution.py:183
  21.3 6.5 %collective-permute-start.5 = (bf16[256,512]{1,0:T(8,128)(2,1)S(1)}, bf16[256,512]{1,0:T(8,128)(2,1)S(1)}, u32[]{:S(2)}, u32[]{:S(2)}) collective-permute-start(bf16[256,512]{1,0:T(8,128)(2,1)S(1)} %collective-permute-done.1.refs_2_.refs_5_), channel_id=1, source_target_pairs={{0,4},{4,0},{8,12},{12,8},{16,20},{20,16},{24,28},{28,24},{1,5},{5... | collective-permute-start | bytes 786440 | tf_op jit(solution)/shard_map/ppermute | solution.py:180
  21.3 6.5 %collective-permute-start.4 = (bf16[256,512]{1,0:T(8,128)(2,1)S(1)}, bf16[256,512]{1,0:T(8,128)(2,1)S(1)}, u32[]{:S(2)}, u32[]{:S(2)}) collective-permute-start(bf16[256,512]{1,0:T(8,128)(2,1)S(1)} %collective-permute-done.refs_1_.refs_4_), channel_id=1, source_target_pairs={{0,4},{4,0},{8,12},{12,8},{16,20},{20,16},{24,28},{28,24},{1,5},{5... | collective-permute-start | bytes 786440 | tf_op jit(solution)/shard_map/ppermute | solution.py:180
  27.8 1.5 %collective-permute-start.6 = (bf16[256,512]{1,0:T(8,128)(2,1)S(1)}, bf16[256,512]{1,0:T(8,128)(2,1)S(1)}, u32[]{:S(2)}, u32[]{:S(2)}) collective-permute-start(bf16[256,512]{1,0:T(8,128)(2,1)S(1)} %collective-permute-done.2.refs_3_.refs_6_), channel_id=1, source_target_pairs={{0,4},{4,0},{8,12},{12,8},{16,20},{20,16},{24,28},{28,24},{1,5},{5... | collective-permute-start | bytes 786440 | tf_op jit(solution)/shard_map/ppermute | solution.py:180
  29.9 11.7 %collective-permute-start.9 = (bf16[1040,128]{1,0:T(8,128)(2,1)S(1)}, bf16[1040,128]{1,0:T(8,128)(2,1)S(1)}, u32[]{:S(2)}, u32[]{:S(2)}) collective-permute-start(bf16[1040,128]{1,0:T(8,128)(2,1)S(1)} %get-tuple-element.28), channel_id=1, source_target_pairs={{0,16},{4,20},{8,24},{12,28},{16,0},{20,4},{24,8},{28,12},{1,17},{... | collective-permute-start | bytes 798728 | tf_op jit(solution)/shard_map/ppermute | solution.py:180
  31.7 10.0 %collective-permute-start.10 = (bf16[1040,128]{1,0:T(8,128)(2,1)S(1)}, bf16[1040,128]{1,0:T(8,128)(2,1)S(1)}, u32[]{:S(2)}, u32[]{:S(2)}) collective-permute-start(bf16[1040,128]{1,0:T(8,128)(2,1)S(1)} %get-tuple-element.29), channel_id=1, source_target_pairs={{0,8},{4,12},{8,0},{12,4},{16,24},{20,28},{24,16},{28,20},{1,9},{5... | collective-permute-start | bytes 798728 | tf_op jit(solution)/shard_map/ppermute | solution.py:180
  32.3 11.3 %collective-permute-start.11 = (bf16[1024,128]{1,0:T(8,128)(2,1)S(1)}, bf16[1024,128]{1,0:T(8,128)(2,1)S(1)}, u32[]{:S(2)}, u32[]{:S(2)}) collective-permute-start(bf16[1024,128]{1,0:T(8,128)(2,1)S(1)} %get-tuple-element.32), channel_id=1, source_target_pairs={{0,16},{4,20},{8,24},{12,28},{16,0},{20,4},{24,8},{28,12},{1,17},{... | collective-permute-start | bytes 786440 | tf_op jit(solution)/shard_map/ppermute | solution.py:180
  32.6 11.4 %collective-permute-start.12 = (bf16[1024,128]{1,0:T(8,128)(2,1)S(1)}, bf16[1024,128]{1,0:T(8,128)(2,1)S(1)}, u32[]{:S(2)}, u32[]{:S(2)}) collective-permute-start(bf16[1024,128]{1,0:T(8,128)(2,1)S(1)} %get-tuple-element.33), channel_id=1, source_target_pairs={{0,8},{4,12},{8,0},{12,4},{16,24},{20,28},{24,16},{28,20},{1,9},{5... | collective-permute-start | bytes 786440 | tf_op jit(solution)/shard_map/ppermute | solution.py:180
  45.7 1.6 %collective-permute-start.15 = (bf16[2,2,256,128]{3,2,1,0:T(8,128)(2,1)S(1)}, bf16[2,2,256,128]{3,2,1,0:T(8,128)(2,1)S(1)}, u32[]{:S(2)}, u32[]{:S(2)}) collective-permute-start(bf16[2,2,256,128]{3,2,1,0:T(8,128)(2,1)S(1)} %get-tuple-element.41), channel_id=1, source_target_pairs={{0,4},{4,0},{8,12},{12,8},{16,20},{20,16},{24,28},{28,24},{1,5},{5... | collective-permute-start | bytes 786440 | tf_op jit(solution)/shard_map/ppermute | solution.py:180
  46.1 5.9 %collective-permute-start.13 = (bf16[2,2,256,128]{3,2,1,0:T(8,128)(2,1)S(1)}, bf16[2,2,256,128]{3,2,1,0:T(8,128)(2,1)S(1)}, u32[]{:S(2)}, u32[]{:S(2)}) collective-permute-start(bf16[2,2,256,128]{3,2,1,0:T(8,128)(2,1)S(1)} %get-tuple-element.37), channel_id=1, source_target_pairs={{0,4},{4,0},{8,12},{12,8},{16,20},{20,16},{24,28},{28,24},{1,5},{5... | collective-permute-start | bytes 786440 | tf_op jit(solution)/shard_map/ppermute | solution.py:180
  47.4 13.3 %collective-permute-start.16 = (bf16[2,256,128]{2,1,0:T(8,128)(2,1)S(1)}, bf16[2,256,128]{2,1,0:T(8,128)(2,1)S(1)}, u32[]{:S(2)}, u32[]{:S(2)}) collective-permute-start(bf16[2,256,128]{2,1,0:T(8,128)(2,1)S(1)} %get-tuple-element.42), channel_id=1, source_target_pairs={{0,2},{1,3},{2,0},{3,1},{4,6},{5,7},{6,4},{7,5},{8,10},{9,11},{10,... | collective-permute-start | bytes 393224 | tf_op jit(solution)/shard_map/ppermute | solution.py:183
  50.7 9.9 %collective-permute-start.17 = (bf16[2,256,128]{2,1,0:T(8,128)(2,1)S(1)}, bf16[2,256,128]{2,1,0:T(8,128)(2,1)S(1)}, u32[]{:S(2)}, u32[]{:S(2)}) collective-permute-start(bf16[2,256,128]{2,1,0:T(8,128)(2,1)S(1)} %get-tuple-element.43), channel_id=1, source_target_pairs={{0,3},{1,2},{2,1},{3,0},{4,7},{5,6},{6,5},{7,4},{8,11},{9,10},{10,... | collective-permute-start | bytes 393224 | tf_op jit(solution)/shard_map/ppermute | solution.py:183
  52.0 9.6 %collective-permute-start.14 = (bf16[2,256,128]{2,1,0:T(8,128)(2,1)S(1)}, bf16[2,256,128]{2,1,0:T(8,128)(2,1)S(1)}, u32[]{:S(2)}, u32[]{:S(2)}) collective-permute-start(bf16[2,256,128]{2,1,0:T(8,128)(2,1)S(1)} %get-tuple-element.39), channel_id=1, source_target_pairs={{0,1},{1,0},{2,3},{3,2},{4,5},{5,4},{6,7},{7,6},{8,9},{9,8},{10,11... | collective-permute-start | bytes 393224 | tf_op jit(solution)/shard_map/ppermute | solution.py:183
  61.8 1.4 %collective-permute-start.18 = (bf16[2,256,128]{2,1,0:T(8,128)(2,1)S(1)}, bf16[2,256,128]{2,1,0:T(8,128)(2,1)S(1)}, u32[]{:S(2)}, u32[]{:S(2)}) collective-permute-start(bf16[2,256,128]{2,1,0:T(8,128)(2,1)S(1)} %shard_map.54.half_ref), channel_id=1, source_target_pairs={{0,4},{4,0},{8,12},{12,8},{16,20},{20,16},{24,28},{28,24},{1,5},{5... | collective-permute-start | bytes 393224 | tf_op jit(solution)/shard_map/ppermute | solution.py:180
